TPU v7x, 32 devices: a whole 2x2x4 slice. The times are simulated.
32 devices in a mesh: gx: 4 (over z), gy: 8 (over y, x, core).
Axes of the slice: x: 2, y: 2, z: 4, core: 2. Of those that a mesh axis runs over, the one named last changes fastest.
Arguments:
- queries: bfloat16 [512, 1536], P(('gx', 'gy')), may hold values from -40 to 40
- new_kv: bfloat16 [512, 1024], P(('gx', 'gy')), may hold values from -6 to 6
- cache_pool: bfloat16 [4096, 16, 1024], P(('gx', 'gy')), may hold values from -6 to 6
- cache_len: int32 [512], P(('gx', 'gy')), may hold values from 1 to 512, as said below
- local_pages: int32 [256, 32], P(('gx', 'gy')), may hold values from 0 to 127
- anchor: int32 [256], P(('gx', 'gy')), may hold values from 0 to 7, as said below
- push_pages: int32 [512, 32], P(('gx', 'gy')), may hold values from 0 to 127
- prefill_attn: bfloat16 [3584, 1536], P(('gx', 'gy')), may hold values from -4 to 4
- residual: bfloat16 [4096, 1536], P(('gx', 'gy')), may hold values from -7 to 7
- out_weight: bfloat16 [1536, 1536], P('gx'), may hold values from -0.15625 to 0.15625
- norm_gain: bfloat16 [1536], replicated, may hold values from 0.099609375 to 1.8984375
- router: bfloat16 [1536, 32], replicated, may hold values from -4 to 4
- routes: int32 [4096, 8], P(('gx', 'gy')), may hold values from 0 to 31, all different within a row; in each aligned block of 128 rows (0 to 127, 128 to 255, ...) at most 48 rows name the same one
- gate_up: bfloat16 [1536, 32, 1024], P('gx', 'gy'), may hold values from -0.15625 to 0.15625
- down_proj: bfloat16 [1536, 32, 512], P('gx', 'gy'), may hold values from -0.25 to 0.25
Outputs:
- attended: bfloat16 [512, 1536], P(('gx', 'gy'))
- layer_out: float32 [4096, 1536], P(('gx', 'gy'))
Inputs may be any that keep to these rules, and one draw needn't show every extreme that they name: `cache_len`: every device holds a request with exactly 512 cached tokens. The last 8 requests of a device continue from the device in the same gx row whose gy column is anchor, never from the device itself; one column sends at most 2 of them to one device, and some column sends exactly 2 to each device. `routes`: no expert is named by more than 48 of the rows of one device.
All inputs are finite; a program needn't handle non-finite values.
Results may differ from a plain program's by a relative error of at most 0.0038.
Values may be sent and summed in bfloat16 or wider, within the bound.
No kernel may reach another device: no remote copies, remote signals or barrier semaphores. Data moves between devices by JAX's collectives and lax.ppermute only.
A program may use at most 192 MiB of HBM per device.

v0:
```python
import math

import jax
import jax.numpy as jnp
from jax import lax
from jax.sharding import PartitionSpec as P

D = 1536
HEADS = 24
KV_HEADS = 8
HEAD = 64
EXPERTS = 32
FF = 512
TOP = 8
MAXLEN = 512
R_DEV = 16
LOCAL = 8
MOVED = 8
CAP = 48


def partial_attend(query_heads, keyval, lengths):
    count_req, positions, kv_width = keyval.shape
    kv_count = query_heads.shape[1]
    head_size = query_heads.shape[3]
    half_width = kv_count * head_size
    key_rows = keyval[:, :, :half_width].reshape(count_req, positions, kv_count, head_size)
    value_rows = keyval[:, :, half_width:].reshape(count_req, positions, kv_count, head_size)
    scores = jnp.einsum(
        "nkgh,ntkh->nkgt", query_heads, key_rows, preferred_element_type=jnp.float32
    ) * (1.0 / math.sqrt(head_size))
    valid = (jnp.arange(positions)[None, :] < lengths[:, None])[:, None, None, :]
    masked = jnp.where(valid, scores, -1e30)
    cache_max = jnp.max(masked, axis=3)
    expos = jnp.where(valid, jnp.exp(masked - cache_max[..., None]), 0.0)
    totals = jnp.sum(expos, axis=3)
    weights = expos.astype(jnp.bfloat16)
    mixture = jnp.einsum("nkgt,ntkh->nkgh", weights, value_rows, preferred_element_type=jnp.float32)
    return (cache_max, totals, mixture)


def finish(query_heads, fresh, cache_max, totals, mixture):
    count_req, kv_count, group_size, head_size = query_heads.shape
    half_width = kv_count * head_size
    own_key = fresh[:, :half_width].reshape(count_req, kv_count, head_size)
    own_value = fresh[:, half_width:].reshape(count_req, kv_count, head_size).astype(jnp.float32)
    own_score = jnp.einsum(
        "nkgh,nkh->nkg", query_heads, own_key, preferred_element_type=jnp.float32
    ) * (1.0 / math.sqrt(head_size))
    highest = jnp.maximum(cache_max, own_score)
    old_share = jnp.exp(cache_max - highest)
    new_share = jnp.exp(own_score - highest)
    weighted = old_share[..., None] * mixture + new_share[..., None] * own_value[:, :, None, :]
    output = weighted / (old_share * totals + new_share)[..., None]
    return output.reshape(count_req, kv_count * group_size * head_size).astype(jnp.bfloat16)


def body(
    queries,
    new_kv,
    cache_pool,
    cache_len,
    local_pages,
    anchor,
    push_pages,
    prefill_attn,
    residual,
    out_weight,
    norm_gain,
    router,
    routes,
    gate_up,
    down_proj,
):
    columns = lax.axis_size("gy")
    slot_count = (MOVED + columns - 2) // (columns - 1)
    group_size = HEADS // KV_HEADS
    kv_width = 2 * KV_HEADS * HEAD
    query_heads = queries.reshape(R_DEV, KV_HEADS, group_size, HEAD)
    local_kv = cache_pool[local_pages].reshape(LOCAL, MAXLEN, kv_width)
    matches = (anchor[:, None] == jnp.arange(columns, dtype=jnp.int32)[None, :]).astype(jnp.int32)
    earlier = jnp.sum((jnp.cumsum(matches, axis=0) - 1) * matches, axis=1)
    chosen = anchor * slot_count + earlier
    outgoing = cache_pool[push_pages].reshape(columns, slot_count * MAXLEN, kv_width)
    incoming = lax.all_to_all(outgoing, "gy", split_axis=0, concat_axis=0, tiled=True)
    moved_kv = incoming.reshape(columns * slot_count, MAXLEN, kv_width)[chosen]
    keyval = jnp.concatenate([local_kv, moved_kv], axis=0)
    cache_max, totals, mixture = partial_attend(query_heads, keyval, cache_len)
    attended = finish(query_heads, new_kv, cache_max, totals, mixture)
    tokens = jnp.concatenate([attended, prefill_attn], axis=0)
    row_count = tokens.shape[0]
    full_out, full_pair, full_down = (
        lax.all_gather(out_weight, "gx", axis=0, tiled=True),
        lax.all_gather(gate_up, "gx", axis=0, tiled=True),
        lax.all_gather(down_proj, "gx", axis=0, tiled=True),
    )
    stream = residual.astype(jnp.float32) + jnp.dot(
        tokens, full_out, preferred_element_type=jnp.float32
    )
    normed = (
        stream
        * lax.rsqrt(jnp.mean(stream * stream, axis=1, keepdims=True) + 1e-06)
        * norm_gain.astype(jnp.float32)
    ).astype(jnp.bfloat16)
    logits = jnp.dot(normed, router, preferred_element_type=jnp.float32)
    selector = routes[:, :, None] == jnp.arange(EXPERTS, dtype=jnp.int32)[None, None, :]
    gate_weights = jax.nn.softmax(
        jnp.sum(jnp.where(selector, logits[:, None, :], 0.0), axis=2), axis=1
    )
    flat_routes = routes.reshape(row_count * TOP)
    route_hits = (flat_routes[:, None] == jnp.arange(EXPERTS, dtype=jnp.int32)[None, :]).astype(
        jnp.int32
    )
    places = jnp.sum((jnp.cumsum(route_hits, axis=0) - 1) * route_hits, axis=1)
    targets = flat_routes * CAP + places
    repeated = jnp.repeat(normed, TOP, axis=0)
    experts_dev = full_pair.shape[1]
    outgoing_rows = (
        jnp.zeros((EXPERTS * CAP, D), jnp.bfloat16)
        .at[targets]
        .set(repeated)
        .reshape(columns, experts_dev, CAP, D)
    )
    arrived = lax.all_to_all(outgoing_rows, "gy", split_axis=0, concat_axis=0, tiled=True)
    gate_pair = jnp.einsum("secd,def->secf", arrived, full_pair, preferred_element_type=jnp.float32)
    hidden = (jax.nn.silu(gate_pair[..., :FF]) * gate_pair[..., FF:]).astype(jnp.bfloat16)
    expert_rows = jnp.einsum(
        "secf,def->secd", hidden, full_down, preferred_element_type=jnp.float32
    ).astype(jnp.bfloat16)
    returned = lax.all_to_all(expert_rows, "gy", split_axis=0, concat_axis=0, tiled=True).reshape(
        EXPERTS * CAP, D
    )
    picked = returned[targets].astype(jnp.float32).reshape(row_count, TOP, D)
    layer_out = stream + jnp.sum(gate_weights[:, :, None] * picked, axis=1)
    return (attended, layer_out)


def solution(mesh):
    placed = (
        P(("gx", "gy"), None),
        P(("gx", "gy"), None),
        P(("gx", "gy"), None, None),
        P(("gx", "gy")),
        P(("gx", "gy"), None),
        P(("gx", "gy")),
        P(("gx", "gy"), None),
        P(("gx", "gy"), None),
        P(("gx", "gy"), None),
        P("gx", None),
        P(),
        P(),
        P(("gx", "gy"), None),
        P("gx", "gy", None),
        P("gx", "gy", None),
    )
    return jax.shard_map(
        body,
        mesh=mesh,
        in_specs=placed,
        out_specs=(P(("gx", "gy"), None), P(("gx", "gy"), None)),
        check_vma=False,
    )
```

profile of v0, /device:TPU:0, one launch (start us, length us, event | category | flops | bytes accessed | tf_op | source)
XLA Modules:
  0.0 525.3 jit_solution(18343803945114728888)
XLA Ops:
  7.2 0.7 all-gather.4.cloned.1.call-update
  8.0 4.6 copy.56
  12.6 0.1 reshape.187
  12.7 16.1 %gather_fusion.1 = bf16[512,16,1024]{2,1,0:T(8,128)(2,1)} fusion(bf16[128,16,1024]{2,1,0:T(8,128)(2,1)} %param.17, s32[1024]{0:T(1024)S(1)} %pad_clamp_fusion.1), kind=kCustom, calls=%fused_computation.1 | custom fusion | bytes 33556480 | tf_op jit(solution)/shard_map/gather | solution.py:84
  28.8 5.9 %all-to-all-start = ((bf16[8,1024,1024]{2,1,0:T(8,128)(2,1)}), bf16[8,1024,1024]{2,1,0:T(8,128)(2,1)}, u32[]{:S(2)}, u32[]{:S(2)}) async-start(bf16[8,1024,1024]{2,1,0:T(8,128)(2,1)} %bitcast.59), calls=%async_computation | async-start | bytes 33554432 | tf_op jit(solution)/shard_map/all_to_all | solution.py:85
  34.7 0.2 all-gather.8.cloned.1.call-start
  34.9 1.5 copy.58
  36.4 0.1 copy.52
  36.5 0.1 eq.61
  36.6 0.1 eq.57
  36.7 0.1 reshape.179
  36.9 11.0 %gather_fusion = bf16[256,16,1024]{2,1,0:T(8,128)(2,1)} fusion(bf16[128,16,1024]{2,1,0:T(8,128)(2,1)} %param.17, s32[1024]{0:T(1024)S(1)} %pad_clamp_fusion.2), kind=kCustom, calls=%fused_computation | custom fusion | bytes 16778240 | tf_op jit(solution)/shard_map/gather | solution.py:80
  47.8 0.2 reshape.168
  48.0 0.1 reshape.229
  48.3 9.0 %reduce-window.6 = s32[32,8,128]{2,1,0:T(8,128)S(1)} reduce-window(s32[32,8,128]{2,1,0:T(8,128)S(1)} %fusion.37, s32[]{:T(128)} %constant.15.clone.1), window={size=1x1x128 pad=0_0x0_0x127_0}, to_apply=%region_8.9 | reduce-window | flops 4161536 | bytes 262148 | tf_op jit(solution)/shard_map/reduce-window
  57.3 0.1 slice.42
  57.4 0.1 copy.54
  57.7 0.1 copy.51
  57.8 0.1 mul.116
  57.9 0.2 select_reduce_fusion.1
  58.1 0.1 add_add_fusion
  58.3 0.3 fusion.49
  58.6 160.6 %all-to-all-done = bf16[8,1024,1024]{2,1,0:T(8,128)(2,1)} async-done(((bf16[8,1024,1024]{2,1,0:T(8,128)(2,1)}), bf16[8,1024,1024]{2,1,0:T(8,128)(2,1)}, u32[]{:S(2)}, u32[]{:S(2)}) %all-to-all-start) | async-done | bytes 16777248 | tf_op jit(solution)/shard_map/all_to_all | solution.py:85
  219.3 10.6 %gather_fusion.2 = bf16[8,512,1024]{2,1,0:T(8,128)(2,1)} fusion(bf16[16,512,1024]{2,1,0:T(8,128)(2,1)} %bitcast.2, s32[1024]{0:T(1024)S(1)} %pad_clamp_fusion), kind=kCustom, calls=%fused_computation.2 | custom fusion | bytes 16777248 | tf_op jit(solution)/shard_map/gather | solution.py:86
  229.9 11.6 %fusion.2 = (bf16[16,512,512]{2,1,0:T(8,128)(2,1)}, bf16[16,512,512]{2,1,0:T(8,128)(2,1)}) fusion(bf16[8,512,1024]{2,1,0:T(8,128)(2,1)} %bitcast.60, bf16[8,512,1024]{2,1,0:T(8,128)(2,1)} %gather_fusion.2), kind=kLoop, calls=%fused_computation.9 | loop fusion | flops 33554432 | bytes 33554432 | tf_op jit(solution)/shard_map/concatenate | solution.py:87
  241.5 12.3 %copy.48 = bf16[16,512,512]{1,2,0:T(8,128)(2,1)} copy(bf16[16,512,512]{2,1,0:T(8,128)(2,1)} %get-tuple-element.5) | data formatting | bytes 16777216 | tf_op jit(solution)/shard_map/slice | solution.py:27
  253.9 12.3 %copy.49 = bf16[16,512,512]{1,2,0:T(8,128)(2,1)} copy(bf16[16,512,512]{2,1,0:T(8,128)(2,1)} %get-tuple-element.6) | data formatting | bytes 16777216 | tf_op jit(solution)/shard_map/slice | solution.py:28
  266.2 4.8 fusion.48
  271.0 0.7 fusion.26
  271.8 0.1 copy-done.1
  272.0 2.4 fusion.25
  274.3 0.2 convert_element_type.57
  274.6 3.2 multiply_reduce_fusion
  277.8 0.9 copy-done.2
  278.7 0.1 multiply_convert_fusion
  278.8 8.6 %scatter_custom_fusion = bf16[1536,1536]{1,0:T(8,128)(2,1)} fusion(s32[1024]{0:T(1024)S(1)} %bitcast.68, bf16[]{:T(256)} %constant.26.clone.1, bf16[128,1536]{1,0:T(8,128)(2,1)S(1)} %multiply_convert_fusion), kind=kCustom, calls=%fused_computation.19 | custom fusion | bytes 5111810 | tf_op jit(solution)/shard_map/scatter | solution.py:121
  287.4 59.2 %all_to_all.15 = bf16[8,4,48,1536]{3,2,1,0:T(8,128)(2,1)} all-to-all(bf16[8,4,48,1536]{3,2,1,0:T(8,128)(2,1)} %bitcast.61), channel_id=1, replica_groups=mesh['gx'=4,'gy'=8] {'gy'}, dimensions={0} | all-to-all | bytes 9437184 | tf_op jit(solution)/shard_map/all_to_all | solution.py:124
  346.6 12.2 %fusion.12 = f32[8,4,48,1024]{3,2,0,1:T(8,128)} fusion(bf16[1536,4,1024]{2,0,1:T(8,128)(2,1)} %all-gather.6.cloned.1.call-done, bf16[8,4,48,1536]{3,2,1,0:T(8,128)(2,1)} %all_to_all.15), kind=kOutput, calls=%fused_computation.21 | convolution fusion | flops 4831838208 | bytes 23592960 | tf_op jit(solution)/shard_map/secd,def->secf/dot_general | solution.py:125
  358.8 76.4 %all-gather.8.cloned.1.call-done = bf16[1536,4,512]{2,0,1:T(8,128)(2,1)} async-done(((bf16[384,4,512]{2,0,1:T(8,128)(2,1)}), bf16[1536,4,512]{2,0,1:T(8,128)(2,1)}) %all-gather.8.cloned.1.call-update) | async-done | bytes 6291472 | tf_op jit(solution)/shard_map/all_gather | solution.py:95
  435.2 7.3 %convert_bitcast_fusion = bf16[8,4,48,1536]{3,2,0,1:T(8,128)(2,1)S(1)} fusion(bf16[1536,4,512]{2,0,1:T(8,128)(2,1)} %all-gather.8.cloned.1.call-done, f32[8,4,48,1024]{3,2,0,1:T(8,128)} %fusion.12), kind=kOutput, calls=%fused_computation.16 | convolution fusion | flops 2422996992 | bytes 17301504 | tf_op jit(solution)/shard_map/secf,def->secd/dot_general | solution.py:127
  442.5 2.5 copy.59
  444.9 4.8 all-to-all-start.2
  449.8 0.2 fusion.50
  450.1 0.1 copy.50
  450.2 54.0 %all-to-all-done.2 = bf16[8,4,48,1536]{3,2,1,0:T(8,128)(2,1)} async-done(((bf16[8,4,48,1536]{3,2,1,0:T(8,128)(2,1)}), bf16[8,4,48,1536]{3,2,1,0:T(8,128)(2,1)}, u32[]{:S(2)}, u32[]{:S(2)}) %all-to-all-start.2) | async-done | bytes 4718624 | tf_op jit(solution)/shard_map/all_to_all | solution.py:130
  504.3 9.6 %gather_fusion.3 = bf16[1024,1536]{1,0:T(8,128)(2,1)S(1)} fusion(bf16[1536,1536]{1,0:T(8,128)(2,1)} %bitcast.20, s32[1024]{0:T(1024)S(1)} %broadcast_clamp_fusion), kind=kCustom, calls=%fused_computation.3 | custom fusion | bytes 6295552 | tf_op jit(solution)/shard_map/gather | solution.py:133
  513.9 2.8 fusion.3
  516.7 2.1 add.84
  (60 shorter events, 0.8 us)
Async XLA Ops:
  7.2 442.6 %copy-start = (bf16[1536,32]{0,1:T(8,128)(2,1)S(1)}, bf16[1536,32]{0,1:T(8,128)(2,1)}, u32[]{:S(2)}) copy-start(bf16[1536,32]{0,1:T(8,128)(2,1)} %param.26) | copy-start | bytes 294916
  7.2 5.4 %copy-start.10 = (s32[16,32]{1,0:T(8,128)S(1)}, s32[16,32]{1,0:T(8,128)}, u32[]{:S(2)}) copy-start(s32[16,32]{1,0:T(8,128)} %param.21) | copy-start | bytes 6148
  7.2 267.4 %all-gather.4.cloned.1.call-start = ((), (), s32[]{:S(2)}) async-start(), calls=%async_computation.3 | async-start | bytes 5898240 | tf_op jit(solution)/shard_map/all_gather | solution.py:93
  7.9 338.6 %all-gather.6.cloned.1.call-start = ((), (), s32[]{:S(2)}) async-start(), calls=%async_computation.4 | async-start | bytes 15728640 | tf_op jit(solution)/shard_map/all_gather | solution.py:94
  28.8 6.1 %copy-start.3 = (bf16[384,4,512]{2,1,0:T(4,128)(2,1)S(1)}, bf16[384,4,512]{2,1,0:T(4,128)(2,1)}, u32[]{:S(2)}) copy-start(bf16[384,4,512]{2,1,0:T(4,128)(2,1)} %param.29) | copy-start | bytes 4718596
  28.8 7.7 %copy-start.8 = (s32[128,8]{0,1:T(8,128)S(1)}, s32[128,8]{0,1:T(8,128)}, u32[]{:S(2)}) copy-start(s32[128,8]{0,1:T(8,128)} %param.27) | copy-start | bytes 12292
  28.8 8.0 %copy-start.12 = (s32[8,32]{1,0:T(8,128)S(1)}, s32[8,32]{1,0:T(8,128)}, u32[]{:S(2)}) copy-start(s32[8,32]{1,0:T(8,128)} %param.19) | copy-start | bytes 3076
  28.8 190.5 %all-to-all-start = ((bf16[8,1024,1024]{2,1,0:T(8,128)(2,1)}), bf16[8,1024,1024]{2,1,0:T(8,128)(2,1)}, u32[]{:S(2)}, u32[]{:S(2)}) async-start(bf16[8,1024,1024]{2,1,0:T(8,128)(2,1)} %bitcast.59), calls=%async_computation | async-start | bytes 33554432 | tf_op jit(solution)/shard_map/all_to_all | solution.py:85
  34.7 400.5 %all-gather.8.cloned.1.call-start = ((), (), s32[]{:S(2)}) async-start(), calls=%async_computation.5 | async-start | bytes 7864320 | tf_op jit(solution)/shard_map/all_gather | solution.py:95
  36.8 11.0 %copy-start.7 = (bf16[16,1536]{1,0:T(8,128)(2,1)S(1)}, bf16[16,1536]{1,0:T(8,128)(2,1)}, u32[]{:S(2)}) copy-start(bf16[16,1536]{1,0:T(8,128)(2,1)} %param.15) | copy-start | bytes 147460
  36.8 11.2 %copy-start.9 = (bf16[16,1024]{1,0:T(8,128)(2,1)S(1)}, bf16[16,1024]{1,0:T(8,128)(2,1)}, u32[]{:S(2)}) copy-start(bf16[16,1024]{1,0:T(8,128)(2,1)} %param.16) | copy-start | bytes 98308
  36.8 11.4 %copy-start.11 = (bf16[1536]{0:T(1024)(128)(2,1)S(1)}, bf16[1536]{0:T(1024)(128)(2,1)}, u32[]{:S(2)}) copy-start(bf16[1536]{0:T(1024)(128)(2,1)} %param.25) | copy-start | bytes 9220
  36.8 11.4 %copy-start.13 = (s32[8]{0:T(128)S(1)}, s32[8]{0:T(128)}, u32[]{:S(2)}) copy-start(s32[8]{0:T(128)} %param.20) | copy-start | bytes 100
  36.9 21.4 %copy-start.14 = (s32[16]{0:T(128)S(1)}, s32[16]{0:T(128)}, u32[]{:S(2)}) copy-start(s32[16]{0:T(128)} %param.18) | copy-start | bytes 196
  266.2 5.8 %copy-start.1 = (bf16[16,512,512]{1,2,0:T(8,128)(2,1)S(1)}, bf16[16,512,512]{1,2,0:T(8,128)(2,1)}, u32[]{:S(2)}) copy-start(bf16[16,512,512]{1,2,0:T(8,128)(2,1)} %copy.49) | copy-start | bytes 25165828
  271.0 3.6 copy-start.4
  271.0 3.6 copy-start.5
  274.5 12.9 %copy-start.6 = (bf16[16,1536]{1,0:T(8,128)(2,1)}, bf16[16,1536]{1,0:T(8,128)(2,1)S(1)}, u32[]{:S(2)}) copy-start(bf16[16,1536]{1,0:T(8,128)(2,1)S(1)} %convert_element_type.57) | copy-start | bytes 147460
  277.8 0.9 copy-start.2
  444.9 59.3 %all-to-all-start.2 = ((bf16[8,4,48,1536]{3,2,1,0:T(8,128)(2,1)}), bf16[8,4,48,1536]{3,2,1,0:T(8,128)(2,1)}, u32[]{:S(2)}, u32[]{:S(2)}) async-start(bf16[8,4,48,1536]{3,2,1,0:T(8,128)(2,1)} %copy.59), calls=%async_computation.2 | async-start | bytes 9437184 | tf_op jit(solution)/shard_map/all_to_all | solution.py:130
Sparse Core Ops, SparseCore 0:
  9.6 92.1 all-gather.3
  103.3 216.6 all-gather.5
  321.6 113.5 all-gather.7
where the time goes:
time: 526 us; the launch traced here: 525 us
  waiting for transfers between devices  292 us (56%)
  local copies, waits for them, and re-layouts  91.6 us (17%)
  blocking collectives  59.2 us (11%)
  matrix products  30.4 us (6%)
  other arithmetic  27.2 us (5%)
  between operations  14.1 us (3%)
  starting transfers between devices  11 us (2%)
    all_to_all x1, waiting for transfers between devices, body(): lax.all_to_all(outgoing, 'gy', split_axis=0, concat_axis=0, tiled=True)  161 us
    all_gather x1, waiting for transfers between devices, body(): lax.all_gather(down_proj, 'gx', axis=0, tiled=True)  76.4 us
    all_to_all x1, blocking collectives, body(): lax.all_to_all(outgoing_rows, 'gy', split_axis=0, concat_axis=0, tiled=True)  59.2 us
    all_to_all x1, waiting for transfers between devices, body(): lax.all_to_all(expert_rows, 'gy', split_axis=0, concat_axis=0, tiled=True)  54 us
    gather x1, local copies, waits for them, and re-layouts, body(): cache_pool[push_pages].reshape(columns, slot_count * MAXLEN, kv_width)  16.1 us
    slice x1, local copies, waits for them, and re-layouts, partial_attend(): keyval[:, :, :half_width].reshape(count_req, positions, kv_count, head_size)  12.3 us
    slice x1, local copies, waits for them, and re-layouts, partial_attend(): keyval[:, :, half_width:].reshape(count_req, positions, kv_count, head_size)  12.3 us
    dot_general x1, matrix products, body(): jnp.einsum('secd,def->secf', arrived, full_pair, preferred_element_type=j...  12.2 us
  transfers between devices with their start and end apart: 5, of which 3 were waited for; matrix products, arithmetic and copies ran while one was open for 24% of the time, Pallas kernels for 0%

commit v1 on v0

v1 whole, which is shorter than its diff:
```python
import functools
import math

import jax
import jax.numpy as jnp
from jax import lax
from jax.experimental import pallas as pl
from jax.experimental.pallas import tpu as pltpu
from jax.sharding import PartitionSpec as P

D = 1536
HEADS = 24
KV_HEADS = 8
HEAD = 64
GROUP = HEADS // KV_HEADS
EXPERTS = 32
FF = 512
TOP = 8
PAGE = 16
MAXLEN = 512
NPAGE = 32
R_DEV = 16
LOCAL = 8
MOVED = 8
CAP = 48
LANES = 128
WIDE = D + LANES
PAIRS = KV_HEADS // 2
BIG = 1e30
BF = jnp.bfloat16
F32 = jnp.float32


def vmem():
    return pl.BlockSpec(memory_space=pltpu.VMEM)


def smem():
    return pl.BlockSpec(memory_space=pltpu.SMEM)


def cost(flops, moved):
    return pl.CostEstimate(flops=flops, bytes_accessed=moved, transcendentals=0)


def attend_kernel(ask_ref, query_ref, table_ref, key_ref, value_ref, mix_ref, stat_ref, counts):
    step = pl.program_id(0)
    slots = table_ref.shape[0]
    pages = counts.shape[1] // PAGE

    @pl.when(step == 0)
    def _():
        lengths = ask_ref[:, D:].astype(jnp.int32)
        full, rest = lengths[:, 0:1], lengths[:, 1:2]
        table = table_ref[...]
        page = lax.broadcasted_iota(jnp.int32, (slots, pages), 1)
        whole = jnp.zeros((slots, pages), F32)
        part = jnp.zeros((slots, pages), F32)
        for p in range(NPAGE):
            hit = table[:, p : p + 1] == page
            whole += jnp.where(hit & (full > p), 1.0, 0.0)
            part += jnp.where(hit & (full == p), 1.0, 0.0)
        row = lax.broadcasted_iota(jnp.int32, (pages, pages * PAGE), 1)
        spread = jnp.where(
            row // PAGE == lax.broadcasted_iota(jnp.int32, (pages, pages * PAGE), 0), 1.0, 0.0
        ).astype(BF)
        whole = jnp.dot(whole.astype(BF), spread, preferred_element_type=F32)
        part = jnp.dot(part.astype(BF), spread, preferred_element_type=F32)
        place = lax.broadcasted_iota(jnp.int32, (slots, pages * PAGE), 1) % PAGE
        counts[...] = whole + jnp.where(place < rest, part, 0.0)

    lane = lax.broadcasted_iota(jnp.int32, (slots, LANES), 1)
    rows = []
    for j in range(2 * GROUP):
        side, chunk, half = j // GROUP, j // 2, j % 2
        part = query_ref[:, chunk * LANES : (chunk + 1) * LANES].astype(F32) * (1.0 / math.sqrt(HEAD))
        if side != half:
            part = pltpu.roll(part, HEAD, 1)
        rows.append(jnp.where((lane < HEAD) == (side == 0), part, 0.0).astype(BF))
    heads = jnp.concatenate(rows, axis=0)
    scores = lax.dot_general(
        heads, key_ref[...], (((1,), (1,)), ((), ())), preferred_element_type=F32
    )
    count = jnp.concatenate([counts[...]] * (2 * GROUP), axis=0)
    masked = jnp.where(count > 0.0, scores, -BIG)
    highest = jnp.max(masked, axis=1, keepdims=True)
    expos = jnp.exp(masked - highest)
    totals = jnp.sum(expos * count, axis=1, keepdims=True)
    weights = (expos.astype(BF).astype(F32) * count).astype(BF)
    mixture = jnp.dot(weights, value_ref[...], preferred_element_type=F32)

    @pl.when(step == 0)
    def _():
        stat_ref[...] = jnp.zeros_like(stat_ref)

    stat = stat_ref[...]
    for j in range(2 * GROUP):
        head = step * 2 * GROUP + j
        take = slice(j * slots, (j + 1) * slots)
        stat = jnp.where(lane == head, highest[take], stat)
        stat = jnp.where(lane == head + 64, totals[take], stat)
    stat_ref[...] = stat
    for chunk in range(GROUP):
        halves = []
        for half in range(2):
            j = 2 * chunk + half
            part = mixture[j * slots : (j + 1) * slots]
            if j // GROUP != half:
                part = pltpu.roll(part, HEAD, 1)
            halves.append(part)
        mix_ref[:, chunk * LANES : (chunk + 1) * LANES] = jnp.where(lane < HEAD, halves[0], halves[1])


def attend(ask, table, pool):
    slots = ask.shape[0]
    tokens = pool.shape[0]
    width = 2 * GROUP * HEAD
    return pl.pallas_call(
        attend_kernel,
        grid=(PAIRS,),
        in_specs=[
            pl.BlockSpec((slots, WIDE), lambda s: (0, 0)),
            pl.BlockSpec((slots, width), lambda s: (0, s)),
            pl.BlockSpec((slots, NPAGE), lambda s: (0, 0)),
            pl.BlockSpec((tokens, LANES), lambda s: (0, s)),
            pl.BlockSpec((tokens, LANES), lambda s: (0, PAIRS + s)),
        ],
        out_specs=[
            pl.BlockSpec((slots, width), lambda s: (0, s)),
            pl.BlockSpec((slots, LANES), lambda s: (0, 0)),
        ],
        out_shape=[
            jax.ShapeDtypeStruct((slots, D), F32),
            jax.ShapeDtypeStruct((slots, LANES), F32),
        ],
        scratch_shapes=[pltpu.VMEM((slots, tokens), F32)],
        compiler_params=pltpu.CompilerParams(vmem_limit_bytes=48 * 1024 * 1024),
        cost_estimate=cost(10**9, 24 * 10**6),
        name="attend",
    )(ask, ask, table, pool, pool)


def stream_kernel(
    chosen_ref, query_ref, fresh_ref, mix_ref, stat_ref, back_ref, prefill_ref, residual_ref,
    out_ref, gain_ref, router_ref, routes_ref,
    attended_ref, stream_ref, send_ref, tokens,
):
    count = query_ref.shape[0]
    lane = lax.broadcasted_iota(jnp.int32, (count, LANES), 1)
    low = lane < HEAD
    picked = [back_ref[pl.ds(chosen_ref[m], 1), :] for m in range(MOVED)]
    picked = jnp.concatenate(picked, axis=0)
    mix = jnp.concatenate([mix_ref[:LOCAL, :], picked[:, :D]], axis=0)
    stat = jnp.concatenate([stat_ref[:LOCAL, :], picked[:, D:]], axis=0)
    fresh = fresh_ref[...].astype(F32)

    def spread(first, second, base):
        sides = []
        for half, head in enumerate((first, second)):
            part = fresh[:, base + head // 2 * LANES : base + head // 2 * LANES + LANES]
            sides.append(pltpu.roll(part, HEAD, 1) if head % 2 != half else part)
        return jnp.where(low, sides[0], sides[1])

    def both(first, second):
        return jnp.where(low, first, second)

    for chunk in range(HEADS // 2):
        first, second = 2 * chunk, 2 * chunk + 1
        span = slice(chunk * LANES, (chunk + 1) * LANES)
        keys = spread(first // GROUP, second // GROUP, 0)
        values = spread(first // GROUP, second // GROUP, KV_HEADS * HEAD)
        product = query_ref[:, span].astype(F32) * keys
        scale = 1.0 / math.sqrt(HEAD)
        own = both(
            jnp.sum(jnp.where(low, product, 0.0), axis=1, keepdims=True) * scale,
            jnp.sum(jnp.where(low, 0.0, product), axis=1, keepdims=True) * scale,
        )
        cache_max = both(stat[:, first : first + 1], stat[:, second : second + 1])
        total = both(stat[:, 64 + first : 65 + first], stat[:, 64 + second : 65 + second])
        highest = jnp.maximum(cache_max, own)
        old = jnp.exp(cache_max - highest)
        new = jnp.exp(own - highest)
        output = (old * mix[:, span] + new * values) / (old * total + new)
        tokens[:count, span] = output.astype(BF)
    attended_ref[...] = tokens[:count, :]
    tokens[count:, :] = prefill_ref[...]
    stream = residual_ref[...].astype(F32) + jnp.dot(
        tokens[...], out_ref[...], preferred_element_type=F32
    )
    stream_ref[...] = stream
    normed = (
        stream
        * lax.rsqrt(jnp.mean(stream * stream, axis=1, keepdims=True) + 1e-06)
        * gain_ref[...].astype(F32)
    ).astype(BF)
    send_ref[:, :D] = normed
    logits = jnp.dot(normed, router_ref[...], preferred_element_type=F32)
    rows = logits.shape[0]
    expert = lax.broadcasted_iota(jnp.int32, (rows, LANES), 1)
    routes = routes_ref[...]
    named = expert == routes[:, 0:1]
    for k in range(1, TOP):
        named = named | (expert == routes[:, k : k + 1])
    masked = jnp.where(named, logits, -BIG)
    expos = jnp.where(named, jnp.exp(masked - jnp.max(masked, axis=1, keepdims=True)), 0.0)
    gates = expos / jnp.sum(expos, axis=1, keepdims=True)
    coarse = gates.astype(BF).astype(F32)
    fine = pltpu.roll(gates - coarse, 64, 1)
    send_ref[:, D:] = jnp.where(expert < 64, coarse, fine).astype(BF)


def make_stream(
    chosen, queries, fresh, mix, stat, back, prefill, residual, out_weight, gain, router, routes
):
    rows = residual.shape[0]
    count = queries.shape[0]
    return pl.pallas_call(
        stream_kernel,
        in_specs=[smem()] + [vmem()] * 11,
        out_specs=[vmem()] * 3,
        out_shape=[
            jax.ShapeDtypeStruct((count, D), BF),
            jax.ShapeDtypeStruct((rows, D), F32),
            jax.ShapeDtypeStruct((rows, WIDE), BF),
        ],
        scratch_shapes=[pltpu.VMEM((rows, D), BF)],
        compiler_params=pltpu.CompilerParams(vmem_limit_bytes=48 * 1024 * 1024),
        cost_estimate=cost(2 * 10**9, 24 * 10**6),
        name="stream",
    )(chosen, queries, fresh, mix, stat, back, prefill, residual, out_weight, gain, router, routes)


def expert_kernel(shards, place_ref, first_ref, second_ref, third_ref, *rest):
    weights, (keep_ref, away_ref, rows_ref, hidden_ref) = rest[: 2 * shards], rest[2 * shards :]
    part = D // shards
    one = first_ref.shape[0]
    rows_ref[:one, :] = first_ref[...]
    rows_ref[one : 2 * one, :] = second_ref[...]
    rows_ref[2 * one :, :] = third_ref[...]
    half = 2 * one
    for block, out_ref in enumerate((keep_ref, away_ref)):
        span = slice(block * half, (block + 1) * half)
        gates = rows_ref[span, D:].astype(F32)
        gates = gates + pltpu.roll(gates, 64, 1)
        lane = lax.broadcasted_iota(jnp.int32, gates.shape, 1)
        for side in range(2):
            total = None
            for s in range(shards):
                at = pl.multiple_of(place_ref[s] * part, LANES)
                term = jnp.dot(
                    rows_ref[span, pl.ds(at, part)],
                    weights[side * shards + s][:, : 2 * FF],
                    preferred_element_type=F32,
                )
                total = term if total is None else total + term
            gate = total[:, :FF]
            hidden_ref[side] = (gate / (1.0 + jnp.exp(-gate)) * total[:, FF:]).astype(BF)
        share = [
            jnp.sum(jnp.where(lane == place_ref[shards + side], gates, 0.0), axis=1, keepdims=True)
            for side in range(2)
        ]
        for s in range(shards):
            at = pl.multiple_of(place_ref[s] * part, LANES)
            total = None
            for side in range(2):
                made = lax.dot_general(
                    hidden_ref[side],
                    weights[side * shards + s][:, 2 * FF :],
                    (((1,), (1,)), ((), ())),
                    preferred_element_type=F32,
                )
                made = share[side] * made.astype(BF).astype(F32)
                total = made if total is None else total + made
            out_ref[:, pl.ds(at, part)] = total.astype(BF)


def run_experts(place, first, second, third, weights):
    shards = len(weights) // 2
    one = first.shape[0]
    return pl.pallas_call(
        functools.partial(expert_kernel, shards),
        in_specs=[smem()] + [vmem()] * (3 + 2 * shards),
        out_specs=[vmem()] * 2,
        out_shape=[jax.ShapeDtypeStruct((2 * one, D), BF)] * 2,
        scratch_shapes=[pltpu.VMEM((4 * one, WIDE), BF), pltpu.VMEM((2, 2 * one, FF), BF)],
        compiler_params=pltpu.CompilerParams(vmem_limit_bytes=52 * 1024 * 1024),
        cost_estimate=cost(5 * 10**9, 12 * 10**6),
        name="experts",
    )(place, first, second, third, *weights)


def swap(x, axis, how):
    return lax.ppermute(x, axis, [(i, how(i)) for i in range(lax.axis_size(axis))])


def near(j):
    return j ^ (2 if j % 2 == 0 else 4)


def far(j):
    return j ^ (4 if j % 2 == 0 else 2)


def exchange_experts(gate_up, down_proj):
    planes = lax.axis_size("gx")
    row = lax.axis_index("gx")
    blocks = []
    for k in range(planes):
        slot = row ^ k
        block = jnp.concatenate(
            [
                lax.dynamic_index_in_dim(gate_up, slot, axis=1, keepdims=False),
                lax.dynamic_index_in_dim(down_proj, slot, axis=1, keepdims=False),
            ],
            axis=1,
        )
        blocks.append(swap(block, "gx", lambda i, k=k: i ^ k) if k else block)
    return blocks + [swap(block, "gy", lambda j: j ^ 1) for block in blocks]


def swapped_experts(send, stream, gate_up, down_proj):
    planes = lax.axis_size("gx")
    row, column = lax.axis_index("gx"), lax.axis_index("gy")
    weights = exchange_experts(gate_up, down_proj)
    place = jnp.stack(
        [row ^ k for k in range(planes)]
        + [column * planes + row, (column ^ 1) * planes + row]
    ).astype(jnp.int32)
    rows = send.shape[0]
    chunks = []
    for k in range(planes):
        mine = swap(send, "gx", lambda i, k=k: i ^ k) if k else send
        second = swap(mine, "gy", near)
        third = swap(jnp.concatenate([mine, second], axis=0), "gy", far)
        chunks.append((mine, second, third))
    result = stream
    for k in reversed(range(planes)):
        keep, away = run_experts(place, *chunks[k], weights)
        arrived = swap(away, "gy", far)
        total = keep.astype(F32) + arrived.astype(F32)
        arrived = swap(total[rows:].astype(BF), "gy", near)
        total = total[:rows] + arrived.astype(F32)
        if k:
            total = swap(total.astype(BF), "gx", lambda i, k=k: i ^ k).astype(F32)
        result = result + total
    return result


def gathered_experts(send, stream, routes, gate_up, down_proj):
    columns = lax.axis_size("gy")
    normed = send[:, :D]
    gates = send[:, D : D + EXPERTS].astype(F32) + send[:, D + 64 : D + 64 + EXPERTS].astype(F32)
    gate_weights = jnp.take_along_axis(gates, routes, axis=1)
    row_count = normed.shape[0]
    full_pair = lax.all_gather(gate_up, "gx", axis=0, tiled=True)
    full_down = lax.all_gather(down_proj, "gx", axis=0, tiled=True)
    flat_routes = routes.reshape(row_count * TOP)
    route_hits = (flat_routes[:, None] == jnp.arange(EXPERTS, dtype=jnp.int32)[None, :]).astype(
        jnp.int32
    )
    places = jnp.sum((jnp.cumsum(route_hits, axis=0) - 1) * route_hits, axis=1)
    targets = flat_routes * CAP + places
    repeated = jnp.repeat(normed, TOP, axis=0)
    experts_dev = full_pair.shape[1]
    outgoing_rows = (
        jnp.zeros((EXPERTS * CAP, D), BF)
        .at[targets]
        .set(repeated)
        .reshape(columns, experts_dev, CAP, D)
    )
    arrived = lax.all_to_all(outgoing_rows, "gy", split_axis=0, concat_axis=0, tiled=True)
    gate_pair = jnp.einsum("secd,def->secf", arrived, full_pair, preferred_element_type=F32)
    hidden = (jax.nn.silu(gate_pair[..., :FF]) * gate_pair[..., FF:]).astype(BF)
    expert_rows = jnp.einsum(
        "secf,def->secd", hidden, full_down, preferred_element_type=F32
    ).astype(BF)
    returned = lax.all_to_all(expert_rows, "gy", split_axis=0, concat_axis=0, tiled=True).reshape(
        EXPERTS * CAP, D
    )
    picked = returned[targets].astype(F32).reshape(row_count, TOP, D)
    return stream + jnp.sum(gate_weights[:, :, None] * picked, axis=1)


def gather_out(out_weight):
    columns = lax.axis_size("gy")
    share = out_weight.shape[0] // columns
    mine = lax.dynamic_slice_in_dim(out_weight, lax.axis_index("gy") * share, share, axis=0)
    return lax.all_gather(mine, ("gx", "gy"), axis=0, tiled=True)


def body(
    queries,
    new_kv,
    cache_pool,
    cache_len,
    local_pages,
    anchor,
    push_pages,
    prefill_attn,
    residual,
    out_weight,
    norm_gain,
    router,
    routes,
    gate_up,
    down_proj,
):
    columns = lax.axis_size("gy")
    slot_count = (MOVED + columns - 2) // (columns - 1)
    pool = cache_pool.reshape(-1, cache_pool.shape[2])
    matches = (anchor[:, None] == jnp.arange(columns, dtype=jnp.int32)[None, :]).astype(jnp.int32)
    earlier = jnp.sum((jnp.cumsum(matches, axis=0) - 1) * matches, axis=1)
    chosen = anchor * slot_count + earlier
    lengths = jnp.stack([cache_len // PAGE, cache_len % PAGE], axis=1).astype(BF)
    ask = jnp.concatenate([queries, jnp.pad(lengths, ((0, 0), (0, LANES - 2)))], axis=1)
    slots = columns * slot_count
    where = (chosen[None, :] == jnp.arange(slots, dtype=jnp.int32)[:, None]).astype(BF)
    outgoing = jnp.dot(where, ask[LOCAL:], preferred_element_type=F32).astype(BF)
    incoming = lax.all_to_all(
        outgoing.reshape(columns, slot_count, WIDE), "gy", split_axis=0, concat_axis=0, tiled=True
    ).reshape(slots, WIDE)
    mix, stat = attend(
        jnp.concatenate([ask[:LOCAL], incoming], axis=0),
        jnp.concatenate([local_pages, push_pages], axis=0),
        pool,
    )
    answers = jnp.concatenate([mix[LOCAL:], stat[LOCAL:]], axis=1).reshape(
        columns, slot_count, WIDE
    )
    back = lax.all_to_all(answers, "gy", split_axis=0, concat_axis=0, tiled=True).reshape(
        slots, WIDE
    )
    attended, stream, send = make_stream(
        chosen,
        queries,
        new_kv,
        mix,
        stat,
        back,
        prefill_attn,
        residual,
        gather_out(out_weight),
        norm_gain.reshape(1, D),
        jnp.pad(router, ((0, 0), (0, LANES - EXPERTS))),
        routes,
    )
    planes = lax.axis_size("gx")
    if columns == 8 and planes & (planes - 1) == 0 and gate_up.shape[1] == planes:
        layer_out = swapped_experts(send, stream, gate_up, down_proj)
    else:
        layer_out = gathered_experts(send, stream, routes, gate_up, down_proj)
    return (attended, layer_out)


def solution(mesh):
    placed = (
        P(("gx", "gy"), None),
        P(("gx", "gy"), None),
        P(("gx", "gy"), None, None),
        P(("gx", "gy")),
        P(("gx", "gy"), None),
        P(("gx", "gy")),
        P(("gx", "gy"), None),
        P(("gx", "gy"), None),
        P(("gx", "gy"), None),
        P("gx", None),
        P(),
        P(),
        P(("gx", "gy"), None),
        P("gx", "gy", None),
        P("gx", "gy", None),
    )
    return jax.shard_map(
        body,
        mesh=mesh,
        in_specs=placed,
        out_specs=(P(("gx", "gy"), None), P(("gx", "gy"), None)),
        check_vma=False,
    )
```

time: 526 us -> 330 us (0.63)
  waiting for transfers between devices: 292 us -> 178 us
  local copies, waits for them, and re-layouts: 91.6 us -> 27.5 us
  blocking collectives: 59.2 us -> 0 us
  Pallas kernels: 0 us -> 57.4 us
  matrix products: 30.4 us -> 0.13 us
  starting transfers between devices: 11 us -> 41 us
  other arithmetic: 27.2 us -> 10.3 us
    all_to_all x2, waiting for transfers between devices: 215 us -> 9.47 us  [the longest x1 4.91 us: body(): lax.all_to_all(outgoing.reshape(columns, slot_count, WIDE), 'gy', split_a...]
    ppermute x0 -> x29, waiting for transfers between devices: none -> 83.3 us  [swap(): lax.ppermute(x, axis, [(i, how(i)) for i in range(lax.axis_size(axis))])]
    all_to_all x1 -> x0, blocking collectives: 59.2 us -> none  [body(): lax.all_to_all(outgoing_rows, 'gy', split_axis=0, concat_axis=0, tiled=True)]
    pallas_call x0 -> x6, Pallas kernels: none -> 57.4 us  [the longest x4 47.2 us: run_experts(): pl.pallas_call(functools.partial(expert_kernel, shards), in_specs=[smem()...]
    gather x4 -> x0, local copies, waits for them, and re-layouts: 47.3 us -> none  [the longest x1 16.1 us: body(): cache_pool[push_pages].reshape(columns, slot_count * MAXLEN, kv_width)]
    ppermute x0 -> x29, starting transfers between devices: none -> 33.4 us  [swap(): lax.ppermute(x, axis, [(i, how(i)) for i in range(lax.axis_size(axis))])]
    dot_general x7 -> x1, matrix products: 30.4 us -> 0.13 us  [body(): jnp.dot(where, ask[LOCAL:], preferred_element_type=F32).astype(BF)]
    slice x4 -> x7, local copies, waits for them, and re-layouts: 24.9 us -> 0.18 us  [the longest x4 0.17 us: swapped_experts(): arrived = swap(total[rows:].astype(BF), 'gy', near)]
  transfers between devices with their start and end apart: 5 -> 32, of which waited for: 3 -> 12; matrix products, arithmetic and copies ran while one was open for 24% -> 8% of each run, Pallas kernels for 0% -> 17%
where the time goes in v1:
time: 330 us; the launch traced here: 329 us
  waiting for transfers between devices  178 us (54%)
  Pallas kernels  57.4 us (17%)
  starting transfers between devices  41 us (12%)
  local copies, waits for them, and re-layouts  27.5 us (8%)
  between operations  14.5 us (4%)
  other arithmetic  10.3 us (3%)
    all_gather x1, waiting for transfers between devices, gather_out(): return lax.all_gather(mine, ('gx', 'gy'), axis=0, tiled=True)  85.7 us
    ppermute x29, waiting for transfers between devices, swap(): lax.ppermute(x, axis, [(i, how(i)) for i in range(lax.axis_size(axis))])  83.3 us
    pallas_call x4, Pallas kernels, run_experts(): pl.pallas_call(functools.partial(expert_kernel, shards), in_specs=[smem()...  47.2 us
    ppermute x29, starting transfers between devices, swap(): lax.ppermute(x, axis, [(i, how(i)) for i in range(lax.axis_size(axis))])  33.4 us
    dynamic_slice x1, local copies, waits for them, and re-layouts, exchange_experts(): lax.dynamic_index_in_dim(gate_up, slot, axis=1, keepdims=False)  11 us
    unnamed x54, local copies, waits for them, and re-layouts  10.7 us
  transfers between devices with their start and end apart: 32, of which 12 were waited for; matrix products, arithmetic and copies ran while one was open for 8% of the time, Pallas kernels for 17%

profile of v1, /device:TPU:0, one launch (start us, length us, event | category | flops | bytes accessed | tf_op | source)
XLA Modules:
  0.0 329.3 jit_solution(5315598265076373006)
XLA Ops:
  7.2 1.2 copy-done
  9.2 11.0 %constant_dynamic-slice_fusion.1 = (bf16[384,1,1024]{2,1,0:T(2,128)(2,1)S(1)}, bf16[384,1,1024]{2,1,0:T(2,128)(2,1)S(1)}, bf16[384,1,1024]{2,1,0:T(2,128)(2,1)S(1)}, bf16[384,1,1024]{2,1,0:T(2,128)(2,1)S(1)}) fusion(bf16[384,4,1024]{2,1,0:T(4,128)(2,1)} %param.28, s32[]{:T(128)S(6)} %select_n.39, s32[]{:T(128)S(6)} %select_n.38, s32[]{:T(128)S(6)} %select_n.37, ...), kind=kLoop, calls=%fused_computation.46 | loop fusion | bytes 6291472 | tf_op jit(solution)/shard_map/jit(dynamic_index_in_dim)/dynamic_slice | solution.py:312
  20.4 1.1 copy-done.11
  21.6 3.3 constant_dynamic-slice_fusion
  24.9 1.1 pad_maximum_fusion.1
  26.0 3.1 collective-permute-start.3
  29.4 1.2 pad_maximum_fusion.2
  30.6 2.6 collective-permute-start.4
  33.5 1.1 pad_maximum_fusion.3
  35.0 1.2 pad_maximum_fusion.rest_0_
  37.4 4.0 %all-to-all-start = ((bf16[8,2,1664]{2,1,0:T(2,128)(2,1)}), bf16[8,2,1664]{2,1,0:T(2,128)(2,1)S(1)}, u32[]{:S(2)}, u32[]{:S(2)}) async-start(bf16[8,2,1664]{2,1,0:T(2,128)(2,1)} %reshape.24), calls=%async_computation | async-start | bytes 106496 | tf_op jit(solution)/shard_map/all_to_all | solution.py:419
  41.5 4.9 %all-to-all-done = bf16[8,2,1664]{2,1,0:T(2,128)(2,1)S(1)} async-done(((bf16[8,2,1664]{2,1,0:T(2,128)(2,1)}), bf16[8,2,1664]{2,1,0:T(2,128)(2,1)S(1)}, u32[]{:S(2)}, u32[]{:S(2)}) %all-to-all-start) | async-done | bytes 53280 | tf_op jit(solution)/shard_map/all_to_all | solution.py:419
  46.5 2.2 copy-done.2
  48.6 5.9 %attend.1 = (f32[24,1536]{1,0:T(8,128)S(1)}, f32[24,128]{1,0:T(8,128)S(1)}) custom-call(bf16[24,1664]{1,0:T(8,128)(2,1)S(1)} %pad_maximum_fusion.9.ask_ref.query_ref, bf16[24,1664]{1,0:T(8,128)(2,1)S(1)} %pad_maximum_fusion.9.ask_ref.query_ref, s32[24,32]{1,0:T(8,128)S(1)} %pad_add_fusion.table_ref, bf16[2048,1024]{1,0:T(8,128)(2,1)S(1)} %bitcast.35, ...), custom_call_target="tpu_custom_call" | custom-call | flops 1000000000 | bytes 24000000 | tf_op jit(solution)/shard_map/attend/pallas_call | solution.py:118
  55.3 3.5 %all-to-all-start.1 = ((f32[8,2,1664]{2,1,0:T(2,128)}), f32[8,2,1664]{2,1,0:T(2,128)S(1)}, u32[]{:S(2)}, u32[]{:S(2)}) async-start(f32[8,2,1664]{2,1,0:T(2,128)} %reshape.27), calls=%async_computation.1 | async-start | bytes 212992 | tf_op jit(solution)/shard_map/all_to_all | solution.py:430
  59.3 4.6 %all-to-all-done.1 = f32[8,2,1664]{2,1,0:T(2,128)S(1)} async-done(((f32[8,2,1664]{2,1,0:T(2,128)}), f32[8,2,1664]{2,1,0:T(2,128)S(1)}, u32[]{:S(2)}, u32[]{:S(2)}) %all-to-all-start.1) | async-done | bytes 106528 | tf_op jit(solution)/shard_map/all_to_all | solution.py:430
  63.9 85.7 %all-gather.2.cloned.1.call-done.out_ref = bf16[1536,1536]{1,0:T(8,128)(2,1)} async-done(((bf16[48,1536]{1,0:T(8,128)(2,1)}), bf16[1536,1536]{1,0:T(8,128)(2,1)}) %all-gather.2.cloned.1.call-update) | async-done | bytes 4718608 | tf_op jit(solution)/shard_map/all_gather | solution.py:388
  149.6 4.3 %stream.1 = (bf16[16,1536]{1,0:T(8,128)(2,1)}, f32[128,1536]{1,0:T(8,128)S(1)}, bf16[128,1664]{1,0:T(8,128)(2,1)S(1)}) custom-call(s32[8]{0:T(128)S(1)} %multiply_add_fusion.chosen_ref, bf16[16,1536]{1,0:T(8,128)(2,1)S(1)} %copy-done.7, bf16[16,1024]{1,0:T(8,128)(2,1)S(1)} %copy-done.10, f32[24,1536]{1,0:T(8,128)S(1)} %get-tuple-element.15.mix_ref, ...), custom_call_target="tpu_custom_call" | custom-call | flops 2000000000 | bytes 24000000 | tf_op jit(solution)/shard_map/stream/pallas_call | solution.py:217
  153.9 1.3 collective-permute-start
  155.2 3.1 collective-permute-start.19
  158.3 1.5 collective-permute-start.25
  159.8 8.7 %collective-permute-done.first_ref = bf16[128,1664]{1,0:T(8,128)(2,1)S(1)} collective-permute-done((bf16[128,1664]{1,0:T(8,128)(2,1)S(1)}, bf16[128,1664]{1,0:T(8,128)(2,1)S(1)}, u32[]{:S(2)}, u32[]{:S(2)}) %collective-permute-start) | collective-permute-done | bytes 426016 | tf_op jit(solution)/shard_map/ppermute | solution.py:293
  168.5 1.5 collective-permute-start.1
  169.9 21.4 %collective-permute-done.13.first_ref = bf16[128,1664]{1,0:T(8,128)(2,1)S(1)} collective-permute-done((bf16[128,1664]{1,0:T(8,128)(2,1)S(1)}, bf16[128,1664]{1,0:T(8,128)(2,1)S(1)}, u32[]{:S(2)}, u32[]{:S(2)}) %collective-permute-start.13) | collective-permute-done | bytes 426016 | tf_op jit(solution)/shard_map/ppermute | solution.py:293
  191.3 1.5 collective-permute-start.14
  194.2 1.3 collective-permute-start.20
  197.3 2.2 collective-permute-done.14.second_ref
  199.5 1.7 collective-permute-start.26
  201.3 1.1 pad_maximum_fusion.4
  202.3 4.6 %collective-permute-done.20.second_ref = bf16[128,1664]{1,0:T(8,128)(2,1)} collective-permute-done((bf16[128,1664]{1,0:T(8,128)(2,1)S(1)}, bf16[128,1664]{1,0:T(8,128)(2,1)}, u32[]{:S(2)}, u32[]{:S(2)}) %collective-permute-start.20) | collective-permute-done | bytes 426016 | tf_op jit(solution)/shard_map/ppermute | solution.py:293
  207.0 1.7 collective-permute-start.2
  208.7 1.1 pad_maximum_fusion.6
  210.2 1.7 collective-permute-start.21
  212.5 11.7 %experts.7 = (bf16[256,1536]{1,0:T(8,128)(2,1)S(1)}, bf16[256,1536]{1,0:T(8,128)(2,1)}) custom-call(s32[6]{0:T(128)S(1)} %stack.42.place_ref, bf16[128,1664]{1,0:T(8,128)(2,1)S(1)} %get-tuple-element.19.first_ref, bf16[128,1664]{1,0:T(8,128)(2,1)S(1)} %copy-done.6, bf16[256,1664]{1,0:T(8,128)(2,1)} %collective-permute-done.26.third_ref, ...), custom_call_target="tpu_custom_call" | custom-call | flops 5000000000 | bytes 12000000 | tf_op jit(solution)/shard_map/experts/pallas_call | solution.py:280
  224.2 1.7 collective-permute-start.27
  226.8 11.9 %experts.4 = (bf16[256,1536]{1,0:T(8,128)(2,1)S(1)}, bf16[256,1536]{1,0:T(8,128)(2,1)}) custom-call(s32[6]{0:T(128)S(1)} %stack.42.place_ref, bf16[128,1664]{1,0:T(8,128)(2,1)S(1)} %collective-permute-done.first_ref, bf16[128,1664]{1,0:T(8,128)(2,1)S(1)} %copy-done.4, bf16[256,1664]{1,0:T(8,128)(2,1)} %copy-done.20, ...), custom_call_target="tpu_custom_call" | custom-call | flops 5000000000 | bytes 12000000 | tf_op jit(solution)/shard_map/experts/pallas_call | solution.py:280
  239.9 11.7 %experts.5 = (bf16[256,1536]{1,0:T(8,128)(2,1)S(1)}, bf16[256,1536]{1,0:T(8,128)(2,1)}) custom-call(s32[6]{0:T(128)S(1)} %stack.42.place_ref, bf16[128,1664]{1,0:T(8,128)(2,1)S(1)} %collective-permute-done.13.first_ref, bf16[128,1664]{1,0:T(8,128)(2,1)S(1)} %collective-permute-done.14.second_ref, bf16[256,1664]{1,0:T(8,128)(2,1)} %copy-done.19, ...), custom_call_target="tpu_custom_call" | custom-call | flops 5000000000 | bytes 12000000 | tf_op jit(solution)/shard_map/experts/pallas_call | solution.py:280
  251.7 1.7 collective-permute-start.16
  254.3 11.9 %experts.6 = (bf16[256,1536]{1,0:T(8,128)(2,1)S(1)}, bf16[256,1536]{1,0:T(8,128)(2,1)}) custom-call(s32[6]{0:T(128)S(1)} %stack.42.place_ref, bf16[128,1664]{1,0:T(8,128)(2,1)S(1)} %collective-permute-done.19.first_ref, bf16[128,1664]{1,0:T(8,128)(2,1)} %collective-permute-done.20.second_ref, bf16[256,1664]{1,0:T(8,128)(2,1)} %copy-done.18, ...), custom_call_target="tpu_custom_call" | custom-call | flops 5000000000 | bytes 12000000 | tf_op jit(solution)/shard_map/experts/pallas_call | solution.py:280
  266.8 1.8 collective-permute-start.28
  269.5 1.8 collective-permute-start.17
  271.3 15.4 %collective-permute-done.22 = bf16[256,1536]{1,0:T(8,128)(2,1)S(1)} collective-permute-done((bf16[256,1536]{1,0:T(8,128)(2,1)}, bf16[256,1536]{1,0:T(8,128)(2,1)S(1)}, u32[]{:S(2)}, u32[]{:S(2)}) %collective-permute-start.22) | collective-permute-done | bytes 786464 | tf_op jit(solution)/shard_map/ppermute | solution.py:293
  287.0 2.1 collective-permute-start.23
  289.2 1.2 collective-permute-start.12
  290.6 4.3 %collective-permute-done.23 = bf16[128,1536]{1,0:T(8,128)(2,1)S(1)} collective-permute-done((bf16[128,1536]{1,0:T(8,128)(2,1)S(1)}, bf16[128,1536]{1,0:T(8,128)(2,1)S(1)}, u32[]{:S(2)}, u32[]{:S(2)}) %collective-permute-start.23) | collective-permute-done | bytes 393248 | tf_op jit(solution)/shard_map/ppermute | solution.py:293
  295.1 8.1 %collective-permute-done.12 = bf16[128,1536]{1,0:T(8,128)(2,1)S(1)} collective-permute-done((bf16[128,1536]{1,0:T(8,128)(2,1)S(1)}, bf16[128,1536]{1,0:T(8,128)(2,1)S(1)}, u32[]{:S(2)}, u32[]{:S(2)}) %collective-permute-start.12) | collective-permute-done | bytes 393248 | tf_op jit(solution)/shard_map/ppermute | solution.py:293
  303.2 17.9 %collective-permute-done.18 = bf16[128,1536]{1,0:T(8,128)(2,1)S(1)} collective-permute-done((bf16[128,1536]{1,0:T(8,128)(2,1)S(1)}, bf16[128,1536]{1,0:T(8,128)(2,1)S(1)}, u32[]{:S(2)}, u32[]{:S(2)}) %collective-permute-start.18) | collective-permute-done | bytes 393248 | tf_op jit(solution)/shard_map/ppermute | solution.py:293
  321.1 1.2 fusion
  (122 shorter events, 14.1 us)
Async XLA Ops:
  7.2 142.4 %all-gather.2.cloned.1.call-start = ((), (), s32[]{:S(2)}) async-start(), calls=%async_computation.2 | async-start | bytes 4866048 | tf_op jit(solution)/shard_map/all_gather | solution.py:388
  20.2 1.4 copy-start.11
  26.0 129.1 %collective-permute-start.3 = (bf16[384,1536]{1,0:T(8,128)(2,1)}, bf16[384,1536]{1,0:T(8,128)(2,1)}, u32[]{:S(2)}, u32[]{:S(2)}) collective-permute-start(bf16[384,1536]{1,0:T(8,128)(2,1)} %pad_maximum_fusion.1), channel_id=1, source_target_pairs={{0,8},{8,0},{16,24},{24,16},{1,9},{9,1},{17,25},{25,17},{2,10},{10... | collective-permute-start | bytes 3538952 | tf_op jit(solution)/shard_map/ppermute | solution.py:293
  30.6 124.6 %collective-permute-start.4 = (bf16[384,1536]{1,0:T(8,128)(2,1)}, bf16[384,1536]{1,0:T(8,128)(2,1)}, u32[]{:S(2)}, u32[]{:S(2)}) collective-permute-start(bf16[384,1536]{1,0:T(8,128)(2,1)} %pad_maximum_fusion.2), channel_id=1, source_target_pairs={{0,16},{8,24},{16,0},{24,8},{1,17},{9,25},{17,1},{25,9},{2,18},{10... | collective-permute-start | bytes 3538952 | tf_op jit(solution)/shard_map/ppermute | solution.py:293
  34.6 123.7 %collective-permute-start.5 = (bf16[384,1536]{1,0:T(8,128)(2,1)}, bf16[384,1536]{1,0:T(8,128)(2,1)}, u32[]{:S(2)}, u32[]{:S(2)}) collective-permute-start(bf16[384,1536]{1,0:T(8,128)(2,1)} %pad_maximum_fusion.3), channel_id=1, source_target_pairs={{0,24},{8,16},{16,8},{24,0},{1,25},{9,17},{17,9},{25,1},{2,26},{10... | collective-permute-start | bytes 3538952 | tf_op jit(solution)/shard_map/ppermute | solution.py:293
  34.9 1.3 copy-start.21
  34.9 1.4 copy-start.17
  34.9 1.7 copy-start.7
  35.0 6.5 %copy-start.13 = (s32[16,32]{1,0:T(8,128)S(1)}, s32[16,32]{1,0:T(8,128)}, u32[]{:S(2)}) copy-start(s32[16,32]{1,0:T(8,128)} %param.21) | copy-start | bytes 6148
  35.0 6.5 %copy-start.16 = (s32[8,32]{1,0:T(8,128)S(1)}, s32[8,32]{1,0:T(8,128)}, u32[]{:S(2)}) copy-start(s32[8,32]{1,0:T(8,128)} %param.19) | copy-start | bytes 3076
  36.2 156.7 %collective-permute-start.6 = (bf16[384,1536]{1,0:T(8,128)(2,1)}, bf16[384,1536]{1,0:T(8,128)(2,1)}, u32[]{:S(2)}, u32[]{:S(2)}) collective-permute-start(bf16[384,1536]{1,0:T(8,128)(2,1)} %pad_maximum_fusion.rest_0_), channel_id=1, source_target_pairs={{0,1},{1,0},{2,3},{3,2},{4,5},{5,4},{6,7},{7,6},{8,9},{9,8},{10,11... | collective-permute-start | bytes 3538952 | tf_op jit(solution)/shard_map/ppermute | solution.py:293
  37.4 9.0 %all-to-all-start = ((bf16[8,2,1664]{2,1,0:T(2,128)(2,1)}), bf16[8,2,1664]{2,1,0:T(2,128)(2,1)S(1)}, u32[]{:S(2)}, u32[]{:S(2)}) async-start(bf16[8,2,1664]{2,1,0:T(2,128)(2,1)} %reshape.24), calls=%async_computation | async-start | bytes 106496 | tf_op jit(solution)/shard_map/all_to_all | solution.py:419
  46.4 2.2 copy-start.2
  48.6 10.2 %copy-start.12 = (bf16[1536,32]{0,1:T(8,128)(2,1)S(1)}, bf16[1536,32]{0,1:T(8,128)(2,1)}, u32[]{:S(2)}) copy-start(bf16[1536,32]{0,1:T(8,128)(2,1)} %param.26) | copy-start | bytes 294916
  48.6 10.4 %copy-start.14 = (s32[128,8]{0,1:T(8,128)S(1)}, s32[128,8]{0,1:T(8,128)}, u32[]{:S(2)}) copy-start(s32[128,8]{0,1:T(8,128)} %param.27) | copy-start | bytes 12292
  48.6 10.5 %copy-start.15 = (bf16[1536]{0:T(1024)(128)(2,1)S(1)}, bf16[1536]{0:T(1024)(128)(2,1)}, u32[]{:S(2)}) copy-start(bf16[1536]{0:T(1024)(128)(2,1)} %param.25) | copy-start | bytes 9220
  54.5 95.1 %copy-start.8 = (bf16[128,1536]{1,0:T(8,128)(2,1)S(1)}, bf16[128,1536]{1,0:T(8,128)(2,1)}, u32[]{:S(2)}) copy-start(bf16[128,1536]{1,0:T(8,128)(2,1)} %residual_ref.1) | copy-start | bytes 1179652
  54.5 95.1 %copy-start.9 = (bf16[112,1536]{1,0:T(8,128)(2,1)S(1)}, bf16[112,1536]{1,0:T(8,128)(2,1)}, u32[]{:S(2)}) copy-start(bf16[112,1536]{1,0:T(8,128)(2,1)} %prefill_ref.1) | copy-start | bytes 1032196
  54.5 95.1 %copy-start.10 = (bf16[16,1024]{1,0:T(8,128)(2,1)S(1)}, bf16[16,1024]{1,0:T(8,128)(2,1)}, u32[]{:S(2)}) copy-start(bf16[16,1024]{1,0:T(8,128)(2,1)} %fresh_ref.1) | copy-start | bytes 98308
  55.3 8.6 %all-to-all-start.1 = ((f32[8,2,1664]{2,1,0:T(2,128)}), f32[8,2,1664]{2,1,0:T(2,128)S(1)}, u32[]{:S(2)}, u32[]{:S(2)}) async-start(f32[8,2,1664]{2,1,0:T(2,128)} %reshape.27), calls=%async_computation.1 | async-start | bytes 212992 | tf_op jit(solution)/shard_map/all_to_all | solution.py:430
  153.9 14.6 %collective-permute-start = (bf16[128,1664]{1,0:T(8,128)(2,1)S(1)}, bf16[128,1664]{1,0:T(8,128)(2,1)S(1)}, u32[]{:S(2)}, u32[]{:S(2)}) collective-permute-start(bf16[128,1664]{1,0:T(8,128)(2,1)S(1)} %get-tuple-element.19.first_ref), channel_id=1, source_target_pairs={{0,24},{8,16},{16,8},{24,0},{1,25},{9,17},{17,9},{25,1},{2,26},{10... | collective-permute-start | bytes 1277960 | tf_op jit(solution)/shard_map/ppermute | solution.py:293
  155.2 36.2 %collective-permute-start.13 = (bf16[128,1664]{1,0:T(8,128)(2,1)S(1)}, bf16[128,1664]{1,0:T(8,128)(2,1)S(1)}, u32[]{:S(2)}, u32[]{:S(2)}) collective-permute-start(bf16[128,1664]{1,0:T(8,128)(2,1)S(1)} %get-tuple-element.19.first_ref), channel_id=1, source_target_pairs={{0,16},{8,24},{16,0},{24,8},{1,17},{9,25},{17,1},{25,9},{2,18},{10... | collective-permute-start | bytes 1277960 | tf_op jit(solution)/shard_map/ppermute | solution.py:293
  155.2 37.7 %collective-permute-start.19 = (bf16[128,1664]{1,0:T(8,128)(2,1)S(1)}, bf16[128,1664]{1,0:T(8,128)(2,1)S(1)}, u32[]{:S(2)}, u32[]{:S(2)}) collective-permute-start(bf16[128,1664]{1,0:T(8,128)(2,1)S(1)} %get-tuple-element.19.first_ref), channel_id=1, source_target_pairs={{0,8},{8,0},{16,24},{24,16},{1,9},{9,1},{17,25},{25,17},{2,10},{10... | collective-permute-start | bytes 1277960 | tf_op jit(solution)/shard_map/ppermute | solution.py:293
  158.3 35.1 %collective-permute-start.25 = (bf16[128,1664]{1,0:T(8,128)(2,1)S(1)}, bf16[128,1664]{1,0:T(8,128)(2,1)S(1)}, u32[]{:S(2)}, u32[]{:S(2)}) collective-permute-start(bf16[128,1664]{1,0:T(8,128)(2,1)S(1)} %get-tuple-element.19.first_ref), channel_id=1, source_target_pairs={{0,2},{1,5},{2,0},{3,7},{4,6},{5,1},{6,4},{7,3},{8,10},{9,13},{10,... | collective-permute-start | bytes 1277960 | tf_op jit(solution)/shard_map/ppermute | solution.py:293
  168.5 25.0 %collective-permute-start.1 = (bf16[128,1664]{1,0:T(8,128)(2,1)S(1)}, bf16[128,1664]{1,0:T(8,128)(2,1)S(1)}, u32[]{:S(2)}, u32[]{:S(2)}) collective-permute-start(bf16[128,1664]{1,0:T(8,128)(2,1)S(1)} %collective-permute-done.first_ref), channel_id=1, source_target_pairs={{0,2},{1,5},{2,0},{3,7},{4,6},{5,1},{6,4},{7,3},{8,10},{9,13},{10,... | collective-permute-start | bytes 1277960 | tf_op jit(solution)/shard_map/ppermute | solution.py:293
  191.3 8.1 %collective-permute-start.14 = (bf16[128,1664]{1,0:T(8,128)(2,1)S(1)}, bf16[128,1664]{1,0:T(8,128)(2,1)S(1)}, u32[]{:S(2)}, u32[]{:S(2)}) collective-permute-start(bf16[128,1664]{1,0:T(8,128)(2,1)S(1)} %collective-permute-done.13.first_ref), channel_id=1, source_target_pairs={{0,2},{1,5},{2,0},{3,7},{4,6},{5,1},{6,4},{7,3},{8,10},{9,13},{10,... | collective-permute-start | bytes 1277960 | tf_op jit(solution)/shard_map/ppermute | solution.py:293
  192.9 17.0 %collective-permute-start.7 = (bf16[384,1536]{1,0:T(8,128)(2,1)}, bf16[384,1536]{1,0:T(8,128)(2,1)}, u32[]{:S(2)}, u32[]{:S(2)}) collective-permute-start(bf16[384,1536]{1,0:T(8,128)(2,1)} %collective-permute-done.3.rest_1_), channel_id=1, source_target_pairs={{0,1},{1,0},{2,3},{3,2},{4,5},{5,4},{6,7},{7,6},{8,9},{9,8},{10,11... | collective-permute-start | bytes 3538952 | tf_op jit(solution)/shard_map/ppermute | solution.py:293
  192.9 17.4 %collective-permute-start.8 = (bf16[384,1536]{1,0:T(8,128)(2,1)}, bf16[384,1536]{1,0:T(8,128)(2,1)}, u32[]{:S(2)}, u32[]{:S(2)}) collective-permute-start(bf16[384,1536]{1,0:T(8,128)(2,1)} %collective-permute-done.4.rest_2_), channel_id=1, source_target_pairs={{0,1},{1,0},{2,3},{3,2},{4,5},{5,4},{6,7},{7,6},{8,9},{9,8},{10,11... | collective-permute-start | bytes 3538952 | tf_op jit(solution)/shard_map/ppermute | solution.py:293
  193.4 18.5 %collective-permute-start.9 = (bf16[384,1536]{1,0:T(8,128)(2,1)}, bf16[384,1536]{1,0:T(8,128)(2,1)}, u32[]{:S(2)}, u32[]{:S(2)}) collective-permute-start(bf16[384,1536]{1,0:T(8,128)(2,1)} %collective-permute-done.5.rest_3_), channel_id=1, source_target_pairs={{0,1},{1,0},{2,3},{3,2},{4,5},{5,4},{6,7},{7,6},{8,9},{9,8},{10,11... | collective-permute-start | bytes 3538952 | tf_op jit(solution)/shard_map/ppermute | solution.py:293
  194.2 12.8 %collective-permute-start.20 = (bf16[128,1664]{1,0:T(8,128)(2,1)S(1)}, bf16[128,1664]{1,0:T(8,128)(2,1)}, u32[]{:S(2)}, u32[]{:S(2)}) collective-permute-start(bf16[128,1664]{1,0:T(8,128)(2,1)S(1)} %collective-permute-done.19.first_ref), channel_id=1, source_target_pairs={{0,2},{1,5},{2,0},{3,7},{4,6},{5,1},{6,4},{7,3},{8,10},{9,13},{10,... | collective-permute-start | bytes 1277960 | tf_op jit(solution)/shard_map/ppermute | solution.py:293
  199.5 13.0 %collective-permute-start.26 = (bf16[256,1664]{1,0:T(8,128)(2,1)}, bf16[256,1664]{1,0:T(8,128)(2,1)}, u32[]{:S(2)}, u32[]{:S(2)}) collective-permute-start(bf16[256,1664]{1,0:T(8,128)(2,1)} %pad_maximum_fusion.7), channel_id=1, source_target_pairs={{0,4},{1,3},{2,6},{3,1},{4,0},{5,7},{6,2},{7,5},{8,12},{9,11},{10,... | collective-permute-start | bytes 2555912 | tf_op jit(solution)/shard_map/ppermute | solution.py:293
  202.3 10.1 %copy-start.6 = (bf16[128,1664]{1,0:T(8,128)(2,1)S(1)}, bf16[128,1664]{1,0:T(8,128)(2,1)}, u32[]{:S(2)}) copy-start(bf16[128,1664]{1,0:T(8,128)(2,1)} %copy-done.5) | copy-start | bytes 1277956
  207.0 18.9 %collective-permute-start.2 = (bf16[256,1664]{1,0:T(8,128)(2,1)S(1)}, bf16[256,1664]{1,0:T(8,128)(2,1)S(1)}, u32[]{:S(2)}, u32[]{:S(2)}) collective-permute-start(bf16[256,1664]{1,0:T(8,128)(2,1)S(1)} %pad_maximum_fusion.4), channel_id=1, source_target_pairs={{0,4},{1,3},{2,6},{3,1},{4,0},{5,7},{6,2},{7,5},{8,12},{9,11},{10,... | collective-permute-start | bytes 2555912 | tf_op jit(solution)/shard_map/ppermute | solution.py:293
  209.8 17.0 %copy-start.4 = (bf16[128,1664]{1,0:T(8,128)(2,1)S(1)}, bf16[128,1664]{1,0:T(8,128)(2,1)}, u32[]{:S(2)}) copy-start(bf16[128,1664]{1,0:T(8,128)(2,1)} %copy-done.3) | copy-start | bytes 1277956
  209.8 29.2 %collective-permute-start.15 = (bf16[256,1664]{1,0:T(8,128)(2,1)S(1)}, bf16[256,1664]{1,0:T(8,128)(2,1)S(1)}, u32[]{:S(2)}, u32[]{:S(2)}) collective-permute-start(bf16[256,1664]{1,0:T(8,128)(2,1)S(1)} %pad_maximum_fusion.5), channel_id=1, source_target_pairs={{0,4},{1,3},{2,6},{3,1},{4,0},{5,7},{6,2},{7,5},{8,12},{9,11},{10,... | collective-permute-start | bytes 2555912 | tf_op jit(solution)/shard_map/ppermute | solution.py:293
  210.2 43.2 %collective-permute-start.21 = (bf16[256,1664]{1,0:T(8,128)(2,1)S(1)}, bf16[256,1664]{1,0:T(8,128)(2,1)S(1)}, u32[]{:S(2)}, u32[]{:S(2)}) collective-permute-start(bf16[256,1664]{1,0:T(8,128)(2,1)S(1)} %pad_maximum_fusion.6), channel_id=1, source_target_pairs={{0,4},{1,3},{2,6},{3,1},{4,0},{5,7},{6,2},{7,5},{8,12},{9,11},{10,... | collective-permute-start | bytes 2555912 | tf_op jit(solution)/shard_map/ppermute | solution.py:293
  224.2 42.3 %collective-permute-start.27 = (bf16[256,1536]{1,0:T(8,128)(2,1)}, bf16[256,1536]{1,0:T(8,128)(2,1)S(1)}, u32[]{:S(2)}, u32[]{:S(2)}) collective-permute-start(bf16[256,1536]{1,0:T(8,128)(2,1)} %get-tuple-element.27), channel_id=1, source_target_pairs={{0,4},{1,3},{2,6},{3,1},{4,0},{5,7},{6,2},{7,5},{8,12},{9,11},{10,... | collective-permute-start | bytes 2359304 | tf_op jit(solution)/shard_map/ppermute | solution.py:293
  238.7 29.9 %collective-permute-start.10 = (bf16[256,1536]{1,0:T(8,128)(2,1)}, bf16[256,1536]{1,0:T(8,128)(2,1)S(1)}, u32[]{:S(2)}, u32[]{:S(2)}) collective-permute-start(bf16[256,1536]{1,0:T(8,128)(2,1)} %get-tuple-element.21), channel_id=1, source_target_pairs={{0,4},{1,3},{2,6},{3,1},{4,0},{5,7},{6,2},{7,5},{8,12},{9,11},{10,... | collective-permute-start | bytes 2359304 | tf_op jit(solution)/shard_map/ppermute | solution.py:293
  251.7 17.5 %collective-permute-start.16 = (bf16[256,1536]{1,0:T(8,128)(2,1)}, bf16[256,1536]{1,0:T(8,128)(2,1)S(1)}, u32[]{:S(2)}, u32[]{:S(2)}) collective-permute-start(bf16[256,1536]{1,0:T(8,128)(2,1)} %get-tuple-element.23), channel_id=1, source_target_pairs={{0,4},{1,3},{2,6},{3,1},{4,0},{5,7},{6,2},{7,5},{8,12},{9,11},{10,... | collective-permute-start | bytes 2359304 | tf_op jit(solution)/shard_map/ppermute | solution.py:293
  266.2 20.6 %collective-permute-start.22 = (bf16[256,1536]{1,0:T(8,128)(2,1)}, bf16[256,1536]{1,0:T(8,128)(2,1)S(1)}, u32[]{:S(2)}, u32[]{:S(2)}) collective-permute-start(bf16[256,1536]{1,0:T(8,128)(2,1)} %get-tuple-element.25), channel_id=1, source_target_pairs={{0,4},{1,3},{2,6},{3,1},{4,0},{5,7},{6,2},{7,5},{8,12},{9,11},{10,... | collective-permute-start | bytes 2359304 | tf_op jit(solution)/shard_map/ppermute | solution.py:293
  266.8 28.3 %collective-permute-start.28 = (bf16[128,1536]{1,0:T(8,128)(2,1)S(1)}, bf16[128,1536]{1,0:T(8,128)(2,1)S(1)}, u32[]{:S(2)}, u32[]{:S(2)}) collective-permute-start(bf16[128,1536]{1,0:T(8,128)(2,1)S(1)} %slice.80), channel_id=1, source_target_pairs={{0,2},{1,5},{2,0},{3,7},{4,6},{5,1},{6,4},{7,3},{8,10},{9,13},{10,... | collective-permute-start | bytes 1179656 | tf_op jit(solution)/shard_map/ppermute | solution.py:293
  268.9 20.3 %collective-permute-start.11 = (bf16[128,1536]{1,0:T(8,128)(2,1)S(1)}, bf16[128,1536]{1,0:T(8,128)(2,1)S(1)}, u32[]{:S(2)}, u32[]{:S(2)}) collective-permute-start(bf16[128,1536]{1,0:T(8,128)(2,1)S(1)} %slice.83), channel_id=1, source_target_pairs={{0,2},{1,5},{2,0},{3,7},{4,6},{5,1},{6,4},{7,3},{8,10},{9,13},{10,... | collective-permute-start | bytes 1179656 | tf_op jit(solution)/shard_map/ppermute | solution.py:293
  269.5 21.0 %collective-permute-start.17 = (bf16[128,1536]{1,0:T(8,128)(2,1)S(1)}, bf16[128,1536]{1,0:T(8,128)(2,1)S(1)}, u32[]{:S(2)}, u32[]{:S(2)}) collective-permute-start(bf16[128,1536]{1,0:T(8,128)(2,1)S(1)} %slice.82), channel_id=1, source_target_pairs={{0,2},{1,5},{2,0},{3,7},{4,6},{5,1},{6,4},{7,3},{8,10},{9,13},{10,... | collective-permute-start | bytes 1179656 | tf_op jit(solution)/shard_map/ppermute | solution.py:293
  287.0 7.9 %collective-permute-start.23 = (bf16[128,1536]{1,0:T(8,128)(2,1)S(1)}, bf16[128,1536]{1,0:T(8,128)(2,1)S(1)}, u32[]{:S(2)}, u32[]{:S(2)}) collective-permute-start(bf16[128,1536]{1,0:T(8,128)(2,1)S(1)} %slice.81), channel_id=1, source_target_pairs={{0,2},{1,5},{2,0},{3,7},{4,6},{5,1},{6,4},{7,3},{8,10},{9,13},{10,... | collective-permute-start | bytes 1179656 | tf_op jit(solution)/shard_map/ppermute | solution.py:293
  289.2 14.0 %collective-permute-start.12 = (bf16[128,1536]{1,0:T(8,128)(2,1)S(1)}, bf16[128,1536]{1,0:T(8,128)(2,1)S(1)}, u32[]{:S(2)}, u32[]{:S(2)}) collective-permute-start(bf16[128,1536]{1,0:T(8,128)(2,1)S(1)} %fusion.3), channel_id=1, source_target_pairs={{0,24},{8,16},{16,8},{24,0},{1,25},{9,17},{17,9},{25,1},{2,26},{10... | collective-permute-start | bytes 1179656 | tf_op jit(solution)/shard_map/ppermute | solution.py:293
  290.5 30.5 %collective-permute-start.18 = (bf16[128,1536]{1,0:T(8,128)(2,1)S(1)}, bf16[128,1536]{1,0:T(8,128)(2,1)S(1)}, u32[]{:S(2)}, u32[]{:S(2)}) collective-permute-start(bf16[128,1536]{1,0:T(8,128)(2,1)S(1)} %fusion.2), channel_id=1, source_target_pairs={{0,16},{8,24},{16,0},{24,8},{1,17},{9,25},{17,1},{25,9},{2,18},{10... | collective-permute-start | bytes 1179656 | tf_op jit(solution)/shard_map/ppermute | solution.py:293
  295.0 26.1 %collective-permute-start.24 = (bf16[128,1536]{1,0:T(8,128)(2,1)S(1)}, bf16[128,1536]{1,0:T(8,128)(2,1)S(1)}, u32[]{:S(2)}, u32[]{:S(2)}) collective-permute-start(bf16[128,1536]{1,0:T(8,128)(2,1)S(1)} %fusion.1), channel_id=1, source_target_pairs={{0,8},{8,0},{16,24},{24,16},{1,9},{9,1},{17,25},{25,17},{2,10},{10... | collective-permute-start | bytes 1179656 | tf_op jit(solution)/shard_map/ppermute | solution.py:293
  321.1 1.4 copy-start.1
  (6 other events, 5.5 us)
Sparse Core Ops, SparseCore 0:
  11.5 138.0 all-gather.1

commit v2 on v1

--- a/solution.py
+++ b/solution.py
@@ -141,10 +141,21 @@
 
 
 def stream_kernel(
-    chosen_ref, query_ref, fresh_ref, mix_ref, stat_ref, back_ref, prefill_ref, residual_ref,
-    out_ref, gain_ref, router_ref, routes_ref,
-    attended_ref, stream_ref, send_ref, tokens,
+    pieces, chosen_ref, at_ref, query_ref, fresh_ref, mix_ref, stat_ref, back_ref, prefill_ref,
+    residual_ref, gain_ref, router_ref, routes_ref, *rest
 ):
+    parts, rest = rest[: len(pieces)], rest[len(pieces) :]
+    attended_ref, stream_ref, send_ref, tokens, out_ref, sems = rest
+    copies = []
+    for part, (blocks, rows) in zip(parts, pieces):
+        for block in range(blocks):
+            n = len(copies)
+            at = pl.multiple_of(at_ref[n], 16)
+            copy = pltpu.make_async_copy(
+                part.at[pl.ds(block * rows, rows)], out_ref.at[pl.ds(at, rows)], sems.at[n]
+            )
+            copy.start()
+            copies.append(copy)
     count = query_ref.shape[0]
     lane = lax.broadcasted_iota(jnp.int32, (count, LANES), 1)
     low = lane < HEAD
@@ -184,6 +195,8 @@
         tokens[:count, span] = output.astype(BF)
     attended_ref[...] = tokens[:count, :]
     tokens[count:, :] = prefill_ref[...]
+    for copy in copies:
+        copy.wait()
     stream = residual_ref[...].astype(F32) + jnp.dot(
         tokens[...], out_ref[...], preferred_element_type=F32
     )
@@ -210,68 +223,72 @@
 
 
 def make_stream(
-    chosen, queries, fresh, mix, stat, back, prefill, residual, out_weight, gain, router, routes
+    chosen, queries, fresh, mix, stat, back, prefill, residual, out_parts, gain, router, routes
 ):
     rows = residual.shape[0]
     count = queries.shape[0]
+    at, parts, pieces = out_parts
     return pl.pallas_call(
-        stream_kernel,
-        in_specs=[smem()] + [vmem()] * 11,
+        functools.partial(stream_kernel, pieces),
+        in_specs=[smem()] * 2 + [vmem()] * 10 + [pl.BlockSpec(memory_space=pl.ANY)] * len(parts),
         out_specs=[vmem()] * 3,
         out_shape=[
             jax.ShapeDtypeStruct((count, D), BF),
             jax.ShapeDtypeStruct((rows, D), F32),
             jax.ShapeDtypeStruct((rows, WIDE), BF),
         ],
-        scratch_shapes=[pltpu.VMEM((rows, D), BF)],
+        scratch_shapes=[
+            pltpu.VMEM((rows, D), BF),
+            pltpu.VMEM((D, D), BF),
+            pltpu.SemaphoreType.DMA((sum(blocks for blocks, _ in pieces),)),
+        ],
         compiler_params=pltpu.CompilerParams(vmem_limit_bytes=48 * 1024 * 1024),
         cost_estimate=cost(2 * 10**9, 24 * 10**6),
         name="stream",
-    )(chosen, queries, fresh, mix, stat, back, prefill, residual, out_weight, gain, router, routes)
+    )(chosen, at, queries, fresh, mix, stat, back, prefill, residual, gain, router, routes, *parts)
 
 
 def expert_kernel(shards, place_ref, first_ref, second_ref, third_ref, *rest):
-    weights, (keep_ref, away_ref, rows_ref, hidden_ref) = rest[: 2 * shards], rest[2 * shards :]
+    weights, rest = rest[: 2 * shards], rest[2 * shards :]
+    keep_ref, away_ref, rows_ref, held_ref, sems = rest
     part = D // shards
     one = first_ref.shape[0]
+    copies = []
+    for n in range(2 * shards):
+        at = pl.multiple_of(place_ref[n % shards] * part, LANES)
+        copy = pltpu.make_async_copy(
+            weights[n], held_ref.at[n // shards, pl.ds(at, part)], sems.at[n]
+        )
+        copy.start()
+        copies.append(copy)
     rows_ref[:one, :] = first_ref[...]
     rows_ref[one : 2 * one, :] = second_ref[...]
     rows_ref[2 * one :, :] = third_ref[...]
-    half = 2 * one
-    for block, out_ref in enumerate((keep_ref, away_ref)):
-        span = slice(block * half, (block + 1) * half)
-        gates = rows_ref[span, D:].astype(F32)
-        gates = gates + pltpu.roll(gates, 64, 1)
-        lane = lax.broadcasted_iota(jnp.int32, gates.shape, 1)
-        for side in range(2):
-            total = None
-            for s in range(shards):
-                at = pl.multiple_of(place_ref[s] * part, LANES)
-                term = jnp.dot(
-                    rows_ref[span, pl.ds(at, part)],
-                    weights[side * shards + s][:, : 2 * FF],
-                    preferred_element_type=F32,
-                )
-                total = term if total is None else total + term
-            gate = total[:, :FF]
-            hidden_ref[side] = (gate / (1.0 + jnp.exp(-gate)) * total[:, FF:]).astype(BF)
-        share = [
-            jnp.sum(jnp.where(lane == place_ref[shards + side], gates, 0.0), axis=1, keepdims=True)
-            for side in range(2)
-        ]
-        for s in range(shards):
-            at = pl.multiple_of(place_ref[s] * part, LANES)
-            total = None
-            for side in range(2):
-                made = lax.dot_general(
-                    hidden_ref[side],
-                    weights[side * shards + s][:, 2 * FF :],
-                    (((1,), (1,)), ((), ())),
-                    preferred_element_type=F32,
-                )
-                made = share[side] * made.astype(BF).astype(F32)
-                total = made if total is None else total + made
-            out_ref[:, pl.ds(at, part)] = total.astype(BF)
+    gates = rows_ref[:, D:].astype(F32)
+    gates = gates + pltpu.roll(gates, 64, 1)
+    lane = lax.broadcasted_iota(jnp.int32, gates.shape, 1)
+    total = None
+    for side in range(2):
+        for copy in copies[side * shards : (side + 1) * shards]:
+            copy.wait()
+        pair = jnp.dot(
+            rows_ref[:, :D], held_ref[side, :, : 2 * FF], preferred_element_type=F32
+        )
+        gate = pair[:, :FF]
+        hidden = (gate / (1.0 + jnp.exp(-gate)) * pair[:, FF:]).astype(BF)
+        share = jnp.sum(
+            jnp.where(lane == place_ref[shards + side], gates, 0.0), axis=1, keepdims=True
+        )
+        made = lax.dot_general(
+            hidden,
+            held_ref[side, :, 2 * FF :],
+            (((1,), (1,)), ((), ())),
+            preferred_element_type=F32,
+        )
+        made = share * made.astype(BF).astype(F32)
+        total = made if total is None else total + made
+    keep_ref[...] = total[: 2 * one].astype(BF)
+    away_ref[...] = total[2 * one :].astype(BF)
 
 
 def run_experts(place, first, second, third, weights):
@@ -279,16 +296,62 @@
     one = first.shape[0]
     return pl.pallas_call(
         functools.partial(expert_kernel, shards),
-        in_specs=[smem()] + [vmem()] * (3 + 2 * shards),
+        in_specs=[smem()]
+        + [vmem()] * 3
+        + [pl.BlockSpec(memory_space=pl.ANY)] * (2 * shards),
         out_specs=[vmem()] * 2,
         out_shape=[jax.ShapeDtypeStruct((2 * one, D), BF)] * 2,
-        scratch_shapes=[pltpu.VMEM((4 * one, WIDE), BF), pltpu.VMEM((2, 2 * one, FF), BF)],
+        scratch_shapes=[
+            pltpu.VMEM((4 * one, WIDE), BF),
+            pltpu.VMEM((2, D, 3 * FF), BF),
+            pltpu.SemaphoreType.DMA((2 * shards,)),
+        ],
         compiler_params=pltpu.CompilerParams(vmem_limit_bytes=52 * 1024 * 1024),
         cost_estimate=cost(5 * 10**9, 12 * 10**6),
         name="experts",
     )(place, first, second, third, *weights)
 
 
+def pack_kernel(slot_ref, gate_ref, down_ref, *rest):
+    outs, (held_ref, sems) = rest[:-2], rest[-2:]
+    depth, experts = gate_ref.shape[:2]
+    step = 16
+
+    @pl.loop(0, depth // step)
+    def _(n):
+        at = pl.ds(pl.multiple_of(n * step, step), step)
+        gate = gate_ref[at]
+        down = down_ref[at]
+        for e in range(experts):
+            held_ref[e, at, : 2 * FF] = gate[:, e, :]
+            held_ref[e, at, 2 * FF :] = down[:, e, :]
+
+    copies = []
+    for k, out in enumerate(outs):
+        copy = pltpu.make_async_copy(held_ref.at[slot_ref[k]], out, sems.at[k])
+        copy.start()
+        copies.append(copy)
+    for copy in copies:
+        copy.wait()
+
+
+def pack_experts(slots, gate_up, down_proj):
+    depth, experts = gate_up.shape[:2]
+    return pl.pallas_call(
+        pack_kernel,
+        in_specs=[smem()] + [vmem()] * 2,
+        out_specs=[pl.BlockSpec(memory_space=pl.ANY)] * experts,
+        out_shape=[jax.ShapeDtypeStruct((depth, 3 * FF), BF)] * experts,
+        scratch_shapes=[
+            pltpu.VMEM((experts, depth, 3 * FF), BF),
+            pltpu.SemaphoreType.DMA((experts,)),
+        ],
+        compiler_params=pltpu.CompilerParams(vmem_limit_bytes=32 * 1024 * 1024),
+        cost_estimate=cost(10**6, 10 * 10**6),
+        name="pack",
+    )(slots, gate_up, down_proj)
+
+
 def swap(x, axis, how):
     return lax.ppermute(x, axis, [(i, how(i)) for i in range(lax.axis_size(axis))])
 
@@ -304,17 +367,11 @@
 def exchange_experts(gate_up, down_proj):
     planes = lax.axis_size("gx")
     row = lax.axis_index("gx")
-    blocks = []
-    for k in range(planes):
-        slot = row ^ k
-        block = jnp.concatenate(
-            [
-                lax.dynamic_index_in_dim(gate_up, slot, axis=1, keepdims=False),
-                lax.dynamic_index_in_dim(down_proj, slot, axis=1, keepdims=False),
-            ],
-            axis=1,
-        )
-        blocks.append(swap(block, "gx", lambda i, k=k: i ^ k) if k else block)
+    slots = jnp.stack([row ^ k for k in range(planes)]).astype(jnp.int32)
+    blocks = pack_experts(slots, gate_up, down_proj)
+    blocks = [
+        swap(block, "gx", lambda i, k=k: i ^ k) if k else block for k, block in enumerate(blocks)
+    ]
     return blocks + [swap(block, "gy", lambda j: j ^ 1) for block in blocks]
 
 
@@ -385,7 +442,32 @@
     columns = lax.axis_size("gy")
     share = out_weight.shape[0] // columns
     mine = lax.dynamic_slice_in_dim(out_weight, lax.axis_index("gy") * share, share, axis=0)
-    return lax.all_gather(mine, ("gx", "gy"), axis=0, tiled=True)
+    whole = lax.all_gather(mine, ("gx", "gy"), axis=0, tiled=True)
+    return jnp.zeros((1,), jnp.int32), [whole], ((1, whole.shape[0]),)
+
+
+def swap_out(out_weight):
+    planes, columns = lax.axis_size("gx"), lax.axis_size("gy")
+    row, column = lax.axis_index("gx"), lax.axis_index("gy")
+    depth = out_weight.shape[0]
+    share = depth // columns
+    mine = lax.dynamic_slice_in_dim(out_weight, column * share, share, axis=0)
+    first = jnp.concatenate(
+        [swap(mine, "gx", lambda i, k=k: i ^ k) for k in range(1, planes)], axis=0
+    )
+    second = swap(first, "gy", near)
+    third = swap(jnp.concatenate([first, second], axis=0), "gy", far)
+    parts = [first, second, third]
+    parts = [out_weight] + parts + [swap(part, "gy", lambda j: j ^ 1) for part in parts]
+    near_of = lambda j: jnp.where(j % 2 == 0, j ^ 2, j ^ 4)
+    far_of = lambda j: jnp.where(j % 2 == 0, j ^ 4, j ^ 2)
+    at = [row * depth]
+    for own in (column, column ^ 1):
+        for source in (own, near_of(own), far_of(own), near_of(far_of(own))):
+            at += [(row ^ k) * depth + source * share for k in range(1, planes)]
+    one = (planes - 1, share)
+    two = (2 * (planes - 1), share)
+    return jnp.stack(at).astype(jnp.int32), parts, ((1, depth), one, one, two, one, one, two)
 
 
 def body(
@@ -430,6 +512,8 @@
     back = lax.all_to_all(answers, "gy", split_axis=0, concat_axis=0, tiled=True).reshape(
         slots, WIDE
     )
+    planes = lax.axis_size("gx")
+    swapped = columns == 8 and planes & (planes - 1) == 0 and gate_up.shape[1] == planes
     attended, stream, send = make_stream(
         chosen,
         queries,
@@ -439,13 +523,12 @@
         back,
         prefill_attn,
         residual,
-        gather_out(out_weight),
+        swap_out(out_weight) if swapped else gather_out(out_weight),
         norm_gain.reshape(1, D),
         jnp.pad(router, ((0, 0), (0, LANES - EXPERTS))),
         routes,
     )
-    planes = lax.axis_size("gx")
-    if columns == 8 and planes & (planes - 1) == 0 and gate_up.shape[1] == planes:
+    if swapped:
         layer_out = swapped_experts(send, stream, gate_up, down_proj)
     else:
         layer_out = gathered_experts(send, stream, routes, gate_up, down_proj)

time: 330 us -> 335 us (1.015)
  waiting for transfers between devices: 178 us -> 204 us
  local copies, waits for them, and re-layouts: 27.5 us -> 12.3 us
  between operations: 14.5 us -> 1.19 us
  starting transfers between devices: 41 us -> 49.8 us
  other arithmetic: 10.3 us -> 6.48 us
    ppermute x29 -> x37, waiting for transfers between devices: 83.3 us -> 200 us  [swap(): lax.ppermute(x, axis, [(i, how(i)) for i in range(lax.axis_size(axis))])]
    all_gather x1 -> x0, waiting for transfers between devices: 85.7 us -> none  [gather_out(): return lax.all_gather(mine, ('gx', 'gy'), axis=0, tiled=True)]
    dynamic_slice x3 -> x1, local copies, waits for them, and re-layouts: 14.9 us -> 1.07 us  [swap_out(): mine = lax.dynamic_slice_in_dim(out_weight, column * share, share, axis=0)]
    pallas_call x1 -> x2, Pallas kernels: 4.32 us -> 14.7 us  [the longest x1 8.56 us: pack_experts(): pl.pallas_call(pack_kernel, in_specs=[smem()] + [vmem()] * 2, out_specs=[...]
    ppermute x29 -> x37, starting transfers between devices: 33.4 us -> 42 us  [swap(): lax.ppermute(x, axis, [(i, how(i)) for i in range(lax.axis_size(axis))])]
    pallas_call x4, Pallas kernels: 47.2 us -> 39.9 us  [run_experts(): pl.pallas_call(functools.partial(expert_kernel, shards), in_specs=[smem()...]
    all_to_all x1, waiting for transfers between devices: 4.91 us -> 0.01 us  [body(): lax.all_to_all(outgoing.reshape(columns, slot_count, WIDE), 'gy', split_a...]
    concatenate x4 -> x1, other arithmetic: 4.54 us -> 1 us  [swap_out(): third = swap(jnp.concatenate([first, second], axis=0), 'gy', far)]
  transfers between devices with their start and end apart: 32 -> 39, of which waited for: 12 -> 16; matrix products, arithmetic and copies ran while one was open for 8% -> 2% of each run, Pallas kernels for 17% -> 18%
where the time goes in v2:
time: 335 us
  waiting for transfers between devices  204 us (61%)
  Pallas kernels  60.5 us (18%)
  starting transfers between devices  49.8 us (15%)
  local copies, waits for them, and re-layouts  12.3 us (4%)
  other arithmetic  6.48 us (2%)
    ppermute x37, waiting for transfers between devices, swap(): lax.ppermute(x, axis, [(i, how(i)) for i in range(lax.axis_size(axis))])  200 us
    ppermute x37, starting transfers between devices, swap(): lax.ppermute(x, axis, [(i, how(i)) for i in range(lax.axis_size(axis))])  42 us
    pallas_call x4, Pallas kernels, run_experts(): pl.pallas_call(functools.partial(expert_kernel, shards), in_specs=[smem()...  39.9 us
    unnamed x50, local copies, waits for them, and re-layouts  9.18 us
    pallas_call x1, Pallas kernels, pack_experts(): pl.pallas_call(pack_kernel, in_specs=[smem()] + [vmem()] * 2, out_specs=[...  8.56 us
  transfers between devices with their start and end apart: 39, of which 16 were waited for; matrix products, arithmetic and copies ran while one was open for 2% of the time, Pallas kernels for 18%

profile of v2, /device:TPU:0, one launch (start us, length us, event | category | flops | bytes accessed | tf_op | source)
XLA Modules:
  0.0 334.6 jit_solution(16198234367322890442)
XLA Ops:
  0.7 1.1 constant_dynamic-slice_fusion
  1.7 3.1 collective-permute-start
  4.8 2.6 collective-permute-start.1
  7.4 3.3 collective-permute-done
  10.7 8.1 %collective-permute-done.1 = bf16[48,1536]{1,0:T(8,128)(2,1)S(1)} collective-permute-done((bf16[48,1536]{1,0:T(8,128)(2,1)S(1)}, bf16[48,1536]{1,0:T(8,128)(2,1)S(1)}, u32[]{:S(2)}, u32[]{:S(2)}) %collective-permute-start.1) | collective-permute-done | bytes 147488 | tf_op jit(solution)/shard_map/ppermute | solution.py:356
  18.9 1.6 collective-permute-start.3
  21.1 6.1 %collective-permute-done.3.rest_2_ = bf16[144,1536]{1,0:T(8,128)(2,1)S(1)} collective-permute-done((bf16[144,1536]{1,0:T(8,128)(2,1)S(1)}, bf16[144,1536]{1,0:T(8,128)(2,1)S(1)}, u32[]{:S(2)}, u32[]{:S(2)}) %collective-permute-start.3) | collective-permute-done | bytes 442400 | tf_op jit(solution)/shard_map/ppermute | solution.py:356
  29.0 1.5 collective-permute-start.4
  31.1 11.3 %collective-permute-done.4.rest_3_ = bf16[288,1536]{1,0:T(8,128)(2,1)} collective-permute-done((bf16[288,1536]{1,0:T(8,128)(2,1)}, bf16[288,1536]{1,0:T(8,128)(2,1)}, u32[]{:S(2)}, u32[]{:S(2)}) %collective-permute-start.4) | collective-permute-done | bytes 884768 | tf_op jit(solution)/shard_map/ppermute | solution.py:356
  43.2 3.8 %all-to-all-start = ((bf16[8,2,1664]{2,1,0:T(2,128)(2,1)}), bf16[8,2,1664]{2,1,0:T(2,128)(2,1)S(1)}, u32[]{:S(2)}, u32[]{:S(2)}) async-start(bf16[8,2,1664]{2,1,0:T(2,128)(2,1)} %reshape.24), calls=%async_computation | async-start | bytes 106496 | tf_op jit(solution)/shard_map/all_to_all | solution.py:501
  47.6 1.4 copy-done.2
  49.0 8.6 %pack.1 = (bf16[384,1536]{1,0:T(8,128)(2,1)}, bf16[384,1536]{1,0:T(8,128)(2,1)}, bf16[384,1536]{1,0:T(8,128)(2,1)}, bf16[384,1536]{1,0:T(8,128)(2,1)}) custom-call(s32[4]{0:T(128)S(1)} %pad_add_fusion.1.slot_ref, bf16[384,4,1024]{2,1,0:T(4,128)(2,1)S(1)} %copy-done.1, bf16[384,4,512]{2,1,0:T(4,128)(2,1)S(1)} %copy-done.2), custom_call_target="tpu_custom_call" | custom-call | flops 1000000 | bytes 10000000 | tf_op jit(solution)/shard_map/pack/pallas_call | solution.py:340
  57.6 2.3 collective-permute-start.11
  59.9 1.1 collective-permute-start.12
  61.0 1.4 collective-permute-start.13
  62.5 2.2 copy-done
  64.7 5.8 %attend.1 = (f32[24,1536]{1,0:T(8,128)S(1)}, f32[24,128]{1,0:T(8,128)S(1)}) custom-call(bf16[24,1664]{1,0:T(8,128)(2,1)S(1)} %pad_maximum_fusion.6.ask_ref.query_ref, bf16[24,1664]{1,0:T(8,128)(2,1)S(1)} %pad_maximum_fusion.6.ask_ref.query_ref, s32[24,32]{1,0:T(8,128)S(1)} %pad_add_fusion.table_ref, bf16[2048,1024]{1,0:T(8,128)(2,1)S(1)} %bitcast.36, ...), custom_call_target="tpu_custom_call" | custom-call | flops 1000000000 | bytes 24000000 | tf_op jit(solution)/shard_map/attend/pallas_call | solution.py:118
  71.4 4.0 %all-to-all-start.1 = ((f32[8,2,1664]{2,1,0:T(2,128)}), f32[8,2,1664]{2,1,0:T(2,128)S(1)}, u32[]{:S(2)}, u32[]{:S(2)}) async-start(f32[8,2,1664]{2,1,0:T(2,128)} %reshape.27), calls=%async_computation.1 | async-start | bytes 212992 | tf_op jit(solution)/shard_map/all_to_all | solution.py:512
  75.9 4.7 %all-to-all-done.1 = f32[8,2,1664]{2,1,0:T(2,128)S(1)} async-done(((f32[8,2,1664]{2,1,0:T(2,128)}), f32[8,2,1664]{2,1,0:T(2,128)S(1)}, u32[]{:S(2)}, u32[]{:S(2)}) %all-to-all-start.1) | async-done | bytes 106528 | tf_op jit(solution)/shard_map/all_to_all | solution.py:512
  81.7 6.2 %stream.1 = (bf16[16,1536]{1,0:T(8,128)(2,1)}, f32[128,1536]{1,0:T(8,128)S(1)}, bf16[128,1664]{1,0:T(8,128)(2,1)S(1)}) custom-call(s32[8]{0:T(128)S(1)} %multiply_add_fusion.chosen_ref, s32[25]{0:T(128)S(1)} %stack.143.at_ref, bf16[16,1536]{1,0:T(8,128)(2,1)S(1)} %copy-done.11, bf16[16,1024]{1,0:T(8,128)(2,1)S(1)} %copy-done.14, ...), custom_call_target="tpu_custom_call" | custom-call | flops 2000000000 | bytes 24000000 | tf_op jit(solution)/shard_map/stream/pallas_call | solution.py:231
  87.9 2.5 collective-permute-start.8
  90.4 20.6 %collective-permute-done.11.rest_1_ = bf16[384,1536]{1,0:T(8,128)(2,1)} collective-permute-done((bf16[384,1536]{1,0:T(8,128)(2,1)}, bf16[384,1536]{1,0:T(8,128)(2,1)}, u32[]{:S(2)}, u32[]{:S(2)}) %collective-permute-start.11) | collective-permute-done | bytes 1179680 | tf_op jit(solution)/shard_map/ppermute | solution.py:356
  111.0 47.9 %collective-permute-done.12.rest_2_ = bf16[384,1536]{1,0:T(8,128)(2,1)} collective-permute-done((bf16[384,1536]{1,0:T(8,128)(2,1)}, bf16[384,1536]{1,0:T(8,128)(2,1)}, u32[]{:S(2)}, u32[]{:S(2)}) %collective-permute-start.12) | collective-permute-done | bytes 1179680 | tf_op jit(solution)/shard_map/ppermute | solution.py:356
  158.9 1.7 collective-permute-start.33
  160.9 40.2 %collective-permute-done.21.first_ref = bf16[128,1664]{1,0:T(8,128)(2,1)S(1)} collective-permute-done((bf16[128,1664]{1,0:T(8,128)(2,1)S(1)}, bf16[128,1664]{1,0:T(8,128)(2,1)S(1)}, u32[]{:S(2)}, u32[]{:S(2)}) %collective-permute-start.21) | collective-permute-done | bytes 426016 | tf_op jit(solution)/shard_map/ppermute | solution.py:356
  201.1 2.0 collective-permute-start.22
  206.6 2.6 collective-permute-done.22.second_ref
  209.2 2.0 collective-permute-start.34
  211.3 1.1 pad_maximum_fusion.1
  212.4 4.4 %collective-permute-done.28.second_ref = bf16[128,1664]{1,0:T(8,128)(2,1)S(1)} collective-permute-done((bf16[128,1664]{1,0:T(8,128)(2,1)S(1)}, bf16[128,1664]{1,0:T(8,128)(2,1)S(1)}, u32[]{:S(2)}, u32[]{:S(2)}) %collective-permute-start.28) | collective-permute-done | bytes 426016 | tf_op jit(solution)/shard_map/ppermute | solution.py:356
  216.8 2.3 collective-permute-start.10
  219.3 2.0 collective-permute-start.29
  222.2 9.9 %experts.7 = (bf16[256,1536]{1,0:T(8,128)(2,1)S(1)}, bf16[256,1536]{1,0:T(8,128)(2,1)}) custom-call(s32[6]{0:T(128)S(1)} %stack.153.place_ref, bf16[128,1664]{1,0:T(8,128)(2,1)S(1)} %get-tuple-element.23.first_ref, bf16[128,1664]{1,0:T(8,128)(2,1)S(1)} %copy-done.8, bf16[256,1664]{1,0:T(8,128)(2,1)} %collective-permute-done.34.third_ref, ...), custom_call_target="tpu_custom_call" | custom-call | flops 5000000000 | bytes 12000000 | tf_op jit(solution)/shard_map/experts/pallas_call | solution.py:297
  232.1 2.1 collective-permute-start.35
  234.2 9.9 %experts.4 = (bf16[256,1536]{1,0:T(8,128)(2,1)S(1)}, bf16[256,1536]{1,0:T(8,128)(2,1)}) custom-call(s32[6]{0:T(128)S(1)} %stack.153.place_ref, bf16[128,1664]{1,0:T(8,128)(2,1)S(1)} %collective-permute-done.8.first_ref, bf16[128,1664]{1,0:T(8,128)(2,1)S(1)} %copy-done.6, bf16[256,1664]{1,0:T(8,128)(2,1)} %collective-permute-done.10.third_ref, ...), custom_call_target="tpu_custom_call" | custom-call | flops 5000000000 | bytes 12000000 | tf_op jit(solution)/shard_map/experts/pallas_call | solution.py:297
  245.1 10.2 %experts.5 = (bf16[256,1536]{1,0:T(8,128)(2,1)S(1)}, bf16[256,1536]{1,0:T(8,128)(2,1)}) custom-call(s32[6]{0:T(128)S(1)} %stack.153.place_ref, bf16[128,1664]{1,0:T(8,128)(2,1)S(1)} %collective-permute-done.21.first_ref, bf16[128,1664]{1,0:T(8,128)(2,1)S(1)} %collective-permute-done.22.second_ref, bf16[256,1664]{1,0:T(8,128)(2,1)} %copy-done.22, ...), custom_call_target="tpu_custom_call" | custom-call | flops 5000000000 | bytes 12000000 | tf_op jit(solution)/shard_map/experts/pallas_call | solution.py:297
  255.3 2.1 collective-permute-start.24
  258.2 10.0 %experts.6 = (bf16[256,1536]{1,0:T(8,128)(2,1)S(1)}, bf16[256,1536]{1,0:T(8,128)(2,1)}) custom-call(s32[6]{0:T(128)S(1)} %stack.153.place_ref, bf16[128,1664]{1,0:T(8,128)(2,1)S(1)} %collective-permute-done.27.first_ref, bf16[128,1664]{1,0:T(8,128)(2,1)S(1)} %collective-permute-done.28.second_ref, bf16[256,1664]{1,0:T(8,128)(2,1)} %copy-done.21, ...), custom_call_target="tpu_custom_call" | custom-call | flops 5000000000 | bytes 12000000 | tf_op jit(solution)/shard_map/experts/pallas_call | solution.py:297
  268.6 2.1 collective-permute-start.36
  271.0 7.1 %collective-permute-done.24 = bf16[256,1536]{1,0:T(8,128)(2,1)S(1)} collective-permute-done((bf16[256,1536]{1,0:T(8,128)(2,1)}, bf16[256,1536]{1,0:T(8,128)(2,1)S(1)}, u32[]{:S(2)}, u32[]{:S(2)}) %collective-permute-start.24) | collective-permute-done | bytes 786464 | tf_op jit(solution)/shard_map/ppermute | solution.py:356
  278.4 2.4 collective-permute-start.25
  280.8 14.2 %collective-permute-done.30 = bf16[256,1536]{1,0:T(8,128)(2,1)S(1)} collective-permute-done((bf16[256,1536]{1,0:T(8,128)(2,1)}, bf16[256,1536]{1,0:T(8,128)(2,1)S(1)}, u32[]{:S(2)}, u32[]{:S(2)}) %collective-permute-start.30) | collective-permute-done | bytes 786464 | tf_op jit(solution)/shard_map/ppermute | solution.py:356
  295.3 2.4 collective-permute-start.31
  297.7 2.5 collective-permute-start.20
  300.4 3.0 collective-permute-done.31
  303.6 8.1 %collective-permute-done.20 = bf16[128,1536]{1,0:T(8,128)(2,1)S(1)} collective-permute-done((bf16[128,1536]{1,0:T(8,128)(2,1)S(1)}, bf16[128,1536]{1,0:T(8,128)(2,1)S(1)}, u32[]{:S(2)}, u32[]{:S(2)}) %collective-permute-start.20) | collective-permute-done | bytes 393248 | tf_op jit(solution)/shard_map/ppermute | solution.py:356
  311.7 21.7 %collective-permute-done.26 = bf16[128,1536]{1,0:T(8,128)(2,1)S(1)} collective-permute-done((bf16[128,1536]{1,0:T(8,128)(2,1)S(1)}, bf16[128,1536]{1,0:T(8,128)(2,1)S(1)}, u32[]{:S(2)}, u32[]{:S(2)}) %collective-permute-start.26) | collective-permute-done | bytes 393248 | tf_op jit(solution)/shard_map/ppermute | solution.py:356
  333.4 1.2 fusion
  (130 shorter events, 15.3 us)
Async XLA Ops:
  0.6 30.0 %copy-start.20 = (s32[8]{0:T(128)S(1)}, s32[8]{0:T(128)}, u32[]{:S(2)}) copy-start(s32[8]{0:T(128)} %param.20) | copy-start | bytes 100
  0.6 30.3 %copy-start.11 = (bf16[16,1536]{1,0:T(8,128)(2,1)S(1)}, bf16[16,1536]{1,0:T(8,128)(2,1)}, u32[]{:S(2)}) copy-start(bf16[16,1536]{1,0:T(8,128)(2,1)} %query_ref.1) | copy-start | bytes 147460
  0.7 46.9 %copy-start.1 = (bf16[384,4,1024]{2,1,0:T(4,128)(2,1)S(1)}, bf16[384,4,1024]{2,1,0:T(4,128)(2,1)}, u32[]{:S(2)}) copy-start(bf16[384,4,1024]{2,1,0:T(4,128)(2,1)} %gate_ref.1) | copy-start | bytes 9437188
  1.7 8.9 %collective-permute-start = (bf16[48,1536]{1,0:T(8,128)(2,1)S(1)}, bf16[48,1536]{1,0:T(8,128)(2,1)S(1)}, u32[]{:S(2)}, u32[]{:S(2)}) collective-permute-start(bf16[48,1536]{1,0:T(8,128)(2,1)S(1)} %constant_dynamic-slice_fusion), channel_id=1, source_target_pairs={{0,8},{8,0},{16,24},{24,16},{1,9},{9,1},{17,25},{25,17},{2,10},{10... | collective-permute-start | bytes 442376 | tf_op jit(solution)/shard_map/ppermute | solution.py:356
  4.8 14.0 %collective-permute-start.1 = (bf16[48,1536]{1,0:T(8,128)(2,1)S(1)}, bf16[48,1536]{1,0:T(8,128)(2,1)S(1)}, u32[]{:S(2)}, u32[]{:S(2)}) collective-permute-start(bf16[48,1536]{1,0:T(8,128)(2,1)S(1)} %constant_dynamic-slice_fusion), channel_id=1, source_target_pairs={{0,16},{8,24},{16,0},{24,8},{1,17},{9,25},{17,1},{25,9},{2,18},{10... | collective-permute-start | bytes 442376 | tf_op jit(solution)/shard_map/ppermute | solution.py:356
  7.4 11.4 %collective-permute-start.2 = (bf16[48,1536]{1,0:T(8,128)(2,1)S(1)}, bf16[48,1536]{1,0:T(8,128)(2,1)S(1)}, u32[]{:S(2)}, u32[]{:S(2)}) collective-permute-start(bf16[48,1536]{1,0:T(8,128)(2,1)S(1)} %constant_dynamic-slice_fusion), channel_id=1, source_target_pairs={{0,24},{8,16},{16,8},{24,0},{1,25},{9,17},{17,9},{25,1},{2,26},{10... | collective-permute-start | bytes 442376 | tf_op jit(solution)/shard_map/ppermute | solution.py:356
  18.9 8.4 %collective-permute-start.3 = (bf16[144,1536]{1,0:T(8,128)(2,1)S(1)}, bf16[144,1536]{1,0:T(8,128)(2,1)S(1)}, u32[]{:S(2)}, u32[]{:S(2)}) collective-permute-start(bf16[144,1536]{1,0:T(8,128)(2,1)S(1)} %constant_dynamic-update-slice_fusion.rest_1_), channel_id=1, source_target_pairs={{0,2},{1,5},{2,0},{3,7},{4,6},{5,1},{6,4},{7,3},{8,10},{9,13},{10,... | collective-permute-start | bytes 1327112 | tf_op jit(solution)/shard_map/ppermute | solution.py:356
  29.0 13.4 %collective-permute-start.4 = (bf16[288,1536]{1,0:T(8,128)(2,1)}, bf16[288,1536]{1,0:T(8,128)(2,1)}, u32[]{:S(2)}, u32[]{:S(2)}) collective-permute-start(bf16[288,1536]{1,0:T(8,128)(2,1)} %pad_maximum_fusion), channel_id=1, source_target_pairs={{0,4},{1,3},{2,6},{3,1},{4,0},{5,7},{6,2},{7,5},{8,12},{9,11},{10,... | collective-permute-start | bytes 2654216 | tf_op jit(solution)/shard_map/ppermute | solution.py:356
  31.0 30.0 %collective-permute-start.5 = (bf16[144,1536]{1,0:T(8,128)(2,1)}, bf16[144,1536]{1,0:T(8,128)(2,1)}, u32[]{:S(2)}, u32[]{:S(2)}) collective-permute-start(bf16[144,1536]{1,0:T(8,128)(2,1)} %copy-done.9), channel_id=1, source_target_pairs={{0,1},{1,0},{2,3},{3,2},{4,5},{5,4},{6,7},{7,6},{8,9},{9,8},{10,11... | collective-permute-start | bytes 1327112 | tf_op jit(solution)/shard_map/ppermute | solution.py:356
  42.4 38.3 %collective-permute-start.7 = (bf16[288,1536]{1,0:T(8,128)(2,1)}, bf16[288,1536]{1,0:T(8,128)(2,1)}, u32[]{:S(2)}, u32[]{:S(2)}) collective-permute-start(bf16[288,1536]{1,0:T(8,128)(2,1)} %collective-permute-done.4.rest_3_), channel_id=1, source_target_pairs={{0,1},{1,0},{2,3},{3,2},{4,5},{5,4},{6,7},{7,6},{8,9},{9,8},{10,11... | collective-permute-start | bytes 2654216 | tf_op jit(solution)/shard_map/ppermute | solution.py:356
  43.2 19.2 %all-to-all-start = ((bf16[8,2,1664]{2,1,0:T(2,128)(2,1)}), bf16[8,2,1664]{2,1,0:T(2,128)(2,1)S(1)}, u32[]{:S(2)}, u32[]{:S(2)}) async-start(bf16[8,2,1664]{2,1,0:T(2,128)(2,1)} %reshape.24), calls=%async_computation | async-start | bytes 106496 | tf_op jit(solution)/shard_map/all_to_all | solution.py:501
  47.0 23.6 %collective-permute-start.6 = (bf16[144,1536]{1,0:T(8,128)(2,1)}, bf16[144,1536]{1,0:T(8,128)(2,1)}, u32[]{:S(2)}, u32[]{:S(2)}) collective-permute-start(bf16[144,1536]{1,0:T(8,128)(2,1)} %copy-done.3), channel_id=1, source_target_pairs={{0,1},{1,0},{2,3},{3,2},{4,5},{5,4},{6,7},{7,6},{8,9},{9,8},{10,11... | collective-permute-start | bytes 1327112 | tf_op jit(solution)/shard_map/ppermute | solution.py:356
  49.0 13.4 %copy-start.16 = (s32[16,32]{1,0:T(8,128)S(1)}, s32[16,32]{1,0:T(8,128)}, u32[]{:S(2)}) copy-start(s32[16,32]{1,0:T(8,128)} %param.21) | copy-start | bytes 6148
  49.0 13.4 %copy-start.19 = (s32[8,32]{1,0:T(8,128)S(1)}, s32[8,32]{1,0:T(8,128)}, u32[]{:S(2)}) copy-start(s32[8,32]{1,0:T(8,128)} %param.19) | copy-start | bytes 3076
  57.6 53.4 %collective-permute-start.11 = (bf16[384,1536]{1,0:T(8,128)(2,1)}, bf16[384,1536]{1,0:T(8,128)(2,1)}, u32[]{:S(2)}, u32[]{:S(2)}) collective-permute-start(bf16[384,1536]{1,0:T(8,128)(2,1)} %get-tuple-element.25), channel_id=1, source_target_pairs={{0,8},{8,0},{16,24},{24,16},{1,9},{9,1},{17,25},{25,17},{2,10},{10... | collective-permute-start | bytes 3538952 | tf_op jit(solution)/shard_map/ppermute | solution.py:356
  59.9 98.9 %collective-permute-start.12 = (bf16[384,1536]{1,0:T(8,128)(2,1)}, bf16[384,1536]{1,0:T(8,128)(2,1)}, u32[]{:S(2)}, u32[]{:S(2)}) collective-permute-start(bf16[384,1536]{1,0:T(8,128)(2,1)} %get-tuple-element.26), channel_id=1, source_target_pairs={{0,16},{8,24},{16,0},{24,8},{1,17},{9,25},{17,1},{25,9},{2,18},{10... | collective-permute-start | bytes 3538952 | tf_op jit(solution)/shard_map/ppermute | solution.py:356
  61.0 97.9 %collective-permute-start.13 = (bf16[384,1536]{1,0:T(8,128)(2,1)}, bf16[384,1536]{1,0:T(8,128)(2,1)}, u32[]{:S(2)}, u32[]{:S(2)}) collective-permute-start(bf16[384,1536]{1,0:T(8,128)(2,1)} %get-tuple-element.27), channel_id=1, source_target_pairs={{0,24},{8,16},{16,8},{24,0},{1,25},{9,17},{17,9},{25,1},{2,26},{10... | collective-permute-start | bytes 3538952 | tf_op jit(solution)/shard_map/ppermute | solution.py:356
  64.7 10.7 %copy-start.15 = (bf16[1536,32]{0,1:T(8,128)(2,1)S(1)}, bf16[1536,32]{0,1:T(8,128)(2,1)}, u32[]{:S(2)}) copy-start(bf16[1536,32]{0,1:T(8,128)(2,1)} %param.26) | copy-start | bytes 294916
  64.7 10.9 %copy-start.17 = (s32[128,8]{0,1:T(8,128)S(1)}, s32[128,8]{0,1:T(8,128)}, u32[]{:S(2)}) copy-start(s32[128,8]{0,1:T(8,128)} %param.27) | copy-start | bytes 12292
  70.5 10.2 %copy-start.4 = (bf16[144,1536]{1,0:T(8,128)(2,1)S(1)}, bf16[144,1536]{1,0:T(8,128)(2,1)}, u32[]{:S(2)}) copy-start(bf16[144,1536]{1,0:T(8,128)(2,1)} %copy-done.3) | copy-start | bytes 1327108
  70.6 132.5 %collective-permute-start.14 = (bf16[384,1536]{1,0:T(8,128)(2,1)}, bf16[384,1536]{1,0:T(8,128)(2,1)}, u32[]{:S(2)}, u32[]{:S(2)}) collective-permute-start(bf16[384,1536]{1,0:T(8,128)(2,1)} %get-tuple-element.24.rest_0_), channel_id=1, source_target_pairs={{0,1},{1,0},{2,3},{3,2},{4,5},{5,4},{6,7},{7,6},{8,9},{9,8},{10,11... | collective-permute-start | bytes 3538952 | tf_op jit(solution)/shard_map/ppermute | solution.py:356
  71.4 9.2 %all-to-all-start.1 = ((f32[8,2,1664]{2,1,0:T(2,128)}), f32[8,2,1664]{2,1,0:T(2,128)S(1)}, u32[]{:S(2)}, u32[]{:S(2)}) async-start(f32[8,2,1664]{2,1,0:T(2,128)} %reshape.27), calls=%async_computation.1 | async-start | bytes 212992 | tf_op jit(solution)/shard_map/all_to_all | solution.py:512
  87.9 72.6 %collective-permute-start.8 = (bf16[128,1664]{1,0:T(8,128)(2,1)S(1)}, bf16[128,1664]{1,0:T(8,128)(2,1)S(1)}, u32[]{:S(2)}, u32[]{:S(2)}) collective-permute-start(bf16[128,1664]{1,0:T(8,128)(2,1)S(1)} %get-tuple-element.23.first_ref), channel_id=1, source_target_pairs={{0,24},{8,16},{16,8},{24,0},{1,25},{9,17},{17,9},{25,1},{2,26},{10... | collective-permute-start | bytes 1277960 | tf_op jit(solution)/shard_map/ppermute | solution.py:356
  111.0 90.1 %collective-permute-start.21 = (bf16[128,1664]{1,0:T(8,128)(2,1)S(1)}, bf16[128,1664]{1,0:T(8,128)(2,1)S(1)}, u32[]{:S(2)}, u32[]{:S(2)}) collective-permute-start(bf16[128,1664]{1,0:T(8,128)(2,1)S(1)} %get-tuple-element.23.first_ref), channel_id=1, source_target_pairs={{0,16},{8,24},{16,0},{24,8},{1,17},{9,25},{17,1},{25,9},{2,18},{10... | collective-permute-start | bytes 1277960 | tf_op jit(solution)/shard_map/ppermute | solution.py:356
  158.9 44.2 %collective-permute-start.27 = (bf16[128,1664]{1,0:T(8,128)(2,1)S(1)}, bf16[128,1664]{1,0:T(8,128)(2,1)S(1)}, u32[]{:S(2)}, u32[]{:S(2)}) collective-permute-start(bf16[128,1664]{1,0:T(8,128)(2,1)S(1)} %get-tuple-element.23.first_ref), channel_id=1, source_target_pairs={{0,8},{8,0},{16,24},{24,16},{1,9},{9,1},{17,25},{25,17},{2,10},{10... | collective-permute-start | bytes 1277960 | tf_op jit(solution)/shard_map/ppermute | solution.py:356
  158.9 44.7 %collective-permute-start.33 = (bf16[128,1664]{1,0:T(8,128)(2,1)S(1)}, bf16[128,1664]{1,0:T(8,128)(2,1)S(1)}, u32[]{:S(2)}, u32[]{:S(2)}) collective-permute-start(bf16[128,1664]{1,0:T(8,128)(2,1)S(1)} %get-tuple-element.23.first_ref), channel_id=1, source_target_pairs={{0,2},{1,5},{2,0},{3,7},{4,6},{5,1},{6,4},{7,3},{8,10},{9,13},{10,... | collective-permute-start | bytes 1277960 | tf_op jit(solution)/shard_map/ppermute | solution.py:356
  160.5 43.1 %collective-permute-start.9 = (bf16[128,1664]{1,0:T(8,128)(2,1)S(1)}, bf16[128,1664]{1,0:T(8,128)(2,1)S(1)}, u32[]{:S(2)}, u32[]{:S(2)}) collective-permute-start(bf16[128,1664]{1,0:T(8,128)(2,1)S(1)} %collective-permute-done.8.first_ref), channel_id=1, source_target_pairs={{0,2},{1,5},{2,0},{3,7},{4,6},{5,1},{6,4},{7,3},{8,10},{9,13},{10,... | collective-permute-start | bytes 1277960 | tf_op jit(solution)/shard_map/ppermute | solution.py:356
  201.1 8.1 %collective-permute-start.22 = (bf16[128,1664]{1,0:T(8,128)(2,1)S(1)}, bf16[128,1664]{1,0:T(8,128)(2,1)S(1)}, u32[]{:S(2)}, u32[]{:S(2)}) collective-permute-start(bf16[128,1664]{1,0:T(8,128)(2,1)S(1)} %collective-permute-done.21.first_ref), channel_id=1, source_target_pairs={{0,2},{1,5},{2,0},{3,7},{4,6},{5,1},{6,4},{7,3},{8,10},{9,13},{10,... | collective-permute-start | bytes 1277960 | tf_op jit(solution)/shard_map/ppermute | solution.py:356
  203.1 16.2 %collective-permute-start.15 = (bf16[384,1536]{1,0:T(8,128)(2,1)}, bf16[384,1536]{1,0:T(8,128)(2,1)}, u32[]{:S(2)}, u32[]{:S(2)}) collective-permute-start(bf16[384,1536]{1,0:T(8,128)(2,1)} %collective-permute-done.11.rest_1_), channel_id=1, source_target_pairs={{0,1},{1,0},{2,3},{3,2},{4,5},{5,4},{6,7},{7,6},{8,9},{9,8},{10,11... | collective-permute-start | bytes 3538952 | tf_op jit(solution)/shard_map/ppermute | solution.py:356
  203.1 16.2 %collective-permute-start.16 = (bf16[384,1536]{1,0:T(8,128)(2,1)}, bf16[384,1536]{1,0:T(8,128)(2,1)}, u32[]{:S(2)}, u32[]{:S(2)}) collective-permute-start(bf16[384,1536]{1,0:T(8,128)(2,1)} %collective-permute-done.12.rest_2_), channel_id=1, source_target_pairs={{0,1},{1,0},{2,3},{3,2},{4,5},{5,4},{6,7},{7,6},{8,9},{9,8},{10,11... | collective-permute-start | bytes 3538952 | tf_op jit(solution)/shard_map/ppermute | solution.py:356
  203.6 17.7 %collective-permute-start.17 = (bf16[384,1536]{1,0:T(8,128)(2,1)}, bf16[384,1536]{1,0:T(8,128)(2,1)}, u32[]{:S(2)}, u32[]{:S(2)}) collective-permute-start(bf16[384,1536]{1,0:T(8,128)(2,1)} %collective-permute-done.13.rest_3_), channel_id=1, source_target_pairs={{0,1},{1,0},{2,3},{3,2},{4,5},{5,4},{6,7},{7,6},{8,9},{9,8},{10,11... | collective-permute-start | bytes 3538952 | tf_op jit(solution)/shard_map/ppermute | solution.py:356
  204.5 12.3 %collective-permute-start.28 = (bf16[128,1664]{1,0:T(8,128)(2,1)S(1)}, bf16[128,1664]{1,0:T(8,128)(2,1)S(1)}, u32[]{:S(2)}, u32[]{:S(2)}) collective-permute-start(bf16[128,1664]{1,0:T(8,128)(2,1)S(1)} %collective-permute-done.27.first_ref), channel_id=1, source_target_pairs={{0,2},{1,5},{2,0},{3,7},{4,6},{5,1},{6,4},{7,3},{8,10},{9,13},{10,... | collective-permute-start | bytes 1277960 | tf_op jit(solution)/shard_map/ppermute | solution.py:356
  209.2 13.0 %collective-permute-start.34 = (bf16[256,1664]{1,0:T(8,128)(2,1)}, bf16[256,1664]{1,0:T(8,128)(2,1)}, u32[]{:S(2)}, u32[]{:S(2)}) collective-permute-start(bf16[256,1664]{1,0:T(8,128)(2,1)} %pad_maximum_fusion.4), channel_id=1, source_target_pairs={{0,4},{1,3},{2,6},{3,1},{4,0},{5,7},{6,2},{7,5},{8,12},{9,11},{10,... | collective-permute-start | bytes 2555912 | tf_op jit(solution)/shard_map/ppermute | solution.py:356
  216.8 17.4 %collective-permute-start.10 = (bf16[256,1664]{1,0:T(8,128)(2,1)S(1)}, bf16[256,1664]{1,0:T(8,128)(2,1)}, u32[]{:S(2)}, u32[]{:S(2)}) collective-permute-start(bf16[256,1664]{1,0:T(8,128)(2,1)S(1)} %pad_maximum_fusion.1), channel_id=1, source_target_pairs={{0,4},{1,3},{2,6},{3,1},{4,0},{5,7},{6,2},{7,5},{8,12},{9,11},{10,... | collective-permute-start | bytes 2555912 | tf_op jit(solution)/shard_map/ppermute | solution.py:356
  219.2 15.0 %copy-start.6 = (bf16[128,1664]{1,0:T(8,128)(2,1)S(1)}, bf16[128,1664]{1,0:T(8,128)(2,1)}, u32[]{:S(2)}) copy-start(bf16[128,1664]{1,0:T(8,128)(2,1)} %copy-done.5) | copy-start | bytes 1277956
  219.3 25.0 %collective-permute-start.23 = (bf16[256,1664]{1,0:T(8,128)(2,1)S(1)}, bf16[256,1664]{1,0:T(8,128)(2,1)S(1)}, u32[]{:S(2)}, u32[]{:S(2)}) collective-permute-start(bf16[256,1664]{1,0:T(8,128)(2,1)S(1)} %pad_maximum_fusion.2), channel_id=1, source_target_pairs={{0,4},{1,3},{2,6},{3,1},{4,0},{5,7},{6,2},{7,5},{8,12},{9,11},{10,... | collective-permute-start | bytes 2555912 | tf_op jit(solution)/shard_map/ppermute | solution.py:356
  219.3 38.0 %collective-permute-start.29 = (bf16[256,1664]{1,0:T(8,128)(2,1)S(1)}, bf16[256,1664]{1,0:T(8,128)(2,1)S(1)}, u32[]{:S(2)}, u32[]{:S(2)}) collective-permute-start(bf16[256,1664]{1,0:T(8,128)(2,1)S(1)} %pad_maximum_fusion.3), channel_id=1, source_target_pairs={{0,4},{1,3},{2,6},{3,1},{4,0},{5,7},{6,2},{7,5},{8,12},{9,11},{10,... | collective-permute-start | bytes 2555912 | tf_op jit(solution)/shard_map/ppermute | solution.py:356
  232.1 36.2 %collective-permute-start.35 = (bf16[256,1536]{1,0:T(8,128)(2,1)}, bf16[256,1536]{1,0:T(8,128)(2,1)S(1)}, u32[]{:S(2)}, u32[]{:S(2)}) collective-permute-start(bf16[256,1536]{1,0:T(8,128)(2,1)} %get-tuple-element.35), channel_id=1, source_target_pairs={{0,4},{1,3},{2,6},{3,1},{4,0},{5,7},{6,2},{7,5},{8,12},{9,11},{10,... | collective-permute-start | bytes 2359304 | tf_op jit(solution)/shard_map/ppermute | solution.py:356
  244.1 26.6 %collective-permute-start.18 = (bf16[256,1536]{1,0:T(8,128)(2,1)}, bf16[256,1536]{1,0:T(8,128)(2,1)S(1)}, u32[]{:S(2)}, u32[]{:S(2)}) collective-permute-start(bf16[256,1536]{1,0:T(8,128)(2,1)} %get-tuple-element.29), channel_id=1, source_target_pairs={{0,4},{1,3},{2,6},{3,1},{4,0},{5,7},{6,2},{7,5},{8,12},{9,11},{10,... | collective-permute-start | bytes 2359304 | tf_op jit(solution)/shard_map/ppermute | solution.py:356
  255.3 22.8 %collective-permute-start.24 = (bf16[256,1536]{1,0:T(8,128)(2,1)}, bf16[256,1536]{1,0:T(8,128)(2,1)S(1)}, u32[]{:S(2)}, u32[]{:S(2)}) collective-permute-start(bf16[256,1536]{1,0:T(8,128)(2,1)} %get-tuple-element.31), channel_id=1, source_target_pairs={{0,4},{1,3},{2,6},{3,1},{4,0},{5,7},{6,2},{7,5},{8,12},{9,11},{10,... | collective-permute-start | bytes 2359304 | tf_op jit(solution)/shard_map/ppermute | solution.py:356
  268.2 26.8 %collective-permute-start.30 = (bf16[256,1536]{1,0:T(8,128)(2,1)}, bf16[256,1536]{1,0:T(8,128)(2,1)S(1)}, u32[]{:S(2)}, u32[]{:S(2)}) collective-permute-start(bf16[256,1536]{1,0:T(8,128)(2,1)} %get-tuple-element.33), channel_id=1, source_target_pairs={{0,4},{1,3},{2,6},{3,1},{4,0},{5,7},{6,2},{7,5},{8,12},{9,11},{10,... | collective-permute-start | bytes 2359304 | tf_op jit(solution)/shard_map/ppermute | solution.py:356
  268.6 35.0 %collective-permute-start.36 = (bf16[128,1536]{1,0:T(8,128)(2,1)S(1)}, bf16[128,1536]{1,0:T(8,128)(2,1)S(1)}, u32[]{:S(2)}, u32[]{:S(2)}) collective-permute-start(bf16[128,1536]{1,0:T(8,128)(2,1)S(1)} %slice.80), channel_id=1, source_target_pairs={{0,2},{1,5},{2,0},{3,7},{4,6},{5,1},{6,4},{7,3},{8,10},{9,13},{10,... | collective-permute-start | bytes 1179656 | tf_op jit(solution)/shard_map/ppermute | solution.py:356
  270.9 26.7 %collective-permute-start.19 = (bf16[128,1536]{1,0:T(8,128)(2,1)S(1)}, bf16[128,1536]{1,0:T(8,128)(2,1)S(1)}, u32[]{:S(2)}, u32[]{:S(2)}) collective-permute-start(bf16[128,1536]{1,0:T(8,128)(2,1)S(1)} %slice.83), channel_id=1, source_target_pairs={{0,2},{1,5},{2,0},{3,7},{4,6},{5,1},{6,4},{7,3},{8,10},{9,13},{10,... | collective-permute-start | bytes 1179656 | tf_op jit(solution)/shard_map/ppermute | solution.py:356
  278.4 21.8 %collective-permute-start.25 = (bf16[128,1536]{1,0:T(8,128)(2,1)S(1)}, bf16[128,1536]{1,0:T(8,128)(2,1)S(1)}, u32[]{:S(2)}, u32[]{:S(2)}) collective-permute-start(bf16[128,1536]{1,0:T(8,128)(2,1)S(1)} %slice.82), channel_id=1, source_target_pairs={{0,2},{1,5},{2,0},{3,7},{4,6},{5,1},{6,4},{7,3},{8,10},{9,13},{10,... | collective-permute-start | bytes 1179656 | tf_op jit(solution)/shard_map/ppermute | solution.py:356
  295.3 8.2 %collective-permute-start.31 = (bf16[128,1536]{1,0:T(8,128)(2,1)S(1)}, bf16[128,1536]{1,0:T(8,128)(2,1)S(1)}, u32[]{:S(2)}, u32[]{:S(2)}) collective-permute-start(bf16[128,1536]{1,0:T(8,128)(2,1)S(1)} %slice.81), channel_id=1, source_target_pairs={{0,2},{1,5},{2,0},{3,7},{4,6},{5,1},{6,4},{7,3},{8,10},{9,13},{10,... | collective-permute-start | bytes 1179656 | tf_op jit(solution)/shard_map/ppermute | solution.py:356
  297.7 14.0 %collective-permute-start.20 = (bf16[128,1536]{1,0:T(8,128)(2,1)S(1)}, bf16[128,1536]{1,0:T(8,128)(2,1)S(1)}, u32[]{:S(2)}, u32[]{:S(2)}) collective-permute-start(bf16[128,1536]{1,0:T(8,128)(2,1)S(1)} %fusion.3), channel_id=1, source_target_pairs={{0,24},{8,16},{16,8},{24,0},{1,25},{9,17},{17,9},{25,1},{2,26},{10... | collective-permute-start | bytes 1179656 | tf_op jit(solution)/shard_map/ppermute | solution.py:356
  300.3 33.1 %collective-permute-start.26 = (bf16[128,1536]{1,0:T(8,128)(2,1)S(1)}, bf16[128,1536]{1,0:T(8,128)(2,1)S(1)}, u32[]{:S(2)}, u32[]{:S(2)}) collective-permute-start(bf16[128,1536]{1,0:T(8,128)(2,1)S(1)} %fusion.2), channel_id=1, source_target_pairs={{0,16},{8,24},{16,0},{24,8},{1,17},{9,25},{17,1},{25,9},{2,18},{10... | collective-permute-start | bytes 1179656 | tf_op jit(solution)/shard_map/ppermute | solution.py:356
  303.5 29.9 %collective-permute-start.32 = (bf16[128,1536]{1,0:T(8,128)(2,1)S(1)}, bf16[128,1536]{1,0:T(8,128)(2,1)S(1)}, u32[]{:S(2)}, u32[]{:S(2)}) collective-permute-start(bf16[128,1536]{1,0:T(8,128)(2,1)S(1)} %fusion.1), channel_id=1, source_target_pairs={{0,8},{8,0},{16,24},{24,16},{1,9},{9,1},{17,25},{25,17},{2,10},{10... | collective-permute-start | bytes 1179656 | tf_op jit(solution)/shard_map/ppermute | solution.py:356
  (14 other events, 56.0 us)

commit v3 on v2

--- a/solution.py
+++ b/solution.py
@@ -27,6 +27,8 @@
 WIDE = D + LANES
 PAIRS = KV_HEADS // 2
 BIG = 1e30
+HIDDEN_COST = 6 * 10**9
+DOWN_COST = 10**6
 BF = jnp.bfloat16
 F32 = jnp.float32
 
@@ -43,13 +45,26 @@
     return pl.CostEstimate(flops=flops, bytes_accessed=moved, transcendentals=0)
 
 
-def attend_kernel(ask_ref, query_ref, table_ref, key_ref, value_ref, mix_ref, stat_ref, counts):
+def attend_kernel(
+    me_ref, own_ref, asks_ref, table_ref, key_ref, value_ref, mix_ref, stat_ref, counts, ask_ref
+):
     step = pl.program_id(0)
     slots = table_ref.shape[0]
     pages = counts.shape[1] // PAGE
 
     @pl.when(step == 0)
     def _():
+        away = slots - LOCAL
+        code = asks_ref[:, D:].astype(jnp.int32)
+        sender = lax.broadcasted_iota(jnp.int32, (code.shape[0], 1), 0) // MOVED
+        each = away // (code.shape[0] // MOVED)
+        slot = jnp.where(code[:, 2:3] == me_ref[0], sender * each + code[:, 3:4], -1)
+        take = lax.broadcasted_iota(jnp.int32, (code.shape[0], away), 1) == slot
+        take = jnp.where(take, 1.0, 0.0).astype(BF)
+        ask_ref[:LOCAL, :] = own_ref[...].astype(F32)
+        ask_ref[LOCAL:, :] = lax.dot_general(
+            take, asks_ref[...], (((0,), (0,)), ((), ())), preferred_element_type=F32
+        )
         lengths = ask_ref[:, D:].astype(jnp.int32)
         full, rest = lengths[:, 0:1], lengths[:, 1:2]
         table = table_ref[...]
@@ -73,7 +88,8 @@
     rows = []
     for j in range(2 * GROUP):
         side, chunk, half = j // GROUP, j // 2, j % 2
-        part = query_ref[:, chunk * LANES : (chunk + 1) * LANES].astype(F32) * (1.0 / math.sqrt(HEAD))
+        at = pl.multiple_of(step * (2 * GROUP * HEAD) + chunk * LANES, LANES)
+        part = ask_ref[:, pl.ds(at, LANES)] * (1.0 / math.sqrt(HEAD))
         if side != half:
             part = pltpu.roll(part, HEAD, 1)
         rows.append(jnp.where((lane < HEAD) == (side == 0), part, 0.0).astype(BF))
@@ -111,16 +127,17 @@
         mix_ref[:, chunk * LANES : (chunk + 1) * LANES] = jnp.where(lane < HEAD, halves[0], halves[1])
 
 
-def attend(ask, table, pool):
-    slots = ask.shape[0]
+def attend(me, own, asks, table, pool):
+    slots = table.shape[0]
     tokens = pool.shape[0]
     width = 2 * GROUP * HEAD
     return pl.pallas_call(
         attend_kernel,
         grid=(PAIRS,),
         in_specs=[
-            pl.BlockSpec((slots, WIDE), lambda s: (0, 0)),
-            pl.BlockSpec((slots, width), lambda s: (0, s)),
+            smem(),
+            pl.BlockSpec(own.shape, lambda s: (0, 0)),
+            pl.BlockSpec(asks.shape, lambda s: (0, 0)),
             pl.BlockSpec((slots, NPAGE), lambda s: (0, 0)),
             pl.BlockSpec((tokens, LANES), lambda s: (0, s)),
             pl.BlockSpec((tokens, LANES), lambda s: (0, PAIRS + s)),
@@ -133,11 +150,11 @@
             jax.ShapeDtypeStruct((slots, D), F32),
             jax.ShapeDtypeStruct((slots, LANES), F32),
         ],
-        scratch_shapes=[pltpu.VMEM((slots, tokens), F32)],
+        scratch_shapes=[pltpu.VMEM((slots, tokens), F32), pltpu.VMEM((slots, WIDE), F32)],
         compiler_params=pltpu.CompilerParams(vmem_limit_bytes=48 * 1024 * 1024),
-        cost_estimate=cost(10**9, 24 * 10**6),
+        cost_estimate=cost(7 * 10**9, 10**5),
         name="attend",
-    )(ask, ask, table, pool, pool)
+    )(me, own, asks, table, pool, pool)
 
 
 def stream_kernel(
@@ -243,77 +260,77 @@
             pltpu.SemaphoreType.DMA((sum(blocks for blocks, _ in pieces),)),
         ],
         compiler_params=pltpu.CompilerParams(vmem_limit_bytes=48 * 1024 * 1024),
-        cost_estimate=cost(2 * 10**9, 24 * 10**6),
+        cost_estimate=cost(8 * 10**9, 10**5),
         name="stream",
     )(chosen, at, queries, fresh, mix, stat, back, prefill, residual, gain, router, routes, *parts)
 
 
-def expert_kernel(shards, place_ref, first_ref, second_ref, third_ref, *rest):
-    weights, rest = rest[: 2 * shards], rest[2 * shards :]
-    keep_ref, away_ref, rows_ref, held_ref, sems = rest
-    part = D // shards
-    one = first_ref.shape[0]
-    copies = []
-    for n in range(2 * shards):
-        at = pl.multiple_of(place_ref[n % shards] * part, LANES)
-        copy = pltpu.make_async_copy(
-            weights[n], held_ref.at[n // shards, pl.ds(at, part)], sems.at[n]
-        )
-        copy.start()
-        copies.append(copy)
-    rows_ref[:one, :] = first_ref[...]
-    rows_ref[one : 2 * one, :] = second_ref[...]
-    rows_ref[2 * one :, :] = third_ref[...]
+def hidden_kernel(place_ref, first_ref, second_ref, mine_ref, other_ref, hidden_ref, share_ref, rows_ref):
+    rows = first_ref.shape[0]
+    rows_ref[:rows, :] = first_ref[...]
+    rows_ref[rows:, :] = second_ref[...]
     gates = rows_ref[:, D:].astype(F32)
     gates = gates + pltpu.roll(gates, 64, 1)
     lane = lax.broadcasted_iota(jnp.int32, gates.shape, 1)
+    shares = []
+    for side, held_ref in enumerate((mine_ref, other_ref)):
+        named = jnp.where(lane == place_ref[side], gates, 0.0)
+        shares.append(jnp.sum(named, axis=1, keepdims=True))
+        pair = jnp.dot(rows_ref[:, :D], held_ref[...], preferred_element_type=F32)
+        gate = pair[:, :FF]
+        hidden_ref[:, side * FF : (side + 1) * FF] = (
+            gate / (1.0 + jnp.exp(-gate)) * pair[:, FF:]
+        ).astype(BF)
+    share_ref[...] = jnp.where(lane == 0, shares[0], shares[1])
+
+
+def make_hidden(place, first, second, mine, other):
+    rows = 2 * first.shape[0]
+    return pl.pallas_call(
+        hidden_kernel,
+        in_specs=[smem()] + [vmem()] * 4,
+        out_specs=[vmem()] * 2,
+        out_shape=[
+            jax.ShapeDtypeStruct((rows, 2 * FF), BF),
+            jax.ShapeDtypeStruct((rows, LANES), F32),
+        ],
+        scratch_shapes=[pltpu.VMEM((rows, WIDE), BF)],
+        compiler_params=pltpu.CompilerParams(vmem_limit_bytes=28 * 1024 * 1024),
+        cost_estimate=cost(HIDDEN_COST, 10**5),
+        name="hidden",
+    )(place, first, second, mine, other)
+
+
+def down_kernel(hidden_ref, share_ref, mine_ref, other_ref, keep_ref, away_ref):
     total = None
-    for side in range(2):
-        for copy in copies[side * shards : (side + 1) * shards]:
-            copy.wait()
-        pair = jnp.dot(
-            rows_ref[:, :D], held_ref[side, :, : 2 * FF], preferred_element_type=F32
-        )
-        gate = pair[:, :FF]
-        hidden = (gate / (1.0 + jnp.exp(-gate)) * pair[:, FF:]).astype(BF)
-        share = jnp.sum(
-            jnp.where(lane == place_ref[shards + side], gates, 0.0), axis=1, keepdims=True
-        )
+    for side, held_ref in enumerate((mine_ref, other_ref)):
         made = lax.dot_general(
-            hidden,
-            held_ref[side, :, 2 * FF :],
+            hidden_ref[:, side * FF : (side + 1) * FF],
+            held_ref[...],
             (((1,), (1,)), ((), ())),
             preferred_element_type=F32,
         )
-        made = share * made.astype(BF).astype(F32)
+        made = share_ref[:, side : side + 1] * made.astype(BF).astype(F32)
         total = made if total is None else total + made
-    keep_ref[...] = total[: 2 * one].astype(BF)
-    away_ref[...] = total[2 * one :].astype(BF)
-
-
-def run_experts(place, first, second, third, weights):
-    shards = len(weights) // 2
-    one = first.shape[0]
+    rows = keep_ref.shape[0]
+    keep_ref[...] = total[:rows].astype(BF)
+    away_ref[...] = total[rows:].astype(BF)
+
+
+def make_down(hidden, share, mine, other):
+    rows = hidden.shape[0]
     return pl.pallas_call(
-        functools.partial(expert_kernel, shards),
-        in_specs=[smem()]
-        + [vmem()] * 3
-        + [pl.BlockSpec(memory_space=pl.ANY)] * (2 * shards),
+        down_kernel,
+        in_specs=[vmem()] * 4,
         out_specs=[vmem()] * 2,
-        out_shape=[jax.ShapeDtypeStruct((2 * one, D), BF)] * 2,
-        scratch_shapes=[
-            pltpu.VMEM((4 * one, WIDE), BF),
-            pltpu.VMEM((2, D, 3 * FF), BF),
-            pltpu.SemaphoreType.DMA((2 * shards,)),
-        ],
-        compiler_params=pltpu.CompilerParams(vmem_limit_bytes=52 * 1024 * 1024),
-        cost_estimate=cost(5 * 10**9, 12 * 10**6),
-        name="experts",
-    )(place, first, second, third, *weights)
-
-
-def pack_kernel(slot_ref, gate_ref, down_ref, *rest):
-    outs, (held_ref, sems) = rest[:-2], rest[-2:]
+        out_shape=[jax.ShapeDtypeStruct((rows // 2, D), BF)] * 2,
+        compiler_params=pltpu.CompilerParams(vmem_limit_bytes=28 * 1024 * 1024),
+        cost_estimate=cost(DOWN_COST, 10**5),
+        name="down",
+    )(hidden, share, mine, other)
+
+
+def pack_kernel(gate_ref, down_ref, pair_out, down_out):
     depth, experts = gate_ref.shape[:2]
     step = 16
 
@@ -323,33 +340,21 @@
         gate = gate_ref[at]
         down = down_ref[at]
         for e in range(experts):
-            held_ref[e, at, : 2 * FF] = gate[:, e, :]
-            held_ref[e, at, 2 * FF :] = down[:, e, :]
-
-    copies = []
-    for k, out in enumerate(outs):
-        copy = pltpu.make_async_copy(held_ref.at[slot_ref[k]], out, sems.at[k])
-        copy.start()
-        copies.append(copy)
-    for copy in copies:
-        copy.wait()
-
-
-def pack_experts(slots, gate_up, down_proj):
+            pair_out[e, at, :] = gate[:, e, :]
+            down_out[e, at, :] = down[:, e, :]
+
+
+def pack_experts(gate_up, down_proj):
     depth, experts = gate_up.shape[:2]
     return pl.pallas_call(
         pack_kernel,
-        in_specs=[smem()] + [vmem()] * 2,
-        out_specs=[pl.BlockSpec(memory_space=pl.ANY)] * experts,
-        out_shape=[jax.ShapeDtypeStruct((depth, 3 * FF), BF)] * experts,
-        scratch_shapes=[
-            pltpu.VMEM((experts, depth, 3 * FF), BF),
-            pltpu.SemaphoreType.DMA((experts,)),
-        ],
+        in_specs=[vmem()] * 2,
+        out_specs=[vmem()] * 2,
+        out_shape=[jax.ShapeDtypeStruct((experts, depth, n * FF), BF) for n in (2, 1)],
         compiler_params=pltpu.CompilerParams(vmem_limit_bytes=32 * 1024 * 1024),
-        cost_estimate=cost(10**6, 10 * 10**6),
+        cost_estimate=cost(7 * 10**9, 10**5),
         name="pack",
-    )(slots, gate_up, down_proj)
+    )(gate_up, down_proj)
 
 
 def swap(x, axis, how):
@@ -360,46 +365,67 @@
     return j ^ (2 if j % 2 == 0 else 4)
 
 
+def beside(j):
+    return j ^ 1
+
+
 def far(j):
     return j ^ (4 if j % 2 == 0 else 2)
 
 
-def exchange_experts(gate_up, down_proj):
-    planes = lax.axis_size("gx")
-    row = lax.axis_index("gx")
-    slots = jnp.stack([row ^ k for k in range(planes)]).astype(jnp.int32)
-    blocks = pack_experts(slots, gate_up, down_proj)
-    blocks = [
-        swap(block, "gx", lambda i, k=k: i ^ k) if k else block for k, block in enumerate(blocks)
-    ]
-    return blocks + [swap(block, "gy", lambda j: j ^ 1) for block in blocks]
-
-
-def swapped_experts(send, stream, gate_up, down_proj):
+def exchange(packed):
+    whole = lax.all_to_all(packed, "gx", split_axis=0, concat_axis=0, tiled=True)
+    return whole.reshape(-1, packed.shape[2])
+
+
+def after(x, *others):
+    return lax.optimization_barrier((x, others))[0]
+
+
+def swapped_experts(send, stream, pair, down):
     planes = lax.axis_size("gx")
     row, column = lax.axis_index("gx"), lax.axis_index("gy")
-    weights = exchange_experts(gate_up, down_proj)
-    place = jnp.stack(
-        [row ^ k for k in range(planes)]
-        + [column * planes + row, (column ^ 1) * planes + row]
-    ).astype(jnp.int32)
+    place = jnp.stack([column * planes + row, beside(column) * planes + row]).astype(jnp.int32)
     rows = send.shape[0]
-    chunks = []
-    for k in range(planes):
-        mine = swap(send, "gx", lambda i, k=k: i ^ k) if k else send
-        second = swap(mine, "gy", near)
-        third = swap(jnp.concatenate([mine, second], axis=0), "gy", far)
-        chunks.append((mine, second, third))
-    result = stream
-    for k in reversed(range(planes)):
-        keep, away = run_experts(place, *chunks[k], weights)
-        arrived = swap(away, "gy", far)
-        total = keep.astype(F32) + arrived.astype(F32)
-        arrived = swap(total[rows:].astype(BF), "gy", near)
-        total = total[:rows] + arrived.astype(F32)
-        if k:
-            total = swap(total.astype(BF), "gx", lambda i, k=k: i ^ k).astype(F32)
-        result = result + total
+    across = lambda x, k: swap(x, "gx", lambda i: i ^ k)
+    firsts = [jnp.concatenate([send, swap(send, "gy", near)], axis=0)]
+    moved = [across(after(send, firsts[0]) if k == 1 else send, k) for k in range(1, planes)]
+    other_pair = swap(after(pair, firsts[0]), "gy", beside)
+    down = exchange(after(down, *moved))
+    firsts += [jnp.concatenate([mine, swap(mine, "gy", near)], axis=0) for mine in moved]
+    chunks = [[first, swap(first, "gy", far)] for first in firsts]
+    hidden = []
+    for chunk in chunks:
+        chunk = after(chunk, *hidden[-1:])
+        hidden.append(make_hidden(place, *chunk, pair, other_pair))
+    down, hidden = lax.optimization_barrier((down, hidden))
+    other_down = swap(down, "gy", beside)
+    order = list(reversed(range(planes)))
+    made, last = {}, ()
+    for k in order:
+        made[k] = make_down(*after(hidden[k], *last), down, other_down)
+        last = made[k]
+    arrived = {k: swap(made[k][1], "gy", far) for k in order}
+    total, ends = {}, {}
+    for n in range(planes + 2):
+        if n < planes:
+            k = order[n]
+            keep, came = after((made[k][0], arrived[k]), *last)
+            total[k] = keep.astype(F32) + came.astype(F32)
+            send_on = total[k][rows:].astype(BF)
+            last = (send_on,)
+            ends[k] = swap(send_on, "gy", near)
+        if 1 <= n <= planes:
+            k = order[n - 1]
+            keep, came = after((total[k][:rows], ends[k]), *last)
+            total[k] = keep + came.astype(F32)
+            if k:
+                send_on = total[k].astype(BF)
+                last = (send_on,)
+                ends[k] = across(send_on, k)
+    result = stream + total[0]
+    for k in range(1, planes):
+        result = result + ends[k].astype(F32)
     return result
 
 
@@ -446,19 +472,22 @@
     return jnp.zeros((1,), jnp.int32), [whole], ((1, whole.shape[0]),)
 
 
-def swap_out(out_weight):
+def start_out(out_weight):
+    planes, columns = lax.axis_size("gx"), lax.axis_size("gy")
+    share = out_weight.shape[0] // columns
+    mine = lax.dynamic_slice_in_dim(out_weight, lax.axis_index("gy") * share, share, axis=0)
+    return [swap(mine, "gx", lambda i, k=k: i ^ k) for k in range(1, planes)]
+
+
+def swap_out(out_weight, first):
     planes, columns = lax.axis_size("gx"), lax.axis_size("gy")
     row, column = lax.axis_index("gx"), lax.axis_index("gy")
     depth = out_weight.shape[0]
     share = depth // columns
-    mine = lax.dynamic_slice_in_dim(out_weight, column * share, share, axis=0)
-    first = jnp.concatenate(
-        [swap(mine, "gx", lambda i, k=k: i ^ k) for k in range(1, planes)], axis=0
-    )
     second = swap(first, "gy", near)
     third = swap(jnp.concatenate([first, second], axis=0), "gy", far)
     parts = [first, second, third]
-    parts = [out_weight] + parts + [swap(part, "gy", lambda j: j ^ 1) for part in parts]
+    parts = [out_weight] + parts + [swap(part, "gy", beside) for part in parts]
     near_of = lambda j: jnp.where(j % 2 == 0, j ^ 2, j ^ 4)
     far_of = lambda j: jnp.where(j % 2 == 0, j ^ 4, j ^ 2)
     at = [row * depth]
@@ -492,28 +521,36 @@
     pool = cache_pool.reshape(-1, cache_pool.shape[2])
     matches = (anchor[:, None] == jnp.arange(columns, dtype=jnp.int32)[None, :]).astype(jnp.int32)
     earlier = jnp.sum((jnp.cumsum(matches, axis=0) - 1) * matches, axis=1)
-    chosen = anchor * slot_count + earlier
-    lengths = jnp.stack([cache_len // PAGE, cache_len % PAGE], axis=1).astype(BF)
-    ask = jnp.concatenate([queries, jnp.pad(lengths, ((0, 0), (0, LANES - 2)))], axis=1)
     slots = columns * slot_count
-    where = (chosen[None, :] == jnp.arange(slots, dtype=jnp.int32)[:, None]).astype(BF)
-    outgoing = jnp.dot(where, ask[LOCAL:], preferred_element_type=F32).astype(BF)
-    incoming = lax.all_to_all(
-        outgoing.reshape(columns, slot_count, WIDE), "gy", split_axis=0, concat_axis=0, tiled=True
-    ).reshape(slots, WIDE)
+    column = lax.axis_index("gy")
+    chosen = anchor * slots + column * slot_count + earlier
+    extra = jnp.stack([cache_len[LOCAL:] // PAGE, cache_len[LOCAL:] % PAGE, anchor, earlier], axis=1)
+    extra = jnp.pad(extra.astype(BF), ((0, 0), (0, LANES - 4)))
+    asks = lax.all_gather(
+        jnp.concatenate([queries[LOCAL:], extra], axis=1), "gy", axis=0, tiled=True
+    )
+    extra = jnp.stack([cache_len[:LOCAL] // PAGE, cache_len[:LOCAL] % PAGE], axis=1)
+    extra = jnp.pad(extra.astype(BF), ((0, 0), (0, LANES - 2)))
+    own = jnp.concatenate([queries[:LOCAL], extra], axis=1)
+    planes = lax.axis_size("gx")
+    swapped = columns == 8 and planes & (planes - 1) == 0 and gate_up.shape[1] == planes
+    if swapped:
+        out_parts = start_out(out_weight)
+        pair, down = pack_experts(gate_up, down_proj)
+        out_parts, pair, down = lax.optimization_barrier((out_parts, pair, down))
+        pair = exchange(pair)
+        out_parts = swap_out(out_weight, jnp.concatenate(out_parts, axis=0))
+    else:
+        out_parts = gather_out(out_weight)
     mix, stat = attend(
-        jnp.concatenate([ask[:LOCAL], incoming], axis=0),
+        column.astype(jnp.int32).reshape(1),
+        own,
+        asks,
         jnp.concatenate([local_pages, push_pages], axis=0),
         pool,
     )
-    answers = jnp.concatenate([mix[LOCAL:], stat[LOCAL:]], axis=1).reshape(
-        columns, slot_count, WIDE
-    )
-    back = lax.all_to_all(answers, "gy", split_axis=0, concat_axis=0, tiled=True).reshape(
-        slots, WIDE
-    )
-    planes = lax.axis_size("gx")
-    swapped = columns == 8 and planes & (planes - 1) == 0 and gate_up.shape[1] == planes
+    answers = jnp.concatenate([mix[LOCAL:], stat[LOCAL:]], axis=1)
+    back = lax.all_gather(answers, "gy", axis=0, tiled=True)
     attended, stream, send = make_stream(
         chosen,
         queries,
@@ -523,13 +560,13 @@
         back,
         prefill_attn,
         residual,
-        swap_out(out_weight) if swapped else gather_out(out_weight),
+        out_parts,
         norm_gain.reshape(1, D),
         jnp.pad(router, ((0, 0), (0, LANES - EXPERTS))),
         routes,
     )
     if swapped:
-        layer_out = swapped_experts(send, stream, gate_up, down_proj)
+        layer_out = swapped_experts(send, stream, pair, down)
     else:
         layer_out = gathered_experts(send, stream, routes, gate_up, down_proj)
     return (attended, layer_out)

time: 335 us -> 267 us (0.80)
  waiting for transfers between devices: 204 us -> 87 us
  blocking collectives: 0 us -> 26.4 us
  local copies, waits for them, and re-layouts: 12.3 us -> 30.3 us
  starting transfers between devices: 49.8 us -> 61.6 us
  Pallas kernels: 60.5 us -> 55.4 us
    ppermute x37 -> x32, waiting for transfers between devices: 200 us -> 84.3 us  [swap(): lax.ppermute(x, axis, [(i, how(i)) for i in range(lax.axis_size(axis))])]
    all_gather x0 -> x2, blocking collectives: none -> 26.4 us  [the longest x1 15.8 us: body(): lax.all_gather(jnp.concatenate([queries[LOCAL:], extra], axis=1), 'gy', a...]
    unnamed x50 -> x80, local copies, waits for them, and re-layouts: 9.18 us -> 23.5 us
    all_to_all x2, starting transfers between devices: 7.79 us -> 15.6 us  [exchange(): lax.all_to_all(packed, 'gx', split_axis=0, concat_axis=0, tiled=True)]
    pallas_call x6 -> x10, Pallas kernels: 54.3 us -> 48.1 us  [the longest x4 26.4 us: make_hidden(): pl.pallas_call(hidden_kernel, in_specs=[smem()] + [vmem()] * 4, out_specs...]
    concatenate x1 -> x5, local copies, waits for them, and re-layouts: 0.01 us -> 4.73 us  [the longest x3 4.68 us: swapped_experts(): jnp.concatenate([mine, swap(mine, 'gy', near)], axis=0)]
    ppermute x37 -> x32, starting transfers between devices: 42 us -> 46 us  [swap(): lax.ppermute(x, axis, [(i, how(i)) for i in range(lax.axis_size(axis))])]
  transfers between devices with their start and end apart: 39 -> 34, of which waited for: 16 -> 12; matrix products, arithmetic and copies ran while one was open for 2% -> 5% of each run, Pallas kernels for 18% -> 20%
where the time goes in v3:
time: 267 us; the launch traced here: 266 us
  waiting for transfers between devices  87 us (33%)
  starting transfers between devices  61.6 us (23%)
  Pallas kernels  55.4 us (21%)
  local copies, waits for them, and re-layouts  30.3 us (11%)
  blocking collectives  26.4 us (10%)
  other arithmetic  4.24 us (2%)
    ppermute x32, waiting for transfers between devices, swap(): lax.ppermute(x, axis, [(i, how(i)) for i in range(lax.axis_size(axis))])  84.3 us
    ppermute x32, starting transfers between devices, swap(): lax.ppermute(x, axis, [(i, how(i)) for i in range(lax.axis_size(axis))])  46 us
    pallas_call x4, Pallas kernels, make_hidden(): pl.pallas_call(hidden_kernel, in_specs=[smem()] + [vmem()] * 4, out_specs...  26.4 us
    unnamed x80, local copies, waits for them, and re-layouts  23.5 us
    all_gather x1, blocking collectives, body(): lax.all_gather(jnp.concatenate([queries[LOCAL:], extra], axis=1), 'gy', a...  15.8 us
    all_to_all x2, starting transfers between devices, exchange(): lax.all_to_all(packed, 'gx', split_axis=0, concat_axis=0, tiled=True)  15.6 us
    all_gather x1, blocking collectives, body(): back = lax.all_gather(answers, 'gy', axis=0, tiled=True)  10.5 us
    pallas_call x1, Pallas kernels, pack_experts(): pl.pallas_call(pack_kernel, in_specs=[vmem()] * 2, out_specs=[vmem()] * 2...  8.01 us
  transfers between devices with their start and end apart: 34, of which 12 were waited for; matrix products, arithmetic and copies ran while one was open for 5% of the time, Pallas kernels for 20%

profile of v3, /device:TPU:0, one launch (start us, length us, event | category | flops | bytes accessed | tf_op | source)
XLA Modules:
  0.0 266.1 jit_solution(11269566552113491585)
XLA Ops:
  1.6 3.1 %collective-permute-start = (bf16[48,1536]{1,0:T(8,128)(2,1)S(1)}, bf16[48,1536]{1,0:T(8,128)(2,1)S(1)}, u32[]{:S(2)}, u32[]{:S(2)}) collective-permute-start(bf16[48,1536]{1,0:T(8,128)(2,1)S(1)} %constant_dynamic-slice_fusion), channel_id=1, source_target_pairs={{0,8},{8,0},{16,24},{24,16},{1,9},{9,1},{17,25},{25,17},{2,10},{10... | collective-permute-start | bytes 442376 | tf_op jit(solution)/shard_map/ppermute | solution.py:361
  4.7 2.6 collective-permute-start.1
  8.8 1.9 copy-done.18
  12.1 8.0 %pack.1 = (bf16[4,384,1024]{2,1,0:T(8,128)(2,1)}, bf16[4,384,512]{2,1,0:T(8,128)(2,1)}) custom-call(bf16[384,4,1024]{2,1,0:T(4,128)(2,1)S(1)} %copy-done.18, bf16[384,4,512]{2,1,0:T(4,128)(2,1)S(1)} %copy-done.19), custom_call_target="tpu_custom_call" | custom-call | flops 7000000000 | bytes 100000 | tf_op jit(solution)/shard_map/pack/pallas_call | solution.py:349
  20.5 5.2 %all-to-all-start.1 = ((bf16[4,384,1024]{2,1,0:T(8,128)(2,1)}), bf16[4,384,1024]{2,1,0:T(8,128)(2,1)}, u32[]{:S(2)}, u32[]{:S(2)}) async-start(bf16[4,384,1024]{2,1,0:T(8,128)(2,1)} %get-tuple-element.89), calls=%async_computation.1 | async-start | bytes 6291456 | tf_op jit(solution)/shard_map/all_to_all | solution.py:377
  25.7 1.6 collective-permute-start.3
  27.3 6.8 %collective-permute-done.3.rest_2_ = bf16[144,1536]{1,0:T(8,128)(2,1)S(1)} collective-permute-done((bf16[144,1536]{1,0:T(8,128)(2,1)S(1)}, bf16[144,1536]{1,0:T(8,128)(2,1)S(1)}, u32[]{:S(2)}, u32[]{:S(2)}) %collective-permute-start.3) | collective-permute-done | bytes 442400 | tf_op jit(solution)/shard_map/ppermute | solution.py:361
  34.2 1.6 collective-permute-start.4
  36.2 15.8 %all_gather.6.asks_ref = bf16[64,1664]{1,0:T(8,128)(2,1)S(1)} all-gather(bf16[8,1664]{1,0:T(8,128)(2,1)S(1)} %pad_maximum_fusion.2), channel_id=1, replica_groups=mesh['gx'=4,'gy'=8] {'gy'}, dimensions={0}, use_global_device_ids=true | all-gather | bytes 239616 | tf_op jit(solution)/shard_map/all_gather | solution.py:529
  53.1 2.2 copy-done.17
  55.2 5.9 %attend.1 = (f32[24,1536]{1,0:T(8,128)S(1)}, f32[24,128]{1,0:T(8,128)S(1)}) custom-call(s32[1]{0:T(128)} %bitcast.25.me_ref, bf16[8,1664]{1,0:T(8,128)(2,1)S(1)} %fusion.1.own_ref, bf16[64,1664]{1,0:T(8,128)(2,1)S(1)} %all_gather.6.asks_ref, s32[24,32]{1,0:T(8,128)S(1)} %pad_add_fusion.table_ref, bf16[2048,1024]{1,0:T(8,128)(2,1)S(1)} %bitcast.48, ...), custom_call_target="tpu_custom_call" | custom-call | flops 7000000000 | bytes 100000 | tf_op jit(solution)/shard_map/attend/pallas_call | solution.py:134
  61.9 10.5 %all_gather.7.back_ref = f32[128,1664]{1,0:T(8,128)S(1)} all-gather(f32[16,1664]{1,0:T(8,128)S(1)} %pad_maximum_fusion.1), channel_id=1, replica_groups=mesh['gx'=4,'gy'=8] {'gy'}, dimensions={0}, use_global_device_ids=true | all-gather | bytes 958464 | tf_op jit(solution)/shard_map/all_gather | solution.py:553
  77.4 7.3 %stream.1 = (bf16[16,1536]{1,0:T(8,128)(2,1)}, f32[128,1536]{1,0:T(8,128)S(1)}, bf16[128,1664]{1,0:T(8,128)(2,1)S(1)}) custom-call(s32[8]{0:T(128)S(1)} %get-tuple-element.155.chosen_ref, s32[25]{0:T(128)S(1)} %stack.141.at_ref, bf16[16,1536]{1,0:T(8,128)(2,1)S(1)} %copy-done.16, bf16[16,1024]{1,0:T(8,128)(2,1)S(1)} %copy-done.26, ...), custom_call_target="tpu_custom_call" | custom-call | flops 8000000000 | bytes 100000 | tf_op jit(solution)/shard_map/stream/pallas_call | solution.py:248
  85.4 7.6 %collective-permute-done.8 = bf16[128,1664]{1,0:T(8,128)(2,1)S(1)} collective-permute-done((bf16[128,1664]{1,0:T(8,128)(2,1)S(1)}, bf16[128,1664]{1,0:T(8,128)(2,1)S(1)}, u32[]{:S(2)}, u32[]{:S(2)}) %collective-permute-start.8) | collective-permute-done | bytes 426016 | tf_op jit(solution)/shard_map/ppermute | solution.py:361
  93.0 2.7 %all-to-all-done.1 = bf16[4,384,1024]{2,1,0:T(8,128)(2,1)} async-done(((bf16[4,384,1024]{2,1,0:T(8,128)(2,1)}), bf16[4,384,1024]{2,1,0:T(8,128)(2,1)}, u32[]{:S(2)}, u32[]{:S(2)}) %all-to-all-start.1) | async-done | bytes 3145760 | tf_op jit(solution)/shard_map/all_to_all | solution.py:377
  97.5 1.6 collective-permute-start.9
  99.3 1.5 collective-permute-start.12
  100.8 25.4 %collective-permute-done.10 = bf16[128,1664]{1,0:T(8,128)(2,1)} collective-permute-done((bf16[128,1664]{1,0:T(8,128)(2,1)S(1)}, bf16[128,1664]{1,0:T(8,128)(2,1)}, u32[]{:S(2)}, u32[]{:S(2)}) %collective-permute-start.10) | collective-permute-done | bytes 426016 | tf_op jit(solution)/shard_map/ppermute | solution.py:361
  128.2 1.8 constant_dynamic-update-slice_fusion.8
  131.5 1.8 constant_dynamic-update-slice_fusion.10
  133.3 10.4 %all-to-all-start = ((bf16[4,384,512]{2,1,0:T(8,128)(2,1)}), bf16[4,384,512]{2,1,0:T(8,128)(2,1)S(1)}, u32[]{:S(2)}, u32[]{:S(2)}) async-start(bf16[4,384,512]{2,1,0:T(8,128)(2,1)} %get-tuple-element.86), calls=%async_computation | async-start | bytes 3145728 | tf_op jit(solution)/shard_map/all_to_all | solution.py:377
  145.8 1.5 collective-permute-start.15
  147.3 1.8 constant_dynamic-update-slice_fusion.7.first_ref
  149.7 1.8 constant_dynamic-update-slice_fusion.9.first_ref
  151.5 1.5 collective-permute-start.19
  153.0 6.6 %hidden.4 = (bf16[512,1024]{1,0:T(8,128)(2,1)S(1)}, f32[512,128]{1,0:T(8,128)S(1)}) custom-call(s32[2]{0:T(128)S(1)} %pad_add_fusion.1.place_ref, bf16[256,1664]{1,0:T(8,128)(2,1)S(1)} %copy-done.15, bf16[256,1664]{1,0:T(8,128)(2,1)} %collective-permute-done.12.second_ref, bf16[1536,1024]{1,0:T(8,128)(2,1)} %bitcast.36.mine_ref, ...), custom_call_target="tpu_custom_call" | custom-call | flops 6000000000 | bytes 100000 | tf_op jit(solution)/shard_map/hidden/pallas_call | solution.py:289
  160.4 6.4 %hidden.5 = (bf16[512,1024]{1,0:T(8,128)(2,1)S(1)}, f32[512,128]{1,0:T(8,128)S(1)}) custom-call(s32[2]{0:T(128)S(1)} %pad_add_fusion.1.place_ref, bf16[256,1664]{1,0:T(8,128)(2,1)S(1)} %constant_dynamic-update-slice_fusion.5.first_ref, bf16[256,1664]{1,0:T(8,128)(2,1)S(1)} %collective-permute-done.15.second_ref, bf16[1536,1024]{1,0:T(8,128)(2,1)} %bitcast.36.mine_ref, ...), custom_call_target="tpu_custom_call" | custom-call | flops 6000000000 | bytes 100000 | tf_op jit(solution)/shard_map/hidden/pallas_call | solution.py:289
  168.5 6.6 %hidden.6 = (bf16[512,1024]{1,0:T(8,128)(2,1)S(1)}, f32[512,128]{1,0:T(8,128)S(1)}) custom-call(s32[2]{0:T(128)S(1)} %pad_add_fusion.1.place_ref, bf16[256,1664]{1,0:T(8,128)(2,1)} %constant_dynamic-update-slice_fusion.7.first_ref, bf16[256,1664]{1,0:T(8,128)(2,1)S(1)} %collective-permute-done.17.second_ref, bf16[1536,1024]{1,0:T(8,128)(2,1)} %bitcast.36.mine_ref, ...), custom_call_target="tpu_custom_call" | custom-call | flops 6000000000 | bytes 100000 | tf_op jit(solution)/shard_map/hidden/pallas_call | solution.py:289
  176.9 6.7 %hidden.7 = (bf16[512,1024]{1,0:T(8,128)(2,1)S(1)}, f32[512,128]{1,0:T(8,128)S(1)}) custom-call(s32[2]{0:T(128)S(1)} %pad_add_fusion.1.place_ref, bf16[256,1664]{1,0:T(8,128)(2,1)} %constant_dynamic-update-slice_fusion.9.first_ref, bf16[256,1664]{1,0:T(8,128)(2,1)S(1)} %collective-permute-done.19.second_ref, bf16[1536,1024]{1,0:T(8,128)(2,1)} %bitcast.36.mine_ref, ...), custom_call_target="tpu_custom_call" | custom-call | flops 6000000000 | bytes 100000 | tf_op jit(solution)/shard_map/hidden/pallas_call | solution.py:289
  185.2 3.4 %collective-permute-done.20.other_ref = bf16[1536,512]{1,0:T(8,128)(2,1)S(1)} collective-permute-done((bf16[1536,512]{1,0:T(8,128)(2,1)S(1)}, bf16[1536,512]{1,0:T(8,128)(2,1)S(1)}, u32[]{:S(2)}, u32[]{:S(2)}) %collective-permute-start.20) | collective-permute-done | bytes 1572896 | tf_op jit(solution)/shard_map/ppermute | solution.py:361
  190.8 2.1 down.4
  194.4 1.9 down.5
  197.0 1.9 down.6
  200.4 1.9 down.7
  202.9 2.1 collective-permute-done.23
  205.3 1.6 collective-permute-start.26
  206.9 10.8 %collective-permute-done.22 = bf16[256,1536]{1,0:T(8,128)(2,1)S(1)} collective-permute-done((bf16[256,1536]{1,0:T(8,128)(2,1)S(1)}, bf16[256,1536]{1,0:T(8,128)(2,1)S(1)}, u32[]{:S(2)}, u32[]{:S(2)}) %collective-permute-start.22) | collective-permute-done | bytes 786464 | tf_op jit(solution)/shard_map/ppermute | solution.py:361
  218.0 1.6 collective-permute-start.24
  219.7 3.9 %collective-permute-start.31 = (bf16[128,1536]{1,0:T(8,128)(2,1)S(1)}, bf16[128,1536]{1,0:T(8,128)(2,1)S(1)}, u32[]{:S(2)}, u32[]{:S(2)}) collective-permute-start(bf16[128,1536]{1,0:T(8,128)(2,1)S(1)} %add_convert_fusion.2), channel_id=1, source_target_pairs={{0,24},{8,16},{16,8},{24,0},{1,25},{9,17},{17,9},{25,1},{2,26},{10... | collective-permute-start | bytes 1179656 | tf_op jit(solution)/shard_map/ppermute | solution.py:361
  223.6 6.7 %collective-permute-done.25 = bf16[256,1536]{1,0:T(8,128)(2,1)S(1)} collective-permute-done((bf16[256,1536]{1,0:T(8,128)(2,1)S(1)}, bf16[256,1536]{1,0:T(8,128)(2,1)S(1)}, u32[]{:S(2)}, u32[]{:S(2)}) %collective-permute-start.25) | collective-permute-done | bytes 786464 | tf_op jit(solution)/shard_map/ppermute | solution.py:361
  230.6 1.6 collective-permute-start.28
  232.3 5.0 %collective-permute-start.30 = (bf16[128,1536]{1,0:T(8,128)(2,1)S(1)}, bf16[128,1536]{1,0:T(8,128)(2,1)S(1)}, u32[]{:S(2)}, u32[]{:S(2)}) collective-permute-start(bf16[128,1536]{1,0:T(8,128)(2,1)S(1)} %add_convert_fusion.1), channel_id=1, source_target_pairs={{0,16},{8,24},{16,0},{24,8},{1,17},{9,25},{17,1},{25,9},{2,18},{10... | collective-permute-start | bytes 1179656 | tf_op jit(solution)/shard_map/ppermute | solution.py:361
  237.3 5.6 %collective-permute-done.21 = bf16[256,1536]{1,0:T(8,128)(2,1)S(1)} collective-permute-done((bf16[256,1536]{1,0:T(8,128)(2,1)S(1)}, bf16[256,1536]{1,0:T(8,128)(2,1)S(1)}, u32[]{:S(2)}, u32[]{:S(2)}) %collective-permute-start.21) | collective-permute-done | bytes 786464 | tf_op jit(solution)/shard_map/ppermute | solution.py:361
  243.2 1.6 collective-permute-start.27
  244.9 4.1 %collective-permute-start.29 = (bf16[128,1536]{1,0:T(8,128)(2,1)S(1)}, bf16[128,1536]{1,0:T(8,128)(2,1)S(1)}, u32[]{:S(2)}, u32[]{:S(2)}) collective-permute-start(bf16[128,1536]{1,0:T(8,128)(2,1)S(1)} %add_convert_fusion), channel_id=1, source_target_pairs={{0,8},{8,0},{16,24},{24,16},{1,9},{9,1},{17,25},{25,17},{2,10},{10... | collective-permute-start | bytes 1179656 | tf_op jit(solution)/shard_map/ppermute | solution.py:361
  249.0 2.0 collective-permute-done.27
  251.1 5.9 %collective-permute-done.30 = bf16[128,1536]{1,0:T(8,128)(2,1)S(1)} collective-permute-done((bf16[128,1536]{1,0:T(8,128)(2,1)S(1)}, bf16[128,1536]{1,0:T(8,128)(2,1)S(1)}, u32[]{:S(2)}, u32[]{:S(2)}) %collective-permute-start.30) | collective-permute-done | bytes 393248 | tf_op jit(solution)/shard_map/ppermute | solution.py:361
  256.9 8.0 %collective-permute-done.29 = bf16[128,1536]{1,0:T(8,128)(2,1)S(1)} collective-permute-done((bf16[128,1536]{1,0:T(8,128)(2,1)S(1)}, bf16[128,1536]{1,0:T(8,128)(2,1)S(1)}, u32[]{:S(2)}, u32[]{:S(2)}) %collective-permute-start.29) | collective-permute-done | bytes 393248 | tf_op jit(solution)/shard_map/ppermute | solution.py:361
  (163 shorter events, 35.0 us)
Async XLA Ops:
  1.6 18.9 %collective-permute-start = (bf16[48,1536]{1,0:T(8,128)(2,1)S(1)}, bf16[48,1536]{1,0:T(8,128)(2,1)S(1)}, u32[]{:S(2)}, u32[]{:S(2)}) collective-permute-start(bf16[48,1536]{1,0:T(8,128)(2,1)S(1)} %constant_dynamic-slice_fusion), channel_id=1, source_target_pairs={{0,8},{8,0},{16,24},{24,16},{1,9},{9,1},{17,25},{25,17},{2,10},{10... | collective-permute-start | bytes 442376 | tf_op jit(solution)/shard_map/ppermute | solution.py:361
  4.7 15.8 %collective-permute-start.1 = (bf16[48,1536]{1,0:T(8,128)(2,1)S(1)}, bf16[48,1536]{1,0:T(8,128)(2,1)S(1)}, u32[]{:S(2)}, u32[]{:S(2)}) collective-permute-start(bf16[48,1536]{1,0:T(8,128)(2,1)S(1)} %constant_dynamic-slice_fusion), channel_id=1, source_target_pairs={{0,16},{8,24},{16,0},{24,8},{1,17},{9,25},{17,1},{25,9},{2,18},{10... | collective-permute-start | bytes 442376 | tf_op jit(solution)/shard_map/ppermute | solution.py:361
  7.2 13.2 %collective-permute-start.2 = (bf16[48,1536]{1,0:T(8,128)(2,1)S(1)}, bf16[48,1536]{1,0:T(8,128)(2,1)S(1)}, u32[]{:S(2)}, u32[]{:S(2)}) collective-permute-start(bf16[48,1536]{1,0:T(8,128)(2,1)S(1)} %constant_dynamic-slice_fusion), channel_id=1, source_target_pairs={{0,24},{8,16},{16,8},{24,0},{1,25},{9,17},{17,9},{25,1},{2,26},{10... | collective-permute-start | bytes 442376 | tf_op jit(solution)/shard_map/ppermute | solution.py:361
  12.1 8.1 %copy-start.32 = (s32[8]{0:T(128)S(1)}, s32[8]{0:T(128)}, u32[]{:S(2)}) copy-start(s32[8]{0:T(128)} %param.20) | copy-start | bytes 100
  20.4 6.9 %copy-start.16 = (bf16[16,1536]{1,0:T(8,128)(2,1)S(1)}, bf16[16,1536]{1,0:T(8,128)(2,1)}, u32[]{:S(2)}) copy-start(bf16[16,1536]{1,0:T(8,128)(2,1)} %query_ref.1) | copy-start | bytes 147460
  20.5 75.2 %all-to-all-start.1 = ((bf16[4,384,1024]{2,1,0:T(8,128)(2,1)}), bf16[4,384,1024]{2,1,0:T(8,128)(2,1)}, u32[]{:S(2)}, u32[]{:S(2)}) async-start(bf16[4,384,1024]{2,1,0:T(8,128)(2,1)} %get-tuple-element.89), calls=%async_computation.1 | async-start | bytes 6291456 | tf_op jit(solution)/shard_map/all_to_all | solution.py:377
  25.7 26.4 %copy-start.31 = (s32[16,32]{1,0:T(8,128)S(1)}, s32[16,32]{1,0:T(8,128)}, u32[]{:S(2)}) copy-start(s32[16,32]{1,0:T(8,128)} %param.21) | copy-start | bytes 6148
  25.7 26.4 %copy-start.35 = (s32[8,32]{1,0:T(8,128)S(1)}, s32[8,32]{1,0:T(8,128)}, u32[]{:S(2)}) copy-start(s32[8,32]{1,0:T(8,128)} %param.19) | copy-start | bytes 3076
  25.7 8.4 %collective-permute-start.3 = (bf16[144,1536]{1,0:T(8,128)(2,1)S(1)}, bf16[144,1536]{1,0:T(8,128)(2,1)S(1)}, u32[]{:S(2)}, u32[]{:S(2)}) collective-permute-start(bf16[144,1536]{1,0:T(8,128)(2,1)S(1)} %constant_dynamic-update-slice_fusion.rest_1_), channel_id=1, source_target_pairs={{0,2},{1,5},{2,0},{3,7},{4,6},{5,1},{6,4},{7,3},{8,10},{9,13},{10,... | collective-permute-start | bytes 1327112 | tf_op jit(solution)/shard_map/ppermute | solution.py:361
  34.2 18.5 %collective-permute-start.4 = (bf16[288,1536]{1,0:T(8,128)(2,1)S(1)}, bf16[288,1536]{1,0:T(8,128)(2,1)S(1)}, u32[]{:S(2)}, u32[]{:S(2)}) collective-permute-start(bf16[288,1536]{1,0:T(8,128)(2,1)S(1)} %pad_maximum_fusion), channel_id=1, source_target_pairs={{0,4},{1,3},{2,6},{3,1},{4,0},{5,7},{6,2},{7,5},{8,12},{9,11},{10,... | collective-permute-start | bytes 2654216 | tf_op jit(solution)/shard_map/ppermute | solution.py:361
  52.1 20.4 %collective-permute-start.5 = (bf16[144,1536]{1,0:T(8,128)(2,1)S(1)}, bf16[144,1536]{1,0:T(8,128)(2,1)S(1)}, u32[]{:S(2)}, u32[]{:S(2)}) collective-permute-start(bf16[144,1536]{1,0:T(8,128)(2,1)S(1)} %constant_dynamic-update-slice_fusion.rest_1_), channel_id=1, source_target_pairs={{0,1},{1,0},{2,3},{3,2},{4,5},{5,4},{6,7},{7,6},{8,9},{9,8},{10,11... | collective-permute-start | bytes 1327112 | tf_op jit(solution)/shard_map/ppermute | solution.py:361
  52.5 20.7 %collective-permute-start.6 = (bf16[144,1536]{1,0:T(8,128)(2,1)S(1)}, bf16[144,1536]{1,0:T(8,128)(2,1)}, u32[]{:S(2)}, u32[]{:S(2)}) collective-permute-start(bf16[144,1536]{1,0:T(8,128)(2,1)S(1)} %collective-permute-done.3.rest_2_), channel_id=1, source_target_pairs={{0,1},{1,0},{2,3},{3,2},{4,5},{5,4},{6,7},{7,6},{8,9},{9,8},{10,11... | collective-permute-start | bytes 1327112 | tf_op jit(solution)/shard_map/ppermute | solution.py:361
  52.7 8.5 %copy-start.20 = (bf16[288,1536]{1,0:T(8,128)(2,1)}, bf16[288,1536]{1,0:T(8,128)(2,1)S(1)}, u32[]{:S(2)}) copy-start(bf16[288,1536]{1,0:T(8,128)(2,1)S(1)} %collective-permute-done.4.rest_3_) | copy-start | bytes 2654212
  52.7 20.6 %collective-permute-start.7 = (bf16[288,1536]{1,0:T(8,128)(2,1)S(1)}, bf16[288,1536]{1,0:T(8,128)(2,1)}, u32[]{:S(2)}, u32[]{:S(2)}) collective-permute-start(bf16[288,1536]{1,0:T(8,128)(2,1)S(1)} %collective-permute-done.4.rest_3_), channel_id=1, source_target_pairs={{0,1},{1,0},{2,3},{3,2},{4,5},{5,4},{6,7},{7,6},{8,9},{9,8},{10,11... | collective-permute-start | bytes 2654216 | tf_op jit(solution)/shard_map/ppermute | solution.py:361
  55.2 6.1 %copy-start.34 = (bf16[1536]{0:T(1024)(128)(2,1)S(1)}, bf16[1536]{0:T(1024)(128)(2,1)}, u32[]{:S(2)}) copy-start(bf16[1536]{0:T(1024)(128)(2,1)} %param.25) | copy-start | bytes 9220
  55.2 6.1 %copy-start.30 = (bf16[1536,32]{0,1:T(8,128)(2,1)S(1)}, bf16[1536,32]{0,1:T(8,128)(2,1)}, u32[]{:S(2)}) copy-start(bf16[1536,32]{0,1:T(8,128)(2,1)} %param.26) | copy-start | bytes 294916
  55.2 6.4 %copy-start.33 = (s32[128,8]{0,1:T(8,128)S(1)}, s32[128,8]{0,1:T(8,128)}, u32[]{:S(2)}) copy-start(s32[128,8]{0,1:T(8,128)} %param.27) | copy-start | bytes 12292
  61.2 12.1 %copy-start.26 = (bf16[16,1024]{1,0:T(8,128)(2,1)S(1)}, bf16[16,1024]{1,0:T(8,128)(2,1)}, u32[]{:S(2)}) copy-start(bf16[16,1024]{1,0:T(8,128)(2,1)} %fresh_ref.1) | copy-start | bytes 98308
  84.7 8.2 %collective-permute-start.8 = (bf16[128,1664]{1,0:T(8,128)(2,1)S(1)}, bf16[128,1664]{1,0:T(8,128)(2,1)S(1)}, u32[]{:S(2)}, u32[]{:S(2)}) collective-permute-start(bf16[128,1664]{1,0:T(8,128)(2,1)S(1)} %get-tuple-element.85), channel_id=1, source_target_pairs={{0,2},{1,5},{2,0},{3,7},{4,6},{5,1},{6,4},{7,3},{8,10},{9,13},{10,... | collective-permute-start | bytes 1277960 | tf_op jit(solution)/shard_map/ppermute | solution.py:361
  93.0 40.3 %copy-start.14 = (bf16[256,1664]{1,0:T(8,128)(2,1)}, bf16[256,1664]{1,0:T(8,128)(2,1)S(1)}, u32[]{:S(2)}) copy-start(bf16[256,1664]{1,0:T(8,128)(2,1)S(1)} %constant_dynamic-update-slice_fusion.3.first_ref) | copy-start | bytes 2555908
  95.7 57.3 %collective-permute-start.13 = (bf16[1536,1024]{1,0:T(8,128)(2,1)}, bf16[1536,1024]{1,0:T(8,128)(2,1)}, u32[]{:S(2)}, u32[]{:S(2)}) collective-permute-start(bf16[1536,1024]{1,0:T(8,128)(2,1)} %bitcast.36.mine_ref), channel_id=1, source_target_pairs={{0,1},{1,0},{2,3},{3,2},{4,5},{5,4},{6,7},{7,6},{8,9},{9,8},{10,11... | collective-permute-start | bytes 9437192 | tf_op jit(solution)/shard_map/ppermute | solution.py:361
  95.7 30.5 %collective-permute-start.10 = (bf16[128,1664]{1,0:T(8,128)(2,1)S(1)}, bf16[128,1664]{1,0:T(8,128)(2,1)}, u32[]{:S(2)}, u32[]{:S(2)}) collective-permute-start(bf16[128,1664]{1,0:T(8,128)(2,1)S(1)} %get-tuple-element.85), channel_id=1, source_target_pairs={{0,16},{8,24},{16,0},{24,8},{1,17},{9,25},{17,1},{25,9},{2,18},{10... | collective-permute-start | bytes 1277960 | tf_op jit(solution)/shard_map/ppermute | solution.py:361
  96.1 31.5 %collective-permute-start.11 = (bf16[128,1664]{1,0:T(8,128)(2,1)S(1)}, bf16[128,1664]{1,0:T(8,128)(2,1)}, u32[]{:S(2)}, u32[]{:S(2)}) collective-permute-start(bf16[128,1664]{1,0:T(8,128)(2,1)S(1)} %get-tuple-element.85), channel_id=1, source_target_pairs={{0,24},{8,16},{16,8},{24,0},{1,25},{9,17},{17,9},{25,1},{2,26},{10... | collective-permute-start | bytes 1277960 | tf_op jit(solution)/shard_map/ppermute | solution.py:361
  97.5 32.5 %collective-permute-start.9 = (bf16[128,1664]{1,0:T(8,128)(2,1)S(1)}, bf16[128,1664]{1,0:T(8,128)(2,1)}, u32[]{:S(2)}, u32[]{:S(2)}) collective-permute-start(bf16[128,1664]{1,0:T(8,128)(2,1)S(1)} %get-tuple-element.85), channel_id=1, source_target_pairs={{0,8},{8,0},{16,24},{24,16},{1,9},{9,1},{17,25},{25,17},{2,10},{10... | collective-permute-start | bytes 1277960 | tf_op jit(solution)/shard_map/ppermute | solution.py:361
  99.3 53.7 %collective-permute-start.12 = (bf16[256,1664]{1,0:T(8,128)(2,1)S(1)}, bf16[256,1664]{1,0:T(8,128)(2,1)}, u32[]{:S(2)}, u32[]{:S(2)}) collective-permute-start(bf16[256,1664]{1,0:T(8,128)(2,1)S(1)} %constant_dynamic-update-slice_fusion.3.first_ref), channel_id=1, source_target_pairs={{0,4},{1,3},{2,6},{3,1},{4,0},{5,7},{6,2},{7,5},{8,12},{9,11},{10,... | collective-permute-start | bytes 2555912 | tf_op jit(solution)/shard_map/ppermute | solution.py:361
  126.2 21.2 %collective-permute-start.16 = (bf16[128,1664]{1,0:T(8,128)(2,1)}, bf16[128,1664]{1,0:T(8,128)(2,1)}, u32[]{:S(2)}, u32[]{:S(2)}) collective-permute-start(bf16[128,1664]{1,0:T(8,128)(2,1)} %collective-permute-done.10), channel_id=1, source_target_pairs={{0,2},{1,5},{2,0},{3,7},{4,6},{5,1},{6,4},{7,3},{8,10},{9,13},{10,... | collective-permute-start | bytes 1277960 | tf_op jit(solution)/shard_map/ppermute | solution.py:361
  127.6 22.1 %collective-permute-start.18 = (bf16[128,1664]{1,0:T(8,128)(2,1)}, bf16[128,1664]{1,0:T(8,128)(2,1)}, u32[]{:S(2)}, u32[]{:S(2)}) collective-permute-start(bf16[128,1664]{1,0:T(8,128)(2,1)} %collective-permute-done.11), channel_id=1, source_target_pairs={{0,2},{1,5},{2,0},{3,7},{4,6},{5,1},{6,4},{7,3},{8,10},{9,13},{10,... | collective-permute-start | bytes 1277960 | tf_op jit(solution)/shard_map/ppermute | solution.py:361
  130.0 14.7 %collective-permute-start.14 = (bf16[128,1664]{1,0:T(8,128)(2,1)}, bf16[128,1664]{1,0:T(8,128)(2,1)}, u32[]{:S(2)}, u32[]{:S(2)}) collective-permute-start(bf16[128,1664]{1,0:T(8,128)(2,1)} %collective-permute-done.9), channel_id=1, source_target_pairs={{0,2},{1,5},{2,0},{3,7},{4,6},{5,1},{6,4},{7,3},{8,10},{9,13},{10,... | collective-permute-start | bytes 1277960 | tf_op jit(solution)/shard_map/ppermute | solution.py:361
  133.3 52.0 %all-to-all-start = ((bf16[4,384,512]{2,1,0:T(8,128)(2,1)}), bf16[4,384,512]{2,1,0:T(8,128)(2,1)S(1)}, u32[]{:S(2)}, u32[]{:S(2)}) async-start(bf16[4,384,512]{2,1,0:T(8,128)(2,1)} %get-tuple-element.86), calls=%async_computation | async-start | bytes 3145728 | tf_op jit(solution)/shard_map/all_to_all | solution.py:377
  143.6 9.4 %copy-start.15 = (bf16[256,1664]{1,0:T(8,128)(2,1)S(1)}, bf16[256,1664]{1,0:T(8,128)(2,1)}, u32[]{:S(2)}) copy-start(bf16[256,1664]{1,0:T(8,128)(2,1)} %copy-done.14) | copy-start | bytes 2555908
  145.8 14.6 %collective-permute-start.15 = (bf16[256,1664]{1,0:T(8,128)(2,1)S(1)}, bf16[256,1664]{1,0:T(8,128)(2,1)S(1)}, u32[]{:S(2)}, u32[]{:S(2)}) collective-permute-start(bf16[256,1664]{1,0:T(8,128)(2,1)S(1)} %constant_dynamic-update-slice_fusion.5.first_ref), channel_id=1, source_target_pairs={{0,4},{1,3},{2,6},{3,1},{4,0},{5,7},{6,2},{7,5},{8,12},{9,11},{10,... | collective-permute-start | bytes 2555912 | tf_op jit(solution)/shard_map/ppermute | solution.py:361
  149.1 19.4 %collective-permute-start.17 = (bf16[256,1664]{1,0:T(8,128)(2,1)}, bf16[256,1664]{1,0:T(8,128)(2,1)S(1)}, u32[]{:S(2)}, u32[]{:S(2)}) collective-permute-start(bf16[256,1664]{1,0:T(8,128)(2,1)} %constant_dynamic-update-slice_fusion.7.first_ref), channel_id=1, source_target_pairs={{0,4},{1,3},{2,6},{3,1},{4,0},{5,7},{6,2},{7,5},{8,12},{9,11},{10,... | collective-permute-start | bytes 2555912 | tf_op jit(solution)/shard_map/ppermute | solution.py:361
  151.5 25.3 %collective-permute-start.19 = (bf16[256,1664]{1,0:T(8,128)(2,1)}, bf16[256,1664]{1,0:T(8,128)(2,1)S(1)}, u32[]{:S(2)}, u32[]{:S(2)}) collective-permute-start(bf16[256,1664]{1,0:T(8,128)(2,1)} %constant_dynamic-update-slice_fusion.9.first_ref), channel_id=1, source_target_pairs={{0,4},{1,3},{2,6},{3,1},{4,0},{5,7},{6,2},{7,5},{8,12},{9,11},{10,... | collective-permute-start | bytes 2555912 | tf_op jit(solution)/shard_map/ppermute | solution.py:361
  185.2 3.4 %collective-permute-start.20 = (bf16[1536,512]{1,0:T(8,128)(2,1)S(1)}, bf16[1536,512]{1,0:T(8,128)(2,1)S(1)}, u32[]{:S(2)}, u32[]{:S(2)}) collective-permute-start(bf16[1536,512]{1,0:T(8,128)(2,1)S(1)} %bitcast.43), channel_id=1, source_target_pairs={{0,1},{1,0},{2,3},{3,2},{4,5},{5,4},{6,7},{7,6},{8,9},{9,8},{10,11... | collective-permute-start | bytes 4718600 | tf_op jit(solution)/shard_map/ppermute | solution.py:361
  190.8 3.6 %copy-start.11 = (f32[512,128]{1,0:T(8,128)S(1)}, f32[512,128]{1,0:T(8,128)}, u32[]{:S(2)}) copy-start(f32[512,128]{1,0:T(8,128)} %copy-done.10) | copy-start | bytes 786436
  193.0 12.1 %collective-permute-start.23 = (bf16[256,1536]{1,0:T(8,128)(2,1)S(1)}, bf16[256,1536]{1,0:T(8,128)(2,1)S(1)}, u32[]{:S(2)}, u32[]{:S(2)}) collective-permute-start(bf16[256,1536]{1,0:T(8,128)(2,1)S(1)} %get-tuple-element.117), channel_id=1, source_target_pairs={{0,4},{1,3},{2,6},{3,1},{4,0},{5,7},{6,2},{7,5},{8,12},{9,11},{10,... | collective-permute-start | bytes 2359304 | tf_op jit(solution)/shard_map/ppermute | solution.py:361
  196.3 21.3 %collective-permute-start.22 = (bf16[256,1536]{1,0:T(8,128)(2,1)S(1)}, bf16[256,1536]{1,0:T(8,128)(2,1)S(1)}, u32[]{:S(2)}, u32[]{:S(2)}) collective-permute-start(bf16[256,1536]{1,0:T(8,128)(2,1)S(1)} %get-tuple-element.121), channel_id=1, source_target_pairs={{0,4},{1,3},{2,6},{3,1},{4,0},{5,7},{6,2},{7,5},{8,12},{9,11},{10,... | collective-permute-start | bytes 2359304 | tf_op jit(solution)/shard_map/ppermute | solution.py:361
  198.9 31.4 %collective-permute-start.25 = (bf16[256,1536]{1,0:T(8,128)(2,1)S(1)}, bf16[256,1536]{1,0:T(8,128)(2,1)S(1)}, u32[]{:S(2)}, u32[]{:S(2)}) collective-permute-start(bf16[256,1536]{1,0:T(8,128)(2,1)S(1)} %get-tuple-element.125), channel_id=1, source_target_pairs={{0,4},{1,3},{2,6},{3,1},{4,0},{5,7},{6,2},{7,5},{8,12},{9,11},{10,... | collective-permute-start | bytes 2359304 | tf_op jit(solution)/shard_map/ppermute | solution.py:361
  202.2 40.7 %collective-permute-start.21 = (bf16[256,1536]{1,0:T(8,128)(2,1)S(1)}, bf16[256,1536]{1,0:T(8,128)(2,1)S(1)}, u32[]{:S(2)}, u32[]{:S(2)}) collective-permute-start(bf16[256,1536]{1,0:T(8,128)(2,1)S(1)} %get-tuple-element.129), channel_id=1, source_target_pairs={{0,4},{1,3},{2,6},{3,1},{4,0},{5,7},{6,2},{7,5},{8,12},{9,11},{10,... | collective-permute-start | bytes 2359304 | tf_op jit(solution)/shard_map/ppermute | solution.py:361
  205.2 12.6 %copy-start.27 = (f32[256,1536]{1,0:T(8,128)}, f32[256,1536]{1,0:T(8,128)S(1)}, u32[]{:S(2)}) copy-start(f32[256,1536]{1,0:T(8,128)S(1)} %convert_add_fusion.3) | copy-start | bytes 4718596
  205.3 14.2 %collective-permute-start.26 = (bf16[128,1536]{1,0:T(8,128)(2,1)S(1)}, bf16[128,1536]{1,0:T(8,128)(2,1)S(1)}, u32[]{:S(2)}, u32[]{:S(2)}) collective-permute-start(bf16[128,1536]{1,0:T(8,128)(2,1)S(1)} %slice.81), channel_id=1, source_target_pairs={{0,2},{1,5},{2,0},{3,7},{4,6},{5,1},{6,4},{7,3},{8,10},{9,13},{10,... | collective-permute-start | bytes 1179656 | tf_op jit(solution)/shard_map/ppermute | solution.py:361
  218.0 14.2 %collective-permute-start.24 = (bf16[128,1536]{1,0:T(8,128)(2,1)S(1)}, bf16[128,1536]{1,0:T(8,128)(2,1)S(1)}, u32[]{:S(2)}, u32[]{:S(2)}) collective-permute-start(bf16[128,1536]{1,0:T(8,128)(2,1)S(1)} %slice.80), channel_id=1, source_target_pairs={{0,2},{1,5},{2,0},{3,7},{4,6},{5,1},{6,4},{7,3},{8,10},{9,13},{10,... | collective-permute-start | bytes 1179656 | tf_op jit(solution)/shard_map/ppermute | solution.py:361
  219.7 31.4 %collective-permute-start.31 = (bf16[128,1536]{1,0:T(8,128)(2,1)S(1)}, bf16[128,1536]{1,0:T(8,128)(2,1)S(1)}, u32[]{:S(2)}, u32[]{:S(2)}) collective-permute-start(bf16[128,1536]{1,0:T(8,128)(2,1)S(1)} %add_convert_fusion.2), channel_id=1, source_target_pairs={{0,24},{8,16},{16,8},{24,0},{1,25},{9,17},{17,9},{25,1},{2,26},{10... | collective-permute-start | bytes 1179656 | tf_op jit(solution)/shard_map/ppermute | solution.py:361
  230.6 14.2 %collective-permute-start.28 = (bf16[128,1536]{1,0:T(8,128)(2,1)S(1)}, bf16[128,1536]{1,0:T(8,128)(2,1)S(1)}, u32[]{:S(2)}, u32[]{:S(2)}) collective-permute-start(bf16[128,1536]{1,0:T(8,128)(2,1)S(1)} %slice.79), channel_id=1, source_target_pairs={{0,2},{1,5},{2,0},{3,7},{4,6},{5,1},{6,4},{7,3},{8,10},{9,13},{10,... | collective-permute-start | bytes 1179656 | tf_op jit(solution)/shard_map/ppermute | solution.py:361
  232.3 24.6 %collective-permute-start.30 = (bf16[128,1536]{1,0:T(8,128)(2,1)S(1)}, bf16[128,1536]{1,0:T(8,128)(2,1)S(1)}, u32[]{:S(2)}, u32[]{:S(2)}) collective-permute-start(bf16[128,1536]{1,0:T(8,128)(2,1)S(1)} %add_convert_fusion.1), channel_id=1, source_target_pairs={{0,16},{8,24},{16,0},{24,8},{1,17},{9,25},{17,1},{25,9},{2,18},{10... | collective-permute-start | bytes 1179656 | tf_op jit(solution)/shard_map/ppermute | solution.py:361
  237.3 7.4 %slice-start.2 = ((f32[256,1536]{1,0:T(8,128)}), f32[128,1536]{1,0:T(8,128)S(1)}, s32[]{:S(2)}) async-start(f32[256,1536]{1,0:T(8,128)} %copy-done.29), calls=%async_computation.4 | async-start | bytes 1572864 | tf_op jit(solution)/shard_map/slice | solution.py:420
  243.2 7.8 %collective-permute-start.27 = (bf16[128,1536]{1,0:T(8,128)(2,1)S(1)}, bf16[128,1536]{1,0:T(8,128)(2,1)S(1)}, u32[]{:S(2)}, u32[]{:S(2)}) collective-permute-start(bf16[128,1536]{1,0:T(8,128)(2,1)S(1)} %slice.78), channel_id=1, source_target_pairs={{0,2},{1,5},{2,0},{3,7},{4,6},{5,1},{6,4},{7,3},{8,10},{9,13},{10,... | collective-permute-start | bytes 1179656 | tf_op jit(solution)/shard_map/ppermute | solution.py:361
  244.9 20.1 %collective-permute-start.29 = (bf16[128,1536]{1,0:T(8,128)(2,1)S(1)}, bf16[128,1536]{1,0:T(8,128)(2,1)S(1)}, u32[]{:S(2)}, u32[]{:S(2)}) collective-permute-start(bf16[128,1536]{1,0:T(8,128)(2,1)S(1)} %add_convert_fusion), channel_id=1, source_target_pairs={{0,8},{8,0},{16,24},{24,16},{1,9},{9,1},{17,25},{25,17},{2,10},{10... | collective-permute-start | bytes 1179656 | tf_op jit(solution)/shard_map/ppermute | solution.py:361
  (25 other events, 37.5 us)

commit v4 on v3

--- a/solution.py
+++ b/solution.py
@@ -27,8 +27,9 @@
 WIDE = D + LANES
 PAIRS = KV_HEADS // 2
 BIG = 1e30
-HIDDEN_COST = 6 * 10**9
+HIDDEN_COST = 10**6
 DOWN_COST = 10**6
+VMEM_LIMIT = 60 * 1024 * 1024
 BF = jnp.bfloat16
 F32 = jnp.float32
 
@@ -41,12 +42,16 @@
     return pl.BlockSpec(memory_space=pltpu.SMEM)
 
 
+def anywhere():
+    return pl.BlockSpec(memory_space=pl.ANY)
+
+
 def cost(flops, moved):
     return pl.CostEstimate(flops=flops, bytes_accessed=moved, transcendentals=0)
 
 
 def attend_kernel(
-    me_ref, own_ref, asks_ref, table_ref, key_ref, value_ref, mix_ref, stat_ref, counts, ask_ref
+    me_ref, own_ref, asks_ref, table_ref, key_ref, value_ref, here_ref, reply_ref, counts, ask_ref
 ):
     step = pl.program_id(0)
     slots = table_ref.shape[0]
@@ -105,17 +110,21 @@
     weights = (expos.astype(BF).astype(F32) * count).astype(BF)
     mixture = jnp.dot(weights, value_ref[...], preferred_element_type=F32)
 
+    def put(at, value):
+        here_ref[:, pl.ds(at, LANES)] = value[:LOCAL]
+        reply_ref[:, pl.ds(at, LANES)] = value[LOCAL:]
+
     @pl.when(step == 0)
     def _():
-        stat_ref[...] = jnp.zeros_like(stat_ref)
-
-    stat = stat_ref[...]
+        put(D, jnp.zeros((slots, LANES), F32))
+
+    stat = jnp.concatenate([here_ref[:, D:], reply_ref[:, D:]], axis=0)
     for j in range(2 * GROUP):
         head = step * 2 * GROUP + j
         take = slice(j * slots, (j + 1) * slots)
         stat = jnp.where(lane == head, highest[take], stat)
         stat = jnp.where(lane == head + 64, totals[take], stat)
-    stat_ref[...] = stat
+    put(D, stat)
     for chunk in range(GROUP):
         halves = []
         for half in range(2):
@@ -124,13 +133,13 @@
             if j // GROUP != half:
                 part = pltpu.roll(part, HEAD, 1)
             halves.append(part)
-        mix_ref[:, chunk * LANES : (chunk + 1) * LANES] = jnp.where(lane < HEAD, halves[0], halves[1])
+        at = pl.multiple_of(step * (2 * GROUP * HEAD) + chunk * LANES, LANES)
+        put(at, jnp.where(lane < HEAD, halves[0], halves[1]))
 
 
 def attend(me, own, asks, table, pool):
     slots = table.shape[0]
     tokens = pool.shape[0]
-    width = 2 * GROUP * HEAD
     return pl.pallas_call(
         attend_kernel,
         grid=(PAIRS,),
@@ -143,22 +152,22 @@
             pl.BlockSpec((tokens, LANES), lambda s: (0, PAIRS + s)),
         ],
         out_specs=[
-            pl.BlockSpec((slots, width), lambda s: (0, s)),
-            pl.BlockSpec((slots, LANES), lambda s: (0, 0)),
+            pl.BlockSpec((LOCAL, WIDE), lambda s: (0, 0)),
+            pl.BlockSpec((slots - LOCAL, WIDE), lambda s: (0, 0)),
         ],
         out_shape=[
-            jax.ShapeDtypeStruct((slots, D), F32),
-            jax.ShapeDtypeStruct((slots, LANES), F32),
+            jax.ShapeDtypeStruct((LOCAL, WIDE), F32),
+            jax.ShapeDtypeStruct((slots - LOCAL, WIDE), F32),
         ],
         scratch_shapes=[pltpu.VMEM((slots, tokens), F32), pltpu.VMEM((slots, WIDE), F32)],
-        compiler_params=pltpu.CompilerParams(vmem_limit_bytes=48 * 1024 * 1024),
+        compiler_params=pltpu.CompilerParams(vmem_limit_bytes=VMEM_LIMIT),
         cost_estimate=cost(7 * 10**9, 10**5),
         name="attend",
     )(me, own, asks, table, pool, pool)
 
 
 def stream_kernel(
-    pieces, chosen_ref, at_ref, query_ref, fresh_ref, mix_ref, stat_ref, back_ref, prefill_ref,
+    pieces, chosen_ref, at_ref, query_ref, fresh_ref, here_ref, back_ref, prefill_ref,
     residual_ref, gain_ref, router_ref, routes_ref, *rest
 ):
     parts, rest = rest[: len(pieces)], rest[len(pieces) :]
@@ -178,8 +187,8 @@
     low = lane < HEAD
     picked = [back_ref[pl.ds(chosen_ref[m], 1), :] for m in range(MOVED)]
     picked = jnp.concatenate(picked, axis=0)
-    mix = jnp.concatenate([mix_ref[:LOCAL, :], picked[:, :D]], axis=0)
-    stat = jnp.concatenate([stat_ref[:LOCAL, :], picked[:, D:]], axis=0)
+    mix = jnp.concatenate([here_ref[:, :D], picked[:, :D]], axis=0)
+    stat = jnp.concatenate([here_ref[:, D:], picked[:, D:]], axis=0)
     fresh = fresh_ref[...].astype(F32)
 
     def spread(first, second, base):
@@ -240,14 +249,14 @@
 
 
 def make_stream(
-    chosen, queries, fresh, mix, stat, back, prefill, residual, out_parts, gain, router, routes
+    chosen, queries, fresh, here, back, prefill, residual, out_parts, gain, router, routes
 ):
     rows = residual.shape[0]
     count = queries.shape[0]
-    at, parts, pieces = out_parts
+    at, parts, pieces, _ = out_parts
     return pl.pallas_call(
         functools.partial(stream_kernel, pieces),
-        in_specs=[smem()] * 2 + [vmem()] * 10 + [pl.BlockSpec(memory_space=pl.ANY)] * len(parts),
+        in_specs=[smem()] * 2 + [vmem()] * 9 + [pl.BlockSpec(memory_space=pltpu.HBM)] * len(parts),
         out_specs=[vmem()] * 3,
         out_shape=[
             jax.ShapeDtypeStruct((count, D), BF),
@@ -259,13 +268,14 @@
             pltpu.VMEM((D, D), BF),
             pltpu.SemaphoreType.DMA((sum(blocks for blocks, _ in pieces),)),
         ],
-        compiler_params=pltpu.CompilerParams(vmem_limit_bytes=48 * 1024 * 1024),
+        compiler_params=pltpu.CompilerParams(vmem_limit_bytes=VMEM_LIMIT),
         cost_estimate=cost(8 * 10**9, 10**5),
         name="stream",
-    )(chosen, at, queries, fresh, mix, stat, back, prefill, residual, gain, router, routes, *parts)
-
-
-def hidden_kernel(place_ref, first_ref, second_ref, mine_ref, other_ref, hidden_ref, share_ref, rows_ref):
+    )(chosen, at, queries, fresh, here, back, prefill, residual, gain, router, routes, *parts)
+
+
+def hidden_kernel(place_ref, first_ref, second_ref, mine_ref, other_ref, *rest):
+    hidden_ref, share_ref, rows_ref = rest[-3:]
     rows = first_ref.shape[0]
     rows_ref[:rows, :] = first_ref[...]
     rows_ref[rows:, :] = second_ref[...]
@@ -284,11 +294,11 @@
     share_ref[...] = jnp.where(lane == 0, shares[0], shares[1])
 
 
-def make_hidden(place, first, second, mine, other):
+def make_hidden(place, first, second, mine, other, *earlier):
     rows = 2 * first.shape[0]
     return pl.pallas_call(
         hidden_kernel,
-        in_specs=[smem()] + [vmem()] * 4,
+        in_specs=[smem()] + [vmem()] * 4 + [anywhere()] * len(earlier),
         out_specs=[vmem()] * 2,
         out_shape=[
             jax.ShapeDtypeStruct((rows, 2 * FF), BF),
@@ -298,10 +308,11 @@
         compiler_params=pltpu.CompilerParams(vmem_limit_bytes=28 * 1024 * 1024),
         cost_estimate=cost(HIDDEN_COST, 10**5),
         name="hidden",
-    )(place, first, second, mine, other)
-
-
-def down_kernel(hidden_ref, share_ref, mine_ref, other_ref, keep_ref, away_ref):
+    )(place, first, second, mine, other, *earlier)
+
+
+def down_kernel(hidden_ref, share_ref, mine_ref, other_ref, *rest):
+    keep_ref, away_ref = rest[-2:]
     total = None
     for side, held_ref in enumerate((mine_ref, other_ref)):
         made = lax.dot_general(
@@ -317,41 +328,41 @@
     away_ref[...] = total[rows:].astype(BF)
 
 
-def make_down(hidden, share, mine, other):
+def make_down(hidden, share, mine, other, *earlier):
     rows = hidden.shape[0]
     return pl.pallas_call(
         down_kernel,
-        in_specs=[vmem()] * 4,
+        in_specs=[vmem()] * 4 + [anywhere()] * len(earlier),
         out_specs=[vmem()] * 2,
         out_shape=[jax.ShapeDtypeStruct((rows // 2, D), BF)] * 2,
         compiler_params=pltpu.CompilerParams(vmem_limit_bytes=28 * 1024 * 1024),
         cost_estimate=cost(DOWN_COST, 10**5),
         name="down",
-    )(hidden, share, mine, other)
+    )(hidden, share, mine, other, *earlier)
 
 
 def pack_kernel(gate_ref, down_ref, pair_out, down_out):
-    depth, experts = gate_ref.shape[:2]
-    step = 16
-
-    @pl.loop(0, depth // step)
-    def _(n):
-        at = pl.ds(pl.multiple_of(n * step, step), step)
+    for n in range(gate_ref.shape[0] // 16):
+        at = slice(n * 16, (n + 1) * 16)
         gate = gate_ref[at]
         down = down_ref[at]
-        for e in range(experts):
+        for e in range(gate_ref.shape[1]):
             pair_out[e, at, :] = gate[:, e, :]
             down_out[e, at, :] = down[:, e, :]
 
 
 def pack_experts(gate_up, down_proj):
     depth, experts = gate_up.shape[:2]
+    step = depth // 8
+    block = lambda n: pl.BlockSpec((step, experts, n * FF), lambda s: (s, 0, 0))
+    packed = lambda n: pl.BlockSpec((experts, step, n * FF), lambda s: (0, s, 0))
     return pl.pallas_call(
         pack_kernel,
-        in_specs=[vmem()] * 2,
-        out_specs=[vmem()] * 2,
+        grid=(depth // step,),
+        in_specs=[block(2), block(1)],
+        out_specs=[packed(2), packed(1)],
         out_shape=[jax.ShapeDtypeStruct((experts, depth, n * FF), BF) for n in (2, 1)],
-        compiler_params=pltpu.CompilerParams(vmem_limit_bytes=32 * 1024 * 1024),
+        compiler_params=pltpu.CompilerParams(vmem_limit_bytes=VMEM_LIMIT),
         cost_estimate=cost(7 * 10**9, 10**5),
         name="pack",
     )(gate_up, down_proj)
@@ -380,53 +391,113 @@
 
 def after(x, *others):
     return lax.optimization_barrier((x, others))[0]
+
+
+def small_call(kernel, name, arrays, earlier, outs, flops=10**6):
+    return pl.pallas_call(
+        kernel,
+        in_specs=[vmem()] * len(arrays) + [anywhere()] * len(earlier),
+        out_specs=[vmem()] * len(outs),
+        out_shape=[jax.ShapeDtypeStruct(*out) for out in outs],
+        compiler_params=pltpu.CompilerParams(vmem_limit_bytes=16 * 1024 * 1024),
+        cost_estimate=cost(flops, 10**5),
+        name=name,
+    )(*arrays, *earlier)
+
+
+def stack_kernel(count, *refs):
+    out_ref, at = refs[-1], 0
+    for ref in refs[:count]:
+        out_ref[at : at + ref.shape[0], :] = ref[...]
+        at += ref.shape[0]
+
+
+def stack_rows(arrays, *earlier, flops=10**6):
+    shape = (sum(x.shape[0] for x in arrays), arrays[0].shape[1])
+    kernel = functools.partial(stack_kernel, len(arrays))
+    return small_call(kernel, "stack", arrays, earlier, [(shape, BF)], flops)[0]
+
+
+def join_kernel(keep_ref, came_ref, *rest):
+    part_ref, pass_ref = rest[-2:]
+    rows = part_ref.shape[0]
+    total = keep_ref[...].astype(F32) + came_ref[...].astype(F32)
+    part_ref[...] = total[:rows]
+    pass_ref[...] = total[rows:].astype(BF)
+
+
+def join(keep, came, *earlier):
+    shape = (keep.shape[0] // 2, keep.shape[1])
+    return small_call(join_kernel, "join", [keep, came], earlier, [(shape, F32), (shape, BF)])
+
+
+def close_kernel(part_ref, came_ref, *rest):
+    rest[-1][...] = (part_ref[...] + came_ref[...].astype(F32)).astype(BF)
+
+
+def close(part, came, *earlier):
+    return small_call(close_kernel, "close", [part, came], earlier, [(part.shape, BF)])[0]
+
+
+def finish_kernel(stream_ref, part_ref, *rest):
+    total = stream_ref[...] + part_ref[...]
+    for ref in rest[:-1]:
+        total = total + ref[...].astype(F32)
+    rest[-1][...] = total
 
 
 def swapped_experts(send, stream, pair, down):
     planes = lax.axis_size("gx")
     row, column = lax.axis_index("gx"), lax.axis_index("gy")
     place = jnp.stack([column * planes + row, beside(column) * planes + row]).astype(jnp.int32)
-    rows = send.shape[0]
     across = lambda x, k: swap(x, "gx", lambda i: i ^ k)
-    firsts = [jnp.concatenate([send, swap(send, "gy", near)], axis=0)]
-    moved = [across(after(send, firsts[0]) if k == 1 else send, k) for k in range(1, planes)]
-    other_pair = swap(after(pair, firsts[0]), "gy", beside)
-    down = exchange(after(down, *moved))
-    firsts += [jnp.concatenate([mine, swap(mine, "gy", near)], axis=0) for mine in moved]
-    chunks = [[first, swap(first, "gy", far)] for first in firsts]
-    hidden = []
-    for chunk in chunks:
-        chunk = after(chunk, *hidden[-1:])
-        hidden.append(make_hidden(place, *chunk, pair, other_pair))
-    down, hidden = lax.optimization_barrier((down, hidden))
+
+    first = [stack_rows([send, swap(send, "gy", near)])]
+    mine = [send] + [across(send, k) for k in range(1, planes)]
+    other_pair = swap(after(pair, first[0]), "gy", beside)
+    first += [
+        stack_rows([mine[k], swap(mine[k], "gy", near)], flops=10**6)
+        for k in range(1, planes)
+    ]
+    second = [swap(x, "gy", far) for x in first]
+    hidden, last = [], ()
+    for k in range(planes):
+        hidden.append(make_hidden(place, first[k], second[k], pair, other_pair, *last))
+        last = (hidden[k][1],)
+    down = exchange(after(down, second[0], *first[1:]))
+    down = after(down, hidden[-1][1])
     other_down = swap(down, "gy", beside)
+
+    made, arrived, parts, ends = {}, {}, {}, {}
+    last = ()
+
+    def put(k):
+        made[k] = make_down(*hidden[k], down, other_down, *last)
+        arrived[k] = swap(made[k][1], "gy", far)
+        return (made[k][0],)
+
+    def turn(k, *earlier):
+        parts[k], passed = join(made[k][0], arrived[k], *last, *earlier)
+        ends[k] = swap(passed, "gy", near)
+        return (passed,)
+
+    def leave(k):
+        passed = close(parts[k], ends[k], *last)
+        ends[k] = across(passed, k)
+        return (passed,)
+
     order = list(reversed(range(planes)))
-    made, last = {}, ()
-    for k in order:
-        made[k] = make_down(*after(hidden[k], *last), down, other_down)
-        last = made[k]
-    arrived = {k: swap(made[k][1], "gy", far) for k in order}
-    total, ends = {}, {}
-    for n in range(planes + 2):
-        if n < planes:
-            k = order[n]
-            keep, came = after((made[k][0], arrived[k]), *last)
-            total[k] = keep.astype(F32) + came.astype(F32)
-            send_on = total[k][rows:].astype(BF)
-            last = (send_on,)
-            ends[k] = swap(send_on, "gy", near)
-        if 1 <= n <= planes:
-            k = order[n - 1]
-            keep, came = after((total[k][:rows], ends[k]), *last)
-            total[k] = keep + came.astype(F32)
-            if k:
-                send_on = total[k].astype(BF)
-                last = (send_on,)
-                ends[k] = across(send_on, k)
-    result = stream + total[0]
-    for k in range(1, planes):
-        result = result + ends[k].astype(F32)
-    return result
+    last = put(order[0])
+    last = put(order[1])
+    last = turn(order[0])
+    for n in range(2, planes):
+        last = put(order[n])
+        last = leave(order[n - 2])
+        last = turn(order[n - 1]) if n < 3 else turn(order[n - 1], ends[order[0]])
+    last = leave(order[-2])
+    last = turn(order[-1])
+    arrays = [stream, parts[0], ends[0]] + [ends[k] for k in range(1, planes)]
+    return small_call(finish_kernel, "finish", arrays, (), [(stream.shape, F32)])[0]
 
 
 def gathered_experts(send, stream, routes, gate_up, down_proj):
@@ -469,7 +540,7 @@
     share = out_weight.shape[0] // columns
     mine = lax.dynamic_slice_in_dim(out_weight, lax.axis_index("gy") * share, share, axis=0)
     whole = lax.all_gather(mine, ("gx", "gy"), axis=0, tiled=True)
-    return jnp.zeros((1,), jnp.int32), [whole], ((1, whole.shape[0]),)
+    return jnp.zeros((1,), jnp.int32), [whole], ((1, whole.shape[0]),), whole
 
 
 def start_out(out_weight):
@@ -479,15 +550,15 @@
     return [swap(mine, "gx", lambda i, k=k: i ^ k) for k in range(1, planes)]
 
 
-def swap_out(out_weight, first):
+def swap_out(out_weight, first, asks):
     planes, columns = lax.axis_size("gx"), lax.axis_size("gy")
     row, column = lax.axis_index("gx"), lax.axis_index("gy")
     depth = out_weight.shape[0]
     share = depth // columns
     second = swap(first, "gy", near)
-    third = swap(jnp.concatenate([first, second], axis=0), "gy", far)
+    both = stack_rows([first, second], asks)
+    third = swap(both, "gy", far)
     parts = [first, second, third]
-    parts = [out_weight] + parts + [swap(part, "gy", beside) for part in parts]
     near_of = lambda j: jnp.where(j % 2 == 0, j ^ 2, j ^ 4)
     far_of = lambda j: jnp.where(j % 2 == 0, j ^ 4, j ^ 2)
     at = [row * depth]
@@ -496,7 +567,8 @@
             at += [(row ^ k) * depth + source * share for k in range(1, planes)]
     one = (planes - 1, share)
     two = (2 * (planes - 1), share)
-    return jnp.stack(at).astype(jnp.int32), parts, ((1, depth), one, one, two, one, one, two)
+    at = jnp.stack(at).astype(jnp.int32)
+    return at, parts, ((1, depth), one, one, two, one, one, two), both
 
 
 def body(
@@ -539,24 +611,27 @@
         pair, down = pack_experts(gate_up, down_proj)
         out_parts, pair, down = lax.optimization_barrier((out_parts, pair, down))
         pair = exchange(pair)
-        out_parts = swap_out(out_weight, jnp.concatenate(out_parts, axis=0))
+        out_parts = swap_out(out_weight, stack_rows(out_parts), asks)
+        asks = after(asks, out_parts[3])
     else:
         out_parts = gather_out(out_weight)
-    mix, stat = attend(
+    here, reply = attend(
         column.astype(jnp.int32).reshape(1),
         own,
         asks,
         jnp.concatenate([local_pages, push_pages], axis=0),
         pool,
     )
-    answers = jnp.concatenate([mix[LOCAL:], stat[LOCAL:]], axis=1)
-    back = lax.all_gather(answers, "gy", axis=0, tiled=True)
+    if swapped:
+        at, parts, pieces, _ = out_parts
+        others = [swap(part, "gy", beside) for part in after(parts, reply)]
+        out_parts = (at, [out_weight] + parts + others, pieces, None)
+    back = lax.all_gather(reply, "gy", axis=0, tiled=True)
     attended, stream, send = make_stream(
         chosen,
         queries,
         new_kv,
-        mix,
-        stat,
+        here,
         back,
         prefill_attn,
         residual,

time: 267 us -> 263 us (0.985)
  Pallas kernels: 55.4 us -> 68.7 us
  local copies, waits for them, and re-layouts: 30.3 us -> 18.3 us
  waiting for transfers between devices: 87 us -> 76.3 us
  starting transfers between devices: 61.6 us -> 71.6 us
    ppermute x32, starting transfers between devices: 46 us -> 61.5 us  [swap(): lax.ppermute(x, axis, [(i, how(i)) for i in range(lax.axis_size(axis))])]
    pallas_call x9 -> x23, Pallas kernels: 42.1 us -> 55.4 us  [the longest x4 23.3 us: make_hidden(): pl.pallas_call(hidden_kernel, in_specs=[smem()] + [vmem()] * 4 + [anywher...]
    ppermute x32, waiting for transfers between devices: 84.3 us -> 72.2 us  [swap(): lax.ppermute(x, axis, [(i, how(i)) for i in range(lax.axis_size(axis))])]
    unnamed x80 -> x66, local copies, waits for them, and re-layouts: 23.5 us -> 14.8 us
    all_to_all x2, starting transfers between devices: 15.6 us -> 10.1 us  [exchange(): lax.all_to_all(packed, 'gx', split_axis=0, concat_axis=0, tiled=True)]
    concatenate x5 -> x0, local copies, waits for them, and re-layouts: 4.73 us -> none  [the longest x3 4.68 us: swapped_experts(): jnp.concatenate([mine, swap(mine, 'gy', near)], axis=0)]
    all_gather x1, blocking collectives: 15.8 us -> 11.8 us  [body(): lax.all_gather(jnp.concatenate([queries[LOCAL:], extra], axis=1), 'gy', a...]
  transfers between devices with their start and end apart: 34 -> 34, of which waited for: 12 -> 21; matrix products, arithmetic and copies ran while one was open for 5% -> 3% of each run, Pallas kernels for 20% -> 24%
where the time goes in v4:
time: 263 us; the launch traced here: 262 us
  waiting for transfers between devices  76.3 us (29%)
  starting transfers between devices  71.6 us (27%)
  Pallas kernels  68.7 us (26%)
  blocking collectives  24.1 us (9%)
  local copies, waits for them, and re-layouts  18.3 us (7%)
    ppermute x32, waiting for transfers between devices, swap(): lax.ppermute(x, axis, [(i, how(i)) for i in range(lax.axis_size(axis))])  72.2 us
    ppermute x32, starting transfers between devices, swap(): lax.ppermute(x, axis, [(i, how(i)) for i in range(lax.axis_size(axis))])  61.5 us
    pallas_call x4, Pallas kernels, make_hidden(): pl.pallas_call(hidden_kernel, in_specs=[smem()] + [vmem()] * 4 + [anywher...  23.3 us
    unnamed x66, local copies, waits for them, and re-layouts  14.8 us
    pallas_call x4, Pallas kernels, make_down(): pl.pallas_call(down_kernel, in_specs=[vmem()] * 4 + [anywhere()] * len(ea...  13.5 us
    all_gather x1, blocking collectives, body(): back = lax.all_gather(reply, 'gy', axis=0, tiled=True)  12.3 us
    all_gather x1, blocking collectives, body(): lax.all_gather(jnp.concatenate([queries[LOCAL:], extra], axis=1), 'gy', a...  11.8 us
    all_to_all x2, starting transfers between devices, exchange(): lax.all_to_all(packed, 'gx', split_axis=0, concat_axis=0, tiled=True)  10.1 us
  transfers between devices with their start and end apart: 34, of which 21 were waited for; matrix products, arithmetic and copies ran while one was open for 3% of the time, Pallas kernels for 24%

profile of v4, /device:TPU:0, one launch (start us, length us, event | category | flops | bytes accessed | tf_op | source)
XLA Modules:
  0.0 262.2 jit_solution(16437749549349666546)
XLA Ops:
  1.6 3.1 %collective-permute-start = (bf16[48,1536]{1,0:T(8,128)(2,1)S(1)}, bf16[48,1536]{1,0:T(8,128)(2,1)S(1)}, u32[]{:S(2)}, u32[]{:S(2)}) collective-permute-start(bf16[48,1536]{1,0:T(8,128)(2,1)S(1)} %constant_dynamic-slice_fusion), channel_id=1, source_target_pairs={{0,8},{8,0},{16,24},{24,16},{1,9},{9,1},{17,25},{25,17},{2,10},{10... | collective-permute-start | bytes 442376 | tf_op jit(solution)/shard_map/ppermute | solution.py:372
  4.7 2.6 collective-permute-start.1
  7.3 9.4 %pack.1 = (bf16[4,384,1024]{2,1,0:T(8,128)(2,1)}, bf16[4,384,512]{2,1,0:T(8,128)(2,1)}) custom-call(bf16[384,4,1024]{2,1,0:T(4,128)(2,1)} %gate_ref.1, bf16[384,4,512]{2,1,0:T(4,128)(2,1)} %down_ref.1), custom_call_target="tpu_custom_call" | custom-call | flops 7000000000 | bytes 100000 | tf_op jit(solution)/shard_map/pack/pallas_call | solution.py:359
  17.0 1.7 collective-permute-done.1.refs_1_
  19.3 4.7 %all-to-all-start = ((bf16[4,384,1024]{2,1,0:T(8,128)(2,1)}), bf16[4,384,1024]{2,1,0:T(8,128)(2,1)S(1)}, u32[]{:S(2)}, u32[]{:S(2)}) async-start(bf16[4,384,1024]{2,1,0:T(8,128)(2,1)} %get-tuple-element.59), calls=%async_computation | async-start | bytes 6291456 | tf_op jit(solution)/shard_map/all_to_all | solution.py:388
  28.4 11.8 %all_gather.6.refs_2_.asks_ref = bf16[64,1664]{1,0:T(8,128)(2,1)S(1)} all-gather(bf16[8,1664]{1,0:T(8,128)(2,1)S(1)} %pad_maximum_fusion), channel_id=1, replica_groups=mesh['gx'=4,'gy'=8] {'gy'}, dimensions={0}, use_global_device_ids=true | all-gather | bytes 239616 | tf_op jit(solution)/shard_map/all_gather | solution.py:601
  40.8 2.2 stack.159
  45.3 7.0 %attend.1 = (f32[8,1664]{1,0:T(8,128)}, f32[16,1664]{1,0:T(8,128)}) custom-call(s32[1]{0:T(128)} %bitcast.25.me_ref, bf16[8,1664]{1,0:T(8,128)(2,1)} %fusion.1.own_ref, bf16[64,1664]{1,0:T(8,128)(2,1)} %copy-done.18, s32[24,32]{1,0:T(8,128)} %pad_add_fusion.table_ref, bf16[2048,1024]{1,0:T(8,128)(2,1)} %bitcast.48, bf16[2048,1024]{1,0:T(8,128)(2,1)} %bitcast.49), custom_call_target="tpu_custom_call" | custom-call | flops 7000000000 | bytes 100000 | tf_op jit(solution)/shard_map/attend/pallas_call | solution.py:143
  52.3 4.1 %collective-permute-done.4.rest_3_ = bf16[288,1536]{1,0:T(8,128)(2,1)} collective-permute-done((bf16[288,1536]{1,0:T(8,128)(2,1)}, bf16[288,1536]{1,0:T(8,128)(2,1)}, u32[]{:S(2)}, u32[]{:S(2)}) %collective-permute-start.4) | collective-permute-done | bytes 884768 | tf_op jit(solution)/shard_map/ppermute | solution.py:372
  60.8 12.3 %all_gather.7.back_ref = f32[128,1664]{1,0:T(8,128)} all-gather(f32[16,1664]{1,0:T(8,128)} %get-tuple-element.52), channel_id=1, replica_groups=mesh['gx'=4,'gy'=8] {'gy'}, dimensions={0}, use_global_device_ids=true | all-gather | bytes 958464 | tf_op jit(solution)/shard_map/all_gather | solution.py:629
  73.1 6.3 %stream.1 = (bf16[16,1536]{1,0:T(8,128)(2,1)}, f32[128,1536]{1,0:T(8,128)}, bf16[128,1664]{1,0:T(8,128)(2,1)}) custom-call(s32[8]{0:T(128)} %get-tuple-element.97.chosen_ref, s32[25]{0:T(128)} %stack.147.at_ref, bf16[16,1536]{1,0:T(8,128)(2,1)} %query_ref.1, bf16[16,1024]{1,0:T(8,128)(2,1)} %fresh_ref.1, f32[8,1664]{1,0:T(8,128)} %get-tuple-element.51.here_ref, ...), custom_call_target="tpu_custom_call" | custom-call | flops 8000000000 | bytes 100000 | tf_op jit(solution)/shard_map/stream/pallas_call | solution.py:257
  79.4 1.6 collective-permute-start.8
  80.9 2.0 collective-permute-start.11
  83.0 2.4 collective-permute-start.13
  85.3 2.4 collective-permute-done.8.refs_1_
  91.3 4.0 %all-to-all-done = bf16[4,384,1024]{2,1,0:T(8,128)(2,1)S(1)} async-done(((bf16[4,384,1024]{2,1,0:T(8,128)(2,1)}), bf16[4,384,1024]{2,1,0:T(8,128)(2,1)S(1)}, u32[]{:S(2)}, u32[]{:S(2)}) %all-to-all-start) | async-done | bytes 3145760 | tf_op jit(solution)/shard_map/all_to_all | solution.py:388
  95.3 10.1 %collective-permute-done.11.refs_0_ = bf16[128,1664]{1,0:T(8,128)(2,1)} collective-permute-done((bf16[128,1664]{1,0:T(8,128)(2,1)}, bf16[128,1664]{1,0:T(8,128)(2,1)}, u32[]{:S(2)}, u32[]{:S(2)}) %collective-permute-start.11) | collective-permute-done | bytes 426016 | tf_op jit(solution)/shard_map/ppermute | solution.py:372
  105.4 9.2 %collective-permute-start.12 = (bf16[128,1664]{1,0:T(8,128)(2,1)}, bf16[128,1664]{1,0:T(8,128)(2,1)S(1)}, u32[]{:S(2)}, u32[]{:S(2)}) collective-permute-start(bf16[128,1664]{1,0:T(8,128)(2,1)} %collective-permute-done.11.refs_0_), channel_id=1, source_target_pairs={{0,2},{1,5},{2,0},{3,7},{4,6},{5,1},{6,4},{7,3},{8,10},{9,13},{10,... | collective-permute-start | bytes 1277960 | tf_op jit(solution)/shard_map/ppermute | solution.py:372
  114.6 7.7 %collective-permute-done.13.refs_0_ = bf16[128,1664]{1,0:T(8,128)(2,1)} collective-permute-done((bf16[128,1664]{1,0:T(8,128)(2,1)}, bf16[128,1664]{1,0:T(8,128)(2,1)}, u32[]{:S(2)}, u32[]{:S(2)}) %collective-permute-start.13) | collective-permute-done | bytes 426016 | tf_op jit(solution)/shard_map/ppermute | solution.py:372
  126.4 4.3 %collective-permute-done.14.refs_1_ = bf16[128,1664]{1,0:T(8,128)(2,1)S(1)} collective-permute-done((bf16[128,1664]{1,0:T(8,128)(2,1)}, bf16[128,1664]{1,0:T(8,128)(2,1)S(1)}, u32[]{:S(2)}, u32[]{:S(2)}) %collective-permute-start.14) | collective-permute-done | bytes 426016 | tf_op jit(solution)/shard_map/ppermute | solution.py:372
  132.7 2.6 collective-permute-done.16.refs_1_
  137.3 5.4 %all-to-all-start.1 = ((bf16[4,384,512]{2,1,0:T(8,128)(2,1)}), bf16[4,384,512]{2,1,0:T(8,128)(2,1)}, u32[]{:S(2)}, u32[]{:S(2)}) async-start(bf16[4,384,512]{2,1,0:T(8,128)(2,1)} %get-tuple-element.64), calls=%async_computation.1 | async-start | bytes 3145728 | tf_op jit(solution)/shard_map/all_to_all | solution.py:388
  146.3 6.0 %hidden.4 = (bf16[512,1024]{1,0:T(8,128)(2,1)S(1)}, f32[512,128]{1,0:T(8,128)S(1)}) custom-call(s32[2]{0:T(128)S(1)} %pad_add_fusion.1.place_ref, bf16[256,1664]{1,0:T(8,128)(2,1)} %stack.160.first_ref, bf16[256,1664]{1,0:T(8,128)(2,1)} %collective-permute-done.9.second_ref, bf16[1536,1024]{1,0:T(8,128)(2,1)S(1)} %bitcast.44, ...), custom_call_target="tpu_custom_call" | custom-call | flops 1000000 | bytes 100000 | tf_op jit(solution)/shard_map/hidden/pallas_call | solution.py:299
  153.3 2.3 collective-permute-done.19.second_ref
  155.7 5.8 %hidden.5 = (bf16[512,1024]{1,0:T(8,128)(2,1)S(1)}, f32[512,128]{1,0:T(8,128)S(1)}) custom-call(s32[2]{0:T(128)S(1)} %pad_add_fusion.1.place_ref, bf16[256,1664]{1,0:T(8,128)(2,1)S(1)} %copy-done.5, bf16[256,1664]{1,0:T(8,128)(2,1)} %collective-permute-done.19.second_ref, bf16[1536,1024]{1,0:T(8,128)(2,1)S(1)} %bitcast.45, ...), custom_call_target="tpu_custom_call" | custom-call | flops 1000000 | bytes 100000 | tf_op jit(solution)/shard_map/hidden/pallas_call | solution.py:299
  162.4 2.3 collective-permute-done.18.second_ref
  164.8 5.8 %hidden.6 = (bf16[512,1024]{1,0:T(8,128)(2,1)S(1)}, f32[512,128]{1,0:T(8,128)S(1)}) custom-call(s32[2]{0:T(128)S(1)} %pad_add_fusion.1.place_ref, bf16[256,1664]{1,0:T(8,128)(2,1)S(1)} %copy-done.3, bf16[256,1664]{1,0:T(8,128)(2,1)} %collective-permute-done.18.second_ref, bf16[1536,1024]{1,0:T(8,128)(2,1)S(1)} %bitcast.46, ...), custom_call_target="tpu_custom_call" | custom-call | flops 1000000 | bytes 100000 | tf_op jit(solution)/shard_map/hidden/pallas_call | solution.py:299
  171.6 2.3 collective-permute-done.17.second_ref
  173.9 5.7 %hidden.7 = (bf16[512,1024]{1,0:T(8,128)(2,1)S(1)}, f32[512,128]{1,0:T(8,128)S(1)}) custom-call(s32[2]{0:T(128)S(1)} %pad_add_fusion.1.place_ref, bf16[256,1664]{1,0:T(8,128)(2,1)S(1)} %copy-done.1, bf16[256,1664]{1,0:T(8,128)(2,1)} %collective-permute-done.17.second_ref, bf16[1536,1024]{1,0:T(8,128)(2,1)S(1)} %bitcast.47, ...), custom_call_target="tpu_custom_call" | custom-call | flops 1000000 | bytes 100000 | tf_op jit(solution)/shard_map/hidden/pallas_call | solution.py:299
  182.0 3.6 %collective-permute-done.20.other_ref = bf16[1536,512]{1,0:T(8,128)(2,1)S(1)} collective-permute-done((bf16[1536,512]{1,0:T(8,128)(2,1)}, bf16[1536,512]{1,0:T(8,128)(2,1)S(1)}, u32[]{:S(2)}, u32[]{:S(2)}) %collective-permute-start.20) | collective-permute-done | bytes 1572896 | tf_op jit(solution)/shard_map/ppermute | solution.py:372
  187.8 3.6 %down.4 = (bf16[256,1536]{1,0:T(8,128)(2,1)S(1)}, bf16[256,1536]{1,0:T(8,128)(2,1)S(1)}) custom-call(bf16[512,1024]{1,0:T(8,128)(2,1)S(1)} %copy-done.13, f32[512,128]{1,0:T(8,128)S(1)} %copy-done.22, bf16[1536,512]{1,0:T(8,128)(2,1)} %bitcast.36.mine_ref, bf16[1536,512]{1,0:T(8,128)(2,1)S(1)} %collective-permute-done.20.other_ref), custom_call_target="tpu_custom_call" | custom-call | flops 1000000 | bytes 100000 | tf_op jit(solution)/shard_map/down/pallas_call | solution.py:333
  191.4 1.6 collective-permute-start.22
  193.0 3.3 %down.5 = (bf16[256,1536]{1,0:T(8,128)(2,1)S(1)}, bf16[256,1536]{1,0:T(8,128)(2,1)S(1)}) custom-call(bf16[512,1024]{1,0:T(8,128)(2,1)S(1)} %copy-done.11, f32[512,128]{1,0:T(8,128)S(1)} %copy-done.17, bf16[1536,512]{1,0:T(8,128)(2,1)} %bitcast.36.mine_ref, bf16[1536,512]{1,0:T(8,128)(2,1)S(1)} %collective-permute-done.20.other_ref, ...), custom_call_target="tpu_custom_call" | custom-call | flops 1000000 | bytes 100000 | tf_op jit(solution)/shard_map/down/pallas_call | solution.py:333
  196.9 6.6 %collective-permute-done.22.came_ref = bf16[256,1536]{1,0:T(8,128)(2,1)S(1)} collective-permute-done((bf16[256,1536]{1,0:T(8,128)(2,1)S(1)}, bf16[256,1536]{1,0:T(8,128)(2,1)S(1)}, u32[]{:S(2)}, u32[]{:S(2)}) %collective-permute-start.22) | collective-permute-done | bytes 786464 | tf_op jit(solution)/shard_map/ppermute | solution.py:372
  203.7 1.5 collective-permute-start.23
  205.2 3.3 %down.6 = (bf16[256,1536]{1,0:T(8,128)(2,1)S(1)}, bf16[256,1536]{1,0:T(8,128)(2,1)S(1)}) custom-call(bf16[512,1024]{1,0:T(8,128)(2,1)S(1)} %copy-done.9, f32[512,128]{1,0:T(8,128)S(1)} %copy-done.15, bf16[1536,512]{1,0:T(8,128)(2,1)} %bitcast.36.mine_ref, bf16[1536,512]{1,0:T(8,128)(2,1)S(1)} %collective-permute-done.20.other_ref, ...), custom_call_target="tpu_custom_call" | custom-call | flops 1000000 | bytes 100000 | tf_op jit(solution)/shard_map/down/pallas_call | solution.py:333
  208.5 1.6 collective-permute-start.25
  210.1 5.7 %collective-permute-done.23.came_ref = bf16[128,1536]{1,0:T(8,128)(2,1)S(1)} collective-permute-done((bf16[128,1536]{1,0:T(8,128)(2,1)S(1)}, bf16[128,1536]{1,0:T(8,128)(2,1)S(1)}, u32[]{:S(2)}, u32[]{:S(2)}) %collective-permute-start.23) | collective-permute-done | bytes 393248 | tf_op jit(solution)/shard_map/ppermute | solution.py:372
  216.3 1.5 collective-permute-start.26
  217.8 3.8 %collective-permute-start.27 = (bf16[128,1536]{1,0:T(8,128)(2,1)S(1)}, bf16[128,1536]{1,0:T(8,128)(2,1)S(1)}, u32[]{:S(2)}, u32[]{:S(2)}) collective-permute-start(bf16[128,1536]{1,0:T(8,128)(2,1)S(1)} %close.3.rest_0_), channel_id=1, source_target_pairs={{0,24},{8,16},{16,8},{24,0},{1,25},{9,17},{17,9},{25,1},{2,26},{10... | collective-permute-start | bytes 1179656 | tf_op jit(solution)/shard_map/ppermute | solution.py:372
  221.7 3.3 %down.7 = (bf16[256,1536]{1,0:T(8,128)(2,1)S(1)}, bf16[256,1536]{1,0:T(8,128)(2,1)S(1)}) custom-call(bf16[512,1024]{1,0:T(8,128)(2,1)S(1)} %copy-done.7, f32[512,128]{1,0:T(8,128)S(1)} %get-tuple-element.62.rest_0_.share_ref, bf16[1536,512]{1,0:T(8,128)(2,1)} %bitcast.36.mine_ref, bf16[1536,512]{1,0:T(8,128)(2,1)S(1)} %collective-permute-done.20.other_ref, ...), custom_call_target="tpu_custom_call" | custom-call | flops 1000000 | bytes 100000 | tf_op jit(solution)/shard_map/down/pallas_call | solution.py:333
  225.0 1.6 collective-permute-start.24
  226.6 1.9 collective-permute-done.26.came_ref
  229.8 1.6 collective-permute-start.28
  231.3 9.5 %collective-permute-start.31 = (bf16[128,1536]{1,0:T(8,128)(2,1)S(1)}, bf16[128,1536]{1,0:T(8,128)(2,1)S(1)}, u32[]{:S(2)}, u32[]{:S(2)}) collective-permute-start(bf16[128,1536]{1,0:T(8,128)(2,1)S(1)} %close.4.rest_0_), channel_id=1, source_target_pairs={{0,16},{8,24},{16,0},{24,8},{1,17},{9,25},{17,1},{25,9},{2,18},{10... | collective-permute-start | bytes 1179656 | tf_op jit(solution)/shard_map/ppermute | solution.py:372
  243.1 5.2 %collective-permute-start.30 = (bf16[128,1536]{1,0:T(8,128)(2,1)S(1)}, bf16[128,1536]{1,0:T(8,128)(2,1)S(1)}, u32[]{:S(2)}, u32[]{:S(2)}) collective-permute-start(bf16[128,1536]{1,0:T(8,128)(2,1)S(1)} %close.5.rest_0_), channel_id=1, source_target_pairs={{0,8},{8,0},{16,24},{24,16},{1,9},{9,1},{17,25},{25,17},{2,10},{10... | collective-permute-start | bytes 1179656 | tf_op jit(solution)/shard_map/ppermute | solution.py:372
  248.3 7.6 %collective-permute-done.31.rest_2_ = bf16[128,1536]{1,0:T(8,128)(2,1)S(1)} collective-permute-done((bf16[128,1536]{1,0:T(8,128)(2,1)S(1)}, bf16[128,1536]{1,0:T(8,128)(2,1)S(1)}, u32[]{:S(2)}, u32[]{:S(2)}) %collective-permute-start.31) | collective-permute-done | bytes 393248 | tf_op jit(solution)/shard_map/ppermute | solution.py:372
  255.9 5.2 %collective-permute-done.30.rest_1_ = bf16[128,1536]{1,0:T(8,128)(2,1)S(1)} collective-permute-done((bf16[128,1536]{1,0:T(8,128)(2,1)S(1)}, bf16[128,1536]{1,0:T(8,128)(2,1)S(1)}, u32[]{:S(2)}, u32[]{:S(2)}) %collective-permute-start.30) | collective-permute-done | bytes 393248 | tf_op jit(solution)/shard_map/ppermute | solution.py:372
  (135 shorter events, 42.2 us)
Async XLA Ops:
  1.6 15.1 %copy-start.27 = (s32[8]{0:T(128)S(1)}, s32[8]{0:T(128)}, u32[]{:S(2)}) copy-start(s32[8]{0:T(128)} %param.20) | copy-start | bytes 100
  1.6 15.4 %collective-permute-start = (bf16[48,1536]{1,0:T(8,128)(2,1)S(1)}, bf16[48,1536]{1,0:T(8,128)(2,1)S(1)}, u32[]{:S(2)}, u32[]{:S(2)}) collective-permute-start(bf16[48,1536]{1,0:T(8,128)(2,1)S(1)} %constant_dynamic-slice_fusion), channel_id=1, source_target_pairs={{0,8},{8,0},{16,24},{24,16},{1,9},{9,1},{17,25},{25,17},{2,10},{10... | collective-permute-start | bytes 442376 | tf_op jit(solution)/shard_map/ppermute | solution.py:372
  4.7 14.0 %collective-permute-start.1 = (bf16[48,1536]{1,0:T(8,128)(2,1)S(1)}, bf16[48,1536]{1,0:T(8,128)(2,1)S(1)}, u32[]{:S(2)}, u32[]{:S(2)}) collective-permute-start(bf16[48,1536]{1,0:T(8,128)(2,1)S(1)} %constant_dynamic-slice_fusion), channel_id=1, source_target_pairs={{0,16},{8,24},{16,0},{24,8},{1,17},{9,25},{17,1},{25,9},{2,18},{10... | collective-permute-start | bytes 442376 | tf_op jit(solution)/shard_map/ppermute | solution.py:372
  7.3 11.4 %collective-permute-start.2 = (bf16[48,1536]{1,0:T(8,128)(2,1)S(1)}, bf16[48,1536]{1,0:T(8,128)(2,1)S(1)}, u32[]{:S(2)}, u32[]{:S(2)}) collective-permute-start(bf16[48,1536]{1,0:T(8,128)(2,1)S(1)} %constant_dynamic-slice_fusion), channel_id=1, source_target_pairs={{0,24},{8,16},{16,8},{24,0},{1,25},{9,17},{17,9},{25,1},{2,26},{10... | collective-permute-start | bytes 442376 | tf_op jit(solution)/shard_map/ppermute | solution.py:372
  19.3 5.8 %copy-start.25 = (bf16[16,1536]{1,0:T(8,128)(2,1)S(1)}, bf16[16,1536]{1,0:T(8,128)(2,1)}, u32[]{:S(2)}) copy-start(bf16[16,1536]{1,0:T(8,128)(2,1)} %query_ref.1) | copy-start | bytes 147460
  19.3 20.8 %copy-start.26 = (s32[16,32]{1,0:T(8,128)S(1)}, s32[16,32]{1,0:T(8,128)}, u32[]{:S(2)}) copy-start(s32[16,32]{1,0:T(8,128)} %param.21) | copy-start | bytes 6148
  19.3 20.8 %copy-start.30 = (s32[8,32]{1,0:T(8,128)S(1)}, s32[8,32]{1,0:T(8,128)}, u32[]{:S(2)}) copy-start(s32[8,32]{1,0:T(8,128)} %param.19) | copy-start | bytes 3076
  19.3 76.0 %all-to-all-start = ((bf16[4,384,1024]{2,1,0:T(8,128)(2,1)}), bf16[4,384,1024]{2,1,0:T(8,128)(2,1)S(1)}, u32[]{:S(2)}, u32[]{:S(2)}) async-start(bf16[4,384,1024]{2,1,0:T(8,128)(2,1)} %get-tuple-element.59), calls=%async_computation | async-start | bytes 6291456 | tf_op jit(solution)/shard_map/all_to_all | solution.py:388
  26.8 14.0 %collective-permute-start.3 = (bf16[144,1536]{1,0:T(8,128)(2,1)}, bf16[144,1536]{1,0:T(8,128)(2,1)}, u32[]{:S(2)}, u32[]{:S(2)}) collective-permute-start(bf16[144,1536]{1,0:T(8,128)(2,1)} %stack.158.refs_0_.rest_1_), channel_id=1, source_target_pairs={{0,2},{1,5},{2,0},{3,7},{4,6},{5,1},{6,4},{7,3},{8,10},{9,13},{10,... | collective-permute-start | bytes 1327112 | tf_op jit(solution)/shard_map/ppermute | solution.py:372
  43.0 13.4 %collective-permute-start.4 = (bf16[288,1536]{1,0:T(8,128)(2,1)}, bf16[288,1536]{1,0:T(8,128)(2,1)}, u32[]{:S(2)}, u32[]{:S(2)}) collective-permute-start(bf16[288,1536]{1,0:T(8,128)(2,1)} %stack.159), channel_id=1, source_target_pairs={{0,4},{1,3},{2,6},{3,1},{4,0},{5,7},{6,2},{7,5},{8,12},{9,11},{10,... | collective-permute-start | bytes 2654216 | tf_op jit(solution)/shard_map/ppermute | solution.py:372
  45.3 11.6 %copy-start.29 = (bf16[1536]{0:T(1024)(128)(2,1)S(1)}, bf16[1536]{0:T(1024)(128)(2,1)}, u32[]{:S(2)}) copy-start(bf16[1536]{0:T(1024)(128)(2,1)} %param.25) | copy-start | bytes 9220
  45.3 13.3 %copy-start.28 = (s32[128,8]{0,1:T(8,128)S(1)}, s32[128,8]{0,1:T(8,128)}, u32[]{:S(2)}) copy-start(s32[128,8]{0,1:T(8,128)} %param.27) | copy-start | bytes 12292
  56.4 16.7 %collective-permute-start.7 = (bf16[288,1536]{1,0:T(8,128)(2,1)}, bf16[288,1536]{1,0:T(8,128)(2,1)}, u32[]{:S(2)}, u32[]{:S(2)}) collective-permute-start(bf16[288,1536]{1,0:T(8,128)(2,1)} %collective-permute-done.4.rest_3_), channel_id=1, source_target_pairs={{0,1},{1,0},{2,3},{3,2},{4,5},{5,4},{6,7},{7,6},{8,9},{9,8},{10,11... | collective-permute-start | bytes 2654216 | tf_op jit(solution)/shard_map/ppermute | solution.py:372
  56.4 16.7 %collective-permute-start.5 = (bf16[144,1536]{1,0:T(8,128)(2,1)}, bf16[144,1536]{1,0:T(8,128)(2,1)}, u32[]{:S(2)}, u32[]{:S(2)}) collective-permute-start(bf16[144,1536]{1,0:T(8,128)(2,1)} %stack.158.refs_0_.rest_1_), channel_id=1, source_target_pairs={{0,1},{1,0},{2,3},{3,2},{4,5},{5,4},{6,7},{7,6},{8,9},{9,8},{10,11... | collective-permute-start | bytes 1327112 | tf_op jit(solution)/shard_map/ppermute | solution.py:372
  56.9 16.2 %collective-permute-start.6 = (bf16[144,1536]{1,0:T(8,128)(2,1)}, bf16[144,1536]{1,0:T(8,128)(2,1)}, u32[]{:S(2)}, u32[]{:S(2)}) collective-permute-start(bf16[144,1536]{1,0:T(8,128)(2,1)} %collective-permute-done.3.refs_1_.rest_2_), channel_id=1, source_target_pairs={{0,1},{1,0},{2,3},{3,2},{4,5},{5,4},{6,7},{7,6},{8,9},{9,8},{10,11... | collective-permute-start | bytes 1327112 | tf_op jit(solution)/shard_map/ppermute | solution.py:372
  79.4 8.4 %collective-permute-start.8 = (bf16[128,1664]{1,0:T(8,128)(2,1)}, bf16[128,1664]{1,0:T(8,128)(2,1)S(1)}, u32[]{:S(2)}, u32[]{:S(2)}) collective-permute-start(bf16[128,1664]{1,0:T(8,128)(2,1)} %get-tuple-element.58.refs_0_), channel_id=1, source_target_pairs={{0,2},{1,5},{2,0},{3,7},{4,6},{5,1},{6,4},{7,3},{8,10},{9,13},{10,... | collective-permute-start | bytes 1277960 | tf_op jit(solution)/shard_map/ppermute | solution.py:372
  80.9 24.5 %collective-permute-start.11 = (bf16[128,1664]{1,0:T(8,128)(2,1)}, bf16[128,1664]{1,0:T(8,128)(2,1)}, u32[]{:S(2)}, u32[]{:S(2)}) collective-permute-start(bf16[128,1664]{1,0:T(8,128)(2,1)} %get-tuple-element.58.refs_0_), channel_id=1, source_target_pairs={{0,8},{8,0},{16,24},{24,16},{1,9},{9,1},{17,25},{25,17},{2,10},{10... | collective-permute-start | bytes 1277960 | tf_op jit(solution)/shard_map/ppermute | solution.py:372
  83.0 39.4 %collective-permute-start.13 = (bf16[128,1664]{1,0:T(8,128)(2,1)}, bf16[128,1664]{1,0:T(8,128)(2,1)}, u32[]{:S(2)}, u32[]{:S(2)}) collective-permute-start(bf16[128,1664]{1,0:T(8,128)(2,1)} %get-tuple-element.58.refs_0_), channel_id=1, source_target_pairs={{0,16},{8,24},{16,0},{24,8},{1,17},{9,25},{17,1},{25,9},{2,18},{10... | collective-permute-start | bytes 1277960 | tf_op jit(solution)/shard_map/ppermute | solution.py:372
  85.3 38.5 %collective-permute-start.15 = (bf16[128,1664]{1,0:T(8,128)(2,1)}, bf16[128,1664]{1,0:T(8,128)(2,1)}, u32[]{:S(2)}, u32[]{:S(2)}) collective-permute-start(bf16[128,1664]{1,0:T(8,128)(2,1)} %get-tuple-element.58.refs_0_), channel_id=1, source_target_pairs={{0,24},{8,16},{16,8},{24,0},{1,25},{9,17},{17,9},{25,1},{2,26},{10... | collective-permute-start | bytes 1277960 | tf_op jit(solution)/shard_map/ppermute | solution.py:372
  89.8 47.5 %collective-permute-start.9 = (bf16[256,1664]{1,0:T(8,128)(2,1)}, bf16[256,1664]{1,0:T(8,128)(2,1)}, u32[]{:S(2)}, u32[]{:S(2)}) collective-permute-start(bf16[256,1664]{1,0:T(8,128)(2,1)} %stack.160.first_ref), channel_id=1, source_target_pairs={{0,4},{1,3},{2,6},{3,1},{4,0},{5,7},{6,2},{7,5},{8,12},{9,11},{10,... | collective-permute-start | bytes 2555912 | tf_op jit(solution)/shard_map/ppermute | solution.py:372
  95.3 51.0 %collective-permute-start.10 = (bf16[1536,1024]{1,0:T(8,128)(2,1)S(1)}, bf16[1536,1024]{1,0:T(8,128)(2,1)}, u32[]{:S(2)}, u32[]{:S(2)}) collective-permute-start(bf16[1536,1024]{1,0:T(8,128)(2,1)S(1)} %bitcast.43), channel_id=1, source_target_pairs={{0,1},{1,0},{2,3},{3,2},{4,5},{5,4},{6,7},{7,6},{8,9},{9,8},{10,11... | collective-permute-start | bytes 9437192 | tf_op jit(solution)/shard_map/ppermute | solution.py:372
  105.4 19.0 %collective-permute-start.12 = (bf16[128,1664]{1,0:T(8,128)(2,1)}, bf16[128,1664]{1,0:T(8,128)(2,1)S(1)}, u32[]{:S(2)}, u32[]{:S(2)}) collective-permute-start(bf16[128,1664]{1,0:T(8,128)(2,1)} %collective-permute-done.11.refs_0_), channel_id=1, source_target_pairs={{0,2},{1,5},{2,0},{3,7},{4,6},{5,1},{6,4},{7,3},{8,10},{9,13},{10,... | collective-permute-start | bytes 1277960 | tf_op jit(solution)/shard_map/ppermute | solution.py:372
  122.4 8.3 %collective-permute-start.14 = (bf16[128,1664]{1,0:T(8,128)(2,1)}, bf16[128,1664]{1,0:T(8,128)(2,1)S(1)}, u32[]{:S(2)}, u32[]{:S(2)}) collective-permute-start(bf16[128,1664]{1,0:T(8,128)(2,1)} %collective-permute-done.13.refs_0_), channel_id=1, source_target_pairs={{0,2},{1,5},{2,0},{3,7},{4,6},{5,1},{6,4},{7,3},{8,10},{9,13},{10,... | collective-permute-start | bytes 1277960 | tf_op jit(solution)/shard_map/ppermute | solution.py:372
  123.9 11.4 %collective-permute-start.16 = (bf16[128,1664]{1,0:T(8,128)(2,1)}, bf16[128,1664]{1,0:T(8,128)(2,1)S(1)}, u32[]{:S(2)}, u32[]{:S(2)}) collective-permute-start(bf16[128,1664]{1,0:T(8,128)(2,1)} %collective-permute-done.15.refs_0_), channel_id=1, source_target_pairs={{0,2},{1,5},{2,0},{3,7},{4,6},{5,1},{6,4},{7,3},{8,10},{9,13},{10,... | collective-permute-start | bytes 1277960 | tf_op jit(solution)/shard_map/ppermute | solution.py:372
  137.3 44.7 %all-to-all-start.1 = ((bf16[4,384,512]{2,1,0:T(8,128)(2,1)}), bf16[4,384,512]{2,1,0:T(8,128)(2,1)}, u32[]{:S(2)}, u32[]{:S(2)}) async-start(bf16[4,384,512]{2,1,0:T(8,128)(2,1)} %get-tuple-element.64), calls=%async_computation.1 | async-start | bytes 3145728 | tf_op jit(solution)/shard_map/all_to_all | solution.py:388
  142.6 13.0 %collective-permute-start.19 = (bf16[256,1664]{1,0:T(8,128)(2,1)}, bf16[256,1664]{1,0:T(8,128)(2,1)}, u32[]{:S(2)}, u32[]{:S(2)}) collective-permute-start(bf16[256,1664]{1,0:T(8,128)(2,1)} %copy-done.4), channel_id=1, source_target_pairs={{0,4},{1,3},{2,6},{3,1},{4,0},{5,7},{6,2},{7,5},{8,12},{9,11},{10,... | collective-permute-start | bytes 2555912 | tf_op jit(solution)/shard_map/ppermute | solution.py:372
  144.2 20.6 %collective-permute-start.18 = (bf16[256,1664]{1,0:T(8,128)(2,1)}, bf16[256,1664]{1,0:T(8,128)(2,1)}, u32[]{:S(2)}, u32[]{:S(2)}) collective-permute-start(bf16[256,1664]{1,0:T(8,128)(2,1)} %copy-done.2), channel_id=1, source_target_pairs={{0,4},{1,3},{2,6},{3,1},{4,0},{5,7},{6,2},{7,5},{8,12},{9,11},{10,... | collective-permute-start | bytes 2555912 | tf_op jit(solution)/shard_map/ppermute | solution.py:372
  144.7 29.2 %collective-permute-start.17 = (bf16[256,1664]{1,0:T(8,128)(2,1)}, bf16[256,1664]{1,0:T(8,128)(2,1)}, u32[]{:S(2)}, u32[]{:S(2)}) collective-permute-start(bf16[256,1664]{1,0:T(8,128)(2,1)} %copy-done), channel_id=1, source_target_pairs={{0,4},{1,3},{2,6},{3,1},{4,0},{5,7},{6,2},{7,5},{8,12},{9,11},{10,... | collective-permute-start | bytes 2555912 | tf_op jit(solution)/shard_map/ppermute | solution.py:372
  146.3 9.4 %copy-start.5 = (bf16[256,1664]{1,0:T(8,128)(2,1)S(1)}, bf16[256,1664]{1,0:T(8,128)(2,1)}, u32[]{:S(2)}) copy-start(bf16[256,1664]{1,0:T(8,128)(2,1)} %copy-done.4) | copy-start | bytes 2555908
  155.7 9.1 %copy-start.3 = (bf16[256,1664]{1,0:T(8,128)(2,1)S(1)}, bf16[256,1664]{1,0:T(8,128)(2,1)}, u32[]{:S(2)}) copy-start(bf16[256,1664]{1,0:T(8,128)(2,1)} %copy-done.2) | copy-start | bytes 2555908
  162.4 8.1 %copy-start.14 = (f32[512,128]{1,0:T(8,128)}, f32[512,128]{1,0:T(8,128)S(1)}, u32[]{:S(2)}) copy-start(f32[512,128]{1,0:T(8,128)S(1)} %get-tuple-element.65.rest_0_.share_ref) | copy-start | bytes 786436
  164.8 9.1 %copy-start.1 = (bf16[256,1664]{1,0:T(8,128)(2,1)S(1)}, bf16[256,1664]{1,0:T(8,128)(2,1)}, u32[]{:S(2)}) copy-start(bf16[256,1664]{1,0:T(8,128)(2,1)} %copy-done) | copy-start | bytes 2555908
  182.0 3.6 %collective-permute-start.20 = (bf16[1536,512]{1,0:T(8,128)(2,1)}, bf16[1536,512]{1,0:T(8,128)(2,1)S(1)}, u32[]{:S(2)}, u32[]{:S(2)}) collective-permute-start(bf16[1536,512]{1,0:T(8,128)(2,1)} %bitcast.36.mine_ref), channel_id=1, source_target_pairs={{0,1},{1,0},{2,3},{3,2},{4,5},{5,4},{6,7},{7,6},{8,9},{9,8},{10,11... | collective-permute-start | bytes 4718600 | tf_op jit(solution)/shard_map/ppermute | solution.py:372
  191.4 12.1 %collective-permute-start.22 = (bf16[256,1536]{1,0:T(8,128)(2,1)S(1)}, bf16[256,1536]{1,0:T(8,128)(2,1)S(1)}, u32[]{:S(2)}, u32[]{:S(2)}) collective-permute-start(bf16[256,1536]{1,0:T(8,128)(2,1)S(1)} %get-tuple-element.74), channel_id=1, source_target_pairs={{0,4},{1,3},{2,6},{3,1},{4,0},{5,7},{6,2},{7,5},{8,12},{9,11},{10,... | collective-permute-start | bytes 2359304 | tf_op jit(solution)/shard_map/ppermute | solution.py:372
  196.3 8.9 %copy-start.9 = (bf16[512,1024]{1,0:T(8,128)(2,1)S(1)}, bf16[512,1024]{1,0:T(8,128)(2,1)}, u32[]{:S(2)}) copy-start(bf16[512,1024]{1,0:T(8,128)(2,1)} %copy-done.8) | copy-start | bytes 3145732
  196.3 8.9 %copy-start.15 = (f32[512,128]{1,0:T(8,128)S(1)}, f32[512,128]{1,0:T(8,128)}, u32[]{:S(2)}) copy-start(f32[512,128]{1,0:T(8,128)} %copy-done.14) | copy-start | bytes 786436
  196.3 19.8 %collective-permute-start.21 = (bf16[256,1536]{1,0:T(8,128)(2,1)S(1)}, bf16[256,1536]{1,0:T(8,128)(2,1)S(1)}, u32[]{:S(2)}, u32[]{:S(2)}) collective-permute-start(bf16[256,1536]{1,0:T(8,128)(2,1)S(1)} %get-tuple-element.73), channel_id=1, source_target_pairs={{0,4},{1,3},{2,6},{3,1},{4,0},{5,7},{6,2},{7,5},{8,12},{9,11},{10,... | collective-permute-start | bytes 2359304 | tf_op jit(solution)/shard_map/ppermute | solution.py:372
  203.7 12.1 %collective-permute-start.23 = (bf16[128,1536]{1,0:T(8,128)(2,1)S(1)}, bf16[128,1536]{1,0:T(8,128)(2,1)S(1)}, u32[]{:S(2)}, u32[]{:S(2)}) collective-permute-start(bf16[128,1536]{1,0:T(8,128)(2,1)S(1)} %get-tuple-element.76.rest_0_), channel_id=1, source_target_pairs={{0,2},{1,5},{2,0},{3,7},{4,6},{5,1},{6,4},{7,3},{8,10},{9,13},{10,... | collective-permute-start | bytes 1179656 | tf_op jit(solution)/shard_map/ppermute | solution.py:372
  208.5 20.3 %collective-permute-start.25 = (bf16[256,1536]{1,0:T(8,128)(2,1)S(1)}, bf16[256,1536]{1,0:T(8,128)(2,1)S(1)}, u32[]{:S(2)}, u32[]{:S(2)}) collective-permute-start(bf16[256,1536]{1,0:T(8,128)(2,1)S(1)} %get-tuple-element.82), channel_id=1, source_target_pairs={{0,4},{1,3},{2,6},{3,1},{4,0},{5,7},{6,2},{7,5},{8,12},{9,11},{10,... | collective-permute-start | bytes 2359304 | tf_op jit(solution)/shard_map/ppermute | solution.py:372
  215.9 5.8 %copy-start.7 = (bf16[512,1024]{1,0:T(8,128)(2,1)S(1)}, bf16[512,1024]{1,0:T(8,128)(2,1)}, u32[]{:S(2)}) copy-start(bf16[512,1024]{1,0:T(8,128)(2,1)} %copy-done.6) | copy-start | bytes 3145732
  216.3 12.1 %collective-permute-start.26 = (bf16[128,1536]{1,0:T(8,128)(2,1)S(1)}, bf16[128,1536]{1,0:T(8,128)(2,1)S(1)}, u32[]{:S(2)}, u32[]{:S(2)}) collective-permute-start(bf16[128,1536]{1,0:T(8,128)(2,1)S(1)} %get-tuple-element.79.rest_0_), channel_id=1, source_target_pairs={{0,2},{1,5},{2,0},{3,7},{4,6},{5,1},{6,4},{7,3},{8,10},{9,13},{10,... | collective-permute-start | bytes 1179656 | tf_op jit(solution)/shard_map/ppermute | solution.py:372
  217.8 11.7 %collective-permute-start.27 = (bf16[128,1536]{1,0:T(8,128)(2,1)S(1)}, bf16[128,1536]{1,0:T(8,128)(2,1)S(1)}, u32[]{:S(2)}, u32[]{:S(2)}) collective-permute-start(bf16[128,1536]{1,0:T(8,128)(2,1)S(1)} %close.3.rest_0_), channel_id=1, source_target_pairs={{0,24},{8,16},{16,8},{24,0},{1,25},{9,17},{17,9},{25,1},{2,26},{10... | collective-permute-start | bytes 1179656 | tf_op jit(solution)/shard_map/ppermute | solution.py:372
  225.0 16.4 %collective-permute-start.24 = (bf16[256,1536]{1,0:T(8,128)(2,1)S(1)}, bf16[256,1536]{1,0:T(8,128)(2,1)S(1)}, u32[]{:S(2)}, u32[]{:S(2)}) collective-permute-start(bf16[256,1536]{1,0:T(8,128)(2,1)S(1)} %get-tuple-element.81), channel_id=1, source_target_pairs={{0,4},{1,3},{2,6},{3,1},{4,0},{5,7},{6,2},{7,5},{8,12},{9,11},{10,... | collective-permute-start | bytes 2359304 | tf_op jit(solution)/shard_map/ppermute | solution.py:372
  229.8 11.1 %collective-permute-start.28 = (bf16[128,1536]{1,0:T(8,128)(2,1)S(1)}, bf16[128,1536]{1,0:T(8,128)(2,1)S(1)}, u32[]{:S(2)}, u32[]{:S(2)}) collective-permute-start(bf16[128,1536]{1,0:T(8,128)(2,1)S(1)} %get-tuple-element.85.rest_0_), channel_id=1, source_target_pairs={{0,2},{1,5},{2,0},{3,7},{4,6},{5,1},{6,4},{7,3},{8,10},{9,13},{10,... | collective-permute-start | bytes 1179656 | tf_op jit(solution)/shard_map/ppermute | solution.py:372
  231.3 24.6 %collective-permute-start.31 = (bf16[128,1536]{1,0:T(8,128)(2,1)S(1)}, bf16[128,1536]{1,0:T(8,128)(2,1)S(1)}, u32[]{:S(2)}, u32[]{:S(2)}) collective-permute-start(bf16[128,1536]{1,0:T(8,128)(2,1)S(1)} %close.4.rest_0_), channel_id=1, source_target_pairs={{0,16},{8,24},{16,0},{24,8},{1,17},{9,25},{17,1},{25,9},{2,18},{10... | collective-permute-start | bytes 1179656 | tf_op jit(solution)/shard_map/ppermute | solution.py:372
  240.8 20.2 %copy-start.19 = (f32[128,1536]{1,0:T(8,128)S(1)}, f32[128,1536]{1,0:T(8,128)}, u32[]{:S(2)}) copy-start(f32[128,1536]{1,0:T(8,128)} %get-tuple-element.57.stream_ref) | copy-start | bytes 2359300
  241.6 14.3 %collective-permute-start.29 = (bf16[128,1536]{1,0:T(8,128)(2,1)S(1)}, bf16[128,1536]{1,0:T(8,128)(2,1)S(1)}, u32[]{:S(2)}, u32[]{:S(2)}) collective-permute-start(bf16[128,1536]{1,0:T(8,128)(2,1)S(1)} %get-tuple-element.87), channel_id=1, source_target_pairs={{0,2},{1,5},{2,0},{3,7},{4,6},{5,1},{6,4},{7,3},{8,10},{9,13},{10,... | collective-permute-start | bytes 1179656 | tf_op jit(solution)/shard_map/ppermute | solution.py:372
  243.1 17.9 %collective-permute-start.30 = (bf16[128,1536]{1,0:T(8,128)(2,1)S(1)}, bf16[128,1536]{1,0:T(8,128)(2,1)S(1)}, u32[]{:S(2)}, u32[]{:S(2)}) collective-permute-start(bf16[128,1536]{1,0:T(8,128)(2,1)S(1)} %close.5.rest_0_), channel_id=1, source_target_pairs={{0,8},{8,0},{16,24},{24,16},{1,9},{9,1},{17,25},{25,17},{2,10},{10... | collective-permute-start | bytes 1179656 | tf_op jit(solution)/shard_map/ppermute | solution.py:372
  (18 other events, 34.0 us)

commit v5 on v4

--- a/solution.py
+++ b/solution.py
@@ -274,11 +274,12 @@
     )(chosen, at, queries, fresh, here, back, prefill, residual, gain, router, routes, *parts)
 
 
-def hidden_kernel(place_ref, first_ref, second_ref, mine_ref, other_ref, *rest):
-    hidden_ref, share_ref, rows_ref = rest[-3:]
-    rows = first_ref.shape[0]
-    rows_ref[:rows, :] = first_ref[...]
-    rows_ref[rows:, :] = second_ref[...]
+def hidden_kernel(count, place_ref, *refs):
+    pieces, (mine_ref, other_ref) = refs[:count], refs[count : count + 2]
+    hidden_ref, share_ref, rows_ref = refs[-3:]
+    rows = pieces[0].shape[0]
+    for n, piece in enumerate(pieces):
+        rows_ref[n * rows : (n + 1) * rows, :] = piece[...]
     gates = rows_ref[:, D:].astype(F32)
     gates = gates + pltpu.roll(gates, 64, 1)
     lane = lax.broadcasted_iota(jnp.int32, gates.shape, 1)
@@ -294,11 +295,11 @@
     share_ref[...] = jnp.where(lane == 0, shares[0], shares[1])
 
 
-def make_hidden(place, first, second, mine, other, *earlier):
-    rows = 2 * first.shape[0]
+def make_hidden(place, pieces, mine, other, *earlier):
+    rows = sum(piece.shape[0] for piece in pieces)
     return pl.pallas_call(
-        hidden_kernel,
-        in_specs=[smem()] + [vmem()] * 4 + [anywhere()] * len(earlier),
+        functools.partial(hidden_kernel, len(pieces)),
+        in_specs=[smem()] + [vmem()] * (len(pieces) + 2) + [anywhere()] * len(earlier),
         out_specs=[vmem()] * 2,
         out_shape=[
             jax.ShapeDtypeStruct((rows, 2 * FF), BF),
@@ -308,11 +309,10 @@
         compiler_params=pltpu.CompilerParams(vmem_limit_bytes=28 * 1024 * 1024),
         cost_estimate=cost(HIDDEN_COST, 10**5),
         name="hidden",
-    )(place, first, second, mine, other, *earlier)
-
-
-def down_kernel(hidden_ref, share_ref, mine_ref, other_ref, *rest):
-    keep_ref, away_ref = rest[-2:]
+    )(place, *pieces, mine, other, *earlier)
+
+
+def down_kernel(count, hidden_ref, share_ref, mine_ref, other_ref, *rest):
     total = None
     for side, held_ref in enumerate((mine_ref, other_ref)):
         made = lax.dot_general(
@@ -323,18 +323,18 @@
         )
         made = share_ref[:, side : side + 1] * made.astype(BF).astype(F32)
         total = made if total is None else total + made
-    rows = keep_ref.shape[0]
-    keep_ref[...] = total[:rows].astype(BF)
-    away_ref[...] = total[rows:].astype(BF)
-
-
-def make_down(hidden, share, mine, other, *earlier):
+    for n, out_ref in enumerate(rest[-count:]):
+        rows = out_ref.shape[0]
+        out_ref[...] = total[n * rows : (n + 1) * rows].astype(BF)
+
+
+def make_down(count, hidden, share, mine, other, *earlier):
     rows = hidden.shape[0]
     return pl.pallas_call(
-        down_kernel,
+        functools.partial(down_kernel, count),
         in_specs=[vmem()] * 4 + [anywhere()] * len(earlier),
-        out_specs=[vmem()] * 2,
-        out_shape=[jax.ShapeDtypeStruct((rows // 2, D), BF)] * 2,
+        out_specs=[vmem()] * count,
+        out_shape=[jax.ShapeDtypeStruct((rows // count, D), BF)] * count,
         compiler_params=pltpu.CompilerParams(vmem_limit_bytes=28 * 1024 * 1024),
         cost_estimate=cost(DOWN_COST, 10**5),
         name="down",
@@ -353,7 +353,7 @@
 
 def pack_experts(gate_up, down_proj):
     depth, experts = gate_up.shape[:2]
-    step = depth // 8
+    step = depth // 4
     block = lambda n: pl.BlockSpec((step, experts, n * FF), lambda s: (s, 0, 0))
     packed = lambda n: pl.BlockSpec((experts, step, n * FF), lambda s: (0, s, 0))
     return pl.pallas_call(
@@ -431,12 +431,16 @@
     return small_call(join_kernel, "join", [keep, came], earlier, [(shape, F32), (shape, BF)])
 
 
-def close_kernel(part_ref, came_ref, *rest):
-    rest[-1][...] = (part_ref[...] + came_ref[...].astype(F32)).astype(BF)
+def close_kernel(count, part_ref, *rest):
+    total = part_ref[...]
+    for ref in rest[:count]:
+        total = total + ref[...].astype(F32)
+    rest[-1][...] = total.astype(BF)
 
 
 def close(part, came, *earlier):
-    return small_call(close_kernel, "close", [part, came], earlier, [(part.shape, BF)])[0]
+    kernel = functools.partial(close_kernel, len(came))
+    return small_call(kernel, "close", [part, *came], earlier, [(part.shape, BF)])[0]
 
 
 def finish_kernel(stream_ref, part_ref, *rest):
@@ -452,27 +456,36 @@
     place = jnp.stack([column * planes + row, beside(column) * planes + row]).astype(jnp.int32)
     across = lambda x, k: swap(x, "gx", lambda i: i ^ k)
 
-    first = [stack_rows([send, swap(send, "gy", near)])]
     mine = [send] + [across(send, k) for k in range(1, planes)]
-    other_pair = swap(after(pair, first[0]), "gy", beside)
-    first += [
-        stack_rows([mine[k], swap(mine[k], "gy", near)], flops=10**6)
-        for k in range(1, planes)
-    ]
+    beyond = [swap(x, "gy", near) for x in mine]
+    first = [stack_rows([mine[k], beyond[k]]) for k in range(3)]
     second = [swap(x, "gy", far) for x in first]
-    hidden, last = [], ()
-    for k in range(planes):
-        hidden.append(make_hidden(place, first[k], second[k], pair, other_pair, *last))
-        last = (hidden[k][1],)
-    down = exchange(after(down, second[0], *first[1:]))
-    down = after(down, hidden[-1][1])
-    other_down = swap(down, "gy", beside)
+    other_pair = swap(after(pair, second[0], *first[1:], mine[3]), "gy", beside)
+    down = exchange(after(down, first[0]))
+    hidden, last = {}, ()
+
+    def inner(k, pieces):
+        hidden[k] = make_hidden(place, pieces, pair, other_pair, *last)
+        return (hidden[k][1],)
+
+    last = inner(0, [first[0], second[0]])
+    first.append(stack_rows([mine[3], beyond[3]], *last))
+    second.append(swap(first[3], "gy", far))
+    last = inner(3, [first[3]])
+    last = inner(1, [first[1], second[1]])
+    last = inner(2, [first[2], second[2]])
+    other_down = swap(after(down, hidden[2][1], second[3]), "gy", beside)
+    outer = make_hidden(place, [second[3]], pair, other_pair, *last)
 
     made, arrived, parts, ends = {}, {}, {}, {}
     last = ()
 
     def put(k):
-        made[k] = make_down(*hidden[k], down, other_down, *last)
+        if k == 3:
+            away = make_down(1, *outer, down, other_down)[0]
+            made[k] = [*make_down(1, *hidden[k], down, other_down, away), away]
+        else:
+            made[k] = make_down(2, *hidden[k], down, other_down, *last)
         arrived[k] = swap(made[k][1], "gy", far)
         return (made[k][0],)
 
@@ -481,22 +494,23 @@
         ends[k] = swap(passed, "gy", near)
         return (passed,)
 
-    def leave(k):
-        passed = close(parts[k], ends[k], *last)
-        ends[k] = across(passed, k)
+    def leave(k, *came):
+        passed = close(parts[k], [ends[k], *came], *last)
+        ends[k] = across(passed, 2 if k == 2 else 1)
         return (passed,)
 
-    order = list(reversed(range(planes)))
-    last = put(order[0])
-    last = put(order[1])
-    last = turn(order[0])
-    for n in range(2, planes):
-        last = put(order[n])
-        last = leave(order[n - 2])
-        last = turn(order[n - 1]) if n < 3 else turn(order[n - 1], ends[order[0]])
-    last = leave(order[-2])
-    last = turn(order[-1])
-    arrays = [stream, parts[0], ends[0]] + [ends[k] for k in range(1, planes)]
+    last = put(3)
+    last = put(2)
+    last = turn(3)
+    last = put(1)
+    last = leave(3)
+    last = turn(2)
+    last = put(0)
+    last = leave(2, ends[3])
+    last = turn(1)
+    last = leave(1)
+    last = turn(0)
+    arrays = [stream, parts[0], ends[0], ends[1], ends[2]]
     return small_call(finish_kernel, "finish", arrays, (), [(stream.shape, F32)])[0]
 
 
@@ -591,6 +605,12 @@
     columns = lax.axis_size("gy")
     slot_count = (MOVED + columns - 2) // (columns - 1)
     pool = cache_pool.reshape(-1, cache_pool.shape[2])
+    planes = lax.axis_size("gx")
+    swapped = columns == 8 and planes == 4 and gate_up.shape[1] == planes
+    if swapped:
+        out_parts = start_out(out_weight)
+        pair, down = pack_experts(gate_up, down_proj)
+        cache_len, anchor = after((cache_len, anchor), pair)
     matches = (anchor[:, None] == jnp.arange(columns, dtype=jnp.int32)[None, :]).astype(jnp.int32)
     earlier = jnp.sum((jnp.cumsum(matches, axis=0) - 1) * matches, axis=1)
     slots = columns * slot_count
@@ -604,11 +624,7 @@
     extra = jnp.stack([cache_len[:LOCAL] // PAGE, cache_len[:LOCAL] % PAGE], axis=1)
     extra = jnp.pad(extra.astype(BF), ((0, 0), (0, LANES - 2)))
     own = jnp.concatenate([queries[:LOCAL], extra], axis=1)
-    planes = lax.axis_size("gx")
-    swapped = columns == 8 and planes & (planes - 1) == 0 and gate_up.shape[1] == planes
     if swapped:
-        out_parts = start_out(out_weight)
-        pair, down = pack_experts(gate_up, down_proj)
         out_parts, pair, down = lax.optimization_barrier((out_parts, pair, down))
         pair = exchange(pair)
         out_parts = swap_out(out_weight, stack_rows(out_parts), asks)

time: 263 us -> 250 us (0.951)
  starting transfers between devices: 71.6 us -> 50.2 us
  waiting for transfers between devices: 76.3 us -> 83.3 us
    ppermute x32, starting transfers between devices: 61.5 us -> 38.1 us  [swap(): lax.ppermute(x, axis, [(i, how(i)) for i in range(lax.axis_size(axis))])]
    ppermute x32, waiting for transfers between devices: 72.2 us -> 80.5 us  [swap(): lax.ppermute(x, axis, [(i, how(i)) for i in range(lax.axis_size(axis))])]
    pallas_call x8 -> x10, Pallas kernels: 36.7 us -> 39.5 us  [the longest x5 24.4 us: make_hidden(): pl.pallas_call(functools.partial(hidden_kernel, len(pieces)), in_specs=[s...]
    unnamed x66 -> x74, local copies, waits for them, and re-layouts: 14.8 us -> 16.6 us
  transfers between devices with their start and end apart: 34 -> 34, of which waited for: 21 -> 18; matrix products, arithmetic and copies ran while one was open for 3% -> 3% of each run, Pallas kernels for 24% -> 26%
where the time goes in v5:
time: 250 us; the launch traced here: 249 us
  waiting for transfers between devices  83.3 us (33%)
  Pallas kernels  68.2 us (27%)
  starting transfers between devices  50.2 us (20%)
  blocking collectives  23.9 us (10%)
  local copies, waits for them, and re-layouts  20.1 us (8%)
    ppermute x32, waiting for transfers between devices, swap(): lax.ppermute(x, axis, [(i, how(i)) for i in range(lax.axis_size(axis))])  80.5 us
    ppermute x32, starting transfers between devices, swap(): lax.ppermute(x, axis, [(i, how(i)) for i in range(lax.axis_size(axis))])  38.1 us
    pallas_call x5, Pallas kernels, make_hidden(): pl.pallas_call(functools.partial(hidden_kernel, len(pieces)), in_specs=[s...  24.4 us
    unnamed x74, local copies, waits for them, and re-layouts  16.6 us
    pallas_call x5, Pallas kernels, make_down(): pl.pallas_call(functools.partial(down_kernel, count), in_specs=[vmem()] *...  15.1 us
    all_gather x1, blocking collectives, body(): back = lax.all_gather(reply, 'gy', axis=0, tiled=True)  12.3 us
    all_to_all x2, starting transfers between devices, exchange(): lax.all_to_all(packed, 'gx', split_axis=0, concat_axis=0, tiled=True)  12.1 us
    all_gather x1, blocking collectives, body(): lax.all_gather(jnp.concatenate([queries[LOCAL:], extra], axis=1), 'gy', a...  11.6 us
  transfers between devices with their start and end apart: 34, of which 18 were waited for; matrix products, arithmetic and copies ran while one was open for 3% of the time, Pallas kernels for 26%

profile of v5, /device:TPU:0, one launch (start us, length us, event | category | flops | bytes accessed | tf_op | source)
XLA Modules:
  0.0 249.1 jit_solution(11748690961610379549)
XLA Ops:
  1.6 5.1 %collective-permute-start.2 = (bf16[48,1536]{1,0:T(8,128)(2,1)S(1)}, bf16[48,1536]{1,0:T(8,128)(2,1)S(1)}, u32[]{:S(2)}, u32[]{:S(2)}) collective-permute-start(bf16[48,1536]{1,0:T(8,128)(2,1)S(1)} %constant_dynamic-slice_fusion), channel_id=1, source_target_pairs={{0,24},{8,16},{16,8},{24,0},{1,25},{9,17},{17,9},{25,1},{2,26},{10... | collective-permute-start | bytes 442376 | tf_op jit(solution)/shard_map/ppermute | solution.py:372
  7.3 8.3 %pack.1 = (bf16[4,384,1024]{2,1,0:T(8,128)(2,1)}, bf16[4,384,512]{2,1,0:T(8,128)(2,1)}) custom-call(bf16[384,4,1024]{2,1,0:T(4,128)(2,1)} %gate_ref.1, bf16[384,4,512]{2,1,0:T(4,128)(2,1)} %down_ref.1), custom_call_target="tpu_custom_call" | custom-call | flops 7000000000 | bytes 100000 | tf_op jit(solution)/shard_map/pack/pallas_call | solution.py:359
  17.0 2.2 collective-permute-done.1.refs_1_
  19.8 3.9 %all-to-all-start = ((bf16[4,384,1024]{2,1,0:T(8,128)(2,1)}), bf16[4,384,1024]{2,1,0:T(8,128)(2,1)S(1)}, u32[]{:S(2)}, u32[]{:S(2)}) async-start(bf16[4,384,1024]{2,1,0:T(8,128)(2,1)} %get-tuple-element.63), calls=%async_computation | async-start | bytes 6291456 | tf_op jit(solution)/shard_map/all_to_all | solution.py:388
  27.1 11.6 %all_gather.6.refs_2_.asks_ref = bf16[64,1664]{1,0:T(8,128)(2,1)S(1)} all-gather(bf16[8,1664]{1,0:T(8,128)(2,1)S(1)} %pad_maximum_fusion), channel_id=1, replica_groups=mesh['gx'=4,'gy'=8] {'gy'}, dimensions={0}, use_global_device_ids=true | all-gather | bytes 239616 | tf_op jit(solution)/shard_map/all_gather | solution.py:621
  39.3 2.1 stack.159
  41.4 1.5 collective-permute-start.4
  43.7 7.0 %attend.1 = (f32[8,1664]{1,0:T(8,128)}, f32[16,1664]{1,0:T(8,128)}) custom-call(s32[1]{0:T(128)} %bitcast.25.me_ref, bf16[8,1664]{1,0:T(8,128)(2,1)} %fusion.1.own_ref, bf16[64,1664]{1,0:T(8,128)(2,1)} %copy-done.17, s32[24,32]{1,0:T(8,128)} %pad_add_fusion.table_ref, bf16[2048,1024]{1,0:T(8,128)(2,1)} %bitcast.49, bf16[2048,1024]{1,0:T(8,128)(2,1)} %bitcast.50), custom_call_target="tpu_custom_call" | custom-call | flops 7000000000 | bytes 100000 | tf_op jit(solution)/shard_map/attend/pallas_call | solution.py:143
  50.7 4.1 %collective-permute-done.4.rest_3_ = bf16[288,1536]{1,0:T(8,128)(2,1)} collective-permute-done((bf16[288,1536]{1,0:T(8,128)(2,1)}, bf16[288,1536]{1,0:T(8,128)(2,1)}, u32[]{:S(2)}, u32[]{:S(2)}) %collective-permute-start.4) | collective-permute-done | bytes 884768 | tf_op jit(solution)/shard_map/ppermute | solution.py:372
  59.2 12.3 %all_gather.7.back_ref = f32[128,1664]{1,0:T(8,128)} all-gather(f32[16,1664]{1,0:T(8,128)} %get-tuple-element.56), channel_id=1, replica_groups=mesh['gx'=4,'gy'=8] {'gy'}, dimensions={0}, use_global_device_ids=true | all-gather | bytes 958464 | tf_op jit(solution)/shard_map/all_gather | solution.py:645
  71.5 6.3 %stream.1 = (bf16[16,1536]{1,0:T(8,128)(2,1)}, f32[128,1536]{1,0:T(8,128)}, bf16[128,1664]{1,0:T(8,128)(2,1)}) custom-call(s32[8]{0:T(128)} %get-tuple-element.101.chosen_ref, s32[25]{0:T(128)} %stack.147.at_ref, bf16[16,1536]{1,0:T(8,128)(2,1)} %query_ref.1, bf16[16,1024]{1,0:T(8,128)(2,1)} %fresh_ref.1, f32[8,1664]{1,0:T(8,128)} %get-tuple-element.55.here_ref, ...), custom_call_target="tpu_custom_call" | custom-call | flops 8000000000 | bytes 100000 | tf_op jit(solution)/shard_map/stream/pallas_call | solution.py:257
  77.8 1.6 collective-permute-start.8
  79.4 3.1 %collective-permute-start.12 = (bf16[128,1664]{1,0:T(8,128)(2,1)}, bf16[128,1664]{1,0:T(8,128)(2,1)S(1)}, u32[]{:S(2)}, u32[]{:S(2)}) collective-permute-start(bf16[128,1664]{1,0:T(8,128)(2,1)} %get-tuple-element.62.refs_0_), channel_id=1, source_target_pairs={{0,16},{8,24},{16,0},{24,8},{1,17},{9,25},{17,1},{25,9},{2,18},{10... | collective-permute-start | bytes 1277960 | tf_op jit(solution)/shard_map/ppermute | solution.py:372
  84.0 2.2 collective-permute-done.8.refs_1_
  87.3 1.6 collective-permute-start.9
  88.9 23.4 %collective-permute-done.12.refs_0_ = bf16[128,1664]{1,0:T(8,128)(2,1)S(1)} collective-permute-done((bf16[128,1664]{1,0:T(8,128)(2,1)}, bf16[128,1664]{1,0:T(8,128)(2,1)S(1)}, u32[]{:S(2)}, u32[]{:S(2)}) %collective-permute-start.12) | collective-permute-done | bytes 426016 | tf_op jit(solution)/shard_map/ppermute | solution.py:372
  112.3 1.5 collective-permute-start.13
  115.6 4.7 %collective-permute-done.13.refs_1_ = bf16[128,1664]{1,0:T(8,128)(2,1)S(1)} collective-permute-done((bf16[128,1664]{1,0:T(8,128)(2,1)S(1)}, bf16[128,1664]{1,0:T(8,128)(2,1)S(1)}, u32[]{:S(2)}, u32[]{:S(2)}) %collective-permute-start.13) | collective-permute-done | bytes 426016 | tf_op jit(solution)/shard_map/ppermute | solution.py:372
  121.4 3.6 %collective-permute-done.11.refs_1_ = bf16[128,1664]{1,0:T(8,128)(2,1)S(1)} collective-permute-done((bf16[128,1664]{1,0:T(8,128)(2,1)S(1)}, bf16[128,1664]{1,0:T(8,128)(2,1)S(1)}, u32[]{:S(2)}, u32[]{:S(2)}) %collective-permute-start.11) | collective-permute-done | bytes 426016 | tf_op jit(solution)/shard_map/ppermute | solution.py:372
  128.0 8.1 %all-to-all-start.1 = ((bf16[4,384,512]{2,1,0:T(8,128)(2,1)}), bf16[4,384,512]{2,1,0:T(8,128)(2,1)}, u32[]{:S(2)}, u32[]{:S(2)}) async-start(bf16[4,384,512]{2,1,0:T(8,128)(2,1)} %get-tuple-element.68), calls=%async_computation.1 | async-start | bytes 3145728 | tf_op jit(solution)/shard_map/all_to_all | solution.py:388
  136.2 1.5 collective-permute-start.18
  137.8 1.5 collective-permute-start.17
  142.1 5.5 %hidden.5 = (bf16[512,1024]{1,0:T(8,128)(2,1)S(1)}, f32[512,128]{1,0:T(8,128)S(1)}) custom-call(s32[2]{0:T(128)S(1)} %pad_add_fusion.1.place_ref, bf16[256,1664]{1,0:T(8,128)(2,1)S(1)} %copy-done.3, bf16[256,1664]{1,0:T(8,128)(2,1)S(1)} %copy-done.19, bf16[1536,1024]{1,0:T(8,128)(2,1)S(1)} %bitcast.44, bf16[1536,1024]{1,0:T(8,128)(2,1)} %collective-permute-done.15.refs_3_.refs_2_), custom_call_target="tpu_custom_call" | custom-call | flops 1000000 | bytes 100000 | tf_op jit(solution)/shard_map/hidden/pallas_call | solution.py:300
  148.7 2.0 stack.163.refs_0_
  150.7 2.0 collective-permute-start.19
  152.6 4.0 %hidden.6 = (bf16[256,1024]{1,0:T(8,128)(2,1)S(1)}, f32[256,128]{1,0:T(8,128)S(1)}) custom-call(s32[2]{0:T(128)S(1)} %pad_add_fusion.1.place_ref, bf16[256,1664]{1,0:T(8,128)(2,1)} %stack.163.refs_0_, bf16[1536,1024]{1,0:T(8,128)(2,1)S(1)} %bitcast.45, bf16[1536,1024]{1,0:T(8,128)(2,1)} %collective-permute-done.15.refs_3_.refs_2_, ...), custom_call_target="tpu_custom_call" | custom-call | flops 1000000 | bytes 100000 | tf_op jit(solution)/shard_map/hidden/pallas_call | solution.py:300
  157.4 5.5 %hidden.7 = (bf16[512,1024]{1,0:T(8,128)(2,1)S(1)}, f32[512,128]{1,0:T(8,128)S(1)}) custom-call(s32[2]{0:T(128)S(1)} %pad_add_fusion.1.place_ref, bf16[256,1664]{1,0:T(8,128)(2,1)S(1)} %copy-done.5, bf16[256,1664]{1,0:T(8,128)(2,1)S(1)} %collective-permute-done.17.refs_1_, bf16[1536,1024]{1,0:T(8,128)(2,1)S(1)} %bitcast.46, ...), custom_call_target="tpu_custom_call" | custom-call | flops 1000000 | bytes 100000 | tf_op jit(solution)/shard_map/hidden/pallas_call | solution.py:300
  164.0 5.4 %hidden.8 = (bf16[512,1024]{1,0:T(8,128)(2,1)S(1)}, f32[512,128]{1,0:T(8,128)S(1)}) custom-call(s32[2]{0:T(128)S(1)} %pad_add_fusion.1.place_ref, bf16[256,1664]{1,0:T(8,128)(2,1)S(1)} %copy-done.1, bf16[256,1664]{1,0:T(8,128)(2,1)S(1)} %collective-permute-done.16.refs_1_, bf16[1536,1024]{1,0:T(8,128)(2,1)S(1)} %bitcast.47, ...), custom_call_target="tpu_custom_call" | custom-call | flops 1000000 | bytes 100000 | tf_op jit(solution)/shard_map/hidden/pallas_call | solution.py:300
  171.9 2.7 %all-to-all-done.1 = bf16[4,384,512]{2,1,0:T(8,128)(2,1)} async-done(((bf16[4,384,512]{2,1,0:T(8,128)(2,1)}), bf16[4,384,512]{2,1,0:T(8,128)(2,1)}, u32[]{:S(2)}, u32[]{:S(2)}) %all-to-all-start.1) | async-done | bytes 1572896 | tf_op jit(solution)/shard_map/all_to_all | solution.py:388
  175.6 4.0 %hidden.9 = (bf16[256,1024]{1,0:T(8,128)(2,1)S(1)}, f32[256,128]{1,0:T(8,128)S(1)}) custom-call(s32[2]{0:T(128)S(1)} %pad_add_fusion.1.place_ref, bf16[256,1664]{1,0:T(8,128)(2,1)} %collective-permute-done.19.refs_0_, bf16[1536,1024]{1,0:T(8,128)(2,1)S(1)} %bitcast.48, bf16[1536,1024]{1,0:T(8,128)(2,1)} %collective-permute-done.15.refs_3_.refs_2_, ...), custom_call_target="tpu_custom_call" | custom-call | flops 1000000 | bytes 100000 | tf_op jit(solution)/shard_map/hidden/pallas_call | solution.py:300
  179.6 2.7 %down.5.rest_0_ = bf16[256,1536]{1,0:T(8,128)(2,1)S(1)} custom-call(bf16[256,1024]{1,0:T(8,128)(2,1)S(1)} %get-tuple-element.75.hidden_ref, f32[256,128]{1,0:T(8,128)S(1)} %get-tuple-element.76.share_ref, bf16[1536,512]{1,0:T(8,128)(2,1)} %bitcast.36.mine_ref, bf16[1536,512]{1,0:T(8,128)(2,1)S(1)} %collective-permute-done.20.other_ref), custom_call_target="tpu_custom_call" | custom-call | flops 1000000 | bytes 100000 | tf_op jit(solution)/shard_map/down/pallas_call | solution.py:333
  182.3 1.6 collective-permute-start.22
  183.9 2.5 %down.6.rest_0_.keep_ref = bf16[256,1536]{1,0:T(8,128)(2,1)S(1)} custom-call(bf16[256,1024]{1,0:T(8,128)(2,1)S(1)} %copy-done.22, f32[256,128]{1,0:T(8,128)S(1)} %get-tuple-element.69.refs_4_.share_ref, bf16[1536,512]{1,0:T(8,128)(2,1)} %bitcast.36.mine_ref, bf16[1536,512]{1,0:T(8,128)(2,1)S(1)} %collective-permute-done.20.other_ref, ...), custom_call_target="tpu_custom_call" | custom-call | flops 1000000 | bytes 100000 | tf_op jit(solution)/shard_map/down/pallas_call | solution.py:333
  186.5 3.3 %down.7 = (bf16[256,1536]{1,0:T(8,128)(2,1)S(1)}, bf16[256,1536]{1,0:T(8,128)(2,1)S(1)}) custom-call(bf16[512,1024]{1,0:T(8,128)(2,1)S(1)} %copy-done.11, f32[512,128]{1,0:T(8,128)S(1)} %copy-done.16, bf16[1536,512]{1,0:T(8,128)(2,1)} %bitcast.36.mine_ref, bf16[1536,512]{1,0:T(8,128)(2,1)S(1)} %collective-permute-done.20.other_ref, ...), custom_call_target="tpu_custom_call" | custom-call | flops 1000000 | bytes 100000 | tf_op jit(solution)/shard_map/down/pallas_call | solution.py:333
  190.4 4.0 %collective-permute-done.22.came_ref = bf16[256,1536]{1,0:T(8,128)(2,1)S(1)} collective-permute-done((bf16[256,1536]{1,0:T(8,128)(2,1)S(1)}, bf16[256,1536]{1,0:T(8,128)(2,1)S(1)}, u32[]{:S(2)}, u32[]{:S(2)}) %collective-permute-start.22) | collective-permute-done | bytes 786464 | tf_op jit(solution)/shard_map/ppermute | solution.py:372
  194.6 1.6 collective-permute-start.23
  196.1 3.3 %down.8 = (bf16[256,1536]{1,0:T(8,128)(2,1)S(1)}, bf16[256,1536]{1,0:T(8,128)(2,1)S(1)}) custom-call(bf16[512,1024]{1,0:T(8,128)(2,1)S(1)} %copy-done.9, f32[512,128]{1,0:T(8,128)S(1)} %copy-done.13, bf16[1536,512]{1,0:T(8,128)(2,1)} %bitcast.36.mine_ref, bf16[1536,512]{1,0:T(8,128)(2,1)S(1)} %collective-permute-done.20.other_ref, ...), custom_call_target="tpu_custom_call" | custom-call | flops 1000000 | bytes 100000 | tf_op jit(solution)/shard_map/down/pallas_call | solution.py:333
  199.4 1.6 collective-permute-start.25
  201.0 5.7 %collective-permute-done.23.rest_0_ = bf16[128,1536]{1,0:T(8,128)(2,1)S(1)} collective-permute-done((bf16[128,1536]{1,0:T(8,128)(2,1)S(1)}, bf16[128,1536]{1,0:T(8,128)(2,1)S(1)}, u32[]{:S(2)}, u32[]{:S(2)}) %collective-permute-start.23) | collective-permute-done | bytes 393248 | tf_op jit(solution)/shard_map/ppermute | solution.py:372
  207.2 1.6 collective-permute-start.26
  208.8 3.3 %down.9 = (bf16[256,1536]{1,0:T(8,128)(2,1)S(1)}, bf16[256,1536]{1,0:T(8,128)(2,1)S(1)}) custom-call(bf16[512,1024]{1,0:T(8,128)(2,1)S(1)} %copy-done.7, f32[512,128]{1,0:T(8,128)S(1)} %get-tuple-element.66.refs_2_.refs_3_.share_ref, bf16[1536,512]{1,0:T(8,128)(2,1)} %bitcast.36.mine_ref, bf16[1536,512]{1,0:T(8,128)(2,1)S(1)} %collective-permute-done.20.other_ref, ...), custom_call_target="tpu_custom_call" | custom-call | flops 1000000 | bytes 100000 | tf_op jit(solution)/shard_map/down/pallas_call | solution.py:333
  212.1 1.6 collective-permute-start.24
  213.7 5.7 %collective-permute-done.26.rest_0_ = bf16[128,1536]{1,0:T(8,128)(2,1)S(1)} collective-permute-done((bf16[128,1536]{1,0:T(8,128)(2,1)S(1)}, bf16[128,1536]{1,0:T(8,128)(2,1)S(1)}, u32[]{:S(2)}, u32[]{:S(2)}) %collective-permute-start.26) | collective-permute-done | bytes 393248 | tf_op jit(solution)/shard_map/ppermute | solution.py:372
  219.8 1.6 collective-permute-start.28
  222.1 9.8 %collective-permute-done.28.rest_0_ = bf16[128,1536]{1,0:T(8,128)(2,1)S(1)} collective-permute-done((bf16[128,1536]{1,0:T(8,128)(2,1)S(1)}, bf16[128,1536]{1,0:T(8,128)(2,1)S(1)}, u32[]{:S(2)}, u32[]{:S(2)}) %collective-permute-start.28) | collective-permute-done | bytes 393248 | tf_op jit(solution)/shard_map/ppermute | solution.py:372
  232.5 1.6 collective-permute-start.29
  234.1 5.6 %collective-permute-done.31.rest_2_ = bf16[128,1536]{1,0:T(8,128)(2,1)S(1)} collective-permute-done((bf16[128,1536]{1,0:T(8,128)(2,1)S(1)}, bf16[128,1536]{1,0:T(8,128)(2,1)S(1)}, u32[]{:S(2)}, u32[]{:S(2)}) %collective-permute-start.31) | collective-permute-done | bytes 393248 | tf_op jit(solution)/shard_map/ppermute | solution.py:372
  240.3 7.7 %collective-permute-done.30.rest_1_ = bf16[128,1536]{1,0:T(8,128)(2,1)S(1)} collective-permute-done((bf16[128,1536]{1,0:T(8,128)(2,1)S(1)}, bf16[128,1536]{1,0:T(8,128)(2,1)S(1)}, u32[]{:S(2)}, u32[]{:S(2)}) %collective-permute-start.30) | collective-permute-done | bytes 393248 | tf_op jit(solution)/shard_map/ppermute | solution.py:372
  (145 shorter events, 35.2 us)
Async XLA Ops:
  1.6 15.4 %collective-permute-start.2 = (bf16[48,1536]{1,0:T(8,128)(2,1)S(1)}, bf16[48,1536]{1,0:T(8,128)(2,1)S(1)}, u32[]{:S(2)}, u32[]{:S(2)}) collective-permute-start(bf16[48,1536]{1,0:T(8,128)(2,1)S(1)} %constant_dynamic-slice_fusion), channel_id=1, source_target_pairs={{0,24},{8,16},{16,8},{24,0},{1,25},{9,17},{17,9},{25,1},{2,26},{10... | collective-permute-start | bytes 442376 | tf_op jit(solution)/shard_map/ppermute | solution.py:372
  6.7 12.5 %collective-permute-start.1 = (bf16[48,1536]{1,0:T(8,128)(2,1)S(1)}, bf16[48,1536]{1,0:T(8,128)(2,1)S(1)}, u32[]{:S(2)}, u32[]{:S(2)}) collective-permute-start(bf16[48,1536]{1,0:T(8,128)(2,1)S(1)} %constant_dynamic-slice_fusion), channel_id=1, source_target_pairs={{0,16},{8,24},{16,0},{24,8},{1,17},{9,25},{17,1},{25,9},{2,18},{10... | collective-permute-start | bytes 442376 | tf_op jit(solution)/shard_map/ppermute | solution.py:372
  6.7 12.5 %collective-permute-start = (bf16[48,1536]{1,0:T(8,128)(2,1)S(1)}, bf16[48,1536]{1,0:T(8,128)(2,1)S(1)}, u32[]{:S(2)}, u32[]{:S(2)}) collective-permute-start(bf16[48,1536]{1,0:T(8,128)(2,1)S(1)} %constant_dynamic-slice_fusion), channel_id=1, source_target_pairs={{0,8},{8,0},{16,24},{24,16},{1,9},{9,1},{17,25},{25,17},{2,10},{10... | collective-permute-start | bytes 442376 | tf_op jit(solution)/shard_map/ppermute | solution.py:372
  7.3 8.3 %copy-start.35 = (s32[16]{0:T(128)S(1)}, s32[16]{0:T(128)}, u32[]{:S(2)}) copy-start(s32[16]{0:T(128)} %param.18) | copy-start | bytes 196
  7.3 8.6 %copy-start.31 = (s32[8]{0:T(128)S(1)}, s32[8]{0:T(128)}, u32[]{:S(2)}) copy-start(s32[8]{0:T(128)} %param.20) | copy-start | bytes 100
  19.8 18.8 %copy-start.30 = (s32[16,32]{1,0:T(8,128)S(1)}, s32[16,32]{1,0:T(8,128)}, u32[]{:S(2)}) copy-start(s32[16,32]{1,0:T(8,128)} %param.21) | copy-start | bytes 6148
  19.8 18.8 %copy-start.34 = (s32[8,32]{1,0:T(8,128)S(1)}, s32[8,32]{1,0:T(8,128)}, u32[]{:S(2)}) copy-start(s32[8,32]{1,0:T(8,128)} %param.19) | copy-start | bytes 3076
  19.8 108.2 %all-to-all-start = ((bf16[4,384,1024]{2,1,0:T(8,128)(2,1)}), bf16[4,384,1024]{2,1,0:T(8,128)(2,1)S(1)}, u32[]{:S(2)}, u32[]{:S(2)}) async-start(bf16[4,384,1024]{2,1,0:T(8,128)(2,1)} %get-tuple-element.63), calls=%async_computation | async-start | bytes 6291456 | tf_op jit(solution)/shard_map/all_to_all | solution.py:388
  25.5 13.8 %collective-permute-start.3 = (bf16[144,1536]{1,0:T(8,128)(2,1)}, bf16[144,1536]{1,0:T(8,128)(2,1)}, u32[]{:S(2)}, u32[]{:S(2)}) collective-permute-start(bf16[144,1536]{1,0:T(8,128)(2,1)} %stack.158.refs_0_.rest_1_), channel_id=1, source_target_pairs={{0,2},{1,5},{2,0},{3,7},{4,6},{5,1},{6,4},{7,3},{8,10},{9,13},{10,... | collective-permute-start | bytes 1327112 | tf_op jit(solution)/shard_map/ppermute | solution.py:372
  41.4 13.4 %collective-permute-start.4 = (bf16[288,1536]{1,0:T(8,128)(2,1)}, bf16[288,1536]{1,0:T(8,128)(2,1)}, u32[]{:S(2)}, u32[]{:S(2)}) collective-permute-start(bf16[288,1536]{1,0:T(8,128)(2,1)} %stack.159), channel_id=1, source_target_pairs={{0,4},{1,3},{2,6},{3,1},{4,0},{5,7},{6,2},{7,5},{8,12},{9,11},{10,... | collective-permute-start | bytes 2654216 | tf_op jit(solution)/shard_map/ppermute | solution.py:372
  43.7 11.6 %copy-start.33 = (bf16[1536]{0:T(1024)(128)(2,1)S(1)}, bf16[1536]{0:T(1024)(128)(2,1)}, u32[]{:S(2)}) copy-start(bf16[1536]{0:T(1024)(128)(2,1)} %param.25) | copy-start | bytes 9220
  43.7 12.2 %copy-start.32 = (s32[128,8]{0,1:T(8,128)S(1)}, s32[128,8]{0,1:T(8,128)}, u32[]{:S(2)}) copy-start(s32[128,8]{0,1:T(8,128)} %param.27) | copy-start | bytes 12292
  54.8 16.7 %collective-permute-start.7 = (bf16[288,1536]{1,0:T(8,128)(2,1)}, bf16[288,1536]{1,0:T(8,128)(2,1)}, u32[]{:S(2)}, u32[]{:S(2)}) collective-permute-start(bf16[288,1536]{1,0:T(8,128)(2,1)} %collective-permute-done.4.rest_3_), channel_id=1, source_target_pairs={{0,1},{1,0},{2,3},{3,2},{4,5},{5,4},{6,7},{7,6},{8,9},{9,8},{10,11... | collective-permute-start | bytes 2654216 | tf_op jit(solution)/shard_map/ppermute | solution.py:372
  54.8 16.7 %collective-permute-start.5 = (bf16[144,1536]{1,0:T(8,128)(2,1)}, bf16[144,1536]{1,0:T(8,128)(2,1)}, u32[]{:S(2)}, u32[]{:S(2)}) collective-permute-start(bf16[144,1536]{1,0:T(8,128)(2,1)} %stack.158.refs_0_.rest_1_), channel_id=1, source_target_pairs={{0,1},{1,0},{2,3},{3,2},{4,5},{5,4},{6,7},{7,6},{8,9},{9,8},{10,11... | collective-permute-start | bytes 1327112 | tf_op jit(solution)/shard_map/ppermute | solution.py:372
  55.3 16.2 %collective-permute-start.6 = (bf16[144,1536]{1,0:T(8,128)(2,1)}, bf16[144,1536]{1,0:T(8,128)(2,1)}, u32[]{:S(2)}, u32[]{:S(2)}) collective-permute-start(bf16[144,1536]{1,0:T(8,128)(2,1)} %collective-permute-done.3.refs_1_.rest_2_), channel_id=1, source_target_pairs={{0,1},{1,0},{2,3},{3,2},{4,5},{5,4},{6,7},{7,6},{8,9},{9,8},{10,11... | collective-permute-start | bytes 1327112 | tf_op jit(solution)/shard_map/ppermute | solution.py:372
  77.8 8.4 %collective-permute-start.8 = (bf16[128,1664]{1,0:T(8,128)(2,1)}, bf16[128,1664]{1,0:T(8,128)(2,1)S(1)}, u32[]{:S(2)}, u32[]{:S(2)}) collective-permute-start(bf16[128,1664]{1,0:T(8,128)(2,1)} %get-tuple-element.62.refs_0_), channel_id=1, source_target_pairs={{0,2},{1,5},{2,0},{3,7},{4,6},{5,1},{6,4},{7,3},{8,10},{9,13},{10,... | collective-permute-start | bytes 1277960 | tf_op jit(solution)/shard_map/ppermute | solution.py:372
  79.4 32.9 %collective-permute-start.12 = (bf16[128,1664]{1,0:T(8,128)(2,1)}, bf16[128,1664]{1,0:T(8,128)(2,1)S(1)}, u32[]{:S(2)}, u32[]{:S(2)}) collective-permute-start(bf16[128,1664]{1,0:T(8,128)(2,1)} %get-tuple-element.62.refs_0_), channel_id=1, source_target_pairs={{0,16},{8,24},{16,0},{24,8},{1,17},{9,25},{17,1},{25,9},{2,18},{10... | collective-permute-start | bytes 1277960 | tf_op jit(solution)/shard_map/ppermute | solution.py:372
  82.5 31.2 %collective-permute-start.10 = (bf16[128,1664]{1,0:T(8,128)(2,1)}, bf16[128,1664]{1,0:T(8,128)(2,1)S(1)}, u32[]{:S(2)}, u32[]{:S(2)}) collective-permute-start(bf16[128,1664]{1,0:T(8,128)(2,1)} %get-tuple-element.62.refs_0_), channel_id=1, source_target_pairs={{0,8},{8,0},{16,24},{24,16},{1,9},{9,1},{17,25},{25,17},{2,10},{10... | collective-permute-start | bytes 1277960 | tf_op jit(solution)/shard_map/ppermute | solution.py:372
  87.2 27.1 %copy-start.26 = (bf16[128,1664]{1,0:T(8,128)(2,1)S(1)}, bf16[128,1664]{1,0:T(8,128)(2,1)}, u32[]{:S(2)}) copy-start(bf16[128,1664]{1,0:T(8,128)(2,1)} %get-tuple-element.62.refs_0_) | copy-start | bytes 1277956
  87.3 37.7 %copy-start.2 = (bf16[256,1664]{1,0:T(8,128)(2,1)}, bf16[256,1664]{1,0:T(8,128)(2,1)S(1)}, u32[]{:S(2)}) copy-start(bf16[256,1664]{1,0:T(8,128)(2,1)S(1)} %stack.160.refs_0_) | copy-start | bytes 2555908
  87.3 39.8 %collective-permute-start.9 = (bf16[256,1664]{1,0:T(8,128)(2,1)S(1)}, bf16[256,1664]{1,0:T(8,128)(2,1)S(1)}, u32[]{:S(2)}, u32[]{:S(2)}) collective-permute-start(bf16[256,1664]{1,0:T(8,128)(2,1)S(1)} %stack.160.refs_0_), channel_id=1, source_target_pairs={{0,4},{1,3},{2,6},{3,1},{4,0},{5,7},{6,2},{7,5},{8,12},{9,11},{10,... | collective-permute-start | bytes 2555912 | tf_op jit(solution)/shard_map/ppermute | solution.py:372
  112.3 8.1 %collective-permute-start.13 = (bf16[128,1664]{1,0:T(8,128)(2,1)S(1)}, bf16[128,1664]{1,0:T(8,128)(2,1)S(1)}, u32[]{:S(2)}, u32[]{:S(2)}) collective-permute-start(bf16[128,1664]{1,0:T(8,128)(2,1)S(1)} %collective-permute-done.12.refs_0_), channel_id=1, source_target_pairs={{0,2},{1,5},{2,0},{3,7},{4,6},{5,1},{6,4},{7,3},{8,10},{9,13},{10,... | collective-permute-start | bytes 1277960 | tf_op jit(solution)/shard_map/ppermute | solution.py:372
  113.8 11.2 %collective-permute-start.11 = (bf16[128,1664]{1,0:T(8,128)(2,1)S(1)}, bf16[128,1664]{1,0:T(8,128)(2,1)S(1)}, u32[]{:S(2)}, u32[]{:S(2)}) collective-permute-start(bf16[128,1664]{1,0:T(8,128)(2,1)S(1)} %collective-permute-done.10.refs_0_), channel_id=1, source_target_pairs={{0,2},{1,5},{2,0},{3,7},{4,6},{5,1},{6,4},{7,3},{8,10},{9,13},{10,... | collective-permute-start | bytes 1277960 | tf_op jit(solution)/shard_map/ppermute | solution.py:372
  114.3 12.0 %collective-permute-start.14 = (bf16[128,1664]{1,0:T(8,128)(2,1)S(1)}, bf16[128,1664]{1,0:T(8,128)(2,1)S(1)}, u32[]{:S(2)}, u32[]{:S(2)}) collective-permute-start(bf16[128,1664]{1,0:T(8,128)(2,1)S(1)} %copy-done.26), channel_id=1, source_target_pairs={{0,24},{8,16},{16,8},{24,0},{1,25},{9,17},{17,9},{25,1},{2,26},{10... | collective-permute-start | bytes 1277960 | tf_op jit(solution)/shard_map/ppermute | solution.py:372
  128.0 11.8 %collective-permute-start.15 = (bf16[1536,1024]{1,0:T(8,128)(2,1)S(1)}, bf16[1536,1024]{1,0:T(8,128)(2,1)}, u32[]{:S(2)}, u32[]{:S(2)}) collective-permute-start(bf16[1536,1024]{1,0:T(8,128)(2,1)S(1)} %bitcast.43), channel_id=1, source_target_pairs={{0,1},{1,0},{2,3},{3,2},{4,5},{5,4},{6,7},{7,6},{8,9},{9,8},{10,11... | collective-permute-start | bytes 9437192 | tf_op jit(solution)/shard_map/ppermute | solution.py:372
  128.0 46.6 %all-to-all-start.1 = ((bf16[4,384,512]{2,1,0:T(8,128)(2,1)}), bf16[4,384,512]{2,1,0:T(8,128)(2,1)}, u32[]{:S(2)}, u32[]{:S(2)}) async-start(bf16[4,384,512]{2,1,0:T(8,128)(2,1)} %get-tuple-element.68), calls=%async_computation.1 | async-start | bytes 3145728 | tf_op jit(solution)/shard_map/all_to_all | solution.py:388
  136.2 12.5 %collective-permute-start.18 = (bf16[128,1664]{1,0:T(8,128)(2,1)}, bf16[128,1664]{1,0:T(8,128)(2,1)}, u32[]{:S(2)}, u32[]{:S(2)}) collective-permute-start(bf16[128,1664]{1,0:T(8,128)(2,1)} %copy-done.23), channel_id=1, source_target_pairs={{0,2},{1,5},{2,0},{3,7},{4,6},{5,1},{6,4},{7,3},{8,10},{9,13},{10,... | collective-permute-start | bytes 1277960 | tf_op jit(solution)/shard_map/ppermute | solution.py:372
  137.8 19.7 %collective-permute-start.17 = (bf16[256,1664]{1,0:T(8,128)(2,1)}, bf16[256,1664]{1,0:T(8,128)(2,1)S(1)}, u32[]{:S(2)}, u32[]{:S(2)}) collective-permute-start(bf16[256,1664]{1,0:T(8,128)(2,1)} %copy-done.4), channel_id=1, source_target_pairs={{0,4},{1,3},{2,6},{3,1},{4,0},{5,7},{6,2},{7,5},{8,12},{9,11},{10,... | collective-permute-start | bytes 2555912 | tf_op jit(solution)/shard_map/ppermute | solution.py:372
  139.3 24.8 %collective-permute-start.16 = (bf16[256,1664]{1,0:T(8,128)(2,1)}, bf16[256,1664]{1,0:T(8,128)(2,1)S(1)}, u32[]{:S(2)}, u32[]{:S(2)}) collective-permute-start(bf16[256,1664]{1,0:T(8,128)(2,1)} %copy-done), channel_id=1, source_target_pairs={{0,4},{1,3},{2,6},{3,1},{4,0},{5,7},{6,2},{7,5},{8,12},{9,11},{10,... | collective-permute-start | bytes 2555912 | tf_op jit(solution)/shard_map/ppermute | solution.py:372
  142.1 6.6 %copy-start.24 = (bf16[128,1664]{1,0:T(8,128)(2,1)S(1)}, bf16[128,1664]{1,0:T(8,128)(2,1)}, u32[]{:S(2)}) copy-start(bf16[128,1664]{1,0:T(8,128)(2,1)} %copy-done.23) | copy-start | bytes 1277956
  150.7 6.8 %copy-start.5 = (bf16[256,1664]{1,0:T(8,128)(2,1)S(1)}, bf16[256,1664]{1,0:T(8,128)(2,1)}, u32[]{:S(2)}) copy-start(bf16[256,1664]{1,0:T(8,128)(2,1)} %copy-done.4) | copy-start | bytes 2555908
  150.7 24.0 %collective-permute-start.19 = (bf16[256,1664]{1,0:T(8,128)(2,1)}, bf16[256,1664]{1,0:T(8,128)(2,1)}, u32[]{:S(2)}, u32[]{:S(2)}) collective-permute-start(bf16[256,1664]{1,0:T(8,128)(2,1)} %stack.163.refs_0_), channel_id=1, source_target_pairs={{0,4},{1,3},{2,6},{3,1},{4,0},{5,7},{6,2},{7,5},{8,12},{9,11},{10,... | collective-permute-start | bytes 2555912 | tf_op jit(solution)/shard_map/ppermute | solution.py:372
  157.4 6.6 %copy-start.1 = (bf16[256,1664]{1,0:T(8,128)(2,1)S(1)}, bf16[256,1664]{1,0:T(8,128)(2,1)}, u32[]{:S(2)}) copy-start(bf16[256,1664]{1,0:T(8,128)(2,1)} %copy-done) | copy-start | bytes 2555908
  174.6 5.0 %collective-permute-start.20 = (bf16[1536,512]{1,0:T(8,128)(2,1)}, bf16[1536,512]{1,0:T(8,128)(2,1)S(1)}, u32[]{:S(2)}, u32[]{:S(2)}) collective-permute-start(bf16[1536,512]{1,0:T(8,128)(2,1)} %bitcast.36.mine_ref), channel_id=1, source_target_pairs={{0,1},{1,0},{2,3},{3,2},{4,5},{5,4},{6,7},{7,6},{8,9},{9,8},{10,11... | collective-permute-start | bytes 4718600 | tf_op jit(solution)/shard_map/ppermute | solution.py:372
  182.3 12.1 %collective-permute-start.22 = (bf16[256,1536]{1,0:T(8,128)(2,1)S(1)}, bf16[256,1536]{1,0:T(8,128)(2,1)S(1)}, u32[]{:S(2)}, u32[]{:S(2)}) collective-permute-start(bf16[256,1536]{1,0:T(8,128)(2,1)S(1)} %down.5.rest_0_), channel_id=1, source_target_pairs={{0,4},{1,3},{2,6},{3,1},{4,0},{5,7},{6,2},{7,5},{8,12},{9,11},{10,... | collective-permute-start | bytes 2359304 | tf_op jit(solution)/shard_map/ppermute | solution.py:372
  189.8 6.3 %copy-start.9 = (bf16[512,1024]{1,0:T(8,128)(2,1)S(1)}, bf16[512,1024]{1,0:T(8,128)(2,1)}, u32[]{:S(2)}) copy-start(bf16[512,1024]{1,0:T(8,128)(2,1)} %copy-done.8) | copy-start | bytes 3145732
  189.8 6.3 %copy-start.13 = (f32[512,128]{1,0:T(8,128)S(1)}, f32[512,128]{1,0:T(8,128)}, u32[]{:S(2)}) copy-start(f32[512,128]{1,0:T(8,128)} %copy-done.12) | copy-start | bytes 786436
  189.8 17.2 %collective-permute-start.21 = (bf16[256,1536]{1,0:T(8,128)(2,1)S(1)}, bf16[256,1536]{1,0:T(8,128)(2,1)S(1)}, u32[]{:S(2)}, u32[]{:S(2)}) collective-permute-start(bf16[256,1536]{1,0:T(8,128)(2,1)S(1)} %get-tuple-element.78), channel_id=1, source_target_pairs={{0,4},{1,3},{2,6},{3,1},{4,0},{5,7},{6,2},{7,5},{8,12},{9,11},{10,... | collective-permute-start | bytes 2359304 | tf_op jit(solution)/shard_map/ppermute | solution.py:372
  194.6 12.1 %collective-permute-start.23 = (bf16[128,1536]{1,0:T(8,128)(2,1)S(1)}, bf16[128,1536]{1,0:T(8,128)(2,1)S(1)}, u32[]{:S(2)}, u32[]{:S(2)}) collective-permute-start(bf16[128,1536]{1,0:T(8,128)(2,1)S(1)} %get-tuple-element.80.rest_0_), channel_id=1, source_target_pairs={{0,2},{1,5},{2,0},{3,7},{4,6},{5,1},{6,4},{7,3},{8,10},{9,13},{10,... | collective-permute-start | bytes 1179656 | tf_op jit(solution)/shard_map/ppermute | solution.py:372
  199.4 20.2 %collective-permute-start.25 = (bf16[256,1536]{1,0:T(8,128)(2,1)S(1)}, bf16[256,1536]{1,0:T(8,128)(2,1)S(1)}, u32[]{:S(2)}, u32[]{:S(2)}) collective-permute-start(bf16[256,1536]{1,0:T(8,128)(2,1)S(1)} %get-tuple-element.86), channel_id=1, source_target_pairs={{0,4},{1,3},{2,6},{3,1},{4,0},{5,7},{6,2},{7,5},{8,12},{9,11},{10,... | collective-permute-start | bytes 2359304 | tf_op jit(solution)/shard_map/ppermute | solution.py:372
  207.2 12.1 %collective-permute-start.26 = (bf16[128,1536]{1,0:T(8,128)(2,1)S(1)}, bf16[128,1536]{1,0:T(8,128)(2,1)S(1)}, u32[]{:S(2)}, u32[]{:S(2)}) collective-permute-start(bf16[128,1536]{1,0:T(8,128)(2,1)S(1)} %get-tuple-element.83.rest_0_), channel_id=1, source_target_pairs={{0,2},{1,5},{2,0},{3,7},{4,6},{5,1},{6,4},{7,3},{8,10},{9,13},{10,... | collective-permute-start | bytes 1179656 | tf_op jit(solution)/shard_map/ppermute | solution.py:372
  208.8 10.6 %collective-permute-start.27 = (bf16[128,1536]{1,0:T(8,128)(2,1)S(1)}, bf16[128,1536]{1,0:T(8,128)(2,1)S(1)}, u32[]{:S(2)}, u32[]{:S(2)}) collective-permute-start(bf16[128,1536]{1,0:T(8,128)(2,1)S(1)} %close.3.rest_0_), channel_id=1, source_target_pairs={{0,8},{8,0},{16,24},{24,16},{1,9},{9,1},{17,25},{25,17},{2,10},{10... | collective-permute-start | bytes 1179656 | tf_op jit(solution)/shard_map/ppermute | solution.py:372
  212.1 20.2 %collective-permute-start.24 = (bf16[256,1536]{1,0:T(8,128)(2,1)S(1)}, bf16[256,1536]{1,0:T(8,128)(2,1)S(1)}, u32[]{:S(2)}, u32[]{:S(2)}) collective-permute-start(bf16[256,1536]{1,0:T(8,128)(2,1)S(1)} %get-tuple-element.85), channel_id=1, source_target_pairs={{0,4},{1,3},{2,6},{3,1},{4,0},{5,7},{6,2},{7,5},{8,12},{9,11},{10,... | collective-permute-start | bytes 2359304 | tf_op jit(solution)/shard_map/ppermute | solution.py:372
  219.8 12.0 %collective-permute-start.28 = (bf16[128,1536]{1,0:T(8,128)(2,1)S(1)}, bf16[128,1536]{1,0:T(8,128)(2,1)S(1)}, u32[]{:S(2)}, u32[]{:S(2)}) collective-permute-start(bf16[128,1536]{1,0:T(8,128)(2,1)S(1)} %get-tuple-element.89.rest_1_), channel_id=1, source_target_pairs={{0,2},{1,5},{2,0},{3,7},{4,6},{5,1},{6,4},{7,3},{8,10},{9,13},{10,... | collective-permute-start | bytes 1179656 | tf_op jit(solution)/shard_map/ppermute | solution.py:372
  221.4 18.3 %collective-permute-start.31 = (bf16[128,1536]{1,0:T(8,128)(2,1)S(1)}, bf16[128,1536]{1,0:T(8,128)(2,1)S(1)}, u32[]{:S(2)}, u32[]{:S(2)}) collective-permute-start(bf16[128,1536]{1,0:T(8,128)(2,1)S(1)} %close.4.rest_0_), channel_id=1, source_target_pairs={{0,16},{8,24},{16,0},{24,8},{1,17},{9,25},{17,1},{25,9},{2,18},{10... | collective-permute-start | bytes 1179656 | tf_op jit(solution)/shard_map/ppermute | solution.py:372
  231.9 16.1 %copy-start.20 = (f32[128,1536]{1,0:T(8,128)S(1)}, f32[128,1536]{1,0:T(8,128)}, u32[]{:S(2)}) copy-start(f32[128,1536]{1,0:T(8,128)} %get-tuple-element.61.stream_ref) | copy-start | bytes 2359300
  232.5 7.8 %collective-permute-start.29 = (bf16[128,1536]{1,0:T(8,128)(2,1)S(1)}, bf16[128,1536]{1,0:T(8,128)(2,1)S(1)}, u32[]{:S(2)}, u32[]{:S(2)}) collective-permute-start(bf16[128,1536]{1,0:T(8,128)(2,1)S(1)} %get-tuple-element.91), channel_id=1, source_target_pairs={{0,2},{1,5},{2,0},{3,7},{4,6},{5,1},{6,4},{7,3},{8,10},{9,13},{10,... | collective-permute-start | bytes 1179656 | tf_op jit(solution)/shard_map/ppermute | solution.py:372
  234.0 13.9 %collective-permute-start.30 = (bf16[128,1536]{1,0:T(8,128)(2,1)S(1)}, bf16[128,1536]{1,0:T(8,128)(2,1)S(1)}, u32[]{:S(2)}, u32[]{:S(2)}) collective-permute-start(bf16[128,1536]{1,0:T(8,128)(2,1)S(1)} %close.5.rest_0_), channel_id=1, source_target_pairs={{0,8},{8,0},{16,24},{24,16},{1,9},{9,1},{17,25},{25,17},{2,10},{10... | collective-permute-start | bytes 1179656 | tf_op jit(solution)/shard_map/ppermute | solution.py:372
  (22 other events, 35.2 us)

commit v6 on v5

--- a/solution.py
+++ b/solution.py
@@ -341,31 +341,28 @@
     )(hidden, share, mine, other, *earlier)
 
 
-def pack_kernel(gate_ref, down_ref, pair_out, down_out):
-    for n in range(gate_ref.shape[0] // 16):
+def pack_kernel(block_ref, out_ref):
+    for n in range(block_ref.shape[0] // 16):
         at = slice(n * 16, (n + 1) * 16)
-        gate = gate_ref[at]
-        down = down_ref[at]
-        for e in range(gate_ref.shape[1]):
-            pair_out[e, at, :] = gate[:, e, :]
-            down_out[e, at, :] = down[:, e, :]
-
-
-def pack_experts(gate_up, down_proj):
-    depth, experts = gate_up.shape[:2]
-    step = depth // 4
-    block = lambda n: pl.BlockSpec((step, experts, n * FF), lambda s: (s, 0, 0))
-    packed = lambda n: pl.BlockSpec((experts, step, n * FF), lambda s: (0, s, 0))
+        block = block_ref[at]
+        for e in range(block_ref.shape[1]):
+            out_ref[e, at, :] = block[:, e, :]
+
+
+def pack_experts(weight, steps, *earlier):
+    depth, experts, width = weight.shape
+    step = depth // steps
     return pl.pallas_call(
-        pack_kernel,
-        grid=(depth // step,),
-        in_specs=[block(2), block(1)],
-        out_specs=[packed(2), packed(1)],
-        out_shape=[jax.ShapeDtypeStruct((experts, depth, n * FF), BF) for n in (2, 1)],
+        lambda block_ref, *rest: pack_kernel(block_ref, rest[-1]),
+        grid=(steps,),
+        in_specs=[pl.BlockSpec((step, experts, width), lambda s: (s, 0, 0))]
+        + [anywhere()] * len(earlier),
+        out_specs=pl.BlockSpec((experts, step, width), lambda s: (0, s, 0)),
+        out_shape=jax.ShapeDtypeStruct((experts, depth, width), BF),
         compiler_params=pltpu.CompilerParams(vmem_limit_bytes=VMEM_LIMIT),
-        cost_estimate=cost(7 * 10**9, 10**5),
+        cost_estimate=cost(5 * 10**9, 10**5),
         name="pack",
-    )(gate_up, down_proj)
+    )(weight, *earlier)
 
 
 def swap(x, axis, how):
@@ -609,7 +606,7 @@
     swapped = columns == 8 and planes == 4 and gate_up.shape[1] == planes
     if swapped:
         out_parts = start_out(out_weight)
-        pair, down = pack_experts(gate_up, down_proj)
+        pair = pack_experts(gate_up, 4)
         cache_len, anchor = after((cache_len, anchor), pair)
     matches = (anchor[:, None] == jnp.arange(columns, dtype=jnp.int32)[None, :]).astype(jnp.int32)
     earlier = jnp.sum((jnp.cumsum(matches, axis=0) - 1) * matches, axis=1)
@@ -625,10 +622,11 @@
     extra = jnp.pad(extra.astype(BF), ((0, 0), (0, LANES - 2)))
     own = jnp.concatenate([queries[:LOCAL], extra], axis=1)
     if swapped:
-        out_parts, pair, down = lax.optimization_barrier((out_parts, pair, down))
+
         pair = exchange(pair)
         out_parts = swap_out(out_weight, stack_rows(out_parts), asks)
-        asks = after(asks, out_parts[3])
+        down = pack_experts(down_proj, 2, out_parts[3])
+        asks = after(asks, out_parts[3], down)
     else:
         out_parts = gather_out(out_weight)
     here, reply = attend(

time: 250 us -> 246 us (0.984)
  waiting for transfers between devices: 83.3 us -> 75.2 us
    ppermute x32, waiting for transfers between devices: 80.5 us -> 72.4 us  [swap(): lax.ppermute(x, axis, [(i, how(i)) for i in range(lax.axis_size(axis))])]
    pallas_call x1 -> x2, Pallas kernels: 8.31 us -> 10.3 us  [pack_experts(): pl.pallas_call(lambda block_ref, *rest: pack_kernel(block_ref, rest[-1]),...]
    unnamed x74 -> x70, local copies, waits for them, and re-layouts: 16.6 us -> 15.7 us
  transfers between devices with their start and end apart: 34 -> 34, of which waited for: 18 -> 18; matrix products, arithmetic and copies ran while one was open for 3% -> 3% of each run, Pallas kernels for 26% -> 27%
where the time goes in v6:
time: 246 us; the launch traced here: 244 us
  waiting for transfers between devices  75.2 us (31%)
  Pallas kernels  70.2 us (29%)
  starting transfers between devices  51 us (21%)
  blocking collectives  24 us (10%)
  local copies, waits for them, and re-layouts  20.6 us (8%)
    ppermute x32, waiting for transfers between devices, swap(): lax.ppermute(x, axis, [(i, how(i)) for i in range(lax.axis_size(axis))])  72.4 us
    ppermute x32, starting transfers between devices, swap(): lax.ppermute(x, axis, [(i, how(i)) for i in range(lax.axis_size(axis))])  37.7 us
    pallas_call x5, Pallas kernels, make_hidden(): pl.pallas_call(functools.partial(hidden_kernel, len(pieces)), in_specs=[s...  24.4 us
    unnamed x70, local copies, waits for them, and re-layouts  15.7 us
    pallas_call x5, Pallas kernels, make_down(): pl.pallas_call(functools.partial(down_kernel, count), in_specs=[vmem()] *...  15.1 us
    all_to_all x2, starting transfers between devices, exchange(): lax.all_to_all(packed, 'gx', split_axis=0, concat_axis=0, tiled=True)  13.4 us
    all_gather x1, blocking collectives, body(): back = lax.all_gather(reply, 'gy', axis=0, tiled=True)  12.3 us
    all_gather x1, blocking collectives, body(): lax.all_gather(jnp.concatenate([queries[LOCAL:], extra], axis=1), 'gy', a...  11.7 us
  transfers between devices with their start and end apart: 34, of which 18 were waited for; matrix products, arithmetic and copies ran while one was open for 3% of the time, Pallas kernels for 27%

profile of v6, /device:TPU:0, one launch (start us, length us, event | category | flops | bytes accessed | tf_op | source)
XLA Modules:
  0.0 244.4 jit_solution(8289191614055142422)
XLA Ops:
  0.6 1.6 constant_dynamic-slice_fusion
  2.2 5.0 %collective-permute-start.2 = (bf16[48,1536]{1,0:T(8,128)(2,1)}, bf16[48,1536]{1,0:T(8,128)(2,1)S(1)}, u32[]{:S(2)}, u32[]{:S(2)}) collective-permute-start(bf16[48,1536]{1,0:T(8,128)(2,1)} %constant_dynamic-slice_fusion), channel_id=1, source_target_pairs={{0,24},{8,16},{16,8},{24,0},{1,25},{9,17},{17,9},{25,1},{2,26},{10... | collective-permute-start | bytes 442376 | tf_op jit(solution)/shard_map/ppermute | solution.py:369
  7.8 6.4 %pack.2 = bf16[4,384,1024]{2,1,0:T(8,128)(2,1)} custom-call(bf16[384,4,1024]{2,1,0:T(4,128)(2,1)} %block_ref.2), custom_call_target="tpu_custom_call" | custom-call | flops 5000000000 | bytes 100000 | tf_op jit(solution)/shard_map/pack/pallas_call | solution.py:355
  14.2 5.2 %all-to-all-start = ((bf16[4,384,1024]{2,1,0:T(8,128)(2,1)}), bf16[4,384,1024]{2,1,0:T(8,128)(2,1)S(1)}, u32[]{:S(2)}, u32[]{:S(2)}) async-start(bf16[4,384,1024]{2,1,0:T(8,128)(2,1)} %pack.2), calls=%async_computation | async-start | bytes 6291456 | tf_op jit(solution)/shard_map/all_to_all | solution.py:385
  21.7 1.7 stack.158.refs_0_.rest_1_
  23.4 1.5 collective-permute-start.3
  25.0 11.7 %all_gather.6.refs_2_.asks_ref = bf16[64,1664]{1,0:T(8,128)(2,1)S(1)} all-gather(bf16[8,1664]{1,0:T(8,128)(2,1)S(1)} %pad_maximum_fusion), channel_id=1, replica_groups=mesh['gx'=4,'gy'=8] {'gy'}, dimensions={0}, use_global_device_ids=true | all-gather | bytes 239616 | tf_op jit(solution)/shard_map/all_gather | solution.py:618
  39.9 1.5 collective-permute-start.4
  41.4 4.0 %pack.3 = bf16[4,384,512]{2,1,0:T(8,128)(2,1)} custom-call(bf16[384,4,512]{2,1,0:T(4,128)(2,1)} %block_ref.3, bf16[288,1536]{1,0:T(8,128)(2,1)} %copy-done.17), custom_call_target="tpu_custom_call" | custom-call | flops 5000000000 | bytes 100000 | tf_op jit(solution)/shard_map/pack/pallas_call | solution.py:355
  45.4 7.0 %attend.1 = (f32[8,1664]{1,0:T(8,128)}, f32[16,1664]{1,0:T(8,128)}) custom-call(s32[1]{0:T(128)} %bitcast.25.me_ref, bf16[8,1664]{1,0:T(8,128)(2,1)} %fusion.1.own_ref, bf16[64,1664]{1,0:T(8,128)(2,1)} %copy-done.18, s32[24,32]{1,0:T(8,128)} %pad_add_fusion.table_ref, bf16[2048,1024]{1,0:T(8,128)(2,1)} %bitcast.49, bf16[2048,1024]{1,0:T(8,128)(2,1)} %bitcast.50), custom_call_target="tpu_custom_call" | custom-call | flops 7000000000 | bytes 100000 | tf_op jit(solution)/shard_map/attend/pallas_call | solution.py:143
  57.5 12.3 %all_gather.7.back_ref = f32[128,1664]{1,0:T(8,128)} all-gather(f32[16,1664]{1,0:T(8,128)} %get-tuple-element.44), channel_id=1, replica_groups=mesh['gx'=4,'gy'=8] {'gy'}, dimensions={0}, use_global_device_ids=true | all-gather | bytes 958464 | tf_op jit(solution)/shard_map/all_gather | solution.py:643
  69.8 6.3 %stream.1 = (bf16[16,1536]{1,0:T(8,128)(2,1)}, f32[128,1536]{1,0:T(8,128)}, bf16[128,1664]{1,0:T(8,128)(2,1)}) custom-call(s32[8]{0:T(128)} %get-tuple-element.87.chosen_ref, s32[25]{0:T(128)} %stack.147.at_ref, bf16[16,1536]{1,0:T(8,128)(2,1)} %query_ref.1, bf16[16,1024]{1,0:T(8,128)(2,1)} %fresh_ref.1, f32[8,1664]{1,0:T(8,128)} %get-tuple-element.43.here_ref, ...), custom_call_target="tpu_custom_call" | custom-call | flops 8000000000 | bytes 100000 | tf_op jit(solution)/shard_map/stream/pallas_call | solution.py:257
  76.1 1.6 collective-permute-start.8
  77.6 2.9 %collective-permute-start.12 = (bf16[128,1664]{1,0:T(8,128)(2,1)}, bf16[128,1664]{1,0:T(8,128)(2,1)S(1)}, u32[]{:S(2)}, u32[]{:S(2)}) collective-permute-start(bf16[128,1664]{1,0:T(8,128)(2,1)} %get-tuple-element.50.refs_0_), channel_id=1, source_target_pairs={{0,16},{8,24},{16,0},{24,8},{1,17},{9,25},{17,1},{25,9},{2,18},{10... | collective-permute-start | bytes 1277960 | tf_op jit(solution)/shard_map/ppermute | solution.py:369
  82.0 2.5 %collective-permute-done.8.refs_1_ = bf16[128,1664]{1,0:T(8,128)(2,1)S(1)} collective-permute-done((bf16[128,1664]{1,0:T(8,128)(2,1)}, bf16[128,1664]{1,0:T(8,128)(2,1)S(1)}, u32[]{:S(2)}, u32[]{:S(2)}) %collective-permute-start.8) | collective-permute-done | bytes 426016 | tf_op jit(solution)/shard_map/ppermute | solution.py:369
  85.6 1.6 collective-permute-start.9
  87.1 20.5 %collective-permute-done.12.refs_0_ = bf16[128,1664]{1,0:T(8,128)(2,1)S(1)} collective-permute-done((bf16[128,1664]{1,0:T(8,128)(2,1)}, bf16[128,1664]{1,0:T(8,128)(2,1)S(1)}, u32[]{:S(2)}, u32[]{:S(2)}) %collective-permute-start.12) | collective-permute-done | bytes 426016 | tf_op jit(solution)/shard_map/ppermute | solution.py:369
  111.0 4.7 %collective-permute-done.13.refs_1_ = bf16[128,1664]{1,0:T(8,128)(2,1)S(1)} collective-permute-done((bf16[128,1664]{1,0:T(8,128)(2,1)S(1)}, bf16[128,1664]{1,0:T(8,128)(2,1)S(1)}, u32[]{:S(2)}, u32[]{:S(2)}) %collective-permute-start.13) | collective-permute-done | bytes 426016 | tf_op jit(solution)/shard_map/ppermute | solution.py:369
  116.8 3.6 %collective-permute-done.11.refs_1_ = bf16[128,1664]{1,0:T(8,128)(2,1)S(1)} collective-permute-done((bf16[128,1664]{1,0:T(8,128)(2,1)S(1)}, bf16[128,1664]{1,0:T(8,128)(2,1)S(1)}, u32[]{:S(2)}, u32[]{:S(2)}) %collective-permute-start.11) | collective-permute-done | bytes 426016 | tf_op jit(solution)/shard_map/ppermute | solution.py:369
  123.4 8.1 %all-to-all-start.1 = ((bf16[4,384,512]{2,1,0:T(8,128)(2,1)}), bf16[4,384,512]{2,1,0:T(8,128)(2,1)}, u32[]{:S(2)}, u32[]{:S(2)}) async-start(bf16[4,384,512]{2,1,0:T(8,128)(2,1)} %pack.3), calls=%async_computation.1 | async-start | bytes 3145728 | tf_op jit(solution)/shard_map/all_to_all | solution.py:385
  131.6 1.5 collective-permute-start.18
  133.1 1.5 collective-permute-start.17
  137.5 5.5 %hidden.5 = (bf16[512,1024]{1,0:T(8,128)(2,1)S(1)}, f32[512,128]{1,0:T(8,128)S(1)}) custom-call(s32[2]{0:T(128)S(1)} %pad_add_fusion.1.place_ref, bf16[256,1664]{1,0:T(8,128)(2,1)S(1)} %copy-done.3, bf16[256,1664]{1,0:T(8,128)(2,1)S(1)} %copy-done.20, bf16[1536,1024]{1,0:T(8,128)(2,1)S(1)} %bitcast.44, bf16[1536,1024]{1,0:T(8,128)(2,1)} %collective-permute-done.15.refs_3_.refs_2_), custom_call_target="tpu_custom_call" | custom-call | flops 1000000 | bytes 100000 | tf_op jit(solution)/shard_map/hidden/pallas_call | solution.py:300
  144.1 2.0 stack.163.refs_0_
  146.1 2.0 collective-permute-start.19
  148.0 4.0 %hidden.6 = (bf16[256,1024]{1,0:T(8,128)(2,1)S(1)}, f32[256,128]{1,0:T(8,128)S(1)}) custom-call(s32[2]{0:T(128)S(1)} %pad_add_fusion.1.place_ref, bf16[256,1664]{1,0:T(8,128)(2,1)} %stack.163.refs_0_, bf16[1536,1024]{1,0:T(8,128)(2,1)S(1)} %bitcast.45, bf16[1536,1024]{1,0:T(8,128)(2,1)} %collective-permute-done.15.refs_3_.refs_2_, ...), custom_call_target="tpu_custom_call" | custom-call | flops 1000000 | bytes 100000 | tf_op jit(solution)/shard_map/hidden/pallas_call | solution.py:300
  152.8 5.5 %hidden.7 = (bf16[512,1024]{1,0:T(8,128)(2,1)S(1)}, f32[512,128]{1,0:T(8,128)S(1)}) custom-call(s32[2]{0:T(128)S(1)} %pad_add_fusion.1.place_ref, bf16[256,1664]{1,0:T(8,128)(2,1)S(1)} %copy-done.5, bf16[256,1664]{1,0:T(8,128)(2,1)S(1)} %collective-permute-done.17.refs_1_, bf16[1536,1024]{1,0:T(8,128)(2,1)S(1)} %bitcast.46, ...), custom_call_target="tpu_custom_call" | custom-call | flops 1000000 | bytes 100000 | tf_op jit(solution)/shard_map/hidden/pallas_call | solution.py:300
  159.4 5.4 %hidden.8 = (bf16[512,1024]{1,0:T(8,128)(2,1)S(1)}, f32[512,128]{1,0:T(8,128)S(1)}) custom-call(s32[2]{0:T(128)S(1)} %pad_add_fusion.1.place_ref, bf16[256,1664]{1,0:T(8,128)(2,1)S(1)} %copy-done.1, bf16[256,1664]{1,0:T(8,128)(2,1)S(1)} %collective-permute-done.16.refs_1_, bf16[1536,1024]{1,0:T(8,128)(2,1)S(1)} %bitcast.47, ...), custom_call_target="tpu_custom_call" | custom-call | flops 1000000 | bytes 100000 | tf_op jit(solution)/shard_map/hidden/pallas_call | solution.py:300
  167.2 2.8 %all-to-all-done.1 = bf16[4,384,512]{2,1,0:T(8,128)(2,1)} async-done(((bf16[4,384,512]{2,1,0:T(8,128)(2,1)}), bf16[4,384,512]{2,1,0:T(8,128)(2,1)}, u32[]{:S(2)}, u32[]{:S(2)}) %all-to-all-start.1) | async-done | bytes 1572896 | tf_op jit(solution)/shard_map/all_to_all | solution.py:385
  171.0 4.0 %hidden.9 = (bf16[256,1024]{1,0:T(8,128)(2,1)S(1)}, f32[256,128]{1,0:T(8,128)S(1)}) custom-call(s32[2]{0:T(128)S(1)} %pad_add_fusion.1.place_ref, bf16[256,1664]{1,0:T(8,128)(2,1)} %collective-permute-done.19.refs_0_, bf16[1536,1024]{1,0:T(8,128)(2,1)S(1)} %bitcast.48, bf16[1536,1024]{1,0:T(8,128)(2,1)} %collective-permute-done.15.refs_3_.refs_2_, ...), custom_call_target="tpu_custom_call" | custom-call | flops 1000000 | bytes 100000 | tf_op jit(solution)/shard_map/hidden/pallas_call | solution.py:300
  175.0 2.7 %down.5.rest_0_ = bf16[256,1536]{1,0:T(8,128)(2,1)S(1)} custom-call(bf16[256,1024]{1,0:T(8,128)(2,1)S(1)} %get-tuple-element.61.hidden_ref, f32[256,128]{1,0:T(8,128)S(1)} %get-tuple-element.62.share_ref, bf16[1536,512]{1,0:T(8,128)(2,1)} %bitcast.36.mine_ref, bf16[1536,512]{1,0:T(8,128)(2,1)S(1)} %collective-permute-done.20.other_ref), custom_call_target="tpu_custom_call" | custom-call | flops 1000000 | bytes 100000 | tf_op jit(solution)/shard_map/down/pallas_call | solution.py:333
  177.7 1.6 collective-permute-start.22
  179.3 2.5 %down.6.rest_0_.keep_ref = bf16[256,1536]{1,0:T(8,128)(2,1)S(1)} custom-call(bf16[256,1024]{1,0:T(8,128)(2,1)S(1)} %copy-done.23, f32[256,128]{1,0:T(8,128)S(1)} %get-tuple-element.55.refs_4_.share_ref, bf16[1536,512]{1,0:T(8,128)(2,1)} %bitcast.36.mine_ref, bf16[1536,512]{1,0:T(8,128)(2,1)S(1)} %collective-permute-done.20.other_ref, ...), custom_call_target="tpu_custom_call" | custom-call | flops 1000000 | bytes 100000 | tf_op jit(solution)/shard_map/down/pallas_call | solution.py:333
  181.9 3.3 %down.7 = (bf16[256,1536]{1,0:T(8,128)(2,1)S(1)}, bf16[256,1536]{1,0:T(8,128)(2,1)S(1)}) custom-call(bf16[512,1024]{1,0:T(8,128)(2,1)S(1)} %copy-done.11, f32[512,128]{1,0:T(8,128)S(1)} %copy-done.16, bf16[1536,512]{1,0:T(8,128)(2,1)} %bitcast.36.mine_ref, bf16[1536,512]{1,0:T(8,128)(2,1)S(1)} %collective-permute-done.20.other_ref, ...), custom_call_target="tpu_custom_call" | custom-call | flops 1000000 | bytes 100000 | tf_op jit(solution)/shard_map/down/pallas_call | solution.py:333
  185.8 4.0 %collective-permute-done.22.came_ref = bf16[256,1536]{1,0:T(8,128)(2,1)S(1)} collective-permute-done((bf16[256,1536]{1,0:T(8,128)(2,1)S(1)}, bf16[256,1536]{1,0:T(8,128)(2,1)S(1)}, u32[]{:S(2)}, u32[]{:S(2)}) %collective-permute-start.22) | collective-permute-done | bytes 786464 | tf_op jit(solution)/shard_map/ppermute | solution.py:369
  190.0 1.6 collective-permute-start.23
  191.5 3.3 %down.8 = (bf16[256,1536]{1,0:T(8,128)(2,1)S(1)}, bf16[256,1536]{1,0:T(8,128)(2,1)S(1)}) custom-call(bf16[512,1024]{1,0:T(8,128)(2,1)S(1)} %copy-done.9, f32[512,128]{1,0:T(8,128)S(1)} %copy-done.13, bf16[1536,512]{1,0:T(8,128)(2,1)} %bitcast.36.mine_ref, bf16[1536,512]{1,0:T(8,128)(2,1)S(1)} %collective-permute-done.20.other_ref, ...), custom_call_target="tpu_custom_call" | custom-call | flops 1000000 | bytes 100000 | tf_op jit(solution)/shard_map/down/pallas_call | solution.py:333
  194.8 1.6 collective-permute-start.25
  196.4 5.7 %collective-permute-done.23.rest_0_ = bf16[128,1536]{1,0:T(8,128)(2,1)S(1)} collective-permute-done((bf16[128,1536]{1,0:T(8,128)(2,1)S(1)}, bf16[128,1536]{1,0:T(8,128)(2,1)S(1)}, u32[]{:S(2)}, u32[]{:S(2)}) %collective-permute-start.23) | collective-permute-done | bytes 393248 | tf_op jit(solution)/shard_map/ppermute | solution.py:369
  202.6 1.6 collective-permute-start.26
  204.2 3.3 %down.9 = (bf16[256,1536]{1,0:T(8,128)(2,1)S(1)}, bf16[256,1536]{1,0:T(8,128)(2,1)S(1)}) custom-call(bf16[512,1024]{1,0:T(8,128)(2,1)S(1)} %copy-done.7, f32[512,128]{1,0:T(8,128)S(1)} %get-tuple-element.53.refs_2_.refs_3_.share_ref, bf16[1536,512]{1,0:T(8,128)(2,1)} %bitcast.36.mine_ref, bf16[1536,512]{1,0:T(8,128)(2,1)S(1)} %collective-permute-done.20.other_ref, ...), custom_call_target="tpu_custom_call" | custom-call | flops 1000000 | bytes 100000 | tf_op jit(solution)/shard_map/down/pallas_call | solution.py:333
  207.5 1.6 collective-permute-start.24
  209.0 5.7 %collective-permute-done.26.rest_0_ = bf16[128,1536]{1,0:T(8,128)(2,1)S(1)} collective-permute-done((bf16[128,1536]{1,0:T(8,128)(2,1)S(1)}, bf16[128,1536]{1,0:T(8,128)(2,1)S(1)}, u32[]{:S(2)}, u32[]{:S(2)}) %collective-permute-start.26) | collective-permute-done | bytes 393248 | tf_op jit(solution)/shard_map/ppermute | solution.py:369
  215.2 1.6 collective-permute-start.28
  217.4 9.8 %collective-permute-done.28.rest_0_ = bf16[128,1536]{1,0:T(8,128)(2,1)S(1)} collective-permute-done((bf16[128,1536]{1,0:T(8,128)(2,1)S(1)}, bf16[128,1536]{1,0:T(8,128)(2,1)S(1)}, u32[]{:S(2)}, u32[]{:S(2)}) %collective-permute-start.28) | collective-permute-done | bytes 393248 | tf_op jit(solution)/shard_map/ppermute | solution.py:369
  227.9 1.6 collective-permute-start.29
  229.4 5.6 %collective-permute-done.31.rest_2_ = bf16[128,1536]{1,0:T(8,128)(2,1)S(1)} collective-permute-done((bf16[128,1536]{1,0:T(8,128)(2,1)S(1)}, bf16[128,1536]{1,0:T(8,128)(2,1)S(1)}, u32[]{:S(2)}, u32[]{:S(2)}) %collective-permute-start.31) | collective-permute-done | bytes 393248 | tf_op jit(solution)/shard_map/ppermute | solution.py:369
  235.7 7.7 %collective-permute-done.30.rest_1_ = bf16[128,1536]{1,0:T(8,128)(2,1)S(1)} collective-permute-done((bf16[128,1536]{1,0:T(8,128)(2,1)S(1)}, bf16[128,1536]{1,0:T(8,128)(2,1)S(1)}, u32[]{:S(2)}, u32[]{:S(2)}) %collective-permute-start.30) | collective-permute-done | bytes 393248 | tf_op jit(solution)/shard_map/ppermute | solution.py:369
  (142 shorter events, 35.0 us)
Async XLA Ops:
  2.2 19.4 %collective-permute-start.2 = (bf16[48,1536]{1,0:T(8,128)(2,1)}, bf16[48,1536]{1,0:T(8,128)(2,1)S(1)}, u32[]{:S(2)}, u32[]{:S(2)}) collective-permute-start(bf16[48,1536]{1,0:T(8,128)(2,1)} %constant_dynamic-slice_fusion), channel_id=1, source_target_pairs={{0,24},{8,16},{16,8},{24,0},{1,25},{9,17},{17,9},{25,1},{2,26},{10... | collective-permute-start | bytes 442376 | tf_op jit(solution)/shard_map/ppermute | solution.py:369
  7.3 14.4 %collective-permute-start.1 = (bf16[48,1536]{1,0:T(8,128)(2,1)}, bf16[48,1536]{1,0:T(8,128)(2,1)S(1)}, u32[]{:S(2)}, u32[]{:S(2)}) collective-permute-start(bf16[48,1536]{1,0:T(8,128)(2,1)} %constant_dynamic-slice_fusion), channel_id=1, source_target_pairs={{0,16},{8,24},{16,0},{24,8},{1,17},{9,25},{17,1},{25,9},{2,18},{10... | collective-permute-start | bytes 442376 | tf_op jit(solution)/shard_map/ppermute | solution.py:369
  7.3 14.4 %collective-permute-start = (bf16[48,1536]{1,0:T(8,128)(2,1)}, bf16[48,1536]{1,0:T(8,128)(2,1)}, u32[]{:S(2)}, u32[]{:S(2)}) collective-permute-start(bf16[48,1536]{1,0:T(8,128)(2,1)} %constant_dynamic-slice_fusion), channel_id=1, source_target_pairs={{0,8},{8,0},{16,24},{24,16},{1,9},{9,1},{17,25},{25,17},{2,10},{10... | collective-permute-start | bytes 442376 | tf_op jit(solution)/shard_map/ppermute | solution.py:369
  14.2 6.0 %copy-start.33 = (s32[16]{0:T(128)S(1)}, s32[16]{0:T(128)}, u32[]{:S(2)}) copy-start(s32[16]{0:T(128)} %param.18) | copy-start | bytes 196
  14.2 6.3 %copy-start.29 = (s32[8]{0:T(128)S(1)}, s32[8]{0:T(128)}, u32[]{:S(2)}) copy-start(s32[8]{0:T(128)} %param.20) | copy-start | bytes 100
  14.2 22.6 %copy-start.28 = (s32[16,32]{1,0:T(8,128)S(1)}, s32[16,32]{1,0:T(8,128)}, u32[]{:S(2)}) copy-start(s32[16,32]{1,0:T(8,128)} %param.21) | copy-start | bytes 6148
  14.2 22.6 %copy-start.32 = (s32[8,32]{1,0:T(8,128)S(1)}, s32[8,32]{1,0:T(8,128)}, u32[]{:S(2)}) copy-start(s32[8,32]{1,0:T(8,128)} %param.19) | copy-start | bytes 3076
  14.2 109.2 %all-to-all-start = ((bf16[4,384,1024]{2,1,0:T(8,128)(2,1)}), bf16[4,384,1024]{2,1,0:T(8,128)(2,1)S(1)}, u32[]{:S(2)}, u32[]{:S(2)}) async-start(bf16[4,384,1024]{2,1,0:T(8,128)(2,1)} %pack.2), calls=%async_computation | async-start | bytes 6291456 | tf_op jit(solution)/shard_map/all_to_all | solution.py:385
  23.4 14.6 %collective-permute-start.3 = (bf16[144,1536]{1,0:T(8,128)(2,1)}, bf16[144,1536]{1,0:T(8,128)(2,1)}, u32[]{:S(2)}, u32[]{:S(2)}) collective-permute-start(bf16[144,1536]{1,0:T(8,128)(2,1)} %stack.158.refs_0_.rest_1_), channel_id=1, source_target_pairs={{0,2},{1,5},{2,0},{3,7},{4,6},{5,1},{6,4},{7,3},{8,10},{9,13},{10,... | collective-permute-start | bytes 1327112 | tf_op jit(solution)/shard_map/ppermute | solution.py:369
  39.9 13.1 %collective-permute-start.4 = (bf16[288,1536]{1,0:T(8,128)(2,1)S(1)}, bf16[288,1536]{1,0:T(8,128)(2,1)}, u32[]{:S(2)}, u32[]{:S(2)}) collective-permute-start(bf16[288,1536]{1,0:T(8,128)(2,1)S(1)} %stack.159.rest_0_), channel_id=1, source_target_pairs={{0,4},{1,3},{2,6},{3,1},{4,0},{5,7},{6,2},{7,5},{8,12},{9,11},{10,... | collective-permute-start | bytes 2654216 | tf_op jit(solution)/shard_map/ppermute | solution.py:369
  45.4 8.2 %copy-start.31 = (bf16[1536]{0:T(1024)(128)(2,1)S(1)}, bf16[1536]{0:T(1024)(128)(2,1)}, u32[]{:S(2)}) copy-start(bf16[1536]{0:T(1024)(128)(2,1)} %param.25) | copy-start | bytes 9220
  45.4 8.8 %copy-start.30 = (s32[128,8]{0,1:T(8,128)S(1)}, s32[128,8]{0,1:T(8,128)}, u32[]{:S(2)}) copy-start(s32[128,8]{0,1:T(8,128)} %param.27) | copy-start | bytes 12292
  53.0 16.7 %collective-permute-start.7 = (bf16[288,1536]{1,0:T(8,128)(2,1)}, bf16[288,1536]{1,0:T(8,128)(2,1)}, u32[]{:S(2)}, u32[]{:S(2)}) collective-permute-start(bf16[288,1536]{1,0:T(8,128)(2,1)} %collective-permute-done.4.rest_3_), channel_id=1, source_target_pairs={{0,1},{1,0},{2,3},{3,2},{4,5},{5,4},{6,7},{7,6},{8,9},{9,8},{10,11... | collective-permute-start | bytes 2654216 | tf_op jit(solution)/shard_map/ppermute | solution.py:369
  53.0 16.7 %collective-permute-start.5 = (bf16[144,1536]{1,0:T(8,128)(2,1)}, bf16[144,1536]{1,0:T(8,128)(2,1)}, u32[]{:S(2)}, u32[]{:S(2)}) collective-permute-start(bf16[144,1536]{1,0:T(8,128)(2,1)} %stack.158.refs_0_.rest_1_), channel_id=1, source_target_pairs={{0,1},{1,0},{2,3},{3,2},{4,5},{5,4},{6,7},{7,6},{8,9},{9,8},{10,11... | collective-permute-start | bytes 1327112 | tf_op jit(solution)/shard_map/ppermute | solution.py:369
  53.5 16.2 %collective-permute-start.6 = (bf16[144,1536]{1,0:T(8,128)(2,1)}, bf16[144,1536]{1,0:T(8,128)(2,1)}, u32[]{:S(2)}, u32[]{:S(2)}) collective-permute-start(bf16[144,1536]{1,0:T(8,128)(2,1)} %collective-permute-done.3.refs_1_.rest_2_), channel_id=1, source_target_pairs={{0,1},{1,0},{2,3},{3,2},{4,5},{5,4},{6,7},{7,6},{8,9},{9,8},{10,11... | collective-permute-start | bytes 1327112 | tf_op jit(solution)/shard_map/ppermute | solution.py:369
  76.1 8.4 %collective-permute-start.8 = (bf16[128,1664]{1,0:T(8,128)(2,1)}, bf16[128,1664]{1,0:T(8,128)(2,1)S(1)}, u32[]{:S(2)}, u32[]{:S(2)}) collective-permute-start(bf16[128,1664]{1,0:T(8,128)(2,1)} %get-tuple-element.50.refs_0_), channel_id=1, source_target_pairs={{0,2},{1,5},{2,0},{3,7},{4,6},{5,1},{6,4},{7,3},{8,10},{9,13},{10,... | collective-permute-start | bytes 1277960 | tf_op jit(solution)/shard_map/ppermute | solution.py:369
  77.6 30.0 %collective-permute-start.12 = (bf16[128,1664]{1,0:T(8,128)(2,1)}, bf16[128,1664]{1,0:T(8,128)(2,1)S(1)}, u32[]{:S(2)}, u32[]{:S(2)}) collective-permute-start(bf16[128,1664]{1,0:T(8,128)(2,1)} %get-tuple-element.50.refs_0_), channel_id=1, source_target_pairs={{0,16},{8,24},{16,0},{24,8},{1,17},{9,25},{17,1},{25,9},{2,18},{10... | collective-permute-start | bytes 1277960 | tf_op jit(solution)/shard_map/ppermute | solution.py:369
  80.6 28.6 %collective-permute-start.10 = (bf16[128,1664]{1,0:T(8,128)(2,1)}, bf16[128,1664]{1,0:T(8,128)(2,1)S(1)}, u32[]{:S(2)}, u32[]{:S(2)}) collective-permute-start(bf16[128,1664]{1,0:T(8,128)(2,1)} %get-tuple-element.50.refs_0_), channel_id=1, source_target_pairs={{0,8},{8,0},{16,24},{24,16},{1,9},{9,1},{17,25},{25,17},{2,10},{10... | collective-permute-start | bytes 1277960 | tf_op jit(solution)/shard_map/ppermute | solution.py:369
  85.5 24.2 %copy-start.27 = (bf16[128,1664]{1,0:T(8,128)(2,1)S(1)}, bf16[128,1664]{1,0:T(8,128)(2,1)}, u32[]{:S(2)}) copy-start(bf16[128,1664]{1,0:T(8,128)(2,1)} %get-tuple-element.50.refs_0_) | copy-start | bytes 1277956
  85.6 34.9 %copy-start.2 = (bf16[256,1664]{1,0:T(8,128)(2,1)}, bf16[256,1664]{1,0:T(8,128)(2,1)S(1)}, u32[]{:S(2)}) copy-start(bf16[256,1664]{1,0:T(8,128)(2,1)S(1)} %stack.160.refs_0_) | copy-start | bytes 2555908
  85.6 36.9 %collective-permute-start.9 = (bf16[256,1664]{1,0:T(8,128)(2,1)S(1)}, bf16[256,1664]{1,0:T(8,128)(2,1)S(1)}, u32[]{:S(2)}, u32[]{:S(2)}) collective-permute-start(bf16[256,1664]{1,0:T(8,128)(2,1)S(1)} %stack.160.refs_0_), channel_id=1, source_target_pairs={{0,4},{1,3},{2,6},{3,1},{4,0},{5,7},{6,2},{7,5},{8,12},{9,11},{10,... | collective-permute-start | bytes 2555912 | tf_op jit(solution)/shard_map/ppermute | solution.py:369
  107.7 8.1 %collective-permute-start.13 = (bf16[128,1664]{1,0:T(8,128)(2,1)S(1)}, bf16[128,1664]{1,0:T(8,128)(2,1)S(1)}, u32[]{:S(2)}, u32[]{:S(2)}) collective-permute-start(bf16[128,1664]{1,0:T(8,128)(2,1)S(1)} %collective-permute-done.12.refs_0_), channel_id=1, source_target_pairs={{0,2},{1,5},{2,0},{3,7},{4,6},{5,1},{6,4},{7,3},{8,10},{9,13},{10,... | collective-permute-start | bytes 1277960 | tf_op jit(solution)/shard_map/ppermute | solution.py:369
  109.1 11.2 %collective-permute-start.11 = (bf16[128,1664]{1,0:T(8,128)(2,1)S(1)}, bf16[128,1664]{1,0:T(8,128)(2,1)S(1)}, u32[]{:S(2)}, u32[]{:S(2)}) collective-permute-start(bf16[128,1664]{1,0:T(8,128)(2,1)S(1)} %collective-permute-done.10.refs_0_), channel_id=1, source_target_pairs={{0,2},{1,5},{2,0},{3,7},{4,6},{5,1},{6,4},{7,3},{8,10},{9,13},{10,... | collective-permute-start | bytes 1277960 | tf_op jit(solution)/shard_map/ppermute | solution.py:369
  109.7 12.1 %collective-permute-start.14 = (bf16[128,1664]{1,0:T(8,128)(2,1)S(1)}, bf16[128,1664]{1,0:T(8,128)(2,1)S(1)}, u32[]{:S(2)}, u32[]{:S(2)}) collective-permute-start(bf16[128,1664]{1,0:T(8,128)(2,1)S(1)} %copy-done.27), channel_id=1, source_target_pairs={{0,24},{8,16},{16,8},{24,0},{1,25},{9,17},{17,9},{25,1},{2,26},{10... | collective-permute-start | bytes 1277960 | tf_op jit(solution)/shard_map/ppermute | solution.py:369
  123.4 11.7 %collective-permute-start.15 = (bf16[1536,1024]{1,0:T(8,128)(2,1)S(1)}, bf16[1536,1024]{1,0:T(8,128)(2,1)}, u32[]{:S(2)}, u32[]{:S(2)}) collective-permute-start(bf16[1536,1024]{1,0:T(8,128)(2,1)S(1)} %bitcast.43), channel_id=1, source_target_pairs={{0,1},{1,0},{2,3},{3,2},{4,5},{5,4},{6,7},{7,6},{8,9},{9,8},{10,11... | collective-permute-start | bytes 9437192 | tf_op jit(solution)/shard_map/ppermute | solution.py:369
  123.4 46.6 %all-to-all-start.1 = ((bf16[4,384,512]{2,1,0:T(8,128)(2,1)}), bf16[4,384,512]{2,1,0:T(8,128)(2,1)}, u32[]{:S(2)}, u32[]{:S(2)}) async-start(bf16[4,384,512]{2,1,0:T(8,128)(2,1)} %pack.3), calls=%async_computation.1 | async-start | bytes 3145728 | tf_op jit(solution)/shard_map/all_to_all | solution.py:385
  131.6 12.5 %collective-permute-start.18 = (bf16[128,1664]{1,0:T(8,128)(2,1)}, bf16[128,1664]{1,0:T(8,128)(2,1)}, u32[]{:S(2)}, u32[]{:S(2)}) collective-permute-start(bf16[128,1664]{1,0:T(8,128)(2,1)} %copy-done.24), channel_id=1, source_target_pairs={{0,2},{1,5},{2,0},{3,7},{4,6},{5,1},{6,4},{7,3},{8,10},{9,13},{10,... | collective-permute-start | bytes 1277960 | tf_op jit(solution)/shard_map/ppermute | solution.py:369
  133.1 19.7 %collective-permute-start.17 = (bf16[256,1664]{1,0:T(8,128)(2,1)}, bf16[256,1664]{1,0:T(8,128)(2,1)S(1)}, u32[]{:S(2)}, u32[]{:S(2)}) collective-permute-start(bf16[256,1664]{1,0:T(8,128)(2,1)} %copy-done.4), channel_id=1, source_target_pairs={{0,4},{1,3},{2,6},{3,1},{4,0},{5,7},{6,2},{7,5},{8,12},{9,11},{10,... | collective-permute-start | bytes 2555912 | tf_op jit(solution)/shard_map/ppermute | solution.py:369
  134.7 24.7 %collective-permute-start.16 = (bf16[256,1664]{1,0:T(8,128)(2,1)}, bf16[256,1664]{1,0:T(8,128)(2,1)S(1)}, u32[]{:S(2)}, u32[]{:S(2)}) collective-permute-start(bf16[256,1664]{1,0:T(8,128)(2,1)} %copy-done), channel_id=1, source_target_pairs={{0,4},{1,3},{2,6},{3,1},{4,0},{5,7},{6,2},{7,5},{8,12},{9,11},{10,... | collective-permute-start | bytes 2555912 | tf_op jit(solution)/shard_map/ppermute | solution.py:369
  137.5 6.6 %copy-start.25 = (bf16[128,1664]{1,0:T(8,128)(2,1)S(1)}, bf16[128,1664]{1,0:T(8,128)(2,1)}, u32[]{:S(2)}) copy-start(bf16[128,1664]{1,0:T(8,128)(2,1)} %copy-done.24) | copy-start | bytes 1277956
  146.1 6.8 %copy-start.5 = (bf16[256,1664]{1,0:T(8,128)(2,1)S(1)}, bf16[256,1664]{1,0:T(8,128)(2,1)}, u32[]{:S(2)}) copy-start(bf16[256,1664]{1,0:T(8,128)(2,1)} %copy-done.4) | copy-start | bytes 2555908
  146.1 24.0 %collective-permute-start.19 = (bf16[256,1664]{1,0:T(8,128)(2,1)}, bf16[256,1664]{1,0:T(8,128)(2,1)}, u32[]{:S(2)}, u32[]{:S(2)}) collective-permute-start(bf16[256,1664]{1,0:T(8,128)(2,1)} %stack.163.refs_0_), channel_id=1, source_target_pairs={{0,4},{1,3},{2,6},{3,1},{4,0},{5,7},{6,2},{7,5},{8,12},{9,11},{10,... | collective-permute-start | bytes 2555912 | tf_op jit(solution)/shard_map/ppermute | solution.py:369
  152.8 6.6 %copy-start.1 = (bf16[256,1664]{1,0:T(8,128)(2,1)S(1)}, bf16[256,1664]{1,0:T(8,128)(2,1)}, u32[]{:S(2)}) copy-start(bf16[256,1664]{1,0:T(8,128)(2,1)} %copy-done) | copy-start | bytes 2555908
  170.0 5.0 %collective-permute-start.20 = (bf16[1536,512]{1,0:T(8,128)(2,1)}, bf16[1536,512]{1,0:T(8,128)(2,1)S(1)}, u32[]{:S(2)}, u32[]{:S(2)}) collective-permute-start(bf16[1536,512]{1,0:T(8,128)(2,1)} %bitcast.36.mine_ref), channel_id=1, source_target_pairs={{0,1},{1,0},{2,3},{3,2},{4,5},{5,4},{6,7},{7,6},{8,9},{9,8},{10,11... | collective-permute-start | bytes 4718600 | tf_op jit(solution)/shard_map/ppermute | solution.py:369
  177.7 12.1 %collective-permute-start.22 = (bf16[256,1536]{1,0:T(8,128)(2,1)S(1)}, bf16[256,1536]{1,0:T(8,128)(2,1)S(1)}, u32[]{:S(2)}, u32[]{:S(2)}) collective-permute-start(bf16[256,1536]{1,0:T(8,128)(2,1)S(1)} %down.5.rest_0_), channel_id=1, source_target_pairs={{0,4},{1,3},{2,6},{3,1},{4,0},{5,7},{6,2},{7,5},{8,12},{9,11},{10,... | collective-permute-start | bytes 2359304 | tf_op jit(solution)/shard_map/ppermute | solution.py:369
  185.2 6.3 %copy-start.9 = (bf16[512,1024]{1,0:T(8,128)(2,1)S(1)}, bf16[512,1024]{1,0:T(8,128)(2,1)}, u32[]{:S(2)}) copy-start(bf16[512,1024]{1,0:T(8,128)(2,1)} %copy-done.8) | copy-start | bytes 3145732
  185.2 6.3 %copy-start.13 = (f32[512,128]{1,0:T(8,128)S(1)}, f32[512,128]{1,0:T(8,128)}, u32[]{:S(2)}) copy-start(f32[512,128]{1,0:T(8,128)} %copy-done.12) | copy-start | bytes 786436
  185.2 17.2 %collective-permute-start.21 = (bf16[256,1536]{1,0:T(8,128)(2,1)S(1)}, bf16[256,1536]{1,0:T(8,128)(2,1)S(1)}, u32[]{:S(2)}, u32[]{:S(2)}) collective-permute-start(bf16[256,1536]{1,0:T(8,128)(2,1)S(1)} %get-tuple-element.64), channel_id=1, source_target_pairs={{0,4},{1,3},{2,6},{3,1},{4,0},{5,7},{6,2},{7,5},{8,12},{9,11},{10,... | collective-permute-start | bytes 2359304 | tf_op jit(solution)/shard_map/ppermute | solution.py:369
  190.0 12.1 %collective-permute-start.23 = (bf16[128,1536]{1,0:T(8,128)(2,1)S(1)}, bf16[128,1536]{1,0:T(8,128)(2,1)S(1)}, u32[]{:S(2)}, u32[]{:S(2)}) collective-permute-start(bf16[128,1536]{1,0:T(8,128)(2,1)S(1)} %get-tuple-element.66.rest_0_), channel_id=1, source_target_pairs={{0,2},{1,5},{2,0},{3,7},{4,6},{5,1},{6,4},{7,3},{8,10},{9,13},{10,... | collective-permute-start | bytes 1179656 | tf_op jit(solution)/shard_map/ppermute | solution.py:369
  194.8 20.3 %collective-permute-start.25 = (bf16[256,1536]{1,0:T(8,128)(2,1)S(1)}, bf16[256,1536]{1,0:T(8,128)(2,1)S(1)}, u32[]{:S(2)}, u32[]{:S(2)}) collective-permute-start(bf16[256,1536]{1,0:T(8,128)(2,1)S(1)} %get-tuple-element.72), channel_id=1, source_target_pairs={{0,4},{1,3},{2,6},{3,1},{4,0},{5,7},{6,2},{7,5},{8,12},{9,11},{10,... | collective-permute-start | bytes 2359304 | tf_op jit(solution)/shard_map/ppermute | solution.py:369
  202.6 12.1 %collective-permute-start.26 = (bf16[128,1536]{1,0:T(8,128)(2,1)S(1)}, bf16[128,1536]{1,0:T(8,128)(2,1)S(1)}, u32[]{:S(2)}, u32[]{:S(2)}) collective-permute-start(bf16[128,1536]{1,0:T(8,128)(2,1)S(1)} %get-tuple-element.69.rest_0_), channel_id=1, source_target_pairs={{0,2},{1,5},{2,0},{3,7},{4,6},{5,1},{6,4},{7,3},{8,10},{9,13},{10,... | collective-permute-start | bytes 1179656 | tf_op jit(solution)/shard_map/ppermute | solution.py:369
  204.2 10.6 %collective-permute-start.27 = (bf16[128,1536]{1,0:T(8,128)(2,1)S(1)}, bf16[128,1536]{1,0:T(8,128)(2,1)S(1)}, u32[]{:S(2)}, u32[]{:S(2)}) collective-permute-start(bf16[128,1536]{1,0:T(8,128)(2,1)S(1)} %close.3.rest_0_), channel_id=1, source_target_pairs={{0,8},{8,0},{16,24},{24,16},{1,9},{9,1},{17,25},{25,17},{2,10},{10... | collective-permute-start | bytes 1179656 | tf_op jit(solution)/shard_map/ppermute | solution.py:369
  207.5 20.3 %collective-permute-start.24 = (bf16[256,1536]{1,0:T(8,128)(2,1)S(1)}, bf16[256,1536]{1,0:T(8,128)(2,1)S(1)}, u32[]{:S(2)}, u32[]{:S(2)}) collective-permute-start(bf16[256,1536]{1,0:T(8,128)(2,1)S(1)} %get-tuple-element.71), channel_id=1, source_target_pairs={{0,4},{1,3},{2,6},{3,1},{4,0},{5,7},{6,2},{7,5},{8,12},{9,11},{10,... | collective-permute-start | bytes 2359304 | tf_op jit(solution)/shard_map/ppermute | solution.py:369
  215.2 12.0 %collective-permute-start.28 = (bf16[128,1536]{1,0:T(8,128)(2,1)S(1)}, bf16[128,1536]{1,0:T(8,128)(2,1)S(1)}, u32[]{:S(2)}, u32[]{:S(2)}) collective-permute-start(bf16[128,1536]{1,0:T(8,128)(2,1)S(1)} %get-tuple-element.75.rest_1_), channel_id=1, source_target_pairs={{0,2},{1,5},{2,0},{3,7},{4,6},{5,1},{6,4},{7,3},{8,10},{9,13},{10,... | collective-permute-start | bytes 1179656 | tf_op jit(solution)/shard_map/ppermute | solution.py:369
  216.8 18.2 %collective-permute-start.31 = (bf16[128,1536]{1,0:T(8,128)(2,1)S(1)}, bf16[128,1536]{1,0:T(8,128)(2,1)S(1)}, u32[]{:S(2)}, u32[]{:S(2)}) collective-permute-start(bf16[128,1536]{1,0:T(8,128)(2,1)S(1)} %close.4.rest_0_), channel_id=1, source_target_pairs={{0,16},{8,24},{16,0},{24,8},{1,17},{9,25},{17,1},{25,9},{2,18},{10... | collective-permute-start | bytes 1179656 | tf_op jit(solution)/shard_map/ppermute | solution.py:369
  227.2 16.1 %copy-start.21 = (f32[128,1536]{1,0:T(8,128)S(1)}, f32[128,1536]{1,0:T(8,128)}, u32[]{:S(2)}) copy-start(f32[128,1536]{1,0:T(8,128)} %get-tuple-element.49.stream_ref) | copy-start | bytes 2359300
  227.9 7.8 %collective-permute-start.29 = (bf16[128,1536]{1,0:T(8,128)(2,1)S(1)}, bf16[128,1536]{1,0:T(8,128)(2,1)S(1)}, u32[]{:S(2)}, u32[]{:S(2)}) collective-permute-start(bf16[128,1536]{1,0:T(8,128)(2,1)S(1)} %get-tuple-element.77), channel_id=1, source_target_pairs={{0,2},{1,5},{2,0},{3,7},{4,6},{5,1},{6,4},{7,3},{8,10},{9,13},{10,... | collective-permute-start | bytes 1179656 | tf_op jit(solution)/shard_map/ppermute | solution.py:369
  229.4 13.9 %collective-permute-start.30 = (bf16[128,1536]{1,0:T(8,128)(2,1)S(1)}, bf16[128,1536]{1,0:T(8,128)(2,1)S(1)}, u32[]{:S(2)}, u32[]{:S(2)}) collective-permute-start(bf16[128,1536]{1,0:T(8,128)(2,1)S(1)} %close.5.rest_0_), channel_id=1, source_target_pairs={{0,8},{8,0},{16,24},{24,16},{1,9},{9,1},{17,25},{25,17},{2,10},{10... | collective-permute-start | bytes 1179656 | tf_op jit(solution)/shard_map/ppermute | solution.py:369
  (20 other events, 26.8 us)

commit v7 on v6

--- a/solution.py
+++ b/solution.py
@@ -428,16 +428,24 @@
     return small_call(join_kernel, "join", [keep, came], earlier, [(shape, F32), (shape, BF)])
 
 
-def close_kernel(count, part_ref, *rest):
-    total = part_ref[...]
-    for ref in rest[:count]:
-        total = total + ref[...].astype(F32)
+def close_kernel(want, core_ref, part_ref, came_ref, *rest):
+    total = part_ref[...] + came_ref[...].astype(F32)
+    if want is not None:
+        total = total + jnp.where(core_ref[0] == want, rest[0][...].astype(F32), 0.0)
     rest[-1][...] = total.astype(BF)
 
 
-def close(part, came, *earlier):
-    kernel = functools.partial(close_kernel, len(came))
-    return small_call(kernel, "close", [part, *came], earlier, [(part.shape, BF)])[0]
+def close(want, core, part, came, earlier):
+    arrays = [part, *came]
+    return pl.pallas_call(
+        functools.partial(close_kernel, want),
+        in_specs=[smem()] + [vmem()] * len(arrays) + [anywhere()] * len(earlier),
+        out_specs=vmem(),
+        out_shape=jax.ShapeDtypeStruct(part.shape, BF),
+        compiler_params=pltpu.CompilerParams(vmem_limit_bytes=16 * 1024 * 1024),
+        cost_estimate=cost(10**6, 10**5),
+        name="close",
+    )(core, *arrays, *earlier)
 
 
 def finish_kernel(stream_ref, part_ref, *rest):
@@ -449,9 +457,20 @@
 
 def swapped_experts(send, stream, pair, down):
     planes = lax.axis_size("gx")
+    columns = lax.axis_size("gy")
     row, column = lax.axis_index("gx"), lax.axis_index("gy")
     place = jnp.stack([column * planes + row, beside(column) * planes + row]).astype(jnp.int32)
-    across = lambda x, k: swap(x, "gx", lambda i: i ^ k)
+    core = (column % 2).astype(jnp.int32).reshape(1)
+
+    def across(x, k):
+        even, odd = ((0, 0), (1, 2), (2, 1), (3, 3))[k]
+        pairs = [
+            (i * columns + j, (i ^ (odd if j % 2 else even)) * columns + j)
+            for i in range(planes)
+            for j in range(columns)
+        ]
+        return lax.ppermute(x, ("gx", "gy"), pairs)
+
 
     mine = [send] + [across(send, k) for k in range(1, planes)]
     beyond = [swap(x, "gy", near) for x in mine]
@@ -492,8 +511,9 @@
         return (passed,)
 
     def leave(k, *came):
-        passed = close(parts[k], [ends[k], *came], *last)
-        ends[k] = across(passed, 2 if k == 2 else 1)
+        want = {1: 1, 2: 0}.get(k)
+        passed = close(want, core, parts[k], [ends[k], *came], last)
+        ends[k] = swap(passed, "gx", lambda i: i ^ 1) if k == 3 else across(passed, k)
         return (passed,)
 
     last = put(3)
@@ -505,7 +525,7 @@
     last = put(0)
     last = leave(2, ends[3])
     last = turn(1)
-    last = leave(1)
+    last = leave(1, ends[3])
     last = turn(0)
     arrays = [stream, parts[0], ends[0], ends[1], ends[2]]
     return small_call(finish_kernel, "finish", arrays, (), [(stream.shape, F32)])[0]

time: 246 us -> 243 us (0.988)
  starting transfers between devices: 51 us -> 47 us
    ppermute x0 -> x5, waiting for transfers between devices: none -> 26.2 us  [across(): return lax.ppermute(x, ('gx', 'gy'), pairs)]
    ppermute x32 -> x27, waiting for transfers between devices: 72.4 us -> 46.4 us  [swap(): lax.ppermute(x, axis, [(i, how(i)) for i in range(lax.axis_size(axis))])]
    ppermute x32 -> x27, starting transfers between devices: 37.7 us -> 27.4 us  [swap(): lax.ppermute(x, axis, [(i, how(i)) for i in range(lax.axis_size(axis))])]
    ppermute x0 -> x5, starting transfers between devices: none -> 6.22 us  [across(): return lax.ppermute(x, ('gx', 'gy'), pairs)]
    pallas_call x14 -> x11, Pallas kernels: 7.09 us -> 6.84 us  [small_call(): pl.pallas_call(kernel, in_specs=[vmem()] * len(arrays) + [anywhere()] * l...]
  transfers between devices with their start and end apart: 34 -> 34, of which waited for: 18 -> 17; matrix products, arithmetic and copies ran while one was open for 3% -> 3% of each run, Pallas kernels for 27% -> 27%
where the time goes in v7:
time: 243 us; the launch traced here: 242 us
  waiting for transfers between devices  76.8 us (32%)
  Pallas kernels  70.4 us (29%)
  starting transfers between devices  47 us (19%)
  blocking collectives  24 us (10%)
  local copies, waits for them, and re-layouts  20.6 us (8%)
    ppermute x27, waiting for transfers between devices, swap(): lax.ppermute(x, axis, [(i, how(i)) for i in range(lax.axis_size(axis))])  46.4 us
    ppermute x27, starting transfers between devices, swap(): lax.ppermute(x, axis, [(i, how(i)) for i in range(lax.axis_size(axis))])  27.4 us
    ppermute x5, waiting for transfers between devices, across(): return lax.ppermute(x, ('gx', 'gy'), pairs)  26.2 us
    pallas_call x5, Pallas kernels, make_hidden(): pl.pallas_call(functools.partial(hidden_kernel, len(pieces)), in_specs=[s...  24.4 us
    unnamed x70, local copies, waits for them, and re-layouts  15.7 us
    pallas_call x5, Pallas kernels, make_down(): pl.pallas_call(functools.partial(down_kernel, count), in_specs=[vmem()] *...  15.1 us
    all_to_all x2, starting transfers between devices, exchange(): lax.all_to_all(packed, 'gx', split_axis=0, concat_axis=0, tiled=True)  13.4 us
    all_gather x1, blocking collectives, body(): back = lax.all_gather(reply, 'gy', axis=0, tiled=True)  12.3 us
  transfers between devices with their start and end apart: 34, of which 17 were waited for; matrix products, arithmetic and copies ran while one was open for 3% of the time, Pallas kernels for 27%

profile of v7, /device:TPU:0, one launch (start us, length us, event | category | flops | bytes accessed | tf_op | source)
XLA Modules:
  0.0 242.2 jit_solution(552660602080349206)
XLA Ops:
  0.6 1.6 constant_dynamic-slice_fusion
  2.2 5.0 %collective-permute-start.2 = (bf16[48,1536]{1,0:T(8,128)(2,1)}, bf16[48,1536]{1,0:T(8,128)(2,1)S(1)}, u32[]{:S(2)}, u32[]{:S(2)}) collective-permute-start(bf16[48,1536]{1,0:T(8,128)(2,1)} %constant_dynamic-slice_fusion), channel_id=1, source_target_pairs={{0,24},{8,16},{16,8},{24,0},{1,25},{9,17},{17,9},{25,1},{2,26},{10... | collective-permute-start | bytes 442376 | tf_op jit(solution)/shard_map/ppermute | solution.py:369
  7.8 6.4 %pack.2 = bf16[4,384,1024]{2,1,0:T(8,128)(2,1)} custom-call(bf16[384,4,1024]{2,1,0:T(4,128)(2,1)} %block_ref.2), custom_call_target="tpu_custom_call" | custom-call | flops 5000000000 | bytes 100000 | tf_op jit(solution)/shard_map/pack/pallas_call | solution.py:355
  14.2 5.2 %all-to-all-start = ((bf16[4,384,1024]{2,1,0:T(8,128)(2,1)}), bf16[4,384,1024]{2,1,0:T(8,128)(2,1)S(1)}, u32[]{:S(2)}, u32[]{:S(2)}) async-start(bf16[4,384,1024]{2,1,0:T(8,128)(2,1)} %pack.2), calls=%async_computation | async-start | bytes 6291456 | tf_op jit(solution)/shard_map/all_to_all | solution.py:385
  21.7 1.7 stack.158.refs_0_.rest_1_
  23.4 1.5 collective-permute-start.3
  25.0 11.7 %all_gather.6.refs_2_.asks_ref = bf16[64,1664]{1,0:T(8,128)(2,1)S(1)} all-gather(bf16[8,1664]{1,0:T(8,128)(2,1)S(1)} %pad_maximum_fusion), channel_id=1, replica_groups=mesh['gx'=4,'gy'=8] {'gy'}, dimensions={0}, use_global_device_ids=true | all-gather | bytes 239616 | tf_op jit(solution)/shard_map/all_gather | solution.py:638
  39.9 1.5 collective-permute-start.4
  41.4 4.0 %pack.3 = bf16[4,384,512]{2,1,0:T(8,128)(2,1)} custom-call(bf16[384,4,512]{2,1,0:T(4,128)(2,1)} %block_ref.3, bf16[288,1536]{1,0:T(8,128)(2,1)} %copy-done.17), custom_call_target="tpu_custom_call" | custom-call | flops 5000000000 | bytes 100000 | tf_op jit(solution)/shard_map/pack/pallas_call | solution.py:355
  45.4 7.0 %attend.1 = (f32[8,1664]{1,0:T(8,128)}, f32[16,1664]{1,0:T(8,128)}) custom-call(s32[1]{0:T(128)} %bitcast.25.me_ref, bf16[8,1664]{1,0:T(8,128)(2,1)} %fusion.1.own_ref, bf16[64,1664]{1,0:T(8,128)(2,1)} %copy-done.18, s32[24,32]{1,0:T(8,128)} %pad_add_fusion.table_ref, bf16[2048,1024]{1,0:T(8,128)(2,1)} %bitcast.50, bf16[2048,1024]{1,0:T(8,128)(2,1)} %bitcast.51), custom_call_target="tpu_custom_call" | custom-call | flops 7000000000 | bytes 100000 | tf_op jit(solution)/shard_map/attend/pallas_call | solution.py:143
  57.5 12.3 %all_gather.7.back_ref = f32[128,1664]{1,0:T(8,128)} all-gather(f32[16,1664]{1,0:T(8,128)} %get-tuple-element.44), channel_id=1, replica_groups=mesh['gx'=4,'gy'=8] {'gy'}, dimensions={0}, use_global_device_ids=true | all-gather | bytes 958464 | tf_op jit(solution)/shard_map/all_gather | solution.py:663
  69.8 6.3 %stream.1 = (bf16[16,1536]{1,0:T(8,128)(2,1)}, f32[128,1536]{1,0:T(8,128)}, bf16[128,1664]{1,0:T(8,128)(2,1)}) custom-call(s32[8]{0:T(128)} %get-tuple-element.87.chosen_ref, s32[25]{0:T(128)} %stack.147.at_ref, bf16[16,1536]{1,0:T(8,128)(2,1)} %query_ref.1, bf16[16,1024]{1,0:T(8,128)(2,1)} %fresh_ref.1, f32[8,1664]{1,0:T(8,128)} %get-tuple-element.43.here_ref, ...), custom_call_target="tpu_custom_call" | custom-call | flops 8000000000 | bytes 100000 | tf_op jit(solution)/shard_map/stream/pallas_call | solution.py:257
  76.1 1.6 collective-permute-start.8
  77.6 2.9 %collective-permute-start.12 = (bf16[128,1664]{1,0:T(8,128)(2,1)}, bf16[128,1664]{1,0:T(8,128)(2,1)S(1)}, u32[]{:S(2)}, u32[]{:S(2)}) collective-permute-start(bf16[128,1664]{1,0:T(8,128)(2,1)} %get-tuple-element.50.refs_0_), channel_id=1, source_target_pairs={{0,16},{1,9},{2,18},{3,11},{4,20},{5,13},{6,22},{7,15},{8,24},{9,1... | collective-permute-start | bytes 1277960 | tf_op jit(solution)/shard_map/ppermute | solution.py:472
  80.6 1.5 collective-permute-start.10
  82.0 2.4 %collective-permute-done.8.refs_1_ = bf16[128,1664]{1,0:T(8,128)(2,1)S(1)} collective-permute-done((bf16[128,1664]{1,0:T(8,128)(2,1)}, bf16[128,1664]{1,0:T(8,128)(2,1)S(1)}, u32[]{:S(2)}, u32[]{:S(2)}) %collective-permute-start.8) | collective-permute-done | bytes 426016 | tf_op jit(solution)/shard_map/ppermute | solution.py:369
  85.6 1.6 collective-permute-start.9
  87.1 20.5 %collective-permute-done.12.refs_0_ = bf16[128,1664]{1,0:T(8,128)(2,1)S(1)} collective-permute-done((bf16[128,1664]{1,0:T(8,128)(2,1)}, bf16[128,1664]{1,0:T(8,128)(2,1)S(1)}, u32[]{:S(2)}, u32[]{:S(2)}) %collective-permute-start.12) | collective-permute-done | bytes 426016 | tf_op jit(solution)/shard_map/ppermute | solution.py:472
  107.6 1.5 collective-permute-start.13
  109.6 1.5 collective-permute-start.14
  111.1 4.6 %collective-permute-done.13.refs_1_ = bf16[128,1664]{1,0:T(8,128)(2,1)S(1)} collective-permute-done((bf16[128,1664]{1,0:T(8,128)(2,1)S(1)}, bf16[128,1664]{1,0:T(8,128)(2,1)S(1)}, u32[]{:S(2)}, u32[]{:S(2)}) %collective-permute-start.13) | collective-permute-done | bytes 426016 | tf_op jit(solution)/shard_map/ppermute | solution.py:369
  116.7 3.6 %collective-permute-done.11.refs_1_ = bf16[128,1664]{1,0:T(8,128)(2,1)S(1)} collective-permute-done((bf16[128,1664]{1,0:T(8,128)(2,1)S(1)}, bf16[128,1664]{1,0:T(8,128)(2,1)S(1)}, u32[]{:S(2)}, u32[]{:S(2)}) %collective-permute-start.11) | collective-permute-done | bytes 426016 | tf_op jit(solution)/shard_map/ppermute | solution.py:369
  123.2 8.1 %all-to-all-start.1 = ((bf16[4,384,512]{2,1,0:T(8,128)(2,1)}), bf16[4,384,512]{2,1,0:T(8,128)(2,1)}, u32[]{:S(2)}, u32[]{:S(2)}) async-start(bf16[4,384,512]{2,1,0:T(8,128)(2,1)} %pack.3), calls=%async_computation.1 | async-start | bytes 3145728 | tf_op jit(solution)/shard_map/all_to_all | solution.py:385
  131.3 1.5 collective-permute-start.18
  133.4 1.5 collective-permute-start.16
  137.3 5.5 %hidden.5 = (bf16[512,1024]{1,0:T(8,128)(2,1)S(1)}, f32[512,128]{1,0:T(8,128)S(1)}) custom-call(s32[2]{0:T(128)S(1)} %pad_add_fusion.1.place_ref, bf16[256,1664]{1,0:T(8,128)(2,1)S(1)} %copy-done.3, bf16[256,1664]{1,0:T(8,128)(2,1)S(1)} %copy-done.20, bf16[1536,1024]{1,0:T(8,128)(2,1)S(1)} %bitcast.45, bf16[1536,1024]{1,0:T(8,128)(2,1)} %collective-permute-done.15.refs_3_.refs_2_), custom_call_target="tpu_custom_call" | custom-call | flops 1000000 | bytes 100000 | tf_op jit(solution)/shard_map/hidden/pallas_call | solution.py:300
  144.3 2.0 stack.163.refs_0_
  146.3 4.0 %hidden.6 = (bf16[256,1024]{1,0:T(8,128)(2,1)S(1)}, f32[256,128]{1,0:T(8,128)S(1)}) custom-call(s32[2]{0:T(128)S(1)} %pad_add_fusion.1.place_ref, bf16[256,1664]{1,0:T(8,128)(2,1)} %stack.163.refs_0_, bf16[1536,1024]{1,0:T(8,128)(2,1)S(1)} %bitcast.46, bf16[1536,1024]{1,0:T(8,128)(2,1)} %collective-permute-done.15.refs_3_.refs_2_, ...), custom_call_target="tpu_custom_call" | custom-call | flops 1000000 | bytes 100000 | tf_op jit(solution)/shard_map/hidden/pallas_call | solution.py:300
  151.2 5.5 %hidden.7 = (bf16[512,1024]{1,0:T(8,128)(2,1)S(1)}, f32[512,128]{1,0:T(8,128)S(1)}) custom-call(s32[2]{0:T(128)S(1)} %pad_add_fusion.1.place_ref, bf16[256,1664]{1,0:T(8,128)(2,1)S(1)} %copy-done.5, bf16[256,1664]{1,0:T(8,128)(2,1)S(1)} %collective-permute-done.17.refs_1_, bf16[1536,1024]{1,0:T(8,128)(2,1)S(1)} %bitcast.47, ...), custom_call_target="tpu_custom_call" | custom-call | flops 1000000 | bytes 100000 | tf_op jit(solution)/shard_map/hidden/pallas_call | solution.py:300
  157.8 5.4 %hidden.8 = (bf16[512,1024]{1,0:T(8,128)(2,1)S(1)}, f32[512,128]{1,0:T(8,128)S(1)}) custom-call(s32[2]{0:T(128)S(1)} %pad_add_fusion.1.place_ref, bf16[256,1664]{1,0:T(8,128)(2,1)S(1)} %copy-done.1, bf16[256,1664]{1,0:T(8,128)(2,1)S(1)} %collective-permute-done.16.refs_1_, bf16[1536,1024]{1,0:T(8,128)(2,1)S(1)} %bitcast.48, ...), custom_call_target="tpu_custom_call" | custom-call | flops 1000000 | bytes 100000 | tf_op jit(solution)/shard_map/hidden/pallas_call | solution.py:300
  165.6 4.2 %all-to-all-done.1 = bf16[4,384,512]{2,1,0:T(8,128)(2,1)} async-done(((bf16[4,384,512]{2,1,0:T(8,128)(2,1)}), bf16[4,384,512]{2,1,0:T(8,128)(2,1)}, u32[]{:S(2)}, u32[]{:S(2)}) %all-to-all-start.1) | async-done | bytes 1572896 | tf_op jit(solution)/shard_map/all_to_all | solution.py:385
  170.7 4.0 %hidden.9 = (bf16[256,1024]{1,0:T(8,128)(2,1)S(1)}, f32[256,128]{1,0:T(8,128)S(1)}) custom-call(s32[2]{0:T(128)S(1)} %pad_add_fusion.1.place_ref, bf16[256,1664]{1,0:T(8,128)(2,1)} %collective-permute-done.19.refs_0_, bf16[1536,1024]{1,0:T(8,128)(2,1)S(1)} %bitcast.49, bf16[1536,1024]{1,0:T(8,128)(2,1)} %collective-permute-done.15.refs_3_.refs_2_, ...), custom_call_target="tpu_custom_call" | custom-call | flops 1000000 | bytes 100000 | tf_op jit(solution)/shard_map/hidden/pallas_call | solution.py:300
  174.8 2.7 %down.5.rest_0_ = bf16[256,1536]{1,0:T(8,128)(2,1)S(1)} custom-call(bf16[256,1024]{1,0:T(8,128)(2,1)S(1)} %get-tuple-element.61.hidden_ref, f32[256,128]{1,0:T(8,128)S(1)} %get-tuple-element.62.share_ref, bf16[1536,512]{1,0:T(8,128)(2,1)} %bitcast.36.mine_ref, bf16[1536,512]{1,0:T(8,128)(2,1)S(1)} %collective-permute-done.20.other_ref), custom_call_target="tpu_custom_call" | custom-call | flops 1000000 | bytes 100000 | tf_op jit(solution)/shard_map/down/pallas_call | solution.py:333
  178.1 2.5 %down.6.rest_0_.keep_ref = bf16[256,1536]{1,0:T(8,128)(2,1)S(1)} custom-call(bf16[256,1024]{1,0:T(8,128)(2,1)S(1)} %copy-done.23, f32[256,128]{1,0:T(8,128)S(1)} %get-tuple-element.55.refs_4_.share_ref, bf16[1536,512]{1,0:T(8,128)(2,1)} %bitcast.36.mine_ref, bf16[1536,512]{1,0:T(8,128)(2,1)S(1)} %collective-permute-done.20.other_ref, ...), custom_call_target="tpu_custom_call" | custom-call | flops 1000000 | bytes 100000 | tf_op jit(solution)/shard_map/down/pallas_call | solution.py:333
  180.6 3.3 %down.7 = (bf16[256,1536]{1,0:T(8,128)(2,1)S(1)}, bf16[256,1536]{1,0:T(8,128)(2,1)S(1)}) custom-call(bf16[512,1024]{1,0:T(8,128)(2,1)S(1)} %copy-done.11, f32[512,128]{1,0:T(8,128)S(1)} %copy-done.16, bf16[1536,512]{1,0:T(8,128)(2,1)} %bitcast.36.mine_ref, bf16[1536,512]{1,0:T(8,128)(2,1)S(1)} %collective-permute-done.20.other_ref, ...), custom_call_target="tpu_custom_call" | custom-call | flops 1000000 | bytes 100000 | tf_op jit(solution)/shard_map/down/pallas_call | solution.py:333
  184.0 1.6 collective-permute-start.21
  185.5 4.0 %collective-permute-done.22.came_ref = bf16[256,1536]{1,0:T(8,128)(2,1)S(1)} collective-permute-done((bf16[256,1536]{1,0:T(8,128)(2,1)S(1)}, bf16[256,1536]{1,0:T(8,128)(2,1)S(1)}, u32[]{:S(2)}, u32[]{:S(2)}) %collective-permute-start.22) | collective-permute-done | bytes 786464 | tf_op jit(solution)/shard_map/ppermute | solution.py:369
  189.7 1.6 collective-permute-start.23
  191.3 3.3 %down.8 = (bf16[256,1536]{1,0:T(8,128)(2,1)S(1)}, bf16[256,1536]{1,0:T(8,128)(2,1)S(1)}) custom-call(bf16[512,1024]{1,0:T(8,128)(2,1)S(1)} %copy-done.9, f32[512,128]{1,0:T(8,128)S(1)} %copy-done.13, bf16[1536,512]{1,0:T(8,128)(2,1)} %bitcast.36.mine_ref, bf16[1536,512]{1,0:T(8,128)(2,1)S(1)} %collective-permute-done.20.other_ref, ...), custom_call_target="tpu_custom_call" | custom-call | flops 1000000 | bytes 100000 | tf_op jit(solution)/shard_map/down/pallas_call | solution.py:333
  195.2 6.7 %collective-permute-done.23.came_ref = bf16[128,1536]{1,0:T(8,128)(2,1)S(1)} collective-permute-done((bf16[128,1536]{1,0:T(8,128)(2,1)S(1)}, bf16[128,1536]{1,0:T(8,128)(2,1)S(1)}, u32[]{:S(2)}, u32[]{:S(2)}) %collective-permute-start.23) | collective-permute-done | bytes 393248 | tf_op jit(solution)/shard_map/ppermute | solution.py:369
  202.4 1.6 collective-permute-start.26
  203.9 3.3 %down.9 = (bf16[256,1536]{1,0:T(8,128)(2,1)S(1)}, bf16[256,1536]{1,0:T(8,128)(2,1)S(1)}) custom-call(bf16[512,1024]{1,0:T(8,128)(2,1)S(1)} %copy-done.7, f32[512,128]{1,0:T(8,128)S(1)} %get-tuple-element.53.refs_2_.refs_3_.share_ref, bf16[1536,512]{1,0:T(8,128)(2,1)} %bitcast.36.mine_ref, bf16[1536,512]{1,0:T(8,128)(2,1)S(1)} %collective-permute-done.20.other_ref, ...), custom_call_target="tpu_custom_call" | custom-call | flops 1000000 | bytes 100000 | tf_op jit(solution)/shard_map/down/pallas_call | solution.py:333
  207.8 6.7 %collective-permute-done.26.came_ref = bf16[128,1536]{1,0:T(8,128)(2,1)S(1)} collective-permute-done((bf16[128,1536]{1,0:T(8,128)(2,1)S(1)}, bf16[128,1536]{1,0:T(8,128)(2,1)S(1)}, u32[]{:S(2)}, u32[]{:S(2)}) %collective-permute-start.26) | collective-permute-done | bytes 393248 | tf_op jit(solution)/shard_map/ppermute | solution.py:369
  215.0 1.6 collective-permute-start.28
  216.9 10.1 %collective-permute-done.28.came_ref = bf16[128,1536]{1,0:T(8,128)(2,1)S(1)} collective-permute-done((bf16[128,1536]{1,0:T(8,128)(2,1)S(1)}, bf16[128,1536]{1,0:T(8,128)(2,1)S(1)}, u32[]{:S(2)}, u32[]{:S(2)}) %collective-permute-start.28) | collective-permute-done | bytes 393248 | tf_op jit(solution)/shard_map/ppermute | solution.py:369
  227.6 1.6 collective-permute-start.29
  229.2 6.3 %collective-permute-done.29.rest_0_ = bf16[128,1536]{1,0:T(8,128)(2,1)S(1)} collective-permute-done((bf16[128,1536]{1,0:T(8,128)(2,1)S(1)}, bf16[128,1536]{1,0:T(8,128)(2,1)S(1)}, u32[]{:S(2)}, u32[]{:S(2)}) %collective-permute-start.29) | collective-permute-done | bytes 393248 | tf_op jit(solution)/shard_map/ppermute | solution.py:369
  235.5 5.6 %collective-permute-done.30.rest_1_ = bf16[128,1536]{1,0:T(8,128)(2,1)S(1)} collective-permute-done((bf16[128,1536]{1,0:T(8,128)(2,1)S(1)}, bf16[128,1536]{1,0:T(8,128)(2,1)S(1)}, u32[]{:S(2)}, u32[]{:S(2)}) %collective-permute-start.30) | collective-permute-done | bytes 393248 | tf_op jit(solution)/shard_map/ppermute | solution.py:472
  (142 shorter events, 31.3 us)
Async XLA Ops:
  2.2 19.4 %collective-permute-start.2 = (bf16[48,1536]{1,0:T(8,128)(2,1)}, bf16[48,1536]{1,0:T(8,128)(2,1)S(1)}, u32[]{:S(2)}, u32[]{:S(2)}) collective-permute-start(bf16[48,1536]{1,0:T(8,128)(2,1)} %constant_dynamic-slice_fusion), channel_id=1, source_target_pairs={{0,24},{8,16},{16,8},{24,0},{1,25},{9,17},{17,9},{25,1},{2,26},{10... | collective-permute-start | bytes 442376 | tf_op jit(solution)/shard_map/ppermute | solution.py:369
  7.3 14.4 %collective-permute-start.1 = (bf16[48,1536]{1,0:T(8,128)(2,1)}, bf16[48,1536]{1,0:T(8,128)(2,1)S(1)}, u32[]{:S(2)}, u32[]{:S(2)}) collective-permute-start(bf16[48,1536]{1,0:T(8,128)(2,1)} %constant_dynamic-slice_fusion), channel_id=1, source_target_pairs={{0,16},{8,24},{16,0},{24,8},{1,17},{9,25},{17,1},{25,9},{2,18},{10... | collective-permute-start | bytes 442376 | tf_op jit(solution)/shard_map/ppermute | solution.py:369
  7.3 14.4 %collective-permute-start = (bf16[48,1536]{1,0:T(8,128)(2,1)}, bf16[48,1536]{1,0:T(8,128)(2,1)}, u32[]{:S(2)}, u32[]{:S(2)}) collective-permute-start(bf16[48,1536]{1,0:T(8,128)(2,1)} %constant_dynamic-slice_fusion), channel_id=1, source_target_pairs={{0,8},{8,0},{16,24},{24,16},{1,9},{9,1},{17,25},{25,17},{2,10},{10... | collective-permute-start | bytes 442376 | tf_op jit(solution)/shard_map/ppermute | solution.py:369
  14.2 6.0 %copy-start.33 = (s32[16]{0:T(128)S(1)}, s32[16]{0:T(128)}, u32[]{:S(2)}) copy-start(s32[16]{0:T(128)} %param.18) | copy-start | bytes 196
  14.2 6.3 %copy-start.29 = (s32[8]{0:T(128)S(1)}, s32[8]{0:T(128)}, u32[]{:S(2)}) copy-start(s32[8]{0:T(128)} %param.20) | copy-start | bytes 100
  14.2 22.6 %copy-start.28 = (s32[16,32]{1,0:T(8,128)S(1)}, s32[16,32]{1,0:T(8,128)}, u32[]{:S(2)}) copy-start(s32[16,32]{1,0:T(8,128)} %param.21) | copy-start | bytes 6148
  14.2 22.6 %copy-start.32 = (s32[8,32]{1,0:T(8,128)S(1)}, s32[8,32]{1,0:T(8,128)}, u32[]{:S(2)}) copy-start(s32[8,32]{1,0:T(8,128)} %param.19) | copy-start | bytes 3076
  14.2 109.0 %all-to-all-start = ((bf16[4,384,1024]{2,1,0:T(8,128)(2,1)}), bf16[4,384,1024]{2,1,0:T(8,128)(2,1)S(1)}, u32[]{:S(2)}, u32[]{:S(2)}) async-start(bf16[4,384,1024]{2,1,0:T(8,128)(2,1)} %pack.2), calls=%async_computation | async-start | bytes 6291456 | tf_op jit(solution)/shard_map/all_to_all | solution.py:385
  23.4 14.6 %collective-permute-start.3 = (bf16[144,1536]{1,0:T(8,128)(2,1)}, bf16[144,1536]{1,0:T(8,128)(2,1)}, u32[]{:S(2)}, u32[]{:S(2)}) collective-permute-start(bf16[144,1536]{1,0:T(8,128)(2,1)} %stack.158.refs_0_.rest_1_), channel_id=1, source_target_pairs={{0,2},{1,5},{2,0},{3,7},{4,6},{5,1},{6,4},{7,3},{8,10},{9,13},{10,... | collective-permute-start | bytes 1327112 | tf_op jit(solution)/shard_map/ppermute | solution.py:369
  39.9 13.1 %collective-permute-start.4 = (bf16[288,1536]{1,0:T(8,128)(2,1)S(1)}, bf16[288,1536]{1,0:T(8,128)(2,1)}, u32[]{:S(2)}, u32[]{:S(2)}) collective-permute-start(bf16[288,1536]{1,0:T(8,128)(2,1)S(1)} %stack.159.rest_0_), channel_id=1, source_target_pairs={{0,4},{1,3},{2,6},{3,1},{4,0},{5,7},{6,2},{7,5},{8,12},{9,11},{10,... | collective-permute-start | bytes 2654216 | tf_op jit(solution)/shard_map/ppermute | solution.py:369
  45.4 8.2 %copy-start.31 = (bf16[1536]{0:T(1024)(128)(2,1)S(1)}, bf16[1536]{0:T(1024)(128)(2,1)}, u32[]{:S(2)}) copy-start(bf16[1536]{0:T(1024)(128)(2,1)} %param.25) | copy-start | bytes 9220
  45.4 8.8 %copy-start.30 = (s32[128,8]{0,1:T(8,128)S(1)}, s32[128,8]{0,1:T(8,128)}, u32[]{:S(2)}) copy-start(s32[128,8]{0,1:T(8,128)} %param.27) | copy-start | bytes 12292
  53.0 16.7 %collective-permute-start.7 = (bf16[288,1536]{1,0:T(8,128)(2,1)}, bf16[288,1536]{1,0:T(8,128)(2,1)}, u32[]{:S(2)}, u32[]{:S(2)}) collective-permute-start(bf16[288,1536]{1,0:T(8,128)(2,1)} %collective-permute-done.4.rest_3_), channel_id=1, source_target_pairs={{0,1},{1,0},{2,3},{3,2},{4,5},{5,4},{6,7},{7,6},{8,9},{9,8},{10,11... | collective-permute-start | bytes 2654216 | tf_op jit(solution)/shard_map/ppermute | solution.py:369
  53.0 16.7 %collective-permute-start.5 = (bf16[144,1536]{1,0:T(8,128)(2,1)}, bf16[144,1536]{1,0:T(8,128)(2,1)}, u32[]{:S(2)}, u32[]{:S(2)}) collective-permute-start(bf16[144,1536]{1,0:T(8,128)(2,1)} %stack.158.refs_0_.rest_1_), channel_id=1, source_target_pairs={{0,1},{1,0},{2,3},{3,2},{4,5},{5,4},{6,7},{7,6},{8,9},{9,8},{10,11... | collective-permute-start | bytes 1327112 | tf_op jit(solution)/shard_map/ppermute | solution.py:369
  53.5 16.2 %collective-permute-start.6 = (bf16[144,1536]{1,0:T(8,128)(2,1)}, bf16[144,1536]{1,0:T(8,128)(2,1)}, u32[]{:S(2)}, u32[]{:S(2)}) collective-permute-start(bf16[144,1536]{1,0:T(8,128)(2,1)} %collective-permute-done.3.refs_1_.rest_2_), channel_id=1, source_target_pairs={{0,1},{1,0},{2,3},{3,2},{4,5},{5,4},{6,7},{7,6},{8,9},{9,8},{10,11... | collective-permute-start | bytes 1327112 | tf_op jit(solution)/shard_map/ppermute | solution.py:369
  76.1 8.4 %collective-permute-start.8 = (bf16[128,1664]{1,0:T(8,128)(2,1)}, bf16[128,1664]{1,0:T(8,128)(2,1)S(1)}, u32[]{:S(2)}, u32[]{:S(2)}) collective-permute-start(bf16[128,1664]{1,0:T(8,128)(2,1)} %get-tuple-element.50.refs_0_), channel_id=1, source_target_pairs={{0,2},{1,5},{2,0},{3,7},{4,6},{5,1},{6,4},{7,3},{8,10},{9,13},{10,... | collective-permute-start | bytes 1277960 | tf_op jit(solution)/shard_map/ppermute | solution.py:369
  77.6 29.9 %collective-permute-start.12 = (bf16[128,1664]{1,0:T(8,128)(2,1)}, bf16[128,1664]{1,0:T(8,128)(2,1)S(1)}, u32[]{:S(2)}, u32[]{:S(2)}) collective-permute-start(bf16[128,1664]{1,0:T(8,128)(2,1)} %get-tuple-element.50.refs_0_), channel_id=1, source_target_pairs={{0,16},{1,9},{2,18},{3,11},{4,20},{5,13},{6,22},{7,15},{8,24},{9,1... | collective-permute-start | bytes 1277960 | tf_op jit(solution)/shard_map/ppermute | solution.py:472
  80.6 28.5 %collective-permute-start.10 = (bf16[128,1664]{1,0:T(8,128)(2,1)}, bf16[128,1664]{1,0:T(8,128)(2,1)S(1)}, u32[]{:S(2)}, u32[]{:S(2)}) collective-permute-start(bf16[128,1664]{1,0:T(8,128)(2,1)} %get-tuple-element.50.refs_0_), channel_id=1, source_target_pairs={{0,8},{1,17},{2,10},{3,19},{4,12},{5,21},{6,14},{7,23},{8,0},{9,25... | collective-permute-start | bytes 1277960 | tf_op jit(solution)/shard_map/ppermute | solution.py:472
  85.5 24.1 %copy-start.27 = (bf16[128,1664]{1,0:T(8,128)(2,1)S(1)}, bf16[128,1664]{1,0:T(8,128)(2,1)}, u32[]{:S(2)}) copy-start(bf16[128,1664]{1,0:T(8,128)(2,1)} %get-tuple-element.50.refs_0_) | copy-start | bytes 1277956
  85.6 34.8 %copy-start.2 = (bf16[256,1664]{1,0:T(8,128)(2,1)}, bf16[256,1664]{1,0:T(8,128)(2,1)S(1)}, u32[]{:S(2)}) copy-start(bf16[256,1664]{1,0:T(8,128)(2,1)S(1)} %stack.160.refs_0_) | copy-start | bytes 2555908
  85.6 36.7 %collective-permute-start.9 = (bf16[256,1664]{1,0:T(8,128)(2,1)S(1)}, bf16[256,1664]{1,0:T(8,128)(2,1)S(1)}, u32[]{:S(2)}, u32[]{:S(2)}) collective-permute-start(bf16[256,1664]{1,0:T(8,128)(2,1)S(1)} %stack.160.refs_0_), channel_id=1, source_target_pairs={{0,4},{1,3},{2,6},{3,1},{4,0},{5,7},{6,2},{7,5},{8,12},{9,11},{10,... | collective-permute-start | bytes 2555912 | tf_op jit(solution)/shard_map/ppermute | solution.py:369
  107.6 8.1 %collective-permute-start.13 = (bf16[128,1664]{1,0:T(8,128)(2,1)S(1)}, bf16[128,1664]{1,0:T(8,128)(2,1)S(1)}, u32[]{:S(2)}, u32[]{:S(2)}) collective-permute-start(bf16[128,1664]{1,0:T(8,128)(2,1)S(1)} %collective-permute-done.12.refs_0_), channel_id=1, source_target_pairs={{0,2},{1,5},{2,0},{3,7},{4,6},{5,1},{6,4},{7,3},{8,10},{9,13},{10,... | collective-permute-start | bytes 1277960 | tf_op jit(solution)/shard_map/ppermute | solution.py:369
  109.1 11.2 %collective-permute-start.11 = (bf16[128,1664]{1,0:T(8,128)(2,1)S(1)}, bf16[128,1664]{1,0:T(8,128)(2,1)S(1)}, u32[]{:S(2)}, u32[]{:S(2)}) collective-permute-start(bf16[128,1664]{1,0:T(8,128)(2,1)S(1)} %collective-permute-done.10.refs_0_), channel_id=1, source_target_pairs={{0,2},{1,5},{2,0},{3,7},{4,6},{5,1},{6,4},{7,3},{8,10},{9,13},{10,... | collective-permute-start | bytes 1277960 | tf_op jit(solution)/shard_map/ppermute | solution.py:369
  109.6 11.9 %collective-permute-start.14 = (bf16[128,1664]{1,0:T(8,128)(2,1)S(1)}, bf16[128,1664]{1,0:T(8,128)(2,1)S(1)}, u32[]{:S(2)}, u32[]{:S(2)}) collective-permute-start(bf16[128,1664]{1,0:T(8,128)(2,1)S(1)} %copy-done.27), channel_id=1, source_target_pairs={{0,24},{1,25},{2,26},{3,27},{4,28},{5,29},{6,30},{7,31},{8,16},{9,... | collective-permute-start | bytes 1277960 | tf_op jit(solution)/shard_map/ppermute | solution.py:472
  123.2 11.7 %collective-permute-start.15 = (bf16[1536,1024]{1,0:T(8,128)(2,1)S(1)}, bf16[1536,1024]{1,0:T(8,128)(2,1)}, u32[]{:S(2)}, u32[]{:S(2)}) collective-permute-start(bf16[1536,1024]{1,0:T(8,128)(2,1)S(1)} %bitcast.44), channel_id=1, source_target_pairs={{0,1},{1,0},{2,3},{3,2},{4,5},{5,4},{6,7},{7,6},{8,9},{9,8},{10,11... | collective-permute-start | bytes 9437192 | tf_op jit(solution)/shard_map/ppermute | solution.py:369
  123.2 46.6 %all-to-all-start.1 = ((bf16[4,384,512]{2,1,0:T(8,128)(2,1)}), bf16[4,384,512]{2,1,0:T(8,128)(2,1)}, u32[]{:S(2)}, u32[]{:S(2)}) async-start(bf16[4,384,512]{2,1,0:T(8,128)(2,1)} %pack.3), calls=%async_computation.1 | async-start | bytes 3145728 | tf_op jit(solution)/shard_map/all_to_all | solution.py:385
  131.3 12.9 %collective-permute-start.18 = (bf16[128,1664]{1,0:T(8,128)(2,1)}, bf16[128,1664]{1,0:T(8,128)(2,1)}, u32[]{:S(2)}, u32[]{:S(2)}) collective-permute-start(bf16[128,1664]{1,0:T(8,128)(2,1)} %copy-done.24), channel_id=1, source_target_pairs={{0,2},{1,5},{2,0},{3,7},{4,6},{5,1},{6,4},{7,3},{8,10},{9,13},{10,... | collective-permute-start | bytes 1277960 | tf_op jit(solution)/shard_map/ppermute | solution.py:369
  132.9 18.3 %collective-permute-start.17 = (bf16[256,1664]{1,0:T(8,128)(2,1)}, bf16[256,1664]{1,0:T(8,128)(2,1)S(1)}, u32[]{:S(2)}, u32[]{:S(2)}) collective-permute-start(bf16[256,1664]{1,0:T(8,128)(2,1)} %copy-done.4), channel_id=1, source_target_pairs={{0,4},{1,3},{2,6},{3,1},{4,0},{5,7},{6,2},{7,5},{8,12},{9,11},{10,... | collective-permute-start | bytes 2555912 | tf_op jit(solution)/shard_map/ppermute | solution.py:369
  133.4 24.3 %collective-permute-start.16 = (bf16[256,1664]{1,0:T(8,128)(2,1)}, bf16[256,1664]{1,0:T(8,128)(2,1)S(1)}, u32[]{:S(2)}, u32[]{:S(2)}) collective-permute-start(bf16[256,1664]{1,0:T(8,128)(2,1)} %copy-done), channel_id=1, source_target_pairs={{0,4},{1,3},{2,6},{3,1},{4,0},{5,7},{6,2},{7,5},{8,12},{9,11},{10,... | collective-permute-start | bytes 2555912 | tf_op jit(solution)/shard_map/ppermute | solution.py:369
  137.3 7.0 %copy-start.25 = (bf16[128,1664]{1,0:T(8,128)(2,1)S(1)}, bf16[128,1664]{1,0:T(8,128)(2,1)}, u32[]{:S(2)}) copy-start(bf16[128,1664]{1,0:T(8,128)(2,1)} %copy-done.24) | copy-start | bytes 1277956
  146.3 4.9 %copy-start.5 = (bf16[256,1664]{1,0:T(8,128)(2,1)S(1)}, bf16[256,1664]{1,0:T(8,128)(2,1)}, u32[]{:S(2)}) copy-start(bf16[256,1664]{1,0:T(8,128)(2,1)} %copy-done.4) | copy-start | bytes 2555908
  146.3 23.5 %collective-permute-start.19 = (bf16[256,1664]{1,0:T(8,128)(2,1)}, bf16[256,1664]{1,0:T(8,128)(2,1)}, u32[]{:S(2)}, u32[]{:S(2)}) collective-permute-start(bf16[256,1664]{1,0:T(8,128)(2,1)} %stack.163.refs_0_), channel_id=1, source_target_pairs={{0,4},{1,3},{2,6},{3,1},{4,0},{5,7},{6,2},{7,5},{8,12},{9,11},{10,... | collective-permute-start | bytes 2555912 | tf_op jit(solution)/shard_map/ppermute | solution.py:369
  151.2 6.6 %copy-start.1 = (bf16[256,1664]{1,0:T(8,128)(2,1)S(1)}, bf16[256,1664]{1,0:T(8,128)(2,1)}, u32[]{:S(2)}) copy-start(bf16[256,1664]{1,0:T(8,128)(2,1)} %copy-done) | copy-start | bytes 2555908
  169.8 5.0 %collective-permute-start.20 = (bf16[1536,512]{1,0:T(8,128)(2,1)}, bf16[1536,512]{1,0:T(8,128)(2,1)S(1)}, u32[]{:S(2)}, u32[]{:S(2)}) collective-permute-start(bf16[1536,512]{1,0:T(8,128)(2,1)} %bitcast.36.mine_ref), channel_id=1, source_target_pairs={{0,1},{1,0},{2,3},{3,2},{4,5},{5,4},{6,7},{7,6},{8,9},{9,8},{10,11... | collective-permute-start | bytes 4718600 | tf_op jit(solution)/shard_map/ppermute | solution.py:369
  177.5 12.1 %collective-permute-start.22 = (bf16[256,1536]{1,0:T(8,128)(2,1)S(1)}, bf16[256,1536]{1,0:T(8,128)(2,1)S(1)}, u32[]{:S(2)}, u32[]{:S(2)}) collective-permute-start(bf16[256,1536]{1,0:T(8,128)(2,1)S(1)} %down.5.rest_0_), channel_id=1, source_target_pairs={{0,4},{1,3},{2,6},{3,1},{4,0},{5,7},{6,2},{7,5},{8,12},{9,11},{10,... | collective-permute-start | bytes 2359304 | tf_op jit(solution)/shard_map/ppermute | solution.py:369
  183.9 7.3 %copy-start.9 = (bf16[512,1024]{1,0:T(8,128)(2,1)S(1)}, bf16[512,1024]{1,0:T(8,128)(2,1)}, u32[]{:S(2)}) copy-start(bf16[512,1024]{1,0:T(8,128)(2,1)} %copy-done.8) | copy-start | bytes 3145732
  184.0 7.3 %copy-start.13 = (f32[512,128]{1,0:T(8,128)S(1)}, f32[512,128]{1,0:T(8,128)}, u32[]{:S(2)}) copy-start(f32[512,128]{1,0:T(8,128)} %copy-done.12) | copy-start | bytes 786436
  184.0 18.2 %collective-permute-start.21 = (bf16[256,1536]{1,0:T(8,128)(2,1)S(1)}, bf16[256,1536]{1,0:T(8,128)(2,1)S(1)}, u32[]{:S(2)}, u32[]{:S(2)}) collective-permute-start(bf16[256,1536]{1,0:T(8,128)(2,1)S(1)} %get-tuple-element.64), channel_id=1, source_target_pairs={{0,4},{1,3},{2,6},{3,1},{4,0},{5,7},{6,2},{7,5},{8,12},{9,11},{10,... | collective-permute-start | bytes 2359304 | tf_op jit(solution)/shard_map/ppermute | solution.py:369
  189.7 12.1 %collective-permute-start.23 = (bf16[128,1536]{1,0:T(8,128)(2,1)S(1)}, bf16[128,1536]{1,0:T(8,128)(2,1)S(1)}, u32[]{:S(2)}, u32[]{:S(2)}) collective-permute-start(bf16[128,1536]{1,0:T(8,128)(2,1)S(1)} %get-tuple-element.66.rest_0_), channel_id=1, source_target_pairs={{0,2},{1,5},{2,0},{3,7},{4,6},{5,1},{6,4},{7,3},{8,10},{9,13},{10,... | collective-permute-start | bytes 1179656 | tf_op jit(solution)/shard_map/ppermute | solution.py:369
  194.6 20.3 %collective-permute-start.25 = (bf16[256,1536]{1,0:T(8,128)(2,1)S(1)}, bf16[256,1536]{1,0:T(8,128)(2,1)S(1)}, u32[]{:S(2)}, u32[]{:S(2)}) collective-permute-start(bf16[256,1536]{1,0:T(8,128)(2,1)S(1)} %get-tuple-element.72), channel_id=1, source_target_pairs={{0,4},{1,3},{2,6},{3,1},{4,0},{5,7},{6,2},{7,5},{8,12},{9,11},{10,... | collective-permute-start | bytes 2359304 | tf_op jit(solution)/shard_map/ppermute | solution.py:369
  202.4 12.1 %collective-permute-start.26 = (bf16[128,1536]{1,0:T(8,128)(2,1)S(1)}, bf16[128,1536]{1,0:T(8,128)(2,1)S(1)}, u32[]{:S(2)}, u32[]{:S(2)}) collective-permute-start(bf16[128,1536]{1,0:T(8,128)(2,1)S(1)} %get-tuple-element.69.rest_0_), channel_id=1, source_target_pairs={{0,2},{1,5},{2,0},{3,7},{4,6},{5,1},{6,4},{7,3},{8,10},{9,13},{10,... | collective-permute-start | bytes 1179656 | tf_op jit(solution)/shard_map/ppermute | solution.py:369
  203.9 10.6 %collective-permute-start.27 = (bf16[128,1536]{1,0:T(8,128)(2,1)S(1)}, bf16[128,1536]{1,0:T(8,128)(2,1)S(1)}, u32[]{:S(2)}, u32[]{:S(2)}) collective-permute-start(bf16[128,1536]{1,0:T(8,128)(2,1)S(1)} %close.3.rest_0_), channel_id=1, source_target_pairs={{0,8},{8,0},{16,24},{24,16},{1,9},{9,1},{17,25},{25,17},{2,10},{10... | collective-permute-start | bytes 1179656 | tf_op jit(solution)/shard_map/ppermute | solution.py:369
  207.2 20.3 %collective-permute-start.24 = (bf16[256,1536]{1,0:T(8,128)(2,1)S(1)}, bf16[256,1536]{1,0:T(8,128)(2,1)S(1)}, u32[]{:S(2)}, u32[]{:S(2)}) collective-permute-start(bf16[256,1536]{1,0:T(8,128)(2,1)S(1)} %get-tuple-element.71), channel_id=1, source_target_pairs={{0,4},{1,3},{2,6},{3,1},{4,0},{5,7},{6,2},{7,5},{8,12},{9,11},{10,... | collective-permute-start | bytes 2359304 | tf_op jit(solution)/shard_map/ppermute | solution.py:369
  215.0 12.0 %collective-permute-start.28 = (bf16[128,1536]{1,0:T(8,128)(2,1)S(1)}, bf16[128,1536]{1,0:T(8,128)(2,1)S(1)}, u32[]{:S(2)}, u32[]{:S(2)}) collective-permute-start(bf16[128,1536]{1,0:T(8,128)(2,1)S(1)} %get-tuple-element.75.rest_1_), channel_id=1, source_target_pairs={{0,2},{1,5},{2,0},{3,7},{4,6},{5,1},{6,4},{7,3},{8,10},{9,13},{10,... | collective-permute-start | bytes 1179656 | tf_op jit(solution)/shard_map/ppermute | solution.py:369
  216.6 12.6 %collective-permute-start.31 = (bf16[128,1536]{1,0:T(8,128)(2,1)S(1)}, bf16[128,1536]{1,0:T(8,128)(2,1)S(1)}, u32[]{:S(2)}, u32[]{:S(2)}) collective-permute-start(bf16[128,1536]{1,0:T(8,128)(2,1)S(1)} %close.4.rest_0_), channel_id=1, source_target_pairs={{0,16},{1,9},{2,18},{3,11},{4,20},{5,13},{6,22},{7,15},{8,24},{9,1... | collective-permute-start | bytes 1179656 | tf_op jit(solution)/shard_map/ppermute | solution.py:472
  227.2 13.9 %copy-start.21 = (f32[128,1536]{1,0:T(8,128)S(1)}, f32[128,1536]{1,0:T(8,128)}, u32[]{:S(2)}) copy-start(f32[128,1536]{1,0:T(8,128)} %get-tuple-element.49.stream_ref) | copy-start | bytes 2359300
  227.6 7.8 %collective-permute-start.29 = (bf16[128,1536]{1,0:T(8,128)(2,1)S(1)}, bf16[128,1536]{1,0:T(8,128)(2,1)S(1)}, u32[]{:S(2)}, u32[]{:S(2)}) collective-permute-start(bf16[128,1536]{1,0:T(8,128)(2,1)S(1)} %get-tuple-element.77), channel_id=1, source_target_pairs={{0,2},{1,5},{2,0},{3,7},{4,6},{5,1},{6,4},{7,3},{8,10},{9,13},{10,... | collective-permute-start | bytes 1179656 | tf_op jit(solution)/shard_map/ppermute | solution.py:369
  229.2 11.9 %collective-permute-start.30 = (bf16[128,1536]{1,0:T(8,128)(2,1)S(1)}, bf16[128,1536]{1,0:T(8,128)(2,1)S(1)}, u32[]{:S(2)}, u32[]{:S(2)}) collective-permute-start(bf16[128,1536]{1,0:T(8,128)(2,1)S(1)} %close.5.rest_0_), channel_id=1, source_target_pairs={{0,8},{1,17},{2,10},{3,19},{4,12},{5,21},{6,14},{7,23},{8,0},{9,25... | collective-permute-start | bytes 1179656 | tf_op jit(solution)/shard_map/ppermute | solution.py:472
  (20 other events, 25.8 us)

commit v8 on v7

--- a/solution.py
+++ b/solution.py
@@ -626,7 +626,7 @@
     swapped = columns == 8 and planes == 4 and gate_up.shape[1] == planes
     if swapped:
         out_parts = start_out(out_weight)
-        pair = pack_experts(gate_up, 4)
+        pair = pack_experts(gate_up, 3)
         cache_len, anchor = after((cache_len, anchor), pair)
     matches = (anchor[:, None] == jnp.arange(columns, dtype=jnp.int32)[None, :]).astype(jnp.int32)
     earlier = jnp.sum((jnp.cumsum(matches, axis=0) - 1) * matches, axis=1)

time: 243 us -> 243 us (level)
  transfers between devices with their start and end apart: 34 -> 34, of which waited for: 17 -> 17; matrix products, arithmetic and copies ran while one was open for 3% -> 3% of each run, Pallas kernels for 27% -> 28%
where the time goes in v8:
time: 243 us; the launch traced here: 242 us
  waiting for transfers between devices  76.8 us (32%)
  Pallas kernels  70.4 us (29%)
  starting transfers between devices  47 us (19%)
  blocking collectives  24 us (10%)
  local copies, waits for them, and re-layouts  20.6 us (8%)
    ppermute x27, waiting for transfers between devices, swap(): lax.ppermute(x, axis, [(i, how(i)) for i in range(lax.axis_size(axis))])  46.4 us
    ppermute x27, starting transfers between devices, swap(): lax.ppermute(x, axis, [(i, how(i)) for i in range(lax.axis_size(axis))])  27.4 us
    ppermute x5, waiting for transfers between devices, across(): return lax.ppermute(x, ('gx', 'gy'), pairs)  26.2 us
    pallas_call x5, Pallas kernels, make_hidden(): pl.pallas_call(functools.partial(hidden_kernel, len(pieces)), in_specs=[s...  24.5 us
    unnamed x70, local copies, waits for them, and re-layouts  15.7 us
    pallas_call x5, Pallas kernels, make_down(): pl.pallas_call(functools.partial(down_kernel, count), in_specs=[vmem()] *...  15.1 us
    all_to_all x2, starting transfers between devices, exchange(): lax.all_to_all(packed, 'gx', split_axis=0, concat_axis=0, tiled=True)  13.4 us
    all_gather x1, blocking collectives, body(): back = lax.all_gather(reply, 'gy', axis=0, tiled=True)  12.3 us
  transfers between devices with their start and end apart: 34, of which 17 were waited for; matrix products, arithmetic and copies ran while one was open for 3% of the time, Pallas kernels for 28%

profile of v8, /device:TPU:0, one launch (start us, length us, event | category | flops | bytes accessed | tf_op | source)
XLA Modules:
  0.0 242.1 jit_solution(5964753593375822563)
XLA Ops:
  0.6 1.6 constant_dynamic-slice_fusion
  2.2 5.0 %collective-permute-start.2 = (bf16[48,1536]{1,0:T(8,128)(2,1)}, bf16[48,1536]{1,0:T(8,128)(2,1)S(1)}, u32[]{:S(2)}, u32[]{:S(2)}) collective-permute-start(bf16[48,1536]{1,0:T(8,128)(2,1)} %constant_dynamic-slice_fusion), channel_id=1, source_target_pairs={{0,24},{8,16},{16,8},{24,0},{1,25},{9,17},{17,9},{25,1},{2,26},{10... | collective-permute-start | bytes 442376 | tf_op jit(solution)/shard_map/ppermute | solution.py:369
  7.8 6.4 %pack.2 = bf16[4,384,1024]{2,1,0:T(8,128)(2,1)} custom-call(bf16[384,4,1024]{2,1,0:T(4,128)(2,1)} %block_ref.2), custom_call_target="tpu_custom_call" | custom-call | flops 5000000000 | bytes 100000 | tf_op jit(solution)/shard_map/pack/pallas_call | solution.py:355
  14.2 5.2 %all-to-all-start = ((bf16[4,384,1024]{2,1,0:T(8,128)(2,1)}), bf16[4,384,1024]{2,1,0:T(8,128)(2,1)S(1)}, u32[]{:S(2)}, u32[]{:S(2)}) async-start(bf16[4,384,1024]{2,1,0:T(8,128)(2,1)} %pack.2), calls=%async_computation | async-start | bytes 6291456 | tf_op jit(solution)/shard_map/all_to_all | solution.py:385
  21.7 1.7 stack.158.refs_0_.rest_1_
  23.4 1.5 collective-permute-start.3
  25.0 11.7 %all_gather.6.refs_2_.asks_ref = bf16[64,1664]{1,0:T(8,128)(2,1)S(1)} all-gather(bf16[8,1664]{1,0:T(8,128)(2,1)S(1)} %pad_maximum_fusion), channel_id=1, replica_groups=mesh['gx'=4,'gy'=8] {'gy'}, dimensions={0}, use_global_device_ids=true | all-gather | bytes 239616 | tf_op jit(solution)/shard_map/all_gather | solution.py:638
  39.9 1.5 collective-permute-start.4
  41.4 4.0 %pack.3 = bf16[4,384,512]{2,1,0:T(8,128)(2,1)} custom-call(bf16[384,4,512]{2,1,0:T(4,128)(2,1)} %block_ref.3, bf16[288,1536]{1,0:T(8,128)(2,1)} %copy-done.17), custom_call_target="tpu_custom_call" | custom-call | flops 5000000000 | bytes 100000 | tf_op jit(solution)/shard_map/pack/pallas_call | solution.py:355
  45.3 7.0 %attend.1 = (f32[8,1664]{1,0:T(8,128)}, f32[16,1664]{1,0:T(8,128)}) custom-call(s32[1]{0:T(128)} %bitcast.25.me_ref, bf16[8,1664]{1,0:T(8,128)(2,1)} %fusion.1.own_ref, bf16[64,1664]{1,0:T(8,128)(2,1)} %copy-done.18, s32[24,32]{1,0:T(8,128)} %pad_add_fusion.table_ref, bf16[2048,1024]{1,0:T(8,128)(2,1)} %bitcast.50, bf16[2048,1024]{1,0:T(8,128)(2,1)} %bitcast.51), custom_call_target="tpu_custom_call" | custom-call | flops 7000000000 | bytes 100000 | tf_op jit(solution)/shard_map/attend/pallas_call | solution.py:143
  57.5 12.3 %all_gather.7.back_ref = f32[128,1664]{1,0:T(8,128)} all-gather(f32[16,1664]{1,0:T(8,128)} %get-tuple-element.44), channel_id=1, replica_groups=mesh['gx'=4,'gy'=8] {'gy'}, dimensions={0}, use_global_device_ids=true | all-gather | bytes 958464 | tf_op jit(solution)/shard_map/all_gather | solution.py:663
  69.8 6.3 %stream.1 = (bf16[16,1536]{1,0:T(8,128)(2,1)}, f32[128,1536]{1,0:T(8,128)}, bf16[128,1664]{1,0:T(8,128)(2,1)}) custom-call(s32[8]{0:T(128)} %get-tuple-element.87.chosen_ref, s32[25]{0:T(128)} %stack.147.at_ref, bf16[16,1536]{1,0:T(8,128)(2,1)} %query_ref.1, bf16[16,1024]{1,0:T(8,128)(2,1)} %fresh_ref.1, f32[8,1664]{1,0:T(8,128)} %get-tuple-element.43.here_ref, ...), custom_call_target="tpu_custom_call" | custom-call | flops 8000000000 | bytes 100000 | tf_op jit(solution)/shard_map/stream/pallas_call | solution.py:257
  76.0 1.6 collective-permute-start.8
  77.6 2.9 %collective-permute-start.12 = (bf16[128,1664]{1,0:T(8,128)(2,1)}, bf16[128,1664]{1,0:T(8,128)(2,1)S(1)}, u32[]{:S(2)}, u32[]{:S(2)}) collective-permute-start(bf16[128,1664]{1,0:T(8,128)(2,1)} %get-tuple-element.50.refs_0_), channel_id=1, source_target_pairs={{0,16},{1,9},{2,18},{3,11},{4,20},{5,13},{6,22},{7,15},{8,24},{9,1... | collective-permute-start | bytes 1277960 | tf_op jit(solution)/shard_map/ppermute | solution.py:472
  80.5 1.5 collective-permute-start.10
  82.0 2.4 collective-permute-done.8.refs_1_
  85.5 1.6 collective-permute-start.9
  87.1 20.5 %collective-permute-done.12.refs_0_ = bf16[128,1664]{1,0:T(8,128)(2,1)S(1)} collective-permute-done((bf16[128,1664]{1,0:T(8,128)(2,1)}, bf16[128,1664]{1,0:T(8,128)(2,1)S(1)}, u32[]{:S(2)}, u32[]{:S(2)}) %collective-permute-start.12) | collective-permute-done | bytes 426016 | tf_op jit(solution)/shard_map/ppermute | solution.py:472
  107.6 1.5 collective-permute-start.13
  109.6 1.5 collective-permute-start.14
  111.1 4.6 %collective-permute-done.13.refs_1_ = bf16[128,1664]{1,0:T(8,128)(2,1)S(1)} collective-permute-done((bf16[128,1664]{1,0:T(8,128)(2,1)S(1)}, bf16[128,1664]{1,0:T(8,128)(2,1)S(1)}, u32[]{:S(2)}, u32[]{:S(2)}) %collective-permute-start.13) | collective-permute-done | bytes 426016 | tf_op jit(solution)/shard_map/ppermute | solution.py:369
  116.7 3.6 %collective-permute-done.11.refs_1_ = bf16[128,1664]{1,0:T(8,128)(2,1)S(1)} collective-permute-done((bf16[128,1664]{1,0:T(8,128)(2,1)S(1)}, bf16[128,1664]{1,0:T(8,128)(2,1)S(1)}, u32[]{:S(2)}, u32[]{:S(2)}) %collective-permute-start.11) | collective-permute-done | bytes 426016 | tf_op jit(solution)/shard_map/ppermute | solution.py:369
  123.2 8.1 %all-to-all-start.1 = ((bf16[4,384,512]{2,1,0:T(8,128)(2,1)}), bf16[4,384,512]{2,1,0:T(8,128)(2,1)}, u32[]{:S(2)}, u32[]{:S(2)}) async-start(bf16[4,384,512]{2,1,0:T(8,128)(2,1)} %pack.3), calls=%async_computation.1 | async-start | bytes 3145728 | tf_op jit(solution)/shard_map/all_to_all | solution.py:385
  131.3 1.5 collective-permute-start.18
  133.4 1.5 collective-permute-start.16
  137.2 5.5 %hidden.5 = (bf16[512,1024]{1,0:T(8,128)(2,1)S(1)}, f32[512,128]{1,0:T(8,128)S(1)}) custom-call(s32[2]{0:T(128)S(1)} %pad_add_fusion.1.place_ref, bf16[256,1664]{1,0:T(8,128)(2,1)S(1)} %copy-done.3, bf16[256,1664]{1,0:T(8,128)(2,1)S(1)} %copy-done.20, bf16[1536,1024]{1,0:T(8,128)(2,1)S(1)} %bitcast.45, bf16[1536,1024]{1,0:T(8,128)(2,1)} %collective-permute-done.15.refs_3_.refs_2_), custom_call_target="tpu_custom_call" | custom-call | flops 1000000 | bytes 100000 | tf_op jit(solution)/shard_map/hidden/pallas_call | solution.py:300
  144.3 2.0 stack.163.refs_0_
  146.3 4.0 %hidden.6 = (bf16[256,1024]{1,0:T(8,128)(2,1)S(1)}, f32[256,128]{1,0:T(8,128)S(1)}) custom-call(s32[2]{0:T(128)S(1)} %pad_add_fusion.1.place_ref, bf16[256,1664]{1,0:T(8,128)(2,1)} %stack.163.refs_0_, bf16[1536,1024]{1,0:T(8,128)(2,1)S(1)} %bitcast.46, bf16[1536,1024]{1,0:T(8,128)(2,1)} %collective-permute-done.15.refs_3_.refs_2_, ...), custom_call_target="tpu_custom_call" | custom-call | flops 1000000 | bytes 100000 | tf_op jit(solution)/shard_map/hidden/pallas_call | solution.py:300
  151.2 5.5 %hidden.7 = (bf16[512,1024]{1,0:T(8,128)(2,1)S(1)}, f32[512,128]{1,0:T(8,128)S(1)}) custom-call(s32[2]{0:T(128)S(1)} %pad_add_fusion.1.place_ref, bf16[256,1664]{1,0:T(8,128)(2,1)S(1)} %copy-done.5, bf16[256,1664]{1,0:T(8,128)(2,1)S(1)} %collective-permute-done.17.refs_1_, bf16[1536,1024]{1,0:T(8,128)(2,1)S(1)} %bitcast.47, ...), custom_call_target="tpu_custom_call" | custom-call | flops 1000000 | bytes 100000 | tf_op jit(solution)/shard_map/hidden/pallas_call | solution.py:300
  157.7 5.4 %hidden.8 = (bf16[512,1024]{1,0:T(8,128)(2,1)S(1)}, f32[512,128]{1,0:T(8,128)S(1)}) custom-call(s32[2]{0:T(128)S(1)} %pad_add_fusion.1.place_ref, bf16[256,1664]{1,0:T(8,128)(2,1)S(1)} %copy-done.1, bf16[256,1664]{1,0:T(8,128)(2,1)S(1)} %collective-permute-done.16.refs_1_, bf16[1536,1024]{1,0:T(8,128)(2,1)S(1)} %bitcast.48, ...), custom_call_target="tpu_custom_call" | custom-call | flops 1000000 | bytes 100000 | tf_op jit(solution)/shard_map/hidden/pallas_call | solution.py:300
  165.6 4.2 %all-to-all-done.1 = bf16[4,384,512]{2,1,0:T(8,128)(2,1)} async-done(((bf16[4,384,512]{2,1,0:T(8,128)(2,1)}), bf16[4,384,512]{2,1,0:T(8,128)(2,1)}, u32[]{:S(2)}, u32[]{:S(2)}) %all-to-all-start.1) | async-done | bytes 1572896 | tf_op jit(solution)/shard_map/all_to_all | solution.py:385
  170.7 4.0 %hidden.9 = (bf16[256,1024]{1,0:T(8,128)(2,1)S(1)}, f32[256,128]{1,0:T(8,128)S(1)}) custom-call(s32[2]{0:T(128)S(1)} %pad_add_fusion.1.place_ref, bf16[256,1664]{1,0:T(8,128)(2,1)} %collective-permute-done.19.refs_0_, bf16[1536,1024]{1,0:T(8,128)(2,1)S(1)} %bitcast.49, bf16[1536,1024]{1,0:T(8,128)(2,1)} %collective-permute-done.15.refs_3_.refs_2_, ...), custom_call_target="tpu_custom_call" | custom-call | flops 1000000 | bytes 100000 | tf_op jit(solution)/shard_map/hidden/pallas_call | solution.py:300
  174.8 2.7 %down.5.rest_0_ = bf16[256,1536]{1,0:T(8,128)(2,1)S(1)} custom-call(bf16[256,1024]{1,0:T(8,128)(2,1)S(1)} %get-tuple-element.61.hidden_ref, f32[256,128]{1,0:T(8,128)S(1)} %get-tuple-element.62.share_ref, bf16[1536,512]{1,0:T(8,128)(2,1)} %bitcast.36.mine_ref, bf16[1536,512]{1,0:T(8,128)(2,1)S(1)} %collective-permute-done.20.other_ref), custom_call_target="tpu_custom_call" | custom-call | flops 1000000 | bytes 100000 | tf_op jit(solution)/shard_map/down/pallas_call | solution.py:333
  178.1 2.5 %down.6.rest_0_.keep_ref = bf16[256,1536]{1,0:T(8,128)(2,1)S(1)} custom-call(bf16[256,1024]{1,0:T(8,128)(2,1)S(1)} %copy-done.23, f32[256,128]{1,0:T(8,128)S(1)} %get-tuple-element.55.refs_4_.share_ref, bf16[1536,512]{1,0:T(8,128)(2,1)} %bitcast.36.mine_ref, bf16[1536,512]{1,0:T(8,128)(2,1)S(1)} %collective-permute-done.20.other_ref, ...), custom_call_target="tpu_custom_call" | custom-call | flops 1000000 | bytes 100000 | tf_op jit(solution)/shard_map/down/pallas_call | solution.py:333
  180.6 3.3 %down.7 = (bf16[256,1536]{1,0:T(8,128)(2,1)S(1)}, bf16[256,1536]{1,0:T(8,128)(2,1)S(1)}) custom-call(bf16[512,1024]{1,0:T(8,128)(2,1)S(1)} %copy-done.11, f32[512,128]{1,0:T(8,128)S(1)} %copy-done.16, bf16[1536,512]{1,0:T(8,128)(2,1)} %bitcast.36.mine_ref, bf16[1536,512]{1,0:T(8,128)(2,1)S(1)} %collective-permute-done.20.other_ref, ...), custom_call_target="tpu_custom_call" | custom-call | flops 1000000 | bytes 100000 | tf_op jit(solution)/shard_map/down/pallas_call | solution.py:333
  184.0 1.6 collective-permute-start.21
  185.5 4.0 %collective-permute-done.22.came_ref = bf16[256,1536]{1,0:T(8,128)(2,1)S(1)} collective-permute-done((bf16[256,1536]{1,0:T(8,128)(2,1)S(1)}, bf16[256,1536]{1,0:T(8,128)(2,1)S(1)}, u32[]{:S(2)}, u32[]{:S(2)}) %collective-permute-start.22) | collective-permute-done | bytes 786464 | tf_op jit(solution)/shard_map/ppermute | solution.py:369
  189.7 1.6 collective-permute-start.23
  191.3 3.3 %down.8 = (bf16[256,1536]{1,0:T(8,128)(2,1)S(1)}, bf16[256,1536]{1,0:T(8,128)(2,1)S(1)}) custom-call(bf16[512,1024]{1,0:T(8,128)(2,1)S(1)} %copy-done.9, f32[512,128]{1,0:T(8,128)S(1)} %copy-done.13, bf16[1536,512]{1,0:T(8,128)(2,1)} %bitcast.36.mine_ref, bf16[1536,512]{1,0:T(8,128)(2,1)S(1)} %collective-permute-done.20.other_ref, ...), custom_call_target="tpu_custom_call" | custom-call | flops 1000000 | bytes 100000 | tf_op jit(solution)/shard_map/down/pallas_call | solution.py:333
  195.1 6.7 %collective-permute-done.23.came_ref = bf16[128,1536]{1,0:T(8,128)(2,1)S(1)} collective-permute-done((bf16[128,1536]{1,0:T(8,128)(2,1)S(1)}, bf16[128,1536]{1,0:T(8,128)(2,1)S(1)}, u32[]{:S(2)}, u32[]{:S(2)}) %collective-permute-start.23) | collective-permute-done | bytes 393248 | tf_op jit(solution)/shard_map/ppermute | solution.py:369
  202.4 1.6 collective-permute-start.26
  203.9 3.3 %down.9 = (bf16[256,1536]{1,0:T(8,128)(2,1)S(1)}, bf16[256,1536]{1,0:T(8,128)(2,1)S(1)}) custom-call(bf16[512,1024]{1,0:T(8,128)(2,1)S(1)} %copy-done.7, f32[512,128]{1,0:T(8,128)S(1)} %get-tuple-element.53.refs_2_.refs_3_.share_ref, bf16[1536,512]{1,0:T(8,128)(2,1)} %bitcast.36.mine_ref, bf16[1536,512]{1,0:T(8,128)(2,1)S(1)} %collective-permute-done.20.other_ref, ...), custom_call_target="tpu_custom_call" | custom-call | flops 1000000 | bytes 100000 | tf_op jit(solution)/shard_map/down/pallas_call | solution.py:333
  207.8 6.7 %collective-permute-done.26.came_ref = bf16[128,1536]{1,0:T(8,128)(2,1)S(1)} collective-permute-done((bf16[128,1536]{1,0:T(8,128)(2,1)S(1)}, bf16[128,1536]{1,0:T(8,128)(2,1)S(1)}, u32[]{:S(2)}, u32[]{:S(2)}) %collective-permute-start.26) | collective-permute-done | bytes 393248 | tf_op jit(solution)/shard_map/ppermute | solution.py:369
  215.0 1.6 collective-permute-start.28
  216.9 10.1 %collective-permute-done.28.came_ref = bf16[128,1536]{1,0:T(8,128)(2,1)S(1)} collective-permute-done((bf16[128,1536]{1,0:T(8,128)(2,1)S(1)}, bf16[128,1536]{1,0:T(8,128)(2,1)S(1)}, u32[]{:S(2)}, u32[]{:S(2)}) %collective-permute-start.28) | collective-permute-done | bytes 393248 | tf_op jit(solution)/shard_map/ppermute | solution.py:369
  227.6 1.6 collective-permute-start.29
  229.2 6.3 %collective-permute-done.29.rest_0_ = bf16[128,1536]{1,0:T(8,128)(2,1)S(1)} collective-permute-done((bf16[128,1536]{1,0:T(8,128)(2,1)S(1)}, bf16[128,1536]{1,0:T(8,128)(2,1)S(1)}, u32[]{:S(2)}, u32[]{:S(2)}) %collective-permute-start.29) | collective-permute-done | bytes 393248 | tf_op jit(solution)/shard_map/ppermute | solution.py:369
  235.5 5.6 %collective-permute-done.30.rest_1_ = bf16[128,1536]{1,0:T(8,128)(2,1)S(1)} collective-permute-done((bf16[128,1536]{1,0:T(8,128)(2,1)S(1)}, bf16[128,1536]{1,0:T(8,128)(2,1)S(1)}, u32[]{:S(2)}, u32[]{:S(2)}) %collective-permute-start.30) | collective-permute-done | bytes 393248 | tf_op jit(solution)/shard_map/ppermute | solution.py:472
  (142 shorter events, 31.3 us)
Async XLA Ops:
  2.2 19.4 %collective-permute-start.2 = (bf16[48,1536]{1,0:T(8,128)(2,1)}, bf16[48,1536]{1,0:T(8,128)(2,1)S(1)}, u32[]{:S(2)}, u32[]{:S(2)}) collective-permute-start(bf16[48,1536]{1,0:T(8,128)(2,1)} %constant_dynamic-slice_fusion), channel_id=1, source_target_pairs={{0,24},{8,16},{16,8},{24,0},{1,25},{9,17},{17,9},{25,1},{2,26},{10... | collective-permute-start | bytes 442376 | tf_op jit(solution)/shard_map/ppermute | solution.py:369
  7.3 14.4 %collective-permute-start.1 = (bf16[48,1536]{1,0:T(8,128)(2,1)}, bf16[48,1536]{1,0:T(8,128)(2,1)S(1)}, u32[]{:S(2)}, u32[]{:S(2)}) collective-permute-start(bf16[48,1536]{1,0:T(8,128)(2,1)} %constant_dynamic-slice_fusion), channel_id=1, source_target_pairs={{0,16},{8,24},{16,0},{24,8},{1,17},{9,25},{17,1},{25,9},{2,18},{10... | collective-permute-start | bytes 442376 | tf_op jit(solution)/shard_map/ppermute | solution.py:369
  7.3 14.4 %collective-permute-start = (bf16[48,1536]{1,0:T(8,128)(2,1)}, bf16[48,1536]{1,0:T(8,128)(2,1)}, u32[]{:S(2)}, u32[]{:S(2)}) collective-permute-start(bf16[48,1536]{1,0:T(8,128)(2,1)} %constant_dynamic-slice_fusion), channel_id=1, source_target_pairs={{0,8},{8,0},{16,24},{24,16},{1,9},{9,1},{17,25},{25,17},{2,10},{10... | collective-permute-start | bytes 442376 | tf_op jit(solution)/shard_map/ppermute | solution.py:369
  14.2 6.0 %copy-start.33 = (s32[16]{0:T(128)S(1)}, s32[16]{0:T(128)}, u32[]{:S(2)}) copy-start(s32[16]{0:T(128)} %param.18) | copy-start | bytes 196
  14.2 6.3 %copy-start.29 = (s32[8]{0:T(128)S(1)}, s32[8]{0:T(128)}, u32[]{:S(2)}) copy-start(s32[8]{0:T(128)} %param.20) | copy-start | bytes 100
  14.2 22.6 %copy-start.28 = (s32[16,32]{1,0:T(8,128)S(1)}, s32[16,32]{1,0:T(8,128)}, u32[]{:S(2)}) copy-start(s32[16,32]{1,0:T(8,128)} %param.21) | copy-start | bytes 6148
  14.2 22.6 %copy-start.32 = (s32[8,32]{1,0:T(8,128)S(1)}, s32[8,32]{1,0:T(8,128)}, u32[]{:S(2)}) copy-start(s32[8,32]{1,0:T(8,128)} %param.19) | copy-start | bytes 3076
  14.2 109.0 %all-to-all-start = ((bf16[4,384,1024]{2,1,0:T(8,128)(2,1)}), bf16[4,384,1024]{2,1,0:T(8,128)(2,1)S(1)}, u32[]{:S(2)}, u32[]{:S(2)}) async-start(bf16[4,384,1024]{2,1,0:T(8,128)(2,1)} %pack.2), calls=%async_computation | async-start | bytes 6291456 | tf_op jit(solution)/shard_map/all_to_all | solution.py:385
  23.4 14.6 %collective-permute-start.3 = (bf16[144,1536]{1,0:T(8,128)(2,1)}, bf16[144,1536]{1,0:T(8,128)(2,1)}, u32[]{:S(2)}, u32[]{:S(2)}) collective-permute-start(bf16[144,1536]{1,0:T(8,128)(2,1)} %stack.158.refs_0_.rest_1_), channel_id=1, source_target_pairs={{0,2},{1,5},{2,0},{3,7},{4,6},{5,1},{6,4},{7,3},{8,10},{9,13},{10,... | collective-permute-start | bytes 1327112 | tf_op jit(solution)/shard_map/ppermute | solution.py:369
  39.9 13.1 %collective-permute-start.4 = (bf16[288,1536]{1,0:T(8,128)(2,1)S(1)}, bf16[288,1536]{1,0:T(8,128)(2,1)}, u32[]{:S(2)}, u32[]{:S(2)}) collective-permute-start(bf16[288,1536]{1,0:T(8,128)(2,1)S(1)} %stack.159.rest_0_), channel_id=1, source_target_pairs={{0,4},{1,3},{2,6},{3,1},{4,0},{5,7},{6,2},{7,5},{8,12},{9,11},{10,... | collective-permute-start | bytes 2654216 | tf_op jit(solution)/shard_map/ppermute | solution.py:369
  45.3 8.2 %copy-start.31 = (bf16[1536]{0:T(1024)(128)(2,1)S(1)}, bf16[1536]{0:T(1024)(128)(2,1)}, u32[]{:S(2)}) copy-start(bf16[1536]{0:T(1024)(128)(2,1)} %param.25) | copy-start | bytes 9220
  45.3 8.8 %copy-start.30 = (s32[128,8]{0,1:T(8,128)S(1)}, s32[128,8]{0,1:T(8,128)}, u32[]{:S(2)}) copy-start(s32[128,8]{0,1:T(8,128)} %param.27) | copy-start | bytes 12292
  53.0 16.7 %collective-permute-start.7 = (bf16[288,1536]{1,0:T(8,128)(2,1)}, bf16[288,1536]{1,0:T(8,128)(2,1)}, u32[]{:S(2)}, u32[]{:S(2)}) collective-permute-start(bf16[288,1536]{1,0:T(8,128)(2,1)} %collective-permute-done.4.rest_3_), channel_id=1, source_target_pairs={{0,1},{1,0},{2,3},{3,2},{4,5},{5,4},{6,7},{7,6},{8,9},{9,8},{10,11... | collective-permute-start | bytes 2654216 | tf_op jit(solution)/shard_map/ppermute | solution.py:369
  53.0 16.7 %collective-permute-start.5 = (bf16[144,1536]{1,0:T(8,128)(2,1)}, bf16[144,1536]{1,0:T(8,128)(2,1)}, u32[]{:S(2)}, u32[]{:S(2)}) collective-permute-start(bf16[144,1536]{1,0:T(8,128)(2,1)} %stack.158.refs_0_.rest_1_), channel_id=1, source_target_pairs={{0,1},{1,0},{2,3},{3,2},{4,5},{5,4},{6,7},{7,6},{8,9},{9,8},{10,11... | collective-permute-start | bytes 1327112 | tf_op jit(solution)/shard_map/ppermute | solution.py:369
  53.5 16.2 %collective-permute-start.6 = (bf16[144,1536]{1,0:T(8,128)(2,1)}, bf16[144,1536]{1,0:T(8,128)(2,1)}, u32[]{:S(2)}, u32[]{:S(2)}) collective-permute-start(bf16[144,1536]{1,0:T(8,128)(2,1)} %collective-permute-done.3.refs_1_.rest_2_), channel_id=1, source_target_pairs={{0,1},{1,0},{2,3},{3,2},{4,5},{5,4},{6,7},{7,6},{8,9},{9,8},{10,11... | collective-permute-start | bytes 1327112 | tf_op jit(solution)/shard_map/ppermute | solution.py:369
  76.0 8.4 %collective-permute-start.8 = (bf16[128,1664]{1,0:T(8,128)(2,1)}, bf16[128,1664]{1,0:T(8,128)(2,1)S(1)}, u32[]{:S(2)}, u32[]{:S(2)}) collective-permute-start(bf16[128,1664]{1,0:T(8,128)(2,1)} %get-tuple-element.50.refs_0_), channel_id=1, source_target_pairs={{0,2},{1,5},{2,0},{3,7},{4,6},{5,1},{6,4},{7,3},{8,10},{9,13},{10,... | collective-permute-start | bytes 1277960 | tf_op jit(solution)/shard_map/ppermute | solution.py:369
  77.6 29.9 %collective-permute-start.12 = (bf16[128,1664]{1,0:T(8,128)(2,1)}, bf16[128,1664]{1,0:T(8,128)(2,1)S(1)}, u32[]{:S(2)}, u32[]{:S(2)}) collective-permute-start(bf16[128,1664]{1,0:T(8,128)(2,1)} %get-tuple-element.50.refs_0_), channel_id=1, source_target_pairs={{0,16},{1,9},{2,18},{3,11},{4,20},{5,13},{6,22},{7,15},{8,24},{9,1... | collective-permute-start | bytes 1277960 | tf_op jit(solution)/shard_map/ppermute | solution.py:472
  80.5 28.5 %collective-permute-start.10 = (bf16[128,1664]{1,0:T(8,128)(2,1)}, bf16[128,1664]{1,0:T(8,128)(2,1)S(1)}, u32[]{:S(2)}, u32[]{:S(2)}) collective-permute-start(bf16[128,1664]{1,0:T(8,128)(2,1)} %get-tuple-element.50.refs_0_), channel_id=1, source_target_pairs={{0,8},{1,17},{2,10},{3,19},{4,12},{5,21},{6,14},{7,23},{8,0},{9,25... | collective-permute-start | bytes 1277960 | tf_op jit(solution)/shard_map/ppermute | solution.py:472
  85.5 24.1 %copy-start.27 = (bf16[128,1664]{1,0:T(8,128)(2,1)S(1)}, bf16[128,1664]{1,0:T(8,128)(2,1)}, u32[]{:S(2)}) copy-start(bf16[128,1664]{1,0:T(8,128)(2,1)} %get-tuple-element.50.refs_0_) | copy-start | bytes 1277956
  85.5 34.8 %copy-start.2 = (bf16[256,1664]{1,0:T(8,128)(2,1)}, bf16[256,1664]{1,0:T(8,128)(2,1)S(1)}, u32[]{:S(2)}) copy-start(bf16[256,1664]{1,0:T(8,128)(2,1)S(1)} %stack.160.refs_0_) | copy-start | bytes 2555908
  85.5 36.7 %collective-permute-start.9 = (bf16[256,1664]{1,0:T(8,128)(2,1)S(1)}, bf16[256,1664]{1,0:T(8,128)(2,1)S(1)}, u32[]{:S(2)}, u32[]{:S(2)}) collective-permute-start(bf16[256,1664]{1,0:T(8,128)(2,1)S(1)} %stack.160.refs_0_), channel_id=1, source_target_pairs={{0,4},{1,3},{2,6},{3,1},{4,0},{5,7},{6,2},{7,5},{8,12},{9,11},{10,... | collective-permute-start | bytes 2555912 | tf_op jit(solution)/shard_map/ppermute | solution.py:369
  107.6 8.1 %collective-permute-start.13 = (bf16[128,1664]{1,0:T(8,128)(2,1)S(1)}, bf16[128,1664]{1,0:T(8,128)(2,1)S(1)}, u32[]{:S(2)}, u32[]{:S(2)}) collective-permute-start(bf16[128,1664]{1,0:T(8,128)(2,1)S(1)} %collective-permute-done.12.refs_0_), channel_id=1, source_target_pairs={{0,2},{1,5},{2,0},{3,7},{4,6},{5,1},{6,4},{7,3},{8,10},{9,13},{10,... | collective-permute-start | bytes 1277960 | tf_op jit(solution)/shard_map/ppermute | solution.py:369
  109.1 11.2 %collective-permute-start.11 = (bf16[128,1664]{1,0:T(8,128)(2,1)S(1)}, bf16[128,1664]{1,0:T(8,128)(2,1)S(1)}, u32[]{:S(2)}, u32[]{:S(2)}) collective-permute-start(bf16[128,1664]{1,0:T(8,128)(2,1)S(1)} %collective-permute-done.10.refs_0_), channel_id=1, source_target_pairs={{0,2},{1,5},{2,0},{3,7},{4,6},{5,1},{6,4},{7,3},{8,10},{9,13},{10,... | collective-permute-start | bytes 1277960 | tf_op jit(solution)/shard_map/ppermute | solution.py:369
  109.6 11.9 %collective-permute-start.14 = (bf16[128,1664]{1,0:T(8,128)(2,1)S(1)}, bf16[128,1664]{1,0:T(8,128)(2,1)S(1)}, u32[]{:S(2)}, u32[]{:S(2)}) collective-permute-start(bf16[128,1664]{1,0:T(8,128)(2,1)S(1)} %copy-done.27), channel_id=1, source_target_pairs={{0,24},{1,25},{2,26},{3,27},{4,28},{5,29},{6,30},{7,31},{8,16},{9,... | collective-permute-start | bytes 1277960 | tf_op jit(solution)/shard_map/ppermute | solution.py:472
  123.2 11.7 %collective-permute-start.15 = (bf16[1536,1024]{1,0:T(8,128)(2,1)S(1)}, bf16[1536,1024]{1,0:T(8,128)(2,1)}, u32[]{:S(2)}, u32[]{:S(2)}) collective-permute-start(bf16[1536,1024]{1,0:T(8,128)(2,1)S(1)} %bitcast.44), channel_id=1, source_target_pairs={{0,1},{1,0},{2,3},{3,2},{4,5},{5,4},{6,7},{7,6},{8,9},{9,8},{10,11... | collective-permute-start | bytes 9437192 | tf_op jit(solution)/shard_map/ppermute | solution.py:369
  123.2 46.6 %all-to-all-start.1 = ((bf16[4,384,512]{2,1,0:T(8,128)(2,1)}), bf16[4,384,512]{2,1,0:T(8,128)(2,1)}, u32[]{:S(2)}, u32[]{:S(2)}) async-start(bf16[4,384,512]{2,1,0:T(8,128)(2,1)} %pack.3), calls=%async_computation.1 | async-start | bytes 3145728 | tf_op jit(solution)/shard_map/all_to_all | solution.py:385
  131.3 12.9 %collective-permute-start.18 = (bf16[128,1664]{1,0:T(8,128)(2,1)}, bf16[128,1664]{1,0:T(8,128)(2,1)}, u32[]{:S(2)}, u32[]{:S(2)}) collective-permute-start(bf16[128,1664]{1,0:T(8,128)(2,1)} %copy-done.24), channel_id=1, source_target_pairs={{0,2},{1,5},{2,0},{3,7},{4,6},{5,1},{6,4},{7,3},{8,10},{9,13},{10,... | collective-permute-start | bytes 1277960 | tf_op jit(solution)/shard_map/ppermute | solution.py:369
  132.9 18.3 %collective-permute-start.17 = (bf16[256,1664]{1,0:T(8,128)(2,1)}, bf16[256,1664]{1,0:T(8,128)(2,1)S(1)}, u32[]{:S(2)}, u32[]{:S(2)}) collective-permute-start(bf16[256,1664]{1,0:T(8,128)(2,1)} %copy-done.4), channel_id=1, source_target_pairs={{0,4},{1,3},{2,6},{3,1},{4,0},{5,7},{6,2},{7,5},{8,12},{9,11},{10,... | collective-permute-start | bytes 2555912 | tf_op jit(solution)/shard_map/ppermute | solution.py:369
  133.4 24.3 %collective-permute-start.16 = (bf16[256,1664]{1,0:T(8,128)(2,1)}, bf16[256,1664]{1,0:T(8,128)(2,1)S(1)}, u32[]{:S(2)}, u32[]{:S(2)}) collective-permute-start(bf16[256,1664]{1,0:T(8,128)(2,1)} %copy-done), channel_id=1, source_target_pairs={{0,4},{1,3},{2,6},{3,1},{4,0},{5,7},{6,2},{7,5},{8,12},{9,11},{10,... | collective-permute-start | bytes 2555912 | tf_op jit(solution)/shard_map/ppermute | solution.py:369
  137.2 7.0 %copy-start.25 = (bf16[128,1664]{1,0:T(8,128)(2,1)S(1)}, bf16[128,1664]{1,0:T(8,128)(2,1)}, u32[]{:S(2)}) copy-start(bf16[128,1664]{1,0:T(8,128)(2,1)} %copy-done.24) | copy-start | bytes 1277956
  146.2 4.9 %copy-start.5 = (bf16[256,1664]{1,0:T(8,128)(2,1)S(1)}, bf16[256,1664]{1,0:T(8,128)(2,1)}, u32[]{:S(2)}) copy-start(bf16[256,1664]{1,0:T(8,128)(2,1)} %copy-done.4) | copy-start | bytes 2555908
  146.2 23.5 %collective-permute-start.19 = (bf16[256,1664]{1,0:T(8,128)(2,1)}, bf16[256,1664]{1,0:T(8,128)(2,1)}, u32[]{:S(2)}, u32[]{:S(2)}) collective-permute-start(bf16[256,1664]{1,0:T(8,128)(2,1)} %stack.163.refs_0_), channel_id=1, source_target_pairs={{0,4},{1,3},{2,6},{3,1},{4,0},{5,7},{6,2},{7,5},{8,12},{9,11},{10,... | collective-permute-start | bytes 2555912 | tf_op jit(solution)/shard_map/ppermute | solution.py:369
  151.2 6.6 %copy-start.1 = (bf16[256,1664]{1,0:T(8,128)(2,1)S(1)}, bf16[256,1664]{1,0:T(8,128)(2,1)}, u32[]{:S(2)}) copy-start(bf16[256,1664]{1,0:T(8,128)(2,1)} %copy-done) | copy-start | bytes 2555908
  169.8 5.0 %collective-permute-start.20 = (bf16[1536,512]{1,0:T(8,128)(2,1)}, bf16[1536,512]{1,0:T(8,128)(2,1)S(1)}, u32[]{:S(2)}, u32[]{:S(2)}) collective-permute-start(bf16[1536,512]{1,0:T(8,128)(2,1)} %bitcast.36.mine_ref), channel_id=1, source_target_pairs={{0,1},{1,0},{2,3},{3,2},{4,5},{5,4},{6,7},{7,6},{8,9},{9,8},{10,11... | collective-permute-start | bytes 4718600 | tf_op jit(solution)/shard_map/ppermute | solution.py:369
  177.5 12.1 %collective-permute-start.22 = (bf16[256,1536]{1,0:T(8,128)(2,1)S(1)}, bf16[256,1536]{1,0:T(8,128)(2,1)S(1)}, u32[]{:S(2)}, u32[]{:S(2)}) collective-permute-start(bf16[256,1536]{1,0:T(8,128)(2,1)S(1)} %down.5.rest_0_), channel_id=1, source_target_pairs={{0,4},{1,3},{2,6},{3,1},{4,0},{5,7},{6,2},{7,5},{8,12},{9,11},{10,... | collective-permute-start | bytes 2359304 | tf_op jit(solution)/shard_map/ppermute | solution.py:369
  183.9 7.3 %copy-start.9 = (bf16[512,1024]{1,0:T(8,128)(2,1)S(1)}, bf16[512,1024]{1,0:T(8,128)(2,1)}, u32[]{:S(2)}) copy-start(bf16[512,1024]{1,0:T(8,128)(2,1)} %copy-done.8) | copy-start | bytes 3145732
  183.9 7.3 %copy-start.13 = (f32[512,128]{1,0:T(8,128)S(1)}, f32[512,128]{1,0:T(8,128)}, u32[]{:S(2)}) copy-start(f32[512,128]{1,0:T(8,128)} %copy-done.12) | copy-start | bytes 786436
  184.0 18.2 %collective-permute-start.21 = (bf16[256,1536]{1,0:T(8,128)(2,1)S(1)}, bf16[256,1536]{1,0:T(8,128)(2,1)S(1)}, u32[]{:S(2)}, u32[]{:S(2)}) collective-permute-start(bf16[256,1536]{1,0:T(8,128)(2,1)S(1)} %get-tuple-element.64), channel_id=1, source_target_pairs={{0,4},{1,3},{2,6},{3,1},{4,0},{5,7},{6,2},{7,5},{8,12},{9,11},{10,... | collective-permute-start | bytes 2359304 | tf_op jit(solution)/shard_map/ppermute | solution.py:369
  189.7 12.1 %collective-permute-start.23 = (bf16[128,1536]{1,0:T(8,128)(2,1)S(1)}, bf16[128,1536]{1,0:T(8,128)(2,1)S(1)}, u32[]{:S(2)}, u32[]{:S(2)}) collective-permute-start(bf16[128,1536]{1,0:T(8,128)(2,1)S(1)} %get-tuple-element.66.rest_0_), channel_id=1, source_target_pairs={{0,2},{1,5},{2,0},{3,7},{4,6},{5,1},{6,4},{7,3},{8,10},{9,13},{10,... | collective-permute-start | bytes 1179656 | tf_op jit(solution)/shard_map/ppermute | solution.py:369
  194.6 20.3 %collective-permute-start.25 = (bf16[256,1536]{1,0:T(8,128)(2,1)S(1)}, bf16[256,1536]{1,0:T(8,128)(2,1)S(1)}, u32[]{:S(2)}, u32[]{:S(2)}) collective-permute-start(bf16[256,1536]{1,0:T(8,128)(2,1)S(1)} %get-tuple-element.72), channel_id=1, source_target_pairs={{0,4},{1,3},{2,6},{3,1},{4,0},{5,7},{6,2},{7,5},{8,12},{9,11},{10,... | collective-permute-start | bytes 2359304 | tf_op jit(solution)/shard_map/ppermute | solution.py:369
  202.4 12.1 %collective-permute-start.26 = (bf16[128,1536]{1,0:T(8,128)(2,1)S(1)}, bf16[128,1536]{1,0:T(8,128)(2,1)S(1)}, u32[]{:S(2)}, u32[]{:S(2)}) collective-permute-start(bf16[128,1536]{1,0:T(8,128)(2,1)S(1)} %get-tuple-element.69.rest_0_), channel_id=1, source_target_pairs={{0,2},{1,5},{2,0},{3,7},{4,6},{5,1},{6,4},{7,3},{8,10},{9,13},{10,... | collective-permute-start | bytes 1179656 | tf_op jit(solution)/shard_map/ppermute | solution.py:369
  203.9 10.6 %collective-permute-start.27 = (bf16[128,1536]{1,0:T(8,128)(2,1)S(1)}, bf16[128,1536]{1,0:T(8,128)(2,1)S(1)}, u32[]{:S(2)}, u32[]{:S(2)}) collective-permute-start(bf16[128,1536]{1,0:T(8,128)(2,1)S(1)} %close.3.rest_0_), channel_id=1, source_target_pairs={{0,8},{8,0},{16,24},{24,16},{1,9},{9,1},{17,25},{25,17},{2,10},{10... | collective-permute-start | bytes 1179656 | tf_op jit(solution)/shard_map/ppermute | solution.py:369
  207.2 20.3 %collective-permute-start.24 = (bf16[256,1536]{1,0:T(8,128)(2,1)S(1)}, bf16[256,1536]{1,0:T(8,128)(2,1)S(1)}, u32[]{:S(2)}, u32[]{:S(2)}) collective-permute-start(bf16[256,1536]{1,0:T(8,128)(2,1)S(1)} %get-tuple-element.71), channel_id=1, source_target_pairs={{0,4},{1,3},{2,6},{3,1},{4,0},{5,7},{6,2},{7,5},{8,12},{9,11},{10,... | collective-permute-start | bytes 2359304 | tf_op jit(solution)/shard_map/ppermute | solution.py:369
  215.0 12.0 %collective-permute-start.28 = (bf16[128,1536]{1,0:T(8,128)(2,1)S(1)}, bf16[128,1536]{1,0:T(8,128)(2,1)S(1)}, u32[]{:S(2)}, u32[]{:S(2)}) collective-permute-start(bf16[128,1536]{1,0:T(8,128)(2,1)S(1)} %get-tuple-element.75.rest_1_), channel_id=1, source_target_pairs={{0,2},{1,5},{2,0},{3,7},{4,6},{5,1},{6,4},{7,3},{8,10},{9,13},{10,... | collective-permute-start | bytes 1179656 | tf_op jit(solution)/shard_map/ppermute | solution.py:369
  216.5 12.6 %collective-permute-start.31 = (bf16[128,1536]{1,0:T(8,128)(2,1)S(1)}, bf16[128,1536]{1,0:T(8,128)(2,1)S(1)}, u32[]{:S(2)}, u32[]{:S(2)}) collective-permute-start(bf16[128,1536]{1,0:T(8,128)(2,1)S(1)} %close.4.rest_0_), channel_id=1, source_target_pairs={{0,16},{1,9},{2,18},{3,11},{4,20},{5,13},{6,22},{7,15},{8,24},{9,1... | collective-permute-start | bytes 1179656 | tf_op jit(solution)/shard_map/ppermute | solution.py:472
  227.1 13.9 %copy-start.21 = (f32[128,1536]{1,0:T(8,128)S(1)}, f32[128,1536]{1,0:T(8,128)}, u32[]{:S(2)}) copy-start(f32[128,1536]{1,0:T(8,128)} %get-tuple-element.49.stream_ref) | copy-start | bytes 2359300
  227.6 7.8 %collective-permute-start.29 = (bf16[128,1536]{1,0:T(8,128)(2,1)S(1)}, bf16[128,1536]{1,0:T(8,128)(2,1)S(1)}, u32[]{:S(2)}, u32[]{:S(2)}) collective-permute-start(bf16[128,1536]{1,0:T(8,128)(2,1)S(1)} %get-tuple-element.77), channel_id=1, source_target_pairs={{0,2},{1,5},{2,0},{3,7},{4,6},{5,1},{6,4},{7,3},{8,10},{9,13},{10,... | collective-permute-start | bytes 1179656 | tf_op jit(solution)/shard_map/ppermute | solution.py:369
  229.2 11.9 %collective-permute-start.30 = (bf16[128,1536]{1,0:T(8,128)(2,1)S(1)}, bf16[128,1536]{1,0:T(8,128)(2,1)S(1)}, u32[]{:S(2)}, u32[]{:S(2)}) collective-permute-start(bf16[128,1536]{1,0:T(8,128)(2,1)S(1)} %close.5.rest_0_), channel_id=1, source_target_pairs={{0,8},{1,17},{2,10},{3,19},{4,12},{5,21},{6,14},{7,23},{8,0},{9,25... | collective-permute-start | bytes 1179656 | tf_op jit(solution)/shard_map/ppermute | solution.py:472
  (20 other events, 25.8 us)
